TPU v7x, 32 devices: a whole 2x2x4 slice. The times are simulated.
32 devices in a mesh: groups: 2 (over y), expert: 4 (over z), proj: 4 (over x, core).
Axes of the slice: x: 2, y: 2, z: 4, core: 2. Of those that a mesh axis runs over, the one named last changes fastest.
Arguments:
- activations: bfloat16 [4096, 7168], P(('groups', 'expert'), 'proj'), parts along dimension 0, may hold values from -6 to 6
- grad_hidden: bfloat16 [4096, 8, 2048], P(('groups', 'expert'), None, 'proj'), parts along dimension 0, may hold values from -6 to 6
- routes: int32 [4096, 8], P(('groups', 'expert')), parts along dimension 0, may hold values from 0 to 31, all different within a row; in each aligned block of 512 rows (0 to 511, 512 to 1023, ...) at most 256 rows name the same one
- doc_ids: int32 [4096], P(('groups', 'expert')), parts along dimension 0, may hold values from 0 to 31, never falling along the last dimension, each value on 1 to 256 neighbouring positions
- query_grads: bfloat16 [256, 32, 4096], P(None, 'expert', 'proj'), may hold values from -0.009765625 to 0.009765625
- in_projection: bfloat16 [64, 7168], P(None, 'proj'), may hold values from -0.0625 to 0.0625
- out_projection: bfloat16 [64, 2048], P(None, 'proj'), may hold values from -0.125 to 0.125
- inverse_in: float32 [32, 64, 64], P('expert'), may hold values from -1 to 3, as said below
- inverse_out: float32 [32, 64, 64], P('expert'), may hold values from -1 to 3, as said below
Outputs:
- scores: float32 [256, 64], P('proj', ('groups', 'expert')), parts along dimension 1
There are 2 independent parts, one for each index of `groups`. A program takes and returns all parts, laid end to end along the dimension named above; an argument that names none is the same for every part. Nothing has to cross between parts.
Inputs may be any that keep to these rules, and one draw needn't show every extreme that they name: `routes`: each token names 8 different experts. In each aligned block of 512 tokens (the tokens of one device) no expert is named by more than 256 tokens, a bound that some block reaches. `doc_ids`: never falls along the tokens; each of the 32 documents has 1 to 256 tokens, one exactly 256. `inverse_in`: each matrix is symmetric. `inverse_out`: each matrix is symmetric.
All inputs are finite; a program needn't handle non-finite values.
Results may differ from a plain program's by a relative error of at most 0.0065.
Values may be sent and summed in bfloat16 or wider, within the bound.
No kernel may reach another device: no remote copies, remote signals or barrier semaphores. Data moves between devices by JAX's collectives and lax.ppermute only.
A program may use at most 64 MiB of HBM per device.

v0:
```python
import jax
import jax.numpy as jnp
from jax import lax
from jax.sharding import PartitionSpec as P

DOC_DEV = 8


PRECISE = lax.Precision.HIGHEST


def local(
    activations,
    grad_hidden,
    routes,
    doc_ids,
    query_grads,
    in_projection,
    out_projection,
    inverse_in,
    inverse_out,
):
    tok_rows, per_token = routes.shape
    local_experts = inverse_in.shape[0]
    expert_devices = lax.axis_size("expert")
    proj_devices = lax.axis_size("proj")
    total_experts = local_experts * expert_devices
    in_width = in_projection.shape[0]
    out_width = out_projection.shape[0]
    capacity = 2 * tok_rows * per_token // total_experts
    doc_count = DOC_DEV * expert_devices
    share_rows = out_width // proj_devices
    partial_in = lax.dot_general(
        activations, in_projection, (((1,), (1,)), ((), ())), preferred_element_type=jnp.float32
    )
    flat_hidden = grad_hidden.reshape(tok_rows * per_token, grad_hidden.shape[2])
    partial_out = lax.dot_general(
        flat_hidden, out_projection, (((1,), (1,)), ((), ())), preferred_element_type=jnp.float32
    )
    summed_in, summed_out = lax.psum((partial_in, partial_out), "proj")
    rows_in = jnp.repeat(summed_in.astype(jnp.bfloat16), per_token, axis=0)
    payload = jnp.concatenate([rows_in, summed_out.astype(jnp.bfloat16)], axis=1)
    expert_flat = routes.reshape(-1)
    expert_ids = jnp.arange(total_experts, dtype=jnp.int32)
    route_marks = (expert_flat[:, None] == expert_ids[None, :]).astype(jnp.int32)
    slot_rank = jnp.sum(jnp.cumsum(route_marks, axis=0) * route_marks, axis=1) - 1
    owner_device = expert_flat // local_experts
    local_expert = expert_flat % local_experts
    slot_index = (local_expert * expert_devices + owner_device) * capacity + slot_rank
    slot_total = local_experts * expert_devices * capacity
    outgoing = jnp.zeros((slot_total, payload.shape[1]), jnp.bfloat16).at[slot_index].set(payload)
    outgoing_docs = (
        jnp.zeros((slot_total,), jnp.int32).at[slot_index].set(jnp.repeat(doc_ids, per_token))
    )
    outgoing = outgoing.reshape(local_experts, expert_devices, capacity, payload.shape[1])
    outgoing_docs = outgoing_docs.reshape(local_experts, expert_devices, capacity)
    arrived, arrived_docs = (
        lax.all_to_all(outgoing, "expert", split_axis=1, concat_axis=1, tiled=True),
        lax.all_to_all(outgoing_docs, "expert", split_axis=1, concat_axis=1, tiled=True),
    )
    slots_in = arrived[..., :in_width]
    slots_out = arrived[..., in_width:]
    out_rows = lax.dynamic_slice_in_dim(
        inverse_out, lax.axis_index("proj") * share_rows, share_rows, 1
    )
    doc_range = jnp.arange(doc_count, dtype=jnp.int32)

    def expert_scores(expert_index, running_total):

        def select(source):
            return lax.dynamic_index_in_dim(source, expert_index, 0, keepdims=False)

        slot_in = select(slots_in).reshape(-1, in_width)
        slot_out = select(slots_out).reshape(-1, out_width)
        slot_docs = select(arrived_docs).reshape(-1)
        slot_count = slot_in.shape[0]
        conditioned_in = jnp.dot(
            slot_in.astype(jnp.float32), select(inverse_in), precision=PRECISE
        ).astype(jnp.bfloat16)
        conditioned_out = jnp.dot(
            slot_out.astype(jnp.float32), select(out_rows).T, precision=PRECISE
        ).astype(jnp.bfloat16)
        doc_table = (slot_docs[:, None] == doc_range[None, :]).astype(jnp.bfloat16)
        doc_weighted = (doc_table[:, :, None] * conditioned_out[:, None, :]).reshape(
            slot_count, doc_count * share_rows
        )
        example_grads = lax.dot_general(
            doc_weighted,
            conditioned_in,
            (((0,), (0,)), ((), ())),
            preferred_element_type=jnp.float32,
        )
        example_grads = example_grads.astype(jnp.bfloat16).reshape(doc_count, share_rows * in_width)
        queries = lax.dynamic_index_in_dim(query_grads, expert_index, 1, keepdims=False)
        return running_total + lax.dot_general(
            queries, example_grads, (((1,), (1,)), ((), ())), preferred_element_type=jnp.float32
        )

    partial_value = lax.fori_loop(
        0, local_experts, expert_scores, jnp.zeros((query_grads.shape[0], doc_count), jnp.float32)
    )
    by_rows = lax.psum_scatter(partial_value, "proj", scatter_dimension=0, tiled=True)
    scores = lax.psum_scatter(by_rows, "expert", scatter_dimension=1, tiled=True)
    return scores


def solution(mesh):
    in_specs = (
        P(("groups", "expert"), "proj"),
        P(("groups", "expert"), None, "proj"),
        P(("groups", "expert"), None),
        P(("groups", "expert")),
        P(None, "expert", "proj"),
        P(None, "proj"),
        P(None, "proj"),
        P("expert", None, None),
        P("expert", None, None),
    )
    out_specs = P("proj", ("groups", "expert"))
    return jax.shard_map(local, mesh=mesh, in_specs=in_specs, out_specs=out_specs, check_vma=False)
```

profile of v0, /device:TPU:0, one launch (start us, length us, event | category | flops | bytes accessed | tf_op | source)
XLA Modules:
  0.0 221.1 jit_solution(772390349376666197)
XLA Ops:
  6.5 1.0 copy.32
  8.1 1.6 fusion.24
  9.7 9.2 %reduce-window.6 = s32[32,32,128]{2,1,0:T(8,128)S(1)} reduce-window(s32[32,32,128]{2,1,0:T(8,128)S(1)} %fusion.18, s32[]{:T(128)} %constant.83.clone.1), window={size=1x1x128 pad=0_0x0_0x127_0}, to_apply=%region_0.0 | reduce-window | flops 16646144 | bytes 1048580 | tf_op jit(solution)/shard_map/reduce-window
  19.0 0.8 slice_reduce_fusion
  20.5 3.6 %fusion.12 = f32[4096,64]{0,1:T(8,128)S(1)} fusion(bf16[64,512]{1,0:T(8,128)(2,1)S(1)} %copy-done.1, bf16[512,8,512]{2,1,0:T(8,128)(2,1)} %param.12), kind=kOutput, calls=%fused_computation.22 | convolution fusion | flops 268435456 | bytes 5308416 | tf_op jit(solution)/shard_map/dot_general | solution.py:37
  24.1 28.9 %all-reduce.3 = (bf16[4096,64]{0,1:T(8,128)(2,1)}, bf16[512,64]{0,1:T(8,128)(2,1)S(1)}) all-reduce(f32[4096,64]{0,1:T(8,128)S(1)} %fusion.12, f32[512,64]{0,1:T(8,128)S(1)} %fusion.24), channel_id=1, replica_groups=mesh['groups'=2,'expert'=4,'proj'=4] {'proj'}, use_global_device_ids=true, to_apply=%region_4.5 | all-reduce | flops 294912 | bytes 1769472 | tf_op jit(solution)/shard_map/psum | solution.py:40
  53.6 1.1 pad_maximum_fusion
  54.7 1.3 copy.38
  56.2 12.8 %scatter_custom_fusion.1 = bf16[8192,128]{1,0:T(8,128)(2,1)} fusion(s32[4096]{0:T(1024)S(1)} %bitcast.83, bf16[4096,128]{1,0:T(8,128)(2,1)} %copy.38, bf16[]{:T(256)} %constant.85.clone.1), kind=kCustom, calls=%fused_computation.25 | custom fusion | bytes 2097664 | tf_op jit(solution)/shard_map/scatter | solution.py:51
  69.0 3.1 %copy.39 = bf16[8,4,256,128]{3,2,0,1:T(8,128)(2,1)} copy(bf16[8,4,256,128]{3,2,1,0:T(8,128)(2,1)} %bitcast.78) | data formatting | bytes 4194304 | tf_op jit(solution)/shard_map/reshape | solution.py:55
  72.1 5.0 %all-to-all-start.1 = ((bf16[8,4,256,128]{3,2,0,1:T(8,128)(2,1)}), bf16[8,4,256,128]{3,2,0,1:T(8,128)(2,1)}, u32[]{:S(2)}, u32[]{:S(2)}) async-start(bf16[8,4,256,128]{3,2,0,1:T(8,128)(2,1)} %copy.39), calls=%async_computation.1 | async-start | bytes 4194304 | tf_op jit(solution)/shard_map/all_to_all | solution.py:58
  77.4 15.5 %scatter_custom_fusion = s32[8192]{0:T(1024)S(1)} fusion(s32[4096]{0:T(1024)S(1)} %bitcast.84, s32[4096]{0:T(1024)S(1)} %reshape.242, s32[]{:T(128)} %constant.83.clone.1), kind=kCustom, calls=%fused_computation.44 | custom fusion | bytes 32772 | tf_op jit(solution)/shard_map/scatter | solution.py:53
  93.0 0.6 copy.35
  93.6 6.4 %copy.40 = bf16[256,8,1024]{2,0,1:T(8,128)(2,1)} copy(bf16[256,8,1024]{2,1,0:T(8,128)(2,1)} %param.15) | data formatting | bytes 8388608
  100.0 0.8 constant_dynamic-slice_fusion.4
  100.9 24.9 %all-to-all-done.1 = bf16[8,4,256,128]{3,2,0,1:T(8,128)(2,1)} async-done(((bf16[8,4,256,128]{3,2,0,1:T(8,128)(2,1)}), bf16[8,4,256,128]{3,2,0,1:T(8,128)(2,1)}, u32[]{:S(2)}, u32[]{:S(2)}) %all-to-all-start.1) | async-done | bytes 2097184 | tf_op jit(solution)/shard_map/all_to_all | solution.py:58
  125.8 3.3 %all-to-all-start = ((s32[8,4,256]{2,0,1:T(8,128)}), s32[8,4,256]{2,0,1:T(8,128)S(1)}, u32[]{:S(2)}, u32[]{:S(2)}) async-start(s32[8,4,256]{2,0,1:T(8,128)} %copy.35), calls=%async_computation | async-start | bytes 65536 | tf_op jit(solution)/shard_map/all_to_all | solution.py:59
  129.1 5.1 %fusion.23 = (bf16[8,4,256,64]{3,2,0,1:T(8,128)(2,1)}, bf16[8,4,256,64]{3,2,0,1:T(8,128)(2,1)}) fusion(bf16[8,4,256,128]{3,2,0,1:T(8,128)(2,1)} %all-to-all-done.1), kind=kLoop, calls=%fused_computation.49 | loop fusion | bytes 4194304 | tf_op jit(solution)/shard_map/slice | solution.py:61
  134.7 38.4 %while.14 = (s32[]{:T(128)}, f32[256,32]{0,1:T(8,128)S(1)}, bf16[256,8,1024]{2,0,1:T(8,128)(2,1)}, s32[8,4,256]{2,0,1:T(8,128)S(1)}, bf16[8,4,256,64]{3,2,0,1:T(...) while((s32[]{:T(128)}, f32[256,32]{0,1:T(8,128)S(1)}, ...), condition=%wide.region_8.9_spmd.clone, body=%wide.region_7.8_spmd.clone.sunk | while | flops 147521536 | bytes 4509835 | solution.py:99
  134.7 1.1 constant_dynamic-slice_fusion.7
  136.1 1.2 convolution_convert_fusion.7
  138.2 1.3 convolution_add_fusion.2
  139.5 1.1 constant_dynamic-slice_fusion.7
  140.9 1.2 convolution_convert_fusion.7
  143.0 1.3 convolution_add_fusion.2
  144.3 1.1 constant_dynamic-slice_fusion.7
  145.7 1.2 convolution_convert_fusion.7
  147.8 1.3 convolution_add_fusion.2
  149.1 1.1 constant_dynamic-slice_fusion.7
  150.5 1.2 convolution_convert_fusion.7
  152.6 1.3 convolution_add_fusion.2
  153.9 1.1 constant_dynamic-slice_fusion.7
  155.3 1.2 convolution_convert_fusion.7
  157.4 1.3 convolution_add_fusion.2
  158.7 1.1 constant_dynamic-slice_fusion.7
  160.1 1.2 convolution_convert_fusion.7
  162.2 1.3 convolution_add_fusion.2
  163.5 1.1 constant_dynamic-slice_fusion.7
  164.9 1.2 convolution_convert_fusion.7
  167.0 1.3 convolution_add_fusion.2
  168.3 1.1 constant_dynamic-slice_fusion.7
  169.7 1.2 convolution_convert_fusion.7
  171.8 1.3 convolution_add_fusion.2
  173.1 0.7 copy.44
  175.1 19.0 %reduce-scatter.4.cloned.1.call-done = f32[64,32]{1,0:T(8,128)} async-done(((f32[256,32]{1,0:T(8,128)}), f32[64,32]{1,0:T(8,128)}) %reduce-scatter.4.cloned.1.call-update) | async-done | bytes 8208
  194.1 0.8 copy.45
  195.0 18.7 %all-reduce = f32[64,32]{0,1:T(8,128)S(1)} all-reduce(f32[64,32]{0,1:T(8,128)S(1)} %copy.45), channel_id=3, replica_groups=mesh['groups'=2,'expert'=4,'proj'=4] {'expert'}, use_global_device_ids=true, to_apply=%region_10.11.clone | all-reduce | flops 2048 | bytes 16384
  213.7 0.6 constant_dynamic-slice_fusion.3
  (84 shorter events, 12.5 us)
Async XLA Ops:
  6.5 1.5 copy-start
  9.7 10.8 %copy-start.1 = (bf16[64,512]{1,0:T(8,128)(2,1)S(1)}, bf16[64,512]{1,0:T(8,128)(2,1)}, u32[]{:S(2)}) copy-start(bf16[64,512]{1,0:T(8,128)(2,1)} %param.17) | copy-start | bytes 196612
  72.1 5.0 %copy-start.2 = (s32[512]{0:T(512)S(1)}, s32[512]{0:T(512)}, u32[]{:S(2)}) copy-start(s32[512]{0:T(512)} %param.14) | copy-start | bytes 6148
  72.1 53.7 %all-to-all-start.1 = ((bf16[8,4,256,128]{3,2,0,1:T(8,128)(2,1)}), bf16[8,4,256,128]{3,2,0,1:T(8,128)(2,1)}, u32[]{:S(2)}, u32[]{:S(2)}) async-start(bf16[8,4,256,128]{3,2,0,1:T(8,128)(2,1)} %copy.39), calls=%async_computation.1 | async-start | bytes 4194304 | tf_op jit(solution)/shard_map/all_to_all | solution.py:58
  125.8 8.9 %all-to-all-start = ((s32[8,4,256]{2,0,1:T(8,128)}), s32[8,4,256]{2,0,1:T(8,128)S(1)}, u32[]{:S(2)}, u32[]{:S(2)}) async-start(s32[8,4,256]{2,0,1:T(8,128)} %copy.35), calls=%async_computation | async-start | bytes 65536 | tf_op jit(solution)/shard_map/all_to_all | solution.py:59
  129.1 65.0 %reduce-scatter.4.cloned.1.call-start = ((), (), s32[]{:S(2)}) async-start(), calls=%async_computation.3 | async-start | bytes 163840
  134.7 39.2 %copy-start.3 = (u32[32]{0:T(128)S(1)}, u32[32]{0:T(128)}, u32[]{:S(2)}) copy-start(u32[32]{0:T(128)} %constant.99) | copy-start | bytes 388
Sparse Core Ops, SparseCore 0:
  174.0 20.1 reduce-scatter.3
where the time goes:
time: 223 us; the launch traced here: 221 us
  local copies, waits for them, and re-layouts  62.5 us (28%)
  blocking collectives  47.6 us (21%)
  waiting for transfers between devices  44.5 us (20%)
  matrix products  31.3 us (14%)
  between operations  14.2 us (6%)
  other arithmetic  12.1 us (5%)
  starting transfers between devices  8.31 us (4%)
    psum x1, blocking collectives, local(): summed_in, summed_out = lax.psum((partial_in, partial_out), 'proj')  28.9 us
    all_to_all x1, waiting for transfers between devices, local(): lax.all_to_all(outgoing, 'expert', split_axis=1, concat_axis=1, tiled=True)  24.9 us
    unnamed x2, waiting for transfers between devices  19 us
    unnamed x1, blocking collectives  18.7 us
    scatter x1, local copies, waits for them, and re-layouts, local(): jnp.zeros((slot_total,), jnp.int32).at[slot_index]  15.5 us
    scatter x1, local copies, waits for them, and re-layouts, local(): jnp.zeros((slot_total, payload.shape[1]), jnp.bfloat16).at[slot_index]  12.8 us
    dot_general x8, matrix products, expert_scores(): lax.dot_general(queries, example_grads, (((1,), (1,)), ((), ())), preferr...  10.5 us
    unnamed x14, local copies, waits for them, and re-layouts  10.2 us
  transfers between devices with their start and end apart: 3, of which 3 were waited for; matrix products, arithmetic and copies ran while one was open for 13% of the time, Pallas kernels for 0%

commit v1 on v0

v1 whole, which is shorter than its diff:
```python
import functools

import jax
import jax.numpy as jnp
from jax import lax
from jax.experimental import pallas as pl
from jax.experimental.pallas import tpu as pltpu
from jax.sharding import PartitionSpec as P

DOC_DEV = 8
VMEM_BYTES = 48 * 1024 * 1024


def half_lanes(shape, width):
    return lax.broadcasted_iota(jnp.int32, shape, len(shape) - 1) < width


def project_kernel(act_ref, hidden_ref, in_proj_ref, out_proj_ref, wire_ref, rows_ref, *, top):
    quarter = act_ref.shape[0]
    width = in_proj_ref.shape[0]
    twice = jnp.concatenate([out_proj_ref[...], out_proj_ref[...]], axis=0)
    rows_ref[...] = lax.dot_general(
        hidden_ref[...], twice, (((1,), (1,)), ((), ())), preferred_element_type=jnp.float32
    )
    first = half_lanes((quarter, 2 * width), width)
    for pair in range(top // 2):
        even = rows_ref[pl.ds(2 * pair, quarter, stride=top), :]
        odd = rows_ref[pl.ds(2 * pair + 1, quarter, stride=top), :]
        wire_ref[0, pair * quarter : (pair + 1) * quarter, :] = jnp.where(first, even, odd).astype(jnp.bfloat16)
    twice_in = jnp.concatenate([in_proj_ref[...], in_proj_ref[...]], axis=0)
    inner = lax.dot_general(
        act_ref[...], twice_in, (((1,), (1,)), ((), ())), preferred_element_type=jnp.float32
    )
    half = quarter // 2
    wire_ref[0, top // 2 * quarter :, :] = jnp.where(
        half_lanes((half, 2 * width), width), inner[:half], inner[half:]
    ).astype(jnp.bfloat16)


def project(activations, flat_hidden, in_projection, out_projection, quarters, top):
    tokens, model = activations.shape
    width = in_projection.shape[0]
    quarter = tokens // quarters
    wire_rows = top // 2 * quarter + quarter // 2
    return pl.pallas_call(
        functools.partial(project_kernel, top=top),
        grid=(quarters,),
        in_specs=[
            pl.BlockSpec((quarter, model), lambda q: (q, 0)),
            pl.BlockSpec((quarter * top, flat_hidden.shape[1]), lambda q: (q, 0)),
            pl.BlockSpec(in_projection.shape, lambda q: (0, 0)),
            pl.BlockSpec(out_projection.shape, lambda q: (0, 0)),
        ],
        out_specs=pl.BlockSpec((1, wire_rows, 2 * width), lambda q: (q, 0, 0)),
        out_shape=jax.ShapeDtypeStruct((quarters, wire_rows, 2 * width), jnp.bfloat16),
        scratch_shapes=[pltpu.VMEM((quarter * top, 2 * width), jnp.float32)],
        compiler_params=pltpu.CompilerParams(vmem_limit_bytes=VMEM_BYTES),
    )(activations, flat_hidden, in_projection, out_projection)


def condition_kernel(parts_ref, routes_ref, weights_ref, payload_ref, value_ref, name_ref, *, top, width):
    quarter = routes_ref.shape[0]
    groups, dense_width, _ = weights_ref.shape
    shares = payload_ref.shape[0] // groups
    lanes = 2 * width
    experts = dense_width // width
    first = half_lanes((quarter, lanes), width)
    second = 1 - first.astype(jnp.int32)

    def summed(start, size):
        total = parts_ref[0, start : start + size, :].astype(jnp.float32)
        for source in range(1, parts_ref.shape[0]):
            total = total + parts_ref[source, start : start + size, :].astype(jnp.float32)
        return total

    for pair in range(top // 2):
        both = summed(pair * quarter, quarter)
        swapped = pltpu.roll(both, width, 1)
        value_ref[2 * pair] = jnp.where(first, both, swapped)
        value_ref[2 * pair + 1] = jnp.where(first, swapped, both)
    for k in range(top):
        name_ref[k] = jnp.broadcast_to(routes_ref[:, k : k + 1], (quarter, lanes)) - second
    half = quarter // 2
    inner = summed(top // 2 * quarter, half)
    inner = jnp.concatenate([inner[:, :width], inner[:, width:]], axis=0)
    inner = jnp.transpose(inner).astype(jnp.bfloat16)

    def one_group(group, carry):
        dense = []
        for pair in range(experts // 2):
            base = group * experts + 2 * pair
            chosen = jnp.zeros((quarter, lanes), jnp.float32)
            for k in range(top):
                chosen = jnp.where(name_ref[k] == base, value_ref[k], chosen)
            dense.append(chosen.astype(jnp.bfloat16))
        result = jnp.dot(
            jnp.concatenate(dense, axis=1), weights_ref[group], preferred_element_type=jnp.float32
        ).astype(jnp.bfloat16)
        share_width = result.shape[1] // shares
        for share in range(shares):
            payload_ref[group * shares + share, :quarter, :] = result[:, share * share_width : (share + 1) * share_width]
            payload_ref[group * shares + share, quarter:, :] = inner
        return carry

    lax.fori_loop(0, groups, one_group, 0, unroll=groups <= 4)


def condition(parts, quarter_routes, weights, shares, width):
    quarter, top = quarter_routes.shape
    groups = weights.shape[0]
    lanes = 2 * width
    return pl.pallas_call(
        functools.partial(condition_kernel, top=top, width=width),
        out_shape=jax.ShapeDtypeStruct((groups * shares, quarter + width, lanes), jnp.bfloat16),
        scratch_shapes=[
            pltpu.VMEM((top, quarter, lanes), jnp.float32),
            pltpu.VMEM((top, quarter, lanes), jnp.int32),
        ],
        compiler_params=pltpu.CompilerParams(vmem_limit_bytes=VMEM_BYTES),
    )(parts, quarter_routes, weights)


def score_kernel(arrived_ref, docs_ref, queries_ref, out_ref, grads_ref, *, width, doc_count):
    sources, rows, lanes = arrived_ref.shape
    quarter = rows - width
    outer = arrived_ref[:, :quarter, :].reshape(sources * quarter, lanes)
    inner = jnp.concatenate([arrived_ref[s, quarter:, :] for s in range(sources)], axis=1)
    docs = jnp.concatenate([docs_ref[s : s + 1, :] for s in range(sources)], axis=1)
    docs = jnp.broadcast_to(docs, (width, sources * quarter))
    doc_group = 8

    def one_group(group, carry):
        masked = [
            jnp.where(docs == group * doc_group + d, inner, jnp.zeros_like(inner)) for d in range(doc_group)
        ]
        start = pl.multiple_of(group * doc_group * width, doc_group * width)
        grads_ref[pl.ds(start, doc_group * width), :] = jnp.dot(
            jnp.concatenate(masked, axis=0), outer, preferred_element_type=jnp.float32
        )
        return carry

    lax.fori_loop(0, doc_count // doc_group, one_group, 0, unroll=doc_count <= 32)
    flat = jnp.concatenate(
        [grads_ref[pl.ds(j, doc_count, stride=width), :].astype(jnp.bfloat16) for j in range(width)], axis=1
    )
    result = jnp.dot(flat, queries_ref[...], preferred_element_type=jnp.float32)
    owners, shares, owned, columns = out_ref.shape
    for owner in range(owners):
        for share in range(shares):
            out_ref[owner, share] = result[
                owner * owned : (owner + 1) * owned, share * columns : (share + 1) * columns
            ]


def score(arrived, docs, queries, width, owners, shares):
    doc_count = DOC_DEV * owners
    return pl.pallas_call(
        functools.partial(score_kernel, width=width, doc_count=doc_count),
        out_shape=jax.ShapeDtypeStruct((owners, shares, DOC_DEV, queries.shape[1] // shares), jnp.float32),
        scratch_shapes=[pltpu.VMEM((doc_count * width, arrived.shape[2]), jnp.float32)],
        compiler_params=pltpu.CompilerParams(vmem_limit_bytes=VMEM_BYTES),
    )(arrived, docs, queries)


def local(
    activations,
    grad_hidden,
    routes,
    doc_ids,
    query_grads,
    in_projection,
    out_projection,
    inverse_in,
    inverse_out,
):
    tokens, top = routes.shape
    experts, width, _ = inverse_in.shape
    owners = lax.axis_size("expert")
    shares = lax.axis_size("proj")
    quarter = tokens // shares
    query_count = query_grads.shape[0]
    share_rows = width // shares
    doc_count = DOC_DEV * owners
    assert doc_count <= 256

    half = experts // 2
    factors = inverse_out.astype(jnp.bfloat16)
    factors = jnp.concatenate([factors[:half], factors[half:]], axis=2).reshape(half * width, 2 * width)
    doc_rows = doc_ids.astype(jnp.bfloat16).reshape(tokens // 128, 128)
    shared = jnp.concatenate([factors, jnp.pad(doc_rows, ((0, 16 - tokens // 128), (0, 0)))], axis=0)
    shared = jnp.broadcast_to(shared[None], (owners, *shared.shape))
    shared = lax.all_to_all(shared, "expert", 0, 0, tiled=True)
    all_docs = shared[:, half * width : half * width + tokens // 128, :].astype(jnp.int32)
    all_docs = all_docs.reshape(owners * shares, quarter)
    factors = shared[:, : half * width, :].reshape(owners, half, width, 2, width)
    factors = factors.transpose(0, 3, 1, 2, 4).reshape(owners * experts * width, width)

    column = jnp.arange(experts * width)
    source_row = column // (experts * share_rows) * share_rows + column % share_rows
    place = (jnp.arange(width)[:, None] == source_row[None, :]).astype(jnp.bfloat16)
    own = column[:, None] // width == (column[None, :] // share_rows) % experts
    weights = jnp.dot(factors, place, preferred_element_type=jnp.float32).reshape(owners, experts * width, experts * width)
    weights = jnp.where(own[None], weights, 0).astype(jnp.bfloat16)

    flat_hidden = grad_hidden.reshape(tokens * top, grad_hidden.shape[2])
    wire = project(activations, flat_hidden, in_projection, out_projection, shares, top)
    parts = lax.all_to_all(wire, "proj", 0, 0, tiled=True)
    quarter_routes = lax.dynamic_slice_in_dim(routes, lax.axis_index("proj") * quarter, quarter, 0)
    payload = condition(parts, quarter_routes, weights, shares, width)
    arrived = lax.all_to_all(payload, ("expert", "proj"), 0, 0, tiled=True)

    queries = jnp.einsum(
        "qeil,ejl->jeiq",
        query_grads.reshape(query_count, experts, share_rows, width),
        inverse_in.astype(jnp.bfloat16),
        preferred_element_type=jnp.float32,
    ).astype(jnp.bfloat16).reshape(width * experts * share_rows, query_count)

    partial_scores = score(arrived, all_docs, queries, width, owners, shares)
    pieces = lax.all_to_all(
        partial_scores.reshape(owners * shares, DOC_DEV, query_count // shares), ("expert", "proj"), 0, 0, tiled=True
    )
    return jnp.sum(pieces, axis=0).T


def solution(mesh):
    in_specs = (
        P(("groups", "expert"), "proj"),
        P(("groups", "expert"), None, "proj"),
        P(("groups", "expert"), None),
        P(("groups", "expert")),
        P(None, "expert", "proj"),
        P(None, "proj"),
        P(None, "proj"),
        P("expert", None, None),
        P("expert", None, None),
    )
    out_specs = P("proj", ("groups", "expert"))
    return jax.shard_map(local, mesh=mesh, in_specs=in_specs, out_specs=out_specs, check_vma=False)
```

time: 223 us -> 77.9 us (0.35)
  local copies, waits for them, and re-layouts: 62.5 us -> 19.4 us
  blocking collectives: 47.6 us -> 11.9 us
  waiting for transfers between devices: 44.5 us -> 10.5 us
  matrix products: 31.3 us -> 5.11 us
  between operations: 14.2 us -> 0.14 us
  Pallas kernels: 0 us -> 11 us
  other arithmetic: 12.1 us -> 4.05 us
  starting transfers between devices: 8.31 us -> 15 us
    psum x1 -> x0, blocking collectives: 28.9 us -> none  [local(): summed_in, summed_out = lax.psum((partial_in, partial_out), 'proj')]
    scatter x2 -> x0, local copies, waits for them, and re-layouts: 28.3 us -> none  [the longest x1 15.5 us: local(): jnp.zeros((slot_total,), jnp.int32).at[slot_index]]
    dot_general x34 -> x2, matrix products: 31.3 us -> 5.11 us  [the longest x1 3.42 us: local(): jnp.einsum('qeil,ejl->jeiq', query_grads.reshape(query_count, experts, sh...]
    unnamed x2 -> x0, waiting for transfers between devices: 19 us -> none
    unnamed x1 -> x0, blocking collectives: 18.7 us -> none
    all_to_all x2 -> x3, waiting for transfers between devices: 25.4 us -> 10.5 us  [the longest x1 6.57 us: local(): parts = lax.all_to_all(wire, 'proj', 0, 0, tiled=True)]
    all_to_all x0 -> x1, blocking collectives: none -> 11.9 us  [local(): lax.all_to_all(partial_scores.reshape(owners * shares, DOC_DEV, query_cou...]
    pallas_call x0 -> x3, Pallas kernels: none -> 11 us  [the longest x1 5.08 us: project(): pl.pallas_call(functools.partial(project_kernel, top=top), grid=(quarters...]
  transfers between devices with their start and end apart: 3 -> 3, of which waited for: 3 -> 2; matrix products, arithmetic and copies ran while one was open for 13% -> 24% of each run, Pallas kernels for 0% -> 7%
where the time goes in v1:
time: 77.9 us; the launch traced here: 77.1 us
  local copies, waits for them, and re-layouts  19.4 us (25%)
  starting transfers between devices  15 us (19%)
  blocking collectives  11.9 us (15%)
  Pallas kernels  11 us (14%)
  waiting for transfers between devices  10.5 us (13%)
  matrix products  5.11 us (7%)
  other arithmetic  4.05 us (5%)
    unnamed x16, local copies, waits for them, and re-layouts  12.7 us
    all_to_all x1, blocking collectives, local(): lax.all_to_all(partial_scores.reshape(owners * shares, DOC_DEV, query_cou...  11.9 us
    all_to_all x1, waiting for transfers between devices, local(): parts = lax.all_to_all(wire, 'proj', 0, 0, tiled=True)  6.57 us
    all_to_all x1, starting transfers between devices, local(): shared = lax.all_to_all(shared, 'expert', 0, 0, tiled=True)  6.32 us
    all_to_all x1, starting transfers between devices, local(): arrived = lax.all_to_all(payload, ('expert', 'proj'), 0, 0, tiled=True)  5.19 us
    pallas_call x1, Pallas kernels, project(): pl.pallas_call(functools.partial(project_kernel, top=top), grid=(quarters...  5.08 us
    convert_element_type x1, local copies, waits for them, and re-layouts, local(): queries = jnp.einsum('qeil,ejl->jeiq', query_grads.reshape(query_count, e...  4.35 us
    pallas_call x1, Pallas kernels, score(): pl.pallas_call(functools.partial(score_kernel, width=width, doc_count=doc...  4.05 us
  transfers between devices with their start and end apart: 3, of which 2 were waited for; matrix products, arithmetic and copies ran while one was open for 24% of the time, Pallas kernels for 7%

profile of v1, /device:TPU:0, one launch (start us, length us, event | category | flops | bytes accessed | tf_op | source)
XLA Modules:
  0.0 77.1 jit_solution(8306215982439910719)
XLA Ops:
  0.0 0.0 copy-start
  0.0 1.0 %convert_element_type.24 = bf16[8,64,64]{2,1,0:T(8,128)(2,1)S(1)} convert(f32[8,64,64]{2,1,0:T(8,128)} %param.17) | non-fusion elementwise | flops 32768 | bytes 196608 | tf_op jit(solution)/shard_map/convert_element_type | solution.py:187
  1.0 0.7 convert_bitcast_fusion.1
  1.7 0.1 pad_maximum_fusion
  1.8 0.7 broadcast_in_dim.11
  2.6 6.3 %all-to-all-start.1 = ((bf16[4,272,128]{2,1,0:T(8,128)(2,1)}), bf16[4,272,128]{2,1,0:T(8,128)(2,1)S(1)}, u32[]{:S(2)}, u32[]{:S(2)}) async-start(bf16[4,272,128]{2,1,0:T(8,128)(2,1)} %broadcast_in_dim.11), calls=%async_computation.1 | async-start | bytes 557056 | tf_op jit(solution)/shard_map/all_to_all | solution.py:192
  8.9 0.0 copy-start.2
  8.9 1.5 %copy-done.2 = bf16[512,1792]{1,0:T(8,128)(2,1)S(1)} copy-done((bf16[512,1792]{1,0:T(8,128)(2,1)S(1)}, bf16[512,1792]{1,0:T(8,128)(2,1)}, u32[]{:S(2)}) %copy-start.2) | copy-done | bytes 1835032
  10.4 0.0 copy-start.3
  10.4 0.9 %copy-done.3 = bf16[64,1792]{1,0:T(8,128)(2,1)S(1)} copy-done((bf16[64,1792]{1,0:T(8,128)(2,1)S(1)}, bf16[64,1792]{1,0:T(8,128)(2,1)}, u32[]{:S(2)}) %copy-start.3) | copy-done | bytes 229400
  11.3 0.0 copy-start.4
  11.3 0.8 %copy-done.4 = bf16[64,512]{1,0:T(8,128)(2,1)S(1)} copy-done((bf16[64,512]{1,0:T(8,128)(2,1)S(1)}, bf16[64,512]{1,0:T(8,128)(2,1)}, u32[]{:S(2)}) %copy-start.4) | copy-done | bytes 65560
  12.2 5.1 %shard_map.91 = bf16[4,576,128]{2,1,0:T(8,128)(2,1)} custom-call(bf16[512,1792]{1,0:T(8,128)(2,1)S(1)} %copy-done.2, bf16[4096,512]{1,0:T(8,128)(2,1)} %bitcast.28, bf16[64,1792]{1,0:T(8,128)(2,1)S(1)} %copy-done.3, bf16[64,512]{1,0:T(8,128)(2,1)S(1)} %copy-done.4), custom_call_target="tpu_custom_call" | custom-call | tf_op jit(solution)/shard_map/pallas_call | solution.py:45
  17.2 0.9 %broadcast_compare_fusion = pred[512,512]{1,0:T(8,128)(4,1)} fusion(s32[512]{0:T(512)S(1)} %get-tuple-element.7, s32[512]{0:T(512)S(1)} %get-tuple-element.8), kind=kLoop, calls=%fused_computation.2 | loop fusion | flops 262144 | bytes 266240 | tf_op jit(solution)/shard_map/eq | solution.py:201
  18.2 0.0 all-to-all-done.1
  18.2 3.5 %all-to-all-start = ((bf16[4,576,128]{2,1,0:T(8,128)(2,1)}), bf16[4,576,128]{2,1,0:T(8,128)(2,1)S(1)}, u32[]{:S(2)}, u32[]{:S(2)}) async-start(bf16[4,576,128]{2,1,0:T(8,128)(2,1)} %shard_map.91), calls=%async_computation | async-start | bytes 1179648 | tf_op jit(solution)/shard_map/all_to_all | solution.py:207
  21.6 0.0 copy-done
  21.7 0.1 copy.19.routes_ref
  21.8 0.2 reshape.172
  22.1 0.5 copy.15
  22.6 0.3 dot_general.8
  22.9 1.7 %select_convert_fusion.weights_ref = bf16[4,512,512]{2,1,0:T(8,128)(2,1)S(1)} fusion(bf16[4,512,64]{1,2,0:T(8,128)(2,1)S(1)} %dot_general.8, pred[512,512]{1,0:T(8,128)(4,1)} %broadcast_compare_fusion, s32[512]{0:T(512)S(1)} %fusion.12), kind=kOutput, calls=%fused_computation.1 | convolution fusion | flops 136347648 | bytes 2623488 | tf_op jit(solution)/shard_map/dot_general | solution.py:202
  24.6 6.6 %all-to-all-done.parts_ref = bf16[4,576,128]{2,1,0:T(8,128)(2,1)S(1)} async-done(((bf16[4,576,128]{2,1,0:T(8,128)(2,1)}), bf16[4,576,128]{2,1,0:T(8,128)(2,1)S(1)}, u32[]{:S(2)}, u32[]{:S(2)}) %all-to-all-start) | async-done | bytes 589856 | tf_op jit(solution)/shard_map/all_to_all | solution.py:207
  31.2 1.8 %shard_map.92 = bf16[16,192,128]{2,1,0:T(8,128)(2,1)} custom-call(bf16[4,576,128]{2,1,0:T(8,128)(2,1)S(1)} %all-to-all-done.parts_ref, s32[128,8]{1,0:T(8,128)S(1)} %copy.19.routes_ref, bf16[4,512,512]{2,1,0:T(8,128)(2,1)S(1)} %select_convert_fusion.weights_ref), custom_call_target="tpu_custom_call" | custom-call | tf_op jit(solution)/shard_map/pallas_call | solution.py:112
  33.0 5.2 %all-to-all-start.2 = ((bf16[16,192,128]{2,1,0:T(8,128)(2,1)}), bf16[16,192,128]{2,1,0:T(8,128)(2,1)S(1)}, u32[]{:S(2)}, u32[]{:S(2)}) async-start(bf16[16,192,128]{2,1,0:T(8,128)(2,1)} %shard_map.92), calls=%async_computation.2 | async-start | bytes 1572864 | tf_op jit(solution)/shard_map/all_to_all | solution.py:210
  38.2 0.0 copy-start.5
  38.2 6.9 %copy.16 = bf16[256,8,1024]{0,2,1:T(8,128)(2,1)} copy(bf16[256,8,1024]{2,1,0:T(8,128)(2,1)} %param.13) | data formatting | bytes 8388608 | tf_op args[4]
  45.1 0.0 copy-done.5
  45.2 3.4 %convert_bitcast_fusion = bf16[64,8,16,256]{3,0,2,1:T(8,128)(2,1)S(1)} fusion(bf16[256,8,16,64]{0,3,2,1:T(8,128)(2,1)} %bitcast.27, f32[8,64,64]{2,1,0:T(8,128)S(1)} %copy-done.5), kind=kOutput, calls=%fused_computation | convolution fusion | flops 270565376 | bytes 8519680 | tf_op jit(solution)/shard_map/qeil,ejl->jeiq/dot_general | solution.py:212
  48.6 4.4 %copy.17 = bf16[64,8,16,256]{3,2,1,0:T(8,128)(2,1)} copy(bf16[64,8,16,256]{3,0,2,1:T(8,128)(2,1)S(1)} %convert_bitcast_fusion) | data formatting | bytes 8388608 | tf_op jit(solution)/shard_map/convert_element_type | solution.py:217
  53.0 3.9 %all-to-all-done.2.arrived_ref = bf16[16,192,128]{2,1,0:T(8,128)(2,1)S(1)} async-done(((bf16[16,192,128]{2,1,0:T(8,128)(2,1)}), bf16[16,192,128]{2,1,0:T(8,128)(2,1)S(1)}, u32[]{:S(2)}, u32[]{:S(2)}) %all-to-all-start.2) | async-done | bytes 786464 | tf_op jit(solution)/shard_map/all_to_all | solution.py:210
  56.9 0.0 copy-start.1
  56.9 2.2 %copy-done.1 = bf16[64,8,16,256]{3,2,1,0:T(8,128)(2,1)S(1)} copy-done((bf16[64,8,16,256]{3,2,1,0:T(8,128)(2,1)S(1)}, bf16[64,8,16,256]{3,2,1,0:T(8,128)(2,1)}, u32[]{:S(2)}) %copy-start.1) | copy-done | bytes 4194328
  59.1 4.1 %shard_map.93 = f32[4,4,8,64]{3,2,1,0:T(8,128)S(1)} custom-call(bf16[16,192,128]{2,1,0:T(8,128)(2,1)S(1)} %all-to-all-done.2.arrived_ref, s32[16,128]{1,0:T(8,128)S(1)} %convert.1.docs_ref, bf16[8192,256]{1,0:T(8,128)(2,1)S(1)} %bitcast.25), custom_call_target="tpu_custom_call" | custom-call | tf_op jit(solution)/shard_map/pallas_call | solution.py:157
  63.1 0.1 reshape.182
  63.3 11.9 %all_to_all.20 = f32[16,1,512]{2,1,0:T(1,128)S(1)} all-to-all(f32[16,1,512]{2,1,0:T(1,128)S(1)} %reshape.182), channel_id=1, replica_groups=mesh['groups'=2,'expert'=4,'proj'=4] {'expert','proj'}, dimensions={0} | all-to-all | bytes 65536 | tf_op jit(solution)/shard_map/all_to_all | solution.py:220
  75.2 0.5 broadcast.177
  75.7 0.7 reduce
  76.4 0.1 reshape.183
  76.5 0.6 reduce_sum.9
  (8 shorter events, 0.1 us)
Async XLA Ops:
  0.0 21.7 %copy-start = (s32[512,8]{0,1:T(8,128)S(1)}, s32[512,8]{0,1:T(8,128)}, u32[]{:S(2)}) copy-start(s32[512,8]{0,1:T(8,128)} %param.11) | copy-start | bytes 49156
  2.6 15.6 %all-to-all-start.1 = ((bf16[4,272,128]{2,1,0:T(8,128)(2,1)}), bf16[4,272,128]{2,1,0:T(8,128)(2,1)S(1)}, u32[]{:S(2)}, u32[]{:S(2)}) async-start(bf16[4,272,128]{2,1,0:T(8,128)(2,1)} %broadcast_in_dim.11), calls=%async_computation.1 | async-start | bytes 557056 | tf_op jit(solution)/shard_map/all_to_all | solution.py:192
  8.9 1.5 %copy-start.2 = (bf16[512,1792]{1,0:T(8,128)(2,1)S(1)}, bf16[512,1792]{1,0:T(8,128)(2,1)}, u32[]{:S(2)}) copy-start(bf16[512,1792]{1,0:T(8,128)(2,1)} %act_ref.1) | copy-start | bytes 5505028
  10.4 0.9 %copy-start.3 = (bf16[64,1792]{1,0:T(8,128)(2,1)S(1)}, bf16[64,1792]{1,0:T(8,128)(2,1)}, u32[]{:S(2)}) copy-start(bf16[64,1792]{1,0:T(8,128)(2,1)} %in_proj_ref.1) | copy-start | bytes 688132
  11.3 0.8 %copy-start.4 = (bf16[64,512]{1,0:T(8,128)(2,1)S(1)}, bf16[64,512]{1,0:T(8,128)(2,1)}, u32[]{:S(2)}) copy-start(bf16[64,512]{1,0:T(8,128)(2,1)} %out_proj_ref.1) | copy-start | bytes 196612
  18.2 13.0 %all-to-all-start = ((bf16[4,576,128]{2,1,0:T(8,128)(2,1)}), bf16[4,576,128]{2,1,0:T(8,128)(2,1)S(1)}, u32[]{:S(2)}, u32[]{:S(2)}) async-start(bf16[4,576,128]{2,1,0:T(8,128)(2,1)} %shard_map.91), calls=%async_computation | async-start | bytes 1179648 | tf_op jit(solution)/shard_map/all_to_all | solution.py:207
  33.0 23.9 %all-to-all-start.2 = ((bf16[16,192,128]{2,1,0:T(8,128)(2,1)}), bf16[16,192,128]{2,1,0:T(8,128)(2,1)S(1)}, u32[]{:S(2)}, u32[]{:S(2)}) async-start(bf16[16,192,128]{2,1,0:T(8,128)(2,1)} %shard_map.92), calls=%async_computation.2 | async-start | bytes 1572864 | tf_op jit(solution)/shard_map/all_to_all | solution.py:210
  38.2 7.0 %copy-start.5 = (f32[8,64,64]{2,1,0:T(8,128)S(1)}, f32[8,64,64]{2,1,0:T(8,128)}, u32[]{:S(2)}) copy-start(f32[8,64,64]{2,1,0:T(8,128)} %param.16) | copy-start | bytes 393220
  56.9 2.2 %copy-start.1 = (bf16[64,8,16,256]{3,2,1,0:T(8,128)(2,1)S(1)}, bf16[64,8,16,256]{3,2,1,0:T(8,128)(2,1)}, u32[]{:S(2)}) copy-start(bf16[64,8,16,256]{3,2,1,0:T(8,128)(2,1)} %copy.17) | copy-start | bytes 12582916

commit v2 on v1

--- a/solution.py
+++ b/solution.py
@@ -8,7 +8,7 @@
 from jax.sharding import PartitionSpec as P
 
 DOC_DEV = 8
-VMEM_BYTES = 48 * 1024 * 1024
+VMEM_BYTES = 40 * 1024 * 1024
 
 
 def half_lanes(shape, width):
@@ -32,16 +32,18 @@
         act_ref[...], twice_in, (((1,), (1,)), ((), ())), preferred_element_type=jnp.float32
     )
     half = quarter // 2
-    wire_ref[0, top // 2 * quarter :, :] = jnp.where(
-        half_lanes((half, 2 * width), width), inner[:half], inner[half:]
-    ).astype(jnp.bfloat16)
+    packed = jnp.where(half_lanes((half, 2 * width), width), inner[:half], inner[half:])
+    high = packed.astype(jnp.bfloat16)
+    start = top // 2 * quarter
+    wire_ref[0, start : start + half, :] = high
+    wire_ref[0, start + half :, :] = (packed - high.astype(jnp.float32)).astype(jnp.bfloat16)
 
 
 def project(activations, flat_hidden, in_projection, out_projection, quarters, top):
     tokens, model = activations.shape
     width = in_projection.shape[0]
     quarter = tokens // quarters
-    wire_rows = top // 2 * quarter + quarter // 2
+    wire_rows = top // 2 * quarter + quarter
     return pl.pallas_call(
         functools.partial(project_kernel, top=top),
         grid=(quarters,),
@@ -54,11 +56,13 @@
         out_specs=pl.BlockSpec((1, wire_rows, 2 * width), lambda q: (q, 0, 0)),
         out_shape=jax.ShapeDtypeStruct((quarters, wire_rows, 2 * width), jnp.bfloat16),
         scratch_shapes=[pltpu.VMEM((quarter * top, 2 * width), jnp.float32)],
-        compiler_params=pltpu.CompilerParams(vmem_limit_bytes=VMEM_BYTES),
+        compiler_params=pltpu.CompilerParams(vmem_limit_bytes=60 * 1024 * 1024),
     )(activations, flat_hidden, in_projection, out_projection)
 
 
-def condition_kernel(parts_ref, routes_ref, weights_ref, payload_ref, value_ref, name_ref, *, top, width):
+def condition_kernel(
+    place_ref, parts_ref, routes_ref, weights_ref, payload_ref, value_ref, name_ref, *, top, width
+):
     quarter = routes_ref.shape[0]
     groups, dense_width, _ = weights_ref.shape
     shares = payload_ref.shape[0] // groups
@@ -81,11 +85,12 @@
     for k in range(top):
         name_ref[k] = jnp.broadcast_to(routes_ref[:, k : k + 1], (quarter, lanes)) - second
     half = quarter // 2
-    inner = summed(top // 2 * quarter, half)
+    inner = summed(top // 2 * quarter, half) + summed(top // 2 * quarter + half, half)
     inner = jnp.concatenate([inner[:, :width], inner[:, width:]], axis=0)
     inner = jnp.transpose(inner).astype(jnp.bfloat16)
 
-    def one_group(group, carry):
+    def one_group(step, carry):
+        group = lax.rem(place_ref[0] + groups - step, groups)
         dense = []
         for pair in range(experts // 2):
             base = group * experts + 2 * pair
@@ -94,7 +99,7 @@
                 chosen = jnp.where(name_ref[k] == base, value_ref[k], chosen)
             dense.append(chosen.astype(jnp.bfloat16))
         result = jnp.dot(
-            jnp.concatenate(dense, axis=1), weights_ref[group], preferred_element_type=jnp.float32
+            jnp.concatenate(dense, axis=1), weights_ref[step], preferred_element_type=jnp.float32
         ).astype(jnp.bfloat16)
         share_width = result.shape[1] // shares
         for share in range(shares):
@@ -105,22 +110,26 @@
     lax.fori_loop(0, groups, one_group, 0, unroll=groups <= 4)
 
 
-def condition(parts, quarter_routes, weights, shares, width):
+def condition(place, parts, quarter_routes, weights, shares, width):
     quarter, top = quarter_routes.shape
     groups = weights.shape[0]
     lanes = 2 * width
+    whole = pl.BlockSpec(memory_space=pltpu.VMEM)
     return pl.pallas_call(
         functools.partial(condition_kernel, top=top, width=width),
+        in_specs=[pl.BlockSpec(memory_space=pltpu.SMEM), whole, whole, whole],
         out_shape=jax.ShapeDtypeStruct((groups * shares, quarter + width, lanes), jnp.bfloat16),
         scratch_shapes=[
             pltpu.VMEM((top, quarter, lanes), jnp.float32),
             pltpu.VMEM((top, quarter, lanes), jnp.int32),
         ],
         compiler_params=pltpu.CompilerParams(vmem_limit_bytes=VMEM_BYTES),
-    )(parts, quarter_routes, weights)
-
-
-def score_kernel(arrived_ref, docs_ref, queries_ref, out_ref, grads_ref, *, width, doc_count):
+    )(place, parts, quarter_routes, weights)
+
+
+def score_kernel(arrived_ref, docs_ref, far_ref, out_ref, grads_ref, queries_ref, sem, *, width, doc_count):
+    fetch = pltpu.make_async_copy(far_ref, queries_ref, sem)
+    fetch.start()
     sources, rows, lanes = arrived_ref.shape
     quarter = rows - width
     outer = arrived_ref[:, :quarter, :].reshape(sources * quarter, lanes)
@@ -140,10 +149,15 @@
         return carry
 
     lax.fori_loop(0, doc_count // doc_group, one_group, 0, unroll=doc_count <= 32)
-    flat = jnp.concatenate(
-        [grads_ref[pl.ds(j, doc_count, stride=width), :].astype(jnp.bfloat16) for j in range(width)], axis=1
-    )
+    high, low = [], []
+    for j in range(width):
+        grads = grads_ref[pl.ds(j, doc_count, stride=width), :]
+        high.append(grads.astype(jnp.bfloat16))
+        low.append((grads - high[-1].astype(jnp.float32)).astype(jnp.bfloat16))
+    flat = jnp.concatenate([jnp.concatenate(high, axis=1), jnp.concatenate(low, axis=1)], axis=0)
+    fetch.wait()
     result = jnp.dot(flat, queries_ref[...], preferred_element_type=jnp.float32)
+    result = result[:doc_count] + result[doc_count:]
     owners, shares, owned, columns = out_ref.shape
     for owner in range(owners):
         for share in range(shares):
@@ -157,9 +171,38 @@
     return pl.pallas_call(
         functools.partial(score_kernel, width=width, doc_count=doc_count),
         out_shape=jax.ShapeDtypeStruct((owners, shares, DOC_DEV, queries.shape[1] // shares), jnp.float32),
-        scratch_shapes=[pltpu.VMEM((doc_count * width, arrived.shape[2]), jnp.float32)],
+        in_specs=[
+            pl.BlockSpec(memory_space=pltpu.VMEM),
+            pl.BlockSpec(memory_space=pltpu.VMEM),
+            pl.BlockSpec(memory_space=pl.ANY),
+        ],
+        scratch_shapes=[
+            pltpu.VMEM((doc_count * width, arrived.shape[2]), jnp.float32),
+            pltpu.VMEM(queries.shape, jnp.bfloat16),
+            pltpu.SemaphoreType.DMA,
+        ],
         compiler_params=pltpu.CompilerParams(vmem_limit_bytes=VMEM_BYTES),
     )(arrived, docs, queries)
+
+
+def sum_kernel(pieces_ref, out_ref):
+    total = pieces_ref[0]
+    for source in range(1, pieces_ref.shape[0]):
+        total = total + pieces_ref[source]
+    out_ref[...] = total
+
+
+def sum_pieces(pieces):
+    return pl.pallas_call(
+        sum_kernel, out_shape=jax.ShapeDtypeStruct(pieces.shape[1:], jnp.float32)
+    )(pieces)
+
+
+def gather_turned(block, axis, size):
+    arrived = [block]
+    for step in range(1, size):
+        arrived.append(lax.ppermute(block, axis, [(i, (i + step) % size) for i in range(size)]))
+    return jnp.stack(arrived)
 
 
 def local(
@@ -188,25 +231,26 @@
     factors = jnp.concatenate([factors[:half], factors[half:]], axis=2).reshape(half * width, 2 * width)
     doc_rows = doc_ids.astype(jnp.bfloat16).reshape(tokens // 128, 128)
     shared = jnp.concatenate([factors, jnp.pad(doc_rows, ((0, 16 - tokens // 128), (0, 0)))], axis=0)
-    shared = jnp.broadcast_to(shared[None], (owners, *shared.shape))
-    shared = lax.all_to_all(shared, "expert", 0, 0, tiled=True)
+    place = lax.axis_index("expert")
+    shared = gather_turned(shared, "expert", owners)
     all_docs = shared[:, half * width : half * width + tokens // 128, :].astype(jnp.int32)
+    all_docs = all_docs[(place - jnp.arange(owners)) % owners]
     all_docs = all_docs.reshape(owners * shares, quarter)
     factors = shared[:, : half * width, :].reshape(owners, half, width, 2, width)
     factors = factors.transpose(0, 3, 1, 2, 4).reshape(owners * experts * width, width)
 
     column = jnp.arange(experts * width)
     source_row = column // (experts * share_rows) * share_rows + column % share_rows
-    place = (jnp.arange(width)[:, None] == source_row[None, :]).astype(jnp.bfloat16)
+    spread = (jnp.arange(width)[:, None] == source_row[None, :]).astype(jnp.bfloat16)
     own = column[:, None] // width == (column[None, :] // share_rows) % experts
-    weights = jnp.dot(factors, place, preferred_element_type=jnp.float32).reshape(owners, experts * width, experts * width)
+    weights = jnp.dot(factors, spread, preferred_element_type=jnp.float32).reshape(owners, experts * width, experts * width)
     weights = jnp.where(own[None], weights, 0).astype(jnp.bfloat16)
 
     flat_hidden = grad_hidden.reshape(tokens * top, grad_hidden.shape[2])
     wire = project(activations, flat_hidden, in_projection, out_projection, shares, top)
     parts = lax.all_to_all(wire, "proj", 0, 0, tiled=True)
     quarter_routes = lax.dynamic_slice_in_dim(routes, lax.axis_index("proj") * quarter, quarter, 0)
-    payload = condition(parts, quarter_routes, weights, shares, width)
+    payload = condition(place.reshape(1).astype(jnp.int32), parts, quarter_routes, weights, shares, width)
     arrived = lax.all_to_all(payload, ("expert", "proj"), 0, 0, tiled=True)
 
     queries = jnp.einsum(
@@ -220,7 +264,7 @@
     pieces = lax.all_to_all(
         partial_scores.reshape(owners * shares, DOC_DEV, query_count // shares), ("expert", "proj"), 0, 0, tiled=True
     )
-    return jnp.sum(pieces, axis=0).T
+    return sum_pieces(pieces).T
 
 
 def solution(mesh):

time: 77.9 us -> 75.6 us (0.970)
  Pallas kernels: 11 us -> 14 us
  local copies, waits for them, and re-layouts: 19.4 us -> 16.6 us
  starting transfers between devices: 15 us -> 14.1 us
  waiting for transfers between devices: 10.5 us -> 9.61 us
    ppermute x0 -> x3, starting transfers between devices: none -> 7.01 us  [gather_turned(): lax.ppermute(block, axis, [(i, (i + step) % size) for i in range(size)])]
    all_to_all x1 -> x0, starting transfers between devices: 6.32 us -> none  [local(): shared = lax.all_to_all(shared, 'expert', 0, 0, tiled=True)]
    unnamed x16 -> x10, local copies, waits for them, and re-layouts: 12.7 us -> 10 us
    all_to_all x1, starting transfers between devices: 5.19 us -> 3.61 us  [local(): arrived = lax.all_to_all(payload, ('expert', 'proj'), 0, 0, tiled=True)]
    pallas_call x0 -> x1, Pallas kernels: none -> 1.45 us  [sum_pieces(): pl.pallas_call(sum_kernel, out_shape=jax.ShapeDtypeStruct(pieces.shape[1:...]
    pallas_call x1, Pallas kernels: 4.05 us -> 5.28 us  [score(): pl.pallas_call(functools.partial(score_kernel, width=width, doc_count=doc...]
  transfers between devices with their start and end apart: 3 -> 5, of which waited for: 2 -> 2; matrix products, arithmetic and copies ran while one was open for 24% -> 26% of each run, Pallas kernels for 7% -> 7%
where the time goes in v2:
time: 75.6 us; the launch traced here: 74.9 us
  local copies, waits for them, and re-layouts  16.6 us (22%)
  starting transfers between devices  14.1 us (19%)
  Pallas kernels  14 us (19%)
  blocking collectives  11.9 us (16%)
  waiting for transfers between devices  9.61 us (13%)
  matrix products  5.11 us (7%)
  other arithmetic  3.49 us (5%)
    all_to_all x1, blocking collectives, local(): lax.all_to_all(partial_scores.reshape(owners * shares, DOC_DEV, query_cou...  11.9 us
    unnamed x10, local copies, waits for them, and re-layouts  10 us
    ppermute x3, starting transfers between devices, gather_turned(): lax.ppermute(block, axis, [(i, (i + step) % size) for i in range(size)])  7.01 us
    all_to_all x1, waiting for transfers between devices, local(): parts = lax.all_to_all(wire, 'proj', 0, 0, tiled=True)  6.28 us
    pallas_call x1, Pallas kernels, project(): pl.pallas_call(functools.partial(project_kernel, top=top), grid=(quarters...  5.43 us
    pallas_call x1, Pallas kernels, score(): pl.pallas_call(functools.partial(score_kernel, width=width, doc_count=doc...  5.28 us
    convert_element_type x1, local copies, waits for them, and re-layouts, local(): queries = jnp.einsum('qeil,ejl->jeiq', query_grads.reshape(query_count, e...  4.37 us
    all_to_all x1, starting transfers between devices, local(): arrived = lax.all_to_all(payload, ('expert', 'proj'), 0, 0, tiled=True)  3.61 us
  transfers between devices with their start and end apart: 5, of which 2 were waited for; matrix products, arithmetic and copies ran while one was open for 26% of the time, Pallas kernels for 7%

profile of v2, /device:TPU:0, one launch (start us, length us, event | category | flops | bytes accessed | tf_op | source)
XLA Modules:
  0.0 74.9 jit_solution(4632848593988415511)
XLA Ops:
  0.0 0.0 copy-start
  0.0 1.0 %convert_element_type.26 = bf16[8,64,64]{2,1,0:T(8,128)(2,1)S(1)} convert(f32[8,64,64]{2,1,0:T(8,128)} %param.17) | non-fusion elementwise | flops 32768 | bytes 196608 | tf_op jit(solution)/shard_map/convert_element_type | solution.py:230
  1.0 0.7 convert_bitcast_fusion.1
  1.7 0.1 pad_maximum_fusion.1
  1.8 3.1 %collective-permute-start = (bf16[272,128]{1,0:T(8,128)(2,1)S(1)}, bf16[272,128]{1,0:T(8,128)(2,1)S(1)}, u32[]{:S(2)}, u32[]{:S(2)}) collective-permute-start(bf16[272,128]{1,0:T(8,128)(2,1)S(1)} %get-tuple-element.8), channel_id=1, source_target_pairs={{0,4},{4,8},{8,12},{12,0},{1,5},{5,9},{9,13},{13,1},{2,6},{6,10},{... | collective-permute-start | bytes 208904 | tf_op jit(solution)/shard_map/ppermute | solution.py:204
  4.9 2.6 %collective-permute-start.1 = (bf16[272,128]{1,0:T(8,128)(2,1)S(1)}, bf16[272,128]{1,0:T(8,128)(2,1)S(1)}, u32[]{:S(2)}, u32[]{:S(2)}) collective-permute-start(bf16[272,128]{1,0:T(8,128)(2,1)S(1)} %get-tuple-element.8), channel_id=1, source_target_pairs={{0,8},{4,12},{8,0},{12,4},{1,9},{5,13},{9,1},{13,5},{2,10},{6,14},... | collective-permute-start | bytes 208904 | tf_op jit(solution)/shard_map/ppermute | solution.py:204
  7.5 1.3 %collective-permute-start.2 = (bf16[272,128]{1,0:T(8,128)(2,1)S(1)}, bf16[272,128]{1,0:T(8,128)(2,1)S(1)}, u32[]{:S(2)}, u32[]{:S(2)}) collective-permute-start(bf16[272,128]{1,0:T(8,128)(2,1)S(1)} %get-tuple-element.8), channel_id=1, source_target_pairs={{0,12},{4,0},{8,4},{12,8},{1,13},{5,1},{9,5},{13,9},{2,14},{6,2},{... | collective-permute-start | bytes 208904 | tf_op jit(solution)/shard_map/ppermute | solution.py:204
  8.8 5.4 %shard_map.91 = bf16[4,640,128]{2,1,0:T(8,128)(2,1)} custom-call(bf16[512,1792]{1,0:T(8,128)(2,1)} %act_ref.1, bf16[4096,512]{1,0:T(8,128)(2,1)} %bitcast.36, bf16[64,1792]{1,0:T(8,128)(2,1)} %in_proj_ref.1, bf16[64,512]{1,0:T(8,128)(2,1)} %out_proj_ref.1), custom_call_target="tpu_custom_call" | custom-call | tf_op jit(solution)/shard_map/pallas_call | solution.py:47
  14.3 3.5 %all-to-all-start = ((bf16[4,640,128]{2,1,0:T(8,128)(2,1)}), bf16[4,640,128]{2,1,0:T(8,128)(2,1)S(1)}, u32[]{:S(2)}, u32[]{:S(2)}) async-start(bf16[4,640,128]{2,1,0:T(8,128)(2,1)} %shard_map.91), calls=%async_computation | async-start | bytes 1310720 | tf_op jit(solution)/shard_map/all_to_all | solution.py:251
  17.8 0.0 copy-done
  17.8 0.1 copy.18.routes_ref
  17.9 0.9 %broadcast_compare_fusion = pred[512,512]{1,0:T(8,128)(4,1)} fusion(s32[512]{0:T(512)S(1)} %get-tuple-element.9, s32[512]{0:T(512)S(1)} %get-tuple-element.10), kind=kLoop, calls=%fused_computation.3 | loop fusion | flops 262144 | bytes 266240 | tf_op jit(solution)/shard_map/eq | solution.py:245
  18.8 0.0 collective-permute-done
  18.8 0.0 collective-permute-done.1
  18.8 0.0 collective-permute-done.2
  18.9 0.2 reshape.222
  19.2 0.5 copy.14
  19.7 0.3 dot_general.8
  20.0 1.7 %select_convert_fusion.weights_ref = bf16[4,512,512]{2,1,0:T(8,128)(2,1)S(1)} fusion(bf16[4,512,64]{1,2,0:T(8,128)(2,1)S(1)} %dot_general.8, pred[512,512]{1,0:T(8,128)(4,1)} %broadcast_compare_fusion, s32[512]{0:T(512)S(1)} %fusion.12), kind=kOutput, calls=%fused_computation.2 | convolution fusion | flops 136347648 | bytes 2623488 | tf_op jit(solution)/shard_map/dot_general | solution.py:246
  21.7 6.3 %all-to-all-done.parts_ref = bf16[4,640,128]{2,1,0:T(8,128)(2,1)S(1)} async-done(((bf16[4,640,128]{2,1,0:T(8,128)(2,1)}), bf16[4,640,128]{2,1,0:T(8,128)(2,1)S(1)}, u32[]{:S(2)}, u32[]{:S(2)}) %all-to-all-start) | async-done | bytes 655392 | tf_op jit(solution)/shard_map/all_to_all | solution.py:251
  28.0 1.8 %shard_map.92 = bf16[16,192,128]{2,1,0:T(8,128)(2,1)} custom-call(s32[1]{0:T(128)} %bitcast.place_ref, bf16[4,640,128]{2,1,0:T(8,128)(2,1)S(1)} %all-to-all-done.parts_ref, s32[128,8]{1,0:T(8,128)S(1)} %copy.18.routes_ref, bf16[4,512,512]{2,1,0:T(8,128)(2,1)S(1)} %select_convert_fusion.weights_ref), custom_call_target="tpu_custom_call" | custom-call | tf_op jit(solution)/shard_map/pallas_call | solution.py:118
  29.8 3.6 %all-to-all-start.1 = ((bf16[16,192,128]{2,1,0:T(8,128)(2,1)}), bf16[16,192,128]{2,1,0:T(8,128)(2,1)S(1)}, u32[]{:S(2)}, u32[]{:S(2)}) async-start(bf16[16,192,128]{2,1,0:T(8,128)(2,1)} %shard_map.92), calls=%async_computation.1 | async-start | bytes 1572864 | tf_op jit(solution)/shard_map/all_to_all | solution.py:254
  33.4 0.0 copy-start.2
  33.4 6.9 %copy.15 = bf16[256,8,1024]{0,2,1:T(8,128)(2,1)} copy(bf16[256,8,1024]{2,1,0:T(8,128)(2,1)} %param.13) | data formatting | bytes 8388608 | tf_op args[4]
  40.3 0.0 copy-done.2
  40.3 3.4 %convert_bitcast_fusion = bf16[64,8,16,256]{3,0,2,1:T(8,128)(2,1)S(1)} fusion(bf16[256,8,16,64]{0,3,2,1:T(8,128)(2,1)} %bitcast.35, f32[8,64,64]{2,1,0:T(8,128)S(1)} %copy-done.2), kind=kOutput, calls=%fused_computation.1 | convolution fusion | flops 270565376 | bytes 8519680 | tf_op jit(solution)/shard_map/qeil,ejl->jeiq/dot_general | solution.py:256
  43.8 4.4 %copy.16 = bf16[64,8,16,256]{3,2,1,0:T(8,128)(2,1)} copy(bf16[64,8,16,256]{3,0,2,1:T(8,128)(2,1)S(1)} %convert_bitcast_fusion) | data formatting | bytes 8388608 | tf_op jit(solution)/shard_map/convert_element_type | solution.py:261
  48.2 0.6 gather_fusion
  48.8 3.3 %all-to-all-done.1.arrived_ref = bf16[16,192,128]{2,1,0:T(8,128)(2,1)S(1)} async-done(((bf16[16,192,128]{2,1,0:T(8,128)(2,1)}), bf16[16,192,128]{2,1,0:T(8,128)(2,1)S(1)}, u32[]{:S(2)}, u32[]{:S(2)}) %all-to-all-start.1) | async-done | bytes 786464 | tf_op jit(solution)/shard_map/all_to_all | solution.py:254
  52.1 0.0 copy-start.1
  52.1 2.2 %copy-done.1 = bf16[64,8,16,256]{3,2,1,0:T(8,128)(2,1)S(1)} copy-done((bf16[64,8,16,256]{3,2,1,0:T(8,128)(2,1)S(1)}, bf16[64,8,16,256]{3,2,1,0:T(8,128)(2,1)}, u32[]{:S(2)}) %copy-start.1) | copy-done | bytes 4194328
  54.3 5.3 %shard_map.93 = f32[4,4,8,64]{3,2,1,0:T(8,128)S(1)} custom-call(bf16[16,192,128]{2,1,0:T(8,128)(2,1)S(1)} %all-to-all-done.1.arrived_ref, s32[16,128]{1,0:T(8,128)S(1)} %bitcast.34, bf16[8192,256]{1,0:T(8,128)(2,1)S(1)} %bitcast.32), custom_call_target="tpu_custom_call" | custom-call | tf_op jit(solution)/shard_map/pallas_call | solution.py:171
  59.6 0.1 reshape.237
  59.7 11.9 %all_to_all.15 = f32[16,1,512]{2,1,0:T(1,128)S(1)} all-to-all(f32[16,1,512]{2,1,0:T(1,128)S(1)} %reshape.237), channel_id=1, replica_groups=mesh['groups'=2,'expert'=4,'proj'=4] {'expert','proj'}, dimensions={0} | all-to-all | bytes 65536 | tf_op jit(solution)/shard_map/all_to_all | solution.py:264
  71.5 0.5 broadcast.249
  72.0 0.7 reduce
  72.8 0.7 reshape.238.pieces_ref
  73.5 1.4 %shard_map.94 = f32[8,64]{1,0:T(8,128)} custom-call(f32[16,8,64]{2,1,0:T(8,128)} %reshape.238.pieces_ref), custom_call_target="tpu_custom_call" | custom-call | tf_op jit(solution)/shard_map/pallas_call | solution.py:196
  (10 shorter events, 0.1 us)
Async XLA Ops:
  0.0 17.8 %copy-start = (s32[512,8]{0,1:T(8,128)S(1)}, s32[512,8]{0,1:T(8,128)}, u32[]{:S(2)}) copy-start(s32[512,8]{0,1:T(8,128)} %param.11) | copy-start | bytes 49156
  1.8 17.0 %collective-permute-start = (bf16[272,128]{1,0:T(8,128)(2,1)S(1)}, bf16[272,128]{1,0:T(8,128)(2,1)S(1)}, u32[]{:S(2)}, u32[]{:S(2)}) collective-permute-start(bf16[272,128]{1,0:T(8,128)(2,1)S(1)} %get-tuple-element.8), channel_id=1, source_target_pairs={{0,4},{4,8},{8,12},{12,0},{1,5},{5,9},{9,13},{13,1},{2,6},{6,10},{... | collective-permute-start | bytes 208904 | tf_op jit(solution)/shard_map/ppermute | solution.py:204
  4.9 13.9 %collective-permute-start.1 = (bf16[272,128]{1,0:T(8,128)(2,1)S(1)}, bf16[272,128]{1,0:T(8,128)(2,1)S(1)}, u32[]{:S(2)}, u32[]{:S(2)}) collective-permute-start(bf16[272,128]{1,0:T(8,128)(2,1)S(1)} %get-tuple-element.8), channel_id=1, source_target_pairs={{0,8},{4,12},{8,0},{12,4},{1,9},{5,13},{9,1},{13,5},{2,10},{6,14},... | collective-permute-start | bytes 208904 | tf_op jit(solution)/shard_map/ppermute | solution.py:204
  7.5 11.3 %collective-permute-start.2 = (bf16[272,128]{1,0:T(8,128)(2,1)S(1)}, bf16[272,128]{1,0:T(8,128)(2,1)S(1)}, u32[]{:S(2)}, u32[]{:S(2)}) collective-permute-start(bf16[272,128]{1,0:T(8,128)(2,1)S(1)} %get-tuple-element.8), channel_id=1, source_target_pairs={{0,12},{4,0},{8,4},{12,8},{1,13},{5,1},{9,5},{13,9},{2,14},{6,2},{... | collective-permute-start | bytes 208904 | tf_op jit(solution)/shard_map/ppermute | solution.py:204
  14.3 13.7 %all-to-all-start = ((bf16[4,640,128]{2,1,0:T(8,128)(2,1)}), bf16[4,640,128]{2,1,0:T(8,128)(2,1)S(1)}, u32[]{:S(2)}, u32[]{:S(2)}) async-start(bf16[4,640,128]{2,1,0:T(8,128)(2,1)} %shard_map.91), calls=%async_computation | async-start | bytes 1310720 | tf_op jit(solution)/shard_map/all_to_all | solution.py:251
  29.8 22.3 %all-to-all-start.1 = ((bf16[16,192,128]{2,1,0:T(8,128)(2,1)}), bf16[16,192,128]{2,1,0:T(8,128)(2,1)S(1)}, u32[]{:S(2)}, u32[]{:S(2)}) async-start(bf16[16,192,128]{2,1,0:T(8,128)(2,1)} %shard_map.92), calls=%async_computation.1 | async-start | bytes 1572864 | tf_op jit(solution)/shard_map/all_to_all | solution.py:254
  33.4 6.9 %copy-start.2 = (f32[8,64,64]{2,1,0:T(8,128)S(1)}, f32[8,64,64]{2,1,0:T(8,128)}, u32[]{:S(2)}) copy-start(f32[8,64,64]{2,1,0:T(8,128)} %param.16) | copy-start | bytes 393220
  52.1 2.2 %copy-start.1 = (bf16[64,8,16,256]{3,2,1,0:T(8,128)(2,1)S(1)}, bf16[64,8,16,256]{3,2,1,0:T(8,128)(2,1)}, u32[]{:S(2)}) copy-start(bf16[64,8,16,256]{3,2,1,0:T(8,128)(2,1)} %copy.16) | copy-start | bytes 12582916

commit v3 on v2

v3 whole, which is shorter than its diff:
```python
import functools

import jax
import jax.numpy as jnp
from jax import lax
from jax.experimental import pallas as pl
from jax.experimental.pallas import tpu as pltpu
from jax.sharding import PartitionSpec as P

DOC_DEV = 8
LANES = 128
DOC_ROWS = 16
MIB = 1024 * 1024
VMEM = pl.BlockSpec(memory_space=pltpu.VMEM)
SMEM = pl.BlockSpec(memory_space=pltpu.SMEM)


def low_lanes(rows, width):
    return lax.broadcasted_iota(jnp.int32, (rows, LANES), 1) < width


def split(value):
    high = value.astype(jnp.bfloat16)
    return high, (value - high.astype(jnp.float32)).astype(jnp.bfloat16)


def project_kernel(
    act_ref, hidden_ref, in_proj_ref, out_proj_ref, inverse_ref, docs_ref, wire_ref, shared_ref, rows_ref, *, top
):
    quarter = act_ref.shape[0]
    width = in_proj_ref.shape[0]

    @pl.when(pl.program_id(0) == 0)
    def _():
        half = inverse_ref.shape[0] // 2
        for e in range(half):
            pair = jnp.concatenate([inverse_ref[e], inverse_ref[half + e]], axis=1)
            shared_ref[e * width : (e + 1) * width, :] = pair.astype(jnp.bfloat16)
        docs = docs_ref[...].astype(jnp.float32)
        docs = jnp.concatenate([docs, jnp.zeros((DOC_ROWS - docs.shape[0], LANES), jnp.float32)], axis=0)
        shared_ref[half * width :, :] = docs.astype(jnp.bfloat16)

    twice = jnp.concatenate([out_proj_ref[...], out_proj_ref[...]], axis=0)
    rows_ref[...] = lax.dot_general(
        hidden_ref[...], twice, (((1,), (1,)), ((), ())), preferred_element_type=jnp.float32
    )
    first = low_lanes(quarter, width)
    for pair in range(top // 2):
        even = rows_ref[pl.ds(2 * pair, quarter, stride=top), :]
        odd = rows_ref[pl.ds(2 * pair + 1, quarter, stride=top), :]
        wire_ref[0, pair * quarter : (pair + 1) * quarter, :] = jnp.where(first, even, odd).astype(jnp.bfloat16)
    twice_in = jnp.concatenate([in_proj_ref[...], in_proj_ref[...]], axis=0)
    inner = lax.dot_general(
        act_ref[...], twice_in, (((1,), (1,)), ((), ())), preferred_element_type=jnp.float32
    )
    half = quarter // 2
    high, low = split(jnp.where(low_lanes(half, width), inner[:half], inner[half:]))
    start = top // 2 * quarter
    wire_ref[0, start : start + half, :] = high
    wire_ref[0, start + half :, :] = low


def project(activations, flat_hidden, in_projection, out_projection, inverse_out, doc_rows, quarters, top):
    tokens, model = activations.shape
    width = in_projection.shape[0]
    quarter = tokens // quarters
    wire_rows = top // 2 * quarter + quarter
    shared_rows = inverse_out.shape[0] // 2 * width + DOC_ROWS
    return pl.pallas_call(
        functools.partial(project_kernel, top=top),
        grid=(quarters,),
        in_specs=[
            pl.BlockSpec((quarter, model), lambda q: (q, 0)),
            pl.BlockSpec((quarter * top, flat_hidden.shape[1]), lambda q: (q, 0)),
            pl.BlockSpec(in_projection.shape, lambda q: (0, 0)),
            pl.BlockSpec(out_projection.shape, lambda q: (0, 0)),
            pl.BlockSpec(inverse_out.shape, lambda q: (0, 0, 0)),
            pl.BlockSpec(doc_rows.shape, lambda q: (0, 0)),
        ],
        out_specs=[
            pl.BlockSpec((1, wire_rows, LANES), lambda q: (q, 0, 0)),
            pl.BlockSpec((shared_rows, LANES), lambda q: (0, 0)),
        ],
        out_shape=[
            jax.ShapeDtypeStruct((quarters, wire_rows, LANES), jnp.bfloat16),
            jax.ShapeDtypeStruct((shared_rows, LANES), jnp.bfloat16),
        ],
        scratch_shapes=[pltpu.VMEM((quarter * top, LANES), jnp.float32)],
        compiler_params=pltpu.CompilerParams(vmem_limit_bytes=60 * MIB),
    )(activations, flat_hidden, in_projection, out_projection, inverse_out, doc_rows)


def expand_kernel(place_ref, *refs, width, experts, shares):
    *shared_refs, weights_ref, docs_ref = refs
    owners = len(shared_refs)
    columns = experts * width
    share_rows = width // shares
    half = experts // 2
    lane = lax.broadcasted_iota(jnp.int32, (LANES, columns), 1)
    row = lax.broadcasted_iota(jnp.int32, (LANES, columns), 0)
    source = lane // (experts * share_rows) * share_rows + lane % share_rows
    expert_lane = lax.broadcasted_iota(jnp.int32, (half * width, columns), 1) // share_rows % experts
    expert_row = lax.broadcasted_iota(jnp.int32, (half * width, columns), 0) // width
    for side in range(2):
        spread = (row == source + side * width).astype(jnp.float32).astype(jnp.bfloat16)
        own = expert_lane == expert_row + side * half
        for step in range(owners):
            placed = jnp.dot(
                shared_refs[step][: half * width, :], spread, preferred_element_type=jnp.float32
            )
            weights_ref[step, side * half * width : (side + 1) * half * width, :] = jnp.where(
                own, placed, 0.0
            ).astype(jnp.bfloat16)
    for step in range(owners):
        owner = lax.rem(place_ref[0] + owners - step, owners)
        docs_ref[owner] = shared_refs[step][half * width :, :].astype(jnp.float32).astype(jnp.int32)


def expand(place, shared, width, experts, shares):
    owners = len(shared)
    return pl.pallas_call(
        functools.partial(expand_kernel, width=width, experts=experts, shares=shares),
        in_specs=[SMEM] + [VMEM] * owners,
        out_shape=[
            jax.ShapeDtypeStruct((owners, experts * width, experts * width), jnp.bfloat16),
            jax.ShapeDtypeStruct((owners, DOC_ROWS, LANES), jnp.int32),
        ],
        compiler_params=pltpu.CompilerParams(vmem_limit_bytes=40 * MIB),
    )(place, *shared)


def condition_kernel(
    place_ref, parts_ref, routes_ref, weights_ref, payload_ref, inner_ref, value_ref, name_ref, *, top, width
):
    quarter = routes_ref.shape[0]
    groups, dense_width, _ = weights_ref.shape
    shares = payload_ref.shape[0] // groups
    experts = dense_width // width
    first = low_lanes(quarter, width)
    second = 1 - first.astype(jnp.int32)

    def summed(start, size):
        total = parts_ref[0, start : start + size, :].astype(jnp.float32)
        for source in range(1, parts_ref.shape[0]):
            total = total + parts_ref[source, start : start + size, :].astype(jnp.float32)
        return total

    for pair in range(top // 2):
        both = summed(pair * quarter, quarter)
        swapped = pltpu.roll(both, width, 1)
        value_ref[2 * pair] = jnp.where(first, both, swapped)
        value_ref[2 * pair + 1] = jnp.where(first, swapped, both)
    for k in range(top):
        name_ref[k] = jnp.broadcast_to(routes_ref[:, k : k + 1], (quarter, LANES)) - second
    half = quarter // 2
    inner = summed(top // 2 * quarter, half) + summed(top // 2 * quarter + half, half)
    inner = jnp.concatenate([inner[:, :width], inner[:, width:]], axis=0)
    inner_ref[...] = jnp.transpose(inner).astype(jnp.bfloat16)

    def one_group(step, carry):
        group = lax.rem(place_ref[0] + groups - step, groups)
        dense = []
        for pair in range(experts // 2):
            base = group * experts + 2 * pair
            chosen = jnp.zeros((quarter, LANES), jnp.float32)
            for k in range(top):
                chosen = jnp.where(name_ref[k] == base, value_ref[k], chosen)
            dense.append(chosen.astype(jnp.bfloat16))
        result = jnp.dot(
            jnp.concatenate(dense, axis=1), weights_ref[step], preferred_element_type=jnp.float32
        ).astype(jnp.bfloat16)
        share_width = result.shape[1] // shares
        for share in range(shares):
            payload_ref[group * shares + share] = result[:, share * share_width : (share + 1) * share_width]
        return carry

    lax.fori_loop(0, groups, one_group, 0, unroll=groups <= 4)


def condition(place, parts, quarter_routes, weights, shares, width):
    quarter, top = quarter_routes.shape
    groups = weights.shape[0]
    return pl.pallas_call(
        functools.partial(condition_kernel, top=top, width=width),
        in_specs=[SMEM, VMEM, VMEM, VMEM],
        out_shape=[
            jax.ShapeDtypeStruct((groups * shares, quarter, LANES), jnp.bfloat16),
            jax.ShapeDtypeStruct((width, quarter), jnp.bfloat16),
        ],
        scratch_shapes=[
            pltpu.VMEM((top, quarter, LANES), jnp.float32),
            pltpu.VMEM((top, quarter, LANES), jnp.int32),
        ],
        compiler_params=pltpu.CompilerParams(vmem_limit_bytes=40 * MIB),
    )(place, parts, quarter_routes, weights)


def query_kernel(query_ref, inverse_ref, out_ref, factor_ref, spread_ref, wide_ref):
    count, experts, _ = query_ref.shape
    width = inverse_ref.shape[1]
    step = pl.program_id(0)
    rows = out_ref.shape[0] // width

    @pl.when(step == 0)
    def _():
        zeros = jnp.zeros((width, width), jnp.bfloat16)
        for e in range(experts):
            high, low = split(inverse_ref[e])
            upper = jnp.concatenate([high, zeros, low, zeros], axis=1)
            lower = jnp.concatenate([zeros, high, zeros, low], axis=1)
            factor_ref[e] = jnp.concatenate([upper, lower], axis=0)

    spread_ref[...] = query_ref[...].astype(jnp.float32).reshape(count * experts, LANES)
    for e in range(experts):
        query = spread_ref[pl.ds(e, count, stride=experts), :].astype(jnp.bfloat16)
        result = lax.dot_general(
            factor_ref[e],
            jnp.concatenate([query, query], axis=1),
            (((1,), (1,)), ((), ())),
            preferred_element_type=jnp.float32,
        )
        start = e * (rows // experts) + 2 * step
        for tile in range(wide_ref.shape[0]):
            part = result[:, tile * LANES : (tile + 1) * LANES]
            wide_ref[tile, pl.ds(start, width, stride=rows), :] = part[:width]
            wide_ref[tile, pl.ds(start + 1, width, stride=rows), :] = part[width:]

    @pl.when(step == pl.num_programs(0) - 1)
    def _():
        for tile in range(wide_ref.shape[0]):
            out_ref[:, tile * LANES : (tile + 1) * LANES] = wide_ref[tile].astype(jnp.bfloat16)


def condition_queries(query_grads, inverse_in):
    count, experts, flat = query_grads.shape
    width = inverse_in.shape[1]
    rows = experts * flat
    return pl.pallas_call(
        query_kernel,
        grid=(flat // LANES,),
        in_specs=[
            pl.BlockSpec((count, experts, LANES), lambda c: (0, 0, c)),
            pl.BlockSpec(inverse_in.shape, lambda c: (0, 0, 0)),
        ],
        out_specs=pl.BlockSpec((rows, count), lambda c: (0, 0)),
        out_shape=jax.ShapeDtypeStruct((rows, count), jnp.bfloat16),
        scratch_shapes=[
            pltpu.VMEM((experts, 2 * width, 4 * width), jnp.bfloat16),
            pltpu.VMEM((count * experts, LANES), jnp.float32),
            pltpu.VMEM((count // LANES, rows, LANES), jnp.float32),
        ],
        compiler_params=pltpu.CompilerParams(vmem_limit_bytes=40 * MIB),
    )(query_grads, inverse_in)


def score_kernel(place_ref, arrived_ref, docs_ref, *refs, width, doc_count, shares):
    *inner_refs, queries_ref, out_ref, grads_ref = refs
    owners = arrived_ref.shape[0] // shares
    outer, inner, docs = [], [], []
    for turn in range(shares):
        share = lax.rem(place_ref[1] + shares - turn, shares)
        for step in range(owners):
            owner = lax.rem(place_ref[0] + owners - step, owners)
            outer.append(arrived_ref[owner * shares + share])
            docs.append(docs_ref[owner, pl.ds(share, 1), :])
            inner.append(inner_refs[turn][step])
    outer = jnp.concatenate(outer, axis=0)
    inner = jnp.concatenate(inner, axis=1)
    docs = jnp.broadcast_to(jnp.concatenate(docs, axis=1), inner.shape)
    doc_group = 8

    def one_group(group, carry):
        masked = [
            jnp.where(docs == group * doc_group + d, inner, jnp.zeros_like(inner)) for d in range(doc_group)
        ]
        start = pl.multiple_of(group * doc_group * width, doc_group * width)
        grads_ref[pl.ds(start, doc_group * width), :] = jnp.dot(
            jnp.concatenate(masked, axis=0), outer, preferred_element_type=jnp.float32
        )
        return carry

    lax.fori_loop(0, doc_count // doc_group, one_group, 0, unroll=doc_count <= 32)
    high, low = [], []
    for j in range(width):
        parts = split(grads_ref[pl.ds(j, doc_count, stride=width), :])
        high.append(parts[0])
        low.append(parts[1])
    flat = jnp.concatenate([jnp.concatenate(high, axis=1), jnp.concatenate(low, axis=1)], axis=0)
    result = jnp.dot(flat, queries_ref[...], preferred_element_type=jnp.float32)
    result = result[:doc_count] + result[doc_count:]
    columns = result.shape[1] // shares
    fill = jnp.zeros((DOC_DEV, LANES - columns), jnp.float32)
    for owner in range(owners):
        for share in range(shares):
            piece = result[owner * DOC_DEV : (owner + 1) * DOC_DEV, share * columns : (share + 1) * columns]
            out_ref[owner * shares + share] = jnp.concatenate([piece, fill], axis=1)


def score(place, arrived, docs, inner, queries, width, shares):
    sources = arrived.shape[0]
    doc_count = DOC_DEV * sources // shares
    return pl.pallas_call(
        functools.partial(score_kernel, width=width, doc_count=doc_count, shares=shares),
        in_specs=[SMEM, VMEM, VMEM] + [VMEM] * len(inner) + [VMEM],
        out_shape=jax.ShapeDtypeStruct((sources, DOC_DEV, LANES), jnp.float32),
        scratch_shapes=[pltpu.VMEM((doc_count * width, arrived.shape[2]), jnp.float32)],
        compiler_params=pltpu.CompilerParams(vmem_limit_bytes=40 * MIB),
    )(place, arrived, docs, *inner, queries)


def sum_kernel(pieces_ref, out_ref):
    total = pieces_ref[0]
    for source in range(1, pieces_ref.shape[0]):
        total = total + pieces_ref[source]
    out_ref[...] = total[:, : out_ref.shape[1]]


def sum_pieces(pieces, columns):
    return pl.pallas_call(
        sum_kernel,
        in_specs=[VMEM],
        out_shape=jax.ShapeDtypeStruct((pieces.shape[1], columns), jnp.float32),
    )(pieces)


def gather_turned(block, axis, size):
    arrived = [block]
    for step in range(1, size):
        arrived.append(lax.ppermute(block, axis, [(i, (i + step) % size) for i in range(size)]))
    return arrived


def local(
    activations,
    grad_hidden,
    routes,
    doc_ids,
    query_grads,
    in_projection,
    out_projection,
    inverse_in,
    inverse_out,
):
    tokens, top = routes.shape
    experts, width, _ = inverse_in.shape
    owners = lax.axis_size("expert")
    shares = lax.axis_size("proj")
    quarter = tokens // shares
    assert quarter == LANES and 2 * width == LANES and experts * width // shares == LANES
    assert DOC_DEV * owners <= 256
    place = jnp.stack([lax.axis_index("expert"), lax.axis_index("proj")]).astype(jnp.int32)

    flat_hidden = grad_hidden.reshape(tokens * top, grad_hidden.shape[2])
    wire, shared = project(
        activations,
        flat_hidden,
        in_projection,
        out_projection,
        inverse_out,
        doc_ids.reshape(shares, quarter),
        shares,
        top,
    )
    parts = lax.all_to_all(wire, "proj", 0, 0, tiled=True)
    weights, all_docs = expand(place, gather_turned(shared, "expert", owners), width, experts, shares)
    quarter_routes = lax.dynamic_slice_in_dim(routes, lax.axis_index("proj") * quarter, quarter, 0)
    payload, inner = condition(place, parts, quarter_routes, weights, shares, width)
    arrived = lax.all_to_all(payload, ("expert", "proj"), 0, 0, tiled=True)
    inner = gather_turned(jnp.stack(gather_turned(inner, "expert", owners)), "proj", shares)
    queries = condition_queries(query_grads, inverse_in)
    partial_scores = score(place, arrived, all_docs, inner, queries, width, shares)
    pieces = lax.all_to_all(partial_scores, ("expert", "proj"), 0, 0, tiled=True)
    return sum_pieces(pieces, query_grads.shape[0] // shares).T


def solution(mesh):
    in_specs = (
        P(("groups", "expert"), "proj"),
        P(("groups", "expert"), None, "proj"),
        P(("groups", "expert"), None),
        P(("groups", "expert")),
        P(None, "expert", "proj"),
        P(None, "proj"),
        P(None, "proj"),
        P("expert", None, None),
        P("expert", None, None),
    )
    out_specs = P("proj", ("groups", "expert"))
    return jax.shard_map(local, mesh=mesh, in_specs=in_specs, out_specs=out_specs, check_vma=False)
```

time: 75.6 us -> 83 us (1.098)
  Pallas kernels: 14 us -> 25.5 us
  local copies, waits for them, and re-layouts: 16.6 us -> 7.3 us
  waiting for transfers between devices: 9.61 us -> 18.3 us
  starting transfers between devices: 14.1 us -> 20.7 us
  matrix products: 5.11 us -> 0 us
  other arithmetic: 3.49 us -> 0.09 us
  blocking collectives: 11.9 us -> 10.5 us
    ppermute x3 -> x9, waiting for transfers between devices: 0.01 us -> 18.3 us  [gather_turned(): lax.ppermute(block, axis, [(i, (i + step) % size) for i in range(size)])]
    pallas_call x1 -> x3, Pallas kernels: 1.45 us -> 12.8 us  [the longest x1 10.1 us: condition_queries(): pl.pallas_call(query_kernel, grid=(flat // LANES,), in_specs=[pl.BlockSpe...]
    all_to_all x1, waiting for transfers between devices: 6.28 us -> 0.01 us  [local(): parts = lax.all_to_all(wire, 'proj', 0, 0, tiled=True)]
    dot_general x2 -> x0, matrix products: 5.11 us -> none  [the longest x1 3.42 us: local(): jnp.einsum('qeil,ejl->jeiq', query_grads.reshape(query_count, experts, sh...]
    ppermute x3 -> x9, starting transfers between devices: 7.01 us -> 12 us  [gather_turned(): lax.ppermute(block, axis, [(i, (i + step) % size) for i in range(size)])]
    convert_element_type x1 -> x0, local copies, waits for them, and re-layouts: 4.37 us -> none  [local(): queries = jnp.einsum('qeil,ejl->jeiq', query_grads.reshape(query_count, e...]
    all_to_all x1, waiting for transfers between devices: 3.32 us -> 0.01 us  [local(): arrived = lax.all_to_all(payload, ('expert', 'proj'), 0, 0, tiled=True)]
    unnamed x10 -> x13, local copies, waits for them, and re-layouts: 10 us -> 7.3 us
  transfers between devices with their start and end apart: 5 -> 11, of which waited for: 2 -> 4; matrix products, arithmetic and copies ran while one was open for 26% -> 0% of each run, Pallas kernels for 7% -> 14%
where the time goes in v3:
time: 83 us; the launch traced here: 82.4 us
  Pallas kernels  25.5 us (31%)
  starting transfers between devices  20.7 us (25%)
  waiting for transfers between devices  18.3 us (22%)
  blocking collectives  10.5 us (13%)
  local copies, waits for them, and re-layouts  7.3 us (9%)
    ppermute x9, waiting for transfers between devices, gather_turned(): lax.ppermute(block, axis, [(i, (i + step) % size) for i in range(size)])  18.3 us
    ppermute x9, starting transfers between devices, gather_turned(): lax.ppermute(block, axis, [(i, (i + step) % size) for i in range(size)])  12 us
    all_to_all x1, blocking collectives, local(): lax.all_to_all(partial_scores, ('expert', 'proj'), 0, 0, tiled=True)  10.5 us
    pallas_call x1, Pallas kernels, condition_queries(): pl.pallas_call(query_kernel, grid=(flat // LANES,), in_specs=[pl.BlockSpe...  10.1 us
    unnamed x13, local copies, waits for them, and re-layouts  7.3 us
    pallas_call x1, Pallas kernels, project(): pl.pallas_call(functools.partial(project_kernel, top=top), grid=(quarters...  5.66 us
    pallas_call x1, Pallas kernels, score(): pl.pallas_call(functools.partial(score_kernel, width=width, doc_count=doc...  4.74 us
    all_to_all x1, starting transfers between devices, local(): parts = lax.all_to_all(wire, 'proj', 0, 0, tiled=True)  4.35 us
  transfers between devices with their start and end apart: 11, of which 4 were waited for; matrix products, arithmetic and copies ran while one was open for 0% of the time, Pallas kernels for 14%

profile of v3, /device:TPU:0, one launch (start us, length us, event | category | flops | bytes accessed | tf_op | source)
XLA Modules:
  0.0 82.4 jit_solution(14833509560659850012)
XLA Ops:
  0.0 0.0 copy-start
  0.0 5.7 %shard_map.91 = (bf16[4,640,128]{2,1,0:T(8,128)(2,1)}, bf16[272,128]{1,0:T(8,128)(2,1)}) custom-call(bf16[512,1792]{1,0:T(8,128)(2,1)} %act_ref.1, bf16[4096,512]{1,0:T(8,128)(2,1)} %bitcast.10, bf16[64,1792]{1,0:T(8,128)(2,1)} %in_proj_ref.1, bf16[64,512]{1,0:T(8,128)(2,1)} %out_proj_ref.1, f32[8,64,64]{2,1,0:T(8,128)} %inverse_ref.2, s32[4,128]{1,0:T(4,128)} %bitcast.14), custom_call_target="tpu_custom_call" | custom-call | tf_op jit(solution)/shard_map/pallas_call | solution.py:69
  5.7 0.0 copy-start.4
  5.7 4.3 %all-to-all-start = ((bf16[4,640,128]{2,1,0:T(8,128)(2,1)}), bf16[4,640,128]{2,1,0:T(8,128)(2,1)S(1)}, u32[]{:S(2)}, u32[]{:S(2)}) async-start(bf16[4,640,128]{2,1,0:T(8,128)(2,1)} %get-tuple-element.11), calls=%async_computation | async-start | bytes 1310720 | tf_op jit(solution)/shard_map/all_to_all | solution.py:364
  10.0 4.4 %collective-permute-start.2 = (bf16[272,128]{1,0:T(8,128)(2,1)}, bf16[272,128]{1,0:T(8,128)(2,1)S(1)}, u32[]{:S(2)}, u32[]{:S(2)}) collective-permute-start(bf16[272,128]{1,0:T(8,128)(2,1)} %get-tuple-element.12.refs_0_), channel_id=1, source_target_pairs={{0,12},{4,0},{8,4},{12,8},{1,13},{5,1},{9,5},{13,9},{2,14},{6,2},{... | collective-permute-start | bytes 208904 | tf_op jit(solution)/shard_map/ppermute | solution.py:329
  14.4 0.0 collective-permute-start.1
  14.4 1.0 %collective-permute-start = (bf16[272,128]{1,0:T(8,128)(2,1)}, bf16[272,128]{1,0:T(8,128)(2,1)S(1)}, u32[]{:S(2)}, u32[]{:S(2)}) collective-permute-start(bf16[272,128]{1,0:T(8,128)(2,1)} %get-tuple-element.12.refs_0_), channel_id=1, source_target_pairs={{0,4},{4,8},{8,12},{12,0},{1,5},{5,9},{9,13},{13,1},{2,6},{6,10},{... | collective-permute-start | bytes 208904 | tf_op jit(solution)/shard_map/ppermute | solution.py:329
  15.4 0.0 copy-done
  15.4 0.1 copy.11.routes_ref
  15.5 0.1 pad_add_fusion.place_ref
  15.6 1.7 %collective-permute-done.2.refs_3_ = bf16[272,128]{1,0:T(8,128)(2,1)S(1)} collective-permute-done((bf16[272,128]{1,0:T(8,128)(2,1)}, bf16[272,128]{1,0:T(8,128)(2,1)S(1)}, u32[]{:S(2)}, u32[]{:S(2)}) %collective-permute-start.2) | collective-permute-done | bytes 69664 | tf_op jit(solution)/shard_map/ppermute | solution.py:329
  17.3 4.8 %collective-permute-done.1.refs_2_ = bf16[272,128]{1,0:T(8,128)(2,1)S(1)} collective-permute-done((bf16[272,128]{1,0:T(8,128)(2,1)}, bf16[272,128]{1,0:T(8,128)(2,1)S(1)}, u32[]{:S(2)}, u32[]{:S(2)}) %collective-permute-start.1) | collective-permute-done | bytes 69664 | tf_op jit(solution)/shard_map/ppermute | solution.py:329
  22.0 0.0 collective-permute-done.refs_1_
  22.0 0.0 copy-start.5
  22.1 0.9 %copy-done.5 = bf16[272,128]{1,0:T(8,128)(2,1)S(1)} copy-done((bf16[272,128]{1,0:T(8,128)(2,1)S(1)}, bf16[272,128]{1,0:T(8,128)(2,1)}, u32[]{:S(2)}) %copy-start.5) | copy-done | bytes 69656
  22.9 1.3 %shard_map.92 = (bf16[4,512,512]{2,1,0:T(8,128)(2,1)S(1)}, s32[4,16,128]{2,1,0:T(8,128)S(1)}) custom-call(s32[2]{0:T(128)S(1)} %pad_add_fusion.place_ref, bf16[272,128]{1,0:T(8,128)(2,1)S(1)} %copy-done.5, bf16[272,128]{1,0:T(8,128)(2,1)S(1)} %collective-permute-done.refs_1_, bf16[272,128]{1,0:T(8,128)(2,1)S(1)} %collective-permute-done.1.refs_2_, ...), custom_call_target="tpu_custom_call" | custom-call | tf_op jit(solution)/shard_map/pallas_call | solution.py:121
  24.2 0.0 all-to-all-done.parts_ref
  24.2 2.3 %shard_map.93 = (bf16[16,128,128]{2,1,0:T(8,128)(2,1)}, bf16[64,128]{1,0:T(8,128)(2,1)S(1)}) custom-call(s32[2]{0:T(128)S(1)} %pad_add_fusion.place_ref, bf16[4,640,128]{2,1,0:T(8,128)(2,1)S(1)} %all-to-all-done.parts_ref, s32[128,8]{1,0:T(8,128)S(1)} %copy.11.routes_ref, bf16[4,512,512]{2,1,0:T(8,128)(2,1)S(1)} %get-tuple-element.13.weights_ref), custom_call_target="tpu_custom_call" | custom-call | tf_op jit(solution)/shard_map/pallas_call | solution.py:183
  26.5 4.3 %all-to-all-start.1 = ((bf16[16,128,128]{2,1,0:T(8,128)(2,1)}), bf16[16,128,128]{2,1,0:T(8,128)(2,1)S(1)}, u32[]{:S(2)}, u32[]{:S(2)}) async-start(bf16[16,128,128]{2,1,0:T(8,128)(2,1)} %get-tuple-element.14), calls=%async_computation.1 | async-start | bytes 1048576 | tf_op jit(solution)/shard_map/all_to_all | solution.py:368
  30.8 3.7 %collective-permute-start.5 = (bf16[64,128]{1,0:T(8,128)(2,1)S(1)}, bf16[64,128]{1,0:T(8,128)(2,1)S(1)}, u32[]{:S(2)}, u32[]{:S(2)}) collective-permute-start(bf16[64,128]{1,0:T(8,128)(2,1)S(1)} %get-tuple-element.16), channel_id=1, source_target_pairs={{0,12},{4,0},{8,4},{12,8},{1,13},{5,1},{9,5},{13,9},{2,14},{6,2},{... | collective-permute-start | bytes 49160 | tf_op jit(solution)/shard_map/ppermute | solution.py:329
  34.5 0.0 collective-permute-start.4
  34.5 1.1 %collective-permute-start.3 = (bf16[64,128]{1,0:T(8,128)(2,1)S(1)}, bf16[64,128]{1,0:T(8,128)(2,1)S(1)}, u32[]{:S(2)}, u32[]{:S(2)}) collective-permute-start(bf16[64,128]{1,0:T(8,128)(2,1)S(1)} %get-tuple-element.16), channel_id=1, source_target_pairs={{0,4},{4,8},{8,12},{12,0},{1,5},{5,9},{9,13},{13,1},{2,6},{6,10},{... | collective-permute-start | bytes 49160 | tf_op jit(solution)/shard_map/ppermute | solution.py:329
  35.7 5.2 %collective-permute-done.5 = bf16[64,128]{1,0:T(8,128)(2,1)S(1)} collective-permute-done((bf16[64,128]{1,0:T(8,128)(2,1)S(1)}, bf16[64,128]{1,0:T(8,128)(2,1)S(1)}, u32[]{:S(2)}, u32[]{:S(2)}) %collective-permute-start.5) | collective-permute-done | bytes 16416 | tf_op jit(solution)/shard_map/ppermute | solution.py:329
  40.9 6.6 %collective-permute-done.4 = bf16[64,128]{1,0:T(8,128)(2,1)S(1)} collective-permute-done((bf16[64,128]{1,0:T(8,128)(2,1)S(1)}, bf16[64,128]{1,0:T(8,128)(2,1)S(1)}, u32[]{:S(2)}, u32[]{:S(2)}) %collective-permute-start.4) | collective-permute-done | bytes 16416 | tf_op jit(solution)/shard_map/ppermute | solution.py:329
  47.5 0.0 collective-permute-done.3
  47.5 0.5 collective-permute-start.8
  48.0 1.1 %collective-permute-start.7 = (bf16[4,64,128]{2,1,0:T(8,128)(2,1)S(1)}, bf16[4,64,128]{2,1,0:T(8,128)(2,1)S(1)}, u32[]{:S(2)}, u32[]{:S(2)}) collective-permute-start(bf16[4,64,128]{2,1,0:T(8,128)(2,1)S(1)} %pad_maximum_fusion.refs_0_), channel_id=1, source_target_pairs={{0,2},{1,3},{2,0},{3,1},{4,6},{5,7},{6,4},{7,5},{8,10},{9,11},{10,... | collective-permute-start | bytes 196616 | tf_op jit(solution)/shard_map/ppermute | solution.py:329
  49.1 0.2 collective-permute-start.6
  49.3 0.0 copy-done.4
  49.3 0.0 copy-start.3
  49.3 2.2 %copy-done.3 = bf16[256,8,1024]{2,1,0:T(8,128)(2,1)S(1)} copy-done((bf16[256,8,1024]{2,1,0:T(8,128)(2,1)S(1)}, bf16[256,8,1024]{2,1,0:T(8,128)(2,1)}, u32[]{:S(2)}) %copy-start.3) | copy-done | bytes 4194328
  51.5 10.1 %shard_map.94.refs_4_ = bf16[8192,256]{1,0:T(8,128)(2,1)S(1)} custom-call(bf16[256,8,1024]{2,1,0:T(8,128)(2,1)S(1)} %copy-done.3, f32[8,64,64]{2,1,0:T(8,128)S(1)} %copy-done.4), custom_call_target="tpu_custom_call" | custom-call | tf_op jit(solution)/shard_map/pallas_call | solution.py:238
  61.6 0.0 copy-start.1
  61.6 1.9 %copy-done.1 = bf16[8192,256]{1,0:T(8,128)(2,1)} copy-done((bf16[8192,256]{1,0:T(8,128)(2,1)}, bf16[8192,256]{1,0:T(8,128)(2,1)S(1)}, u32[]{:S(2)}) %copy-start.1) | copy-done | bytes 4194328
  63.5 0.0 collective-permute-done.8.refs_3_
  63.5 0.0 collective-permute-done.7.refs_2_
  63.5 0.0 collective-permute-done.6.refs_1_
  63.5 0.0 all-to-all-done.1.arrived_ref
  63.6 0.0 copy-start.2
  63.6 2.2 %copy-done.2 = bf16[8192,256]{1,0:T(8,128)(2,1)S(1)} copy-done((bf16[8192,256]{1,0:T(8,128)(2,1)S(1)}, bf16[8192,256]{1,0:T(8,128)(2,1)}, u32[]{:S(2)}) %copy-start.2) | copy-done | bytes 4194328
  65.7 4.7 %shard_map.95 = f32[16,8,128]{2,1,0:T(8,128)S(1)} custom-call(s32[2]{0:T(128)S(1)} %pad_add_fusion.place_ref, bf16[16,128,128]{2,1,0:T(8,128)(2,1)S(1)} %all-to-all-done.1.arrived_ref, s32[4,16,128]{2,1,0:T(8,128)S(1)} %get-tuple-element.15.docs_ref, bf16[4,64,128]{2,1,0:T(8,128)(2,1)S(1)} %pad_maximum_fusion.refs_0_, ...), custom_call_target="tpu_custom_call" | custom-call | tf_op jit(solution)/shard_map/pallas_call | solution.py:302
  70.5 10.5 %all_to_all.15.pieces_ref = f32[16,8,128]{2,1,0:T(8,128)} all-to-all(f32[16,8,128]{2,1,0:T(8,128)S(1)} %shard_map.95), channel_id=1, replica_groups=mesh['groups'=2,'expert'=4,'proj'=4] {'expert','proj'}, dimensions={0} | all-to-all | bytes 131072 | tf_op jit(solution)/shard_map/all_to_all | solution.py:372
  81.0 1.4 %shard_map.96 = f32[8,64]{1,0:T(8,128)} custom-call(f32[16,8,128]{2,1,0:T(8,128)} %all_to_all.15.pieces_ref), custom_call_target="tpu_custom_call" | custom-call | tf_op jit(solution)/shard_map/pallas_call | solution.py:319
  (2 shorter events, 0.0 us)
Async XLA Ops:
  0.0 15.4 %copy-start = (s32[512,8]{0,1:T(8,128)S(1)}, s32[512,8]{0,1:T(8,128)}, u32[]{:S(2)}) copy-start(s32[512,8]{0,1:T(8,128)} %param.11) | copy-start | bytes 49156
  5.7 43.6 %copy-start.4 = (f32[8,64,64]{2,1,0:T(8,128)S(1)}, f32[8,64,64]{2,1,0:T(8,128)}, u32[]{:S(2)}) copy-start(f32[8,64,64]{2,1,0:T(8,128)} %inverse_ref.3) | copy-start | bytes 393220
  5.7 18.5 %all-to-all-start = ((bf16[4,640,128]{2,1,0:T(8,128)(2,1)}), bf16[4,640,128]{2,1,0:T(8,128)(2,1)S(1)}, u32[]{:S(2)}, u32[]{:S(2)}) async-start(bf16[4,640,128]{2,1,0:T(8,128)(2,1)} %get-tuple-element.11), calls=%async_computation | async-start | bytes 1310720 | tf_op jit(solution)/shard_map/all_to_all | solution.py:364
  10.0 7.3 %collective-permute-start.2 = (bf16[272,128]{1,0:T(8,128)(2,1)}, bf16[272,128]{1,0:T(8,128)(2,1)S(1)}, u32[]{:S(2)}, u32[]{:S(2)}) collective-permute-start(bf16[272,128]{1,0:T(8,128)(2,1)} %get-tuple-element.12.refs_0_), channel_id=1, source_target_pairs={{0,12},{4,0},{8,4},{12,8},{1,13},{5,1},{9,5},{13,9},{2,14},{6,2},{... | collective-permute-start | bytes 208904 | tf_op jit(solution)/shard_map/ppermute | solution.py:329
  14.4 7.6 %collective-permute-start.1 = (bf16[272,128]{1,0:T(8,128)(2,1)}, bf16[272,128]{1,0:T(8,128)(2,1)S(1)}, u32[]{:S(2)}, u32[]{:S(2)}) collective-permute-start(bf16[272,128]{1,0:T(8,128)(2,1)} %get-tuple-element.12.refs_0_), channel_id=1, source_target_pairs={{0,8},{4,12},{8,0},{12,4},{1,9},{5,13},{9,1},{13,5},{2,10},{6,14},... | collective-permute-start | bytes 208904 | tf_op jit(solution)/shard_map/ppermute | solution.py:329
  14.4 7.6 %collective-permute-start = (bf16[272,128]{1,0:T(8,128)(2,1)}, bf16[272,128]{1,0:T(8,128)(2,1)S(1)}, u32[]{:S(2)}, u32[]{:S(2)}) collective-permute-start(bf16[272,128]{1,0:T(8,128)(2,1)} %get-tuple-element.12.refs_0_), channel_id=1, source_target_pairs={{0,4},{4,8},{8,12},{12,0},{1,5},{5,9},{9,13},{13,1},{2,6},{6,10},{... | collective-permute-start | bytes 208904 | tf_op jit(solution)/shard_map/ppermute | solution.py:329
  22.0 0.9 %copy-start.5 = (bf16[272,128]{1,0:T(8,128)(2,1)S(1)}, bf16[272,128]{1,0:T(8,128)(2,1)}, u32[]{:S(2)}) copy-start(bf16[272,128]{1,0:T(8,128)(2,1)} %get-tuple-element.12.refs_0_) | copy-start | bytes 208900
  26.5 37.0 %all-to-all-start.1 = ((bf16[16,128,128]{2,1,0:T(8,128)(2,1)}), bf16[16,128,128]{2,1,0:T(8,128)(2,1)S(1)}, u32[]{:S(2)}, u32[]{:S(2)}) async-start(bf16[16,128,128]{2,1,0:T(8,128)(2,1)} %get-tuple-element.14), calls=%async_computation.1 | async-start | bytes 1048576 | tf_op jit(solution)/shard_map/all_to_all | solution.py:368
  30.8 10.1 %collective-permute-start.5 = (bf16[64,128]{1,0:T(8,128)(2,1)S(1)}, bf16[64,128]{1,0:T(8,128)(2,1)S(1)}, u32[]{:S(2)}, u32[]{:S(2)}) collective-permute-start(bf16[64,128]{1,0:T(8,128)(2,1)S(1)} %get-tuple-element.16), channel_id=1, source_target_pairs={{0,12},{4,0},{8,4},{12,8},{1,13},{5,1},{9,5},{13,9},{2,14},{6,2},{... | collective-permute-start | bytes 49160 | tf_op jit(solution)/shard_map/ppermute | solution.py:329
  34.5 13.0 %collective-permute-start.4 = (bf16[64,128]{1,0:T(8,128)(2,1)S(1)}, bf16[64,128]{1,0:T(8,128)(2,1)S(1)}, u32[]{:S(2)}, u32[]{:S(2)}) collective-permute-start(bf16[64,128]{1,0:T(8,128)(2,1)S(1)} %get-tuple-element.16), channel_id=1, source_target_pairs={{0,8},{4,12},{8,0},{12,4},{1,9},{5,13},{9,1},{13,5},{2,10},{6,14},... | collective-permute-start | bytes 49160 | tf_op jit(solution)/shard_map/ppermute | solution.py:329
  34.5 13.0 %collective-permute-start.3 = (bf16[64,128]{1,0:T(8,128)(2,1)S(1)}, bf16[64,128]{1,0:T(8,128)(2,1)S(1)}, u32[]{:S(2)}, u32[]{:S(2)}) collective-permute-start(bf16[64,128]{1,0:T(8,128)(2,1)S(1)} %get-tuple-element.16), channel_id=1, source_target_pairs={{0,4},{4,8},{8,12},{12,0},{1,5},{5,9},{9,13},{13,1},{2,6},{6,10},{... | collective-permute-start | bytes 49160 | tf_op jit(solution)/shard_map/ppermute | solution.py:329
  47.5 16.0 %collective-permute-start.8 = (bf16[4,64,128]{2,1,0:T(8,128)(2,1)S(1)}, bf16[4,64,128]{2,1,0:T(8,128)(2,1)S(1)}, u32[]{:S(2)}, u32[]{:S(2)}) collective-permute-start(bf16[4,64,128]{2,1,0:T(8,128)(2,1)S(1)} %pad_maximum_fusion.refs_0_), channel_id=1, source_target_pairs={{0,3},{1,0},{2,1},{3,2},{4,7},{5,4},{6,5},{7,6},{8,11},{9,8},{10,9... | collective-permute-start | bytes 196616 | tf_op jit(solution)/shard_map/ppermute | solution.py:329
  48.0 15.6 %collective-permute-start.7 = (bf16[4,64,128]{2,1,0:T(8,128)(2,1)S(1)}, bf16[4,64,128]{2,1,0:T(8,128)(2,1)S(1)}, u32[]{:S(2)}, u32[]{:S(2)}) collective-permute-start(bf16[4,64,128]{2,1,0:T(8,128)(2,1)S(1)} %pad_maximum_fusion.refs_0_), channel_id=1, source_target_pairs={{0,2},{1,3},{2,0},{3,1},{4,6},{5,7},{6,4},{7,5},{8,10},{9,11},{10,... | collective-permute-start | bytes 196616 | tf_op jit(solution)/shard_map/ppermute | solution.py:329
  49.1 14.4 %collective-permute-start.6 = (bf16[4,64,128]{2,1,0:T(8,128)(2,1)S(1)}, bf16[4,64,128]{2,1,0:T(8,128)(2,1)S(1)}, u32[]{:S(2)}, u32[]{:S(2)}) collective-permute-start(bf16[4,64,128]{2,1,0:T(8,128)(2,1)S(1)} %pad_maximum_fusion.refs_0_), channel_id=1, source_target_pairs={{0,1},{1,2},{2,3},{3,0},{4,5},{5,6},{6,7},{7,4},{8,9},{9,10},{10,1... | collective-permute-start | bytes 196616 | tf_op jit(solution)/shard_map/ppermute | solution.py:329
  49.3 2.2 %copy-start.3 = (bf16[256,8,1024]{2,1,0:T(8,128)(2,1)S(1)}, bf16[256,8,1024]{2,1,0:T(8,128)(2,1)}, u32[]{:S(2)}) copy-start(bf16[256,8,1024]{2,1,0:T(8,128)(2,1)} %query_ref.1) | copy-start | bytes 12582916
  61.6 1.9 %copy-start.1 = (bf16[8192,256]{1,0:T(8,128)(2,1)}, bf16[8192,256]{1,0:T(8,128)(2,1)S(1)}, u32[]{:S(2)}) copy-start(bf16[8192,256]{1,0:T(8,128)(2,1)S(1)} %shard_map.94.refs_4_) | copy-start | bytes 12582916
  63.6 2.2 %copy-start.2 = (bf16[8192,256]{1,0:T(8,128)(2,1)S(1)}, bf16[8192,256]{1,0:T(8,128)(2,1)}, u32[]{:S(2)}) copy-start(bf16[8192,256]{1,0:T(8,128)(2,1)} %copy-done.1) | copy-start | bytes 12582916

commit v4 on v3

--- a/solution.py
+++ b/solution.py
@@ -24,22 +24,34 @@
     return high, (value - high.astype(jnp.float32)).astype(jnp.bfloat16)
 
 
-def project_kernel(
-    act_ref, hidden_ref, in_proj_ref, out_proj_ref, inverse_ref, docs_ref, wire_ref, shared_ref, rows_ref, *, top
-):
+def cost(microseconds):
+    return pl.CostEstimate(flops=0, bytes_accessed=int(microseconds * 3.3e6), transcendentals=0)
+
+
+def pack_shared(inverse_ref, docs_ref, shared_ref):
+    width = inverse_ref.shape[1]
+    half = inverse_ref.shape[0] // 2
+    for e in range(half):
+        pair = jnp.concatenate([inverse_ref[e], inverse_ref[half + e]], axis=1)
+        shared_ref[e * width : (e + 1) * width, :] = pair.astype(jnp.bfloat16)
+    docs = docs_ref[...].astype(jnp.float32)
+    docs = jnp.concatenate([docs, jnp.zeros((DOC_ROWS - docs.shape[0], LANES), jnp.float32)], axis=0)
+    shared_ref[half * width :, :] = docs.astype(jnp.bfloat16)
+
+
+def project_kernel(place_ref, act_ref, hidden_ref, in_proj_ref, out_proj_ref, *refs, top):
+    *pack_refs, rows_ref = refs
+    if len(pack_refs) == 1:
+        wire_ref = pack_refs[0]
+    else:
+        inverse_ref, docs_ref, wire_ref, shared_ref = pack_refs
+
+        @pl.when(pl.program_id(0) == 0)
+        def _():
+            pack_shared(inverse_ref, docs_ref, shared_ref)
+
     quarter = act_ref.shape[0]
     width = in_proj_ref.shape[0]
-
-    @pl.when(pl.program_id(0) == 0)
-    def _():
-        half = inverse_ref.shape[0] // 2
-        for e in range(half):
-            pair = jnp.concatenate([inverse_ref[e], inverse_ref[half + e]], axis=1)
-            shared_ref[e * width : (e + 1) * width, :] = pair.astype(jnp.bfloat16)
-        docs = docs_ref[...].astype(jnp.float32)
-        docs = jnp.concatenate([docs, jnp.zeros((DOC_ROWS - docs.shape[0], LANES), jnp.float32)], axis=0)
-        shared_ref[half * width :, :] = docs.astype(jnp.bfloat16)
-
     twice = jnp.concatenate([out_proj_ref[...], out_proj_ref[...]], axis=0)
     rows_ref[...] = lax.dot_general(
         hidden_ref[...], twice, (((1,), (1,)), ((), ())), preferred_element_type=jnp.float32
@@ -60,39 +72,68 @@
     wire_ref[0, start + half :, :] = low
 
 
-def project(activations, flat_hidden, in_projection, out_projection, inverse_out, doc_rows, quarters, top):
+def project(place, activations, flat_hidden, in_projection, out_projection, quarters, top, turn, packed=()):
     tokens, model = activations.shape
-    width = in_projection.shape[0]
     quarter = tokens // quarters
     wire_rows = top // 2 * quarter + quarter
-    shared_rows = inverse_out.shape[0] // 2 * width + DOC_ROWS
+
+    def rows(g, place_ref):
+        return jnp.bitwise_xor(place_ref[1], turn(g)), 0
+
+    def fixed(array):
+        return pl.BlockSpec(array.shape, lambda g, place_ref: (0,) * array.ndim)
+
+    out_specs = [pl.BlockSpec((1, wire_rows, LANES), lambda g, place_ref: (g, 0, 0))]
+    out_shape = [jax.ShapeDtypeStruct((quarters // 2, wire_rows, LANES), jnp.bfloat16)]
+    if packed:
+        experts, width, _ = packed[0].shape
+        out_shape.append(jax.ShapeDtypeStruct((experts // 2 * width + DOC_ROWS, LANES), jnp.bfloat16))
+        out_specs.append(fixed(out_shape[1]))
     return pl.pallas_call(
         functools.partial(project_kernel, top=top),
-        grid=(quarters,),
-        in_specs=[
-            pl.BlockSpec((quarter, model), lambda q: (q, 0)),
-            pl.BlockSpec((quarter * top, flat_hidden.shape[1]), lambda q: (q, 0)),
-            pl.BlockSpec(in_projection.shape, lambda q: (0, 0)),
-            pl.BlockSpec(out_projection.shape, lambda q: (0, 0)),
-            pl.BlockSpec(inverse_out.shape, lambda q: (0, 0, 0)),
-            pl.BlockSpec(doc_rows.shape, lambda q: (0, 0)),
-        ],
-        out_specs=[
-            pl.BlockSpec((1, wire_rows, LANES), lambda q: (q, 0, 0)),
-            pl.BlockSpec((shared_rows, LANES), lambda q: (0, 0)),
-        ],
-        out_shape=[
-            jax.ShapeDtypeStruct((quarters, wire_rows, LANES), jnp.bfloat16),
-            jax.ShapeDtypeStruct((shared_rows, LANES), jnp.bfloat16),
-        ],
-        scratch_shapes=[pltpu.VMEM((quarter * top, LANES), jnp.float32)],
-        compiler_params=pltpu.CompilerParams(vmem_limit_bytes=60 * MIB),
-    )(activations, flat_hidden, in_projection, out_projection, inverse_out, doc_rows)
-
-
-def expand_kernel(place_ref, *refs, width, experts, shares):
-    *shared_refs, weights_ref, docs_ref = refs
-    owners = len(shared_refs)
+        grid_spec=pltpu.PrefetchScalarGridSpec(
+            num_scalar_prefetch=1,
+            grid=(quarters // 2,),
+            in_specs=[
+                pl.BlockSpec((quarter, model), rows),
+                pl.BlockSpec((quarter * top, flat_hidden.shape[1]), rows),
+                fixed(in_projection),
+                fixed(out_projection),
+            ]
+            + [fixed(array) for array in packed],
+            out_specs=out_specs,
+            scratch_shapes=[pltpu.VMEM((quarter * top, LANES), jnp.float32)],
+        ),
+        out_shape=out_shape,
+        compiler_params=pltpu.CompilerParams(vmem_limit_bytes=57 * MIB),
+        cost_estimate=cost(3),
+    )(place, activations, flat_hidden, in_projection, out_projection, *packed)
+
+
+def combine_kernel(own_ref, other_ref, out_ref, *, value_rows):
+    total = own_ref[0, :value_rows, :].astype(jnp.float32) + other_ref[1, :value_rows, :].astype(jnp.float32)
+    out_ref[:value_rows, :] = total.astype(jnp.bfloat16)
+    half = (out_ref.shape[0] - value_rows) // 2
+    exact = jnp.zeros((half, LANES), jnp.float32)
+    for part in (own_ref[0], other_ref[1]):
+        exact = exact + part[value_rows : value_rows + half].astype(jnp.float32)
+        exact = exact + part[value_rows + half :].astype(jnp.float32)
+    high, low = split(exact)
+    out_ref[value_rows : value_rows + half, :] = high
+    out_ref[value_rows + half :, :] = low
+
+
+def combine(own, other, value_rows):
+    return pl.pallas_call(
+        functools.partial(combine_kernel, value_rows=value_rows),
+        in_specs=[VMEM, VMEM],
+        out_shape=jax.ShapeDtypeStruct(own.shape[1:], jnp.bfloat16),
+        compiler_params=pltpu.CompilerParams(vmem_limit_bytes=40 * MIB),
+        cost_estimate=cost(1),
+    )(own, other)
+
+
+def expand_kernel(place_ref, shared_ref, weights_ref, docs_ref, *, width, experts, shares, turns):
     columns = experts * width
     share_rows = width // shares
     half = experts // 2
@@ -104,33 +145,34 @@
     for side in range(2):
         spread = (row == source + side * width).astype(jnp.float32).astype(jnp.bfloat16)
         own = expert_lane == expert_row + side * half
-        for step in range(owners):
+        for entry, turn in enumerate(turns):
             placed = jnp.dot(
-                shared_refs[step][: half * width, :], spread, preferred_element_type=jnp.float32
+                shared_ref[entry, : half * width, :], spread, preferred_element_type=jnp.float32
             )
-            weights_ref[step, side * half * width : (side + 1) * half * width, :] = jnp.where(
+            weights_ref[turn, side * half * width : (side + 1) * half * width, :] = jnp.where(
                 own, placed, 0.0
             ).astype(jnp.bfloat16)
-    for step in range(owners):
-        owner = lax.rem(place_ref[0] + owners - step, owners)
-        docs_ref[owner] = shared_refs[step][half * width :, :].astype(jnp.float32).astype(jnp.int32)
-
-
-def expand(place, shared, width, experts, shares):
-    owners = len(shared)
-    return pl.pallas_call(
-        functools.partial(expand_kernel, width=width, experts=experts, shares=shares),
-        in_specs=[SMEM] + [VMEM] * owners,
+    for entry, turn in enumerate(turns):
+        owner = jnp.bitwise_xor(place_ref[0], turn)
+        docs_ref[owner] = shared_ref[entry, half * width :, :].astype(jnp.float32).astype(jnp.int32)
+
+
+def expand(place, shared, turns, width, experts, shares):
+    owners = shared.shape[0]
+    return pl.pallas_call(
+        functools.partial(expand_kernel, width=width, experts=experts, shares=shares, turns=turns),
+        in_specs=[SMEM, VMEM],
         out_shape=[
             jax.ShapeDtypeStruct((owners, experts * width, experts * width), jnp.bfloat16),
             jax.ShapeDtypeStruct((owners, DOC_ROWS, LANES), jnp.int32),
         ],
         compiler_params=pltpu.CompilerParams(vmem_limit_bytes=40 * MIB),
-    )(place, *shared)
+        cost_estimate=cost(1.3),
+    )(place, shared)
 
 
 def condition_kernel(
-    place_ref, parts_ref, routes_ref, weights_ref, payload_ref, inner_ref, value_ref, name_ref, *, top, width
+    place_ref, own_ref, near_ref, far_ref, routes_ref, weights_ref, payload_ref, value_ref, name_ref, *, top, width
 ):
     quarter = routes_ref.shape[0]
     groups, dense_width, _ = weights_ref.shape
@@ -140,10 +182,9 @@
     second = 1 - first.astype(jnp.int32)
 
     def summed(start, size):
-        total = parts_ref[0, start : start + size, :].astype(jnp.float32)
-        for source in range(1, parts_ref.shape[0]):
-            total = total + parts_ref[source, start : start + size, :].astype(jnp.float32)
-        return total
+        rows = slice(start, start + size)
+        total = own_ref[1, rows, :].astype(jnp.float32) + near_ref[0, rows, :].astype(jnp.float32)
+        return total + far_ref[rows, :].astype(jnp.float32)
 
     for pair in range(top // 2):
         both = summed(pair * quarter, quarter)
@@ -155,10 +196,10 @@
     half = quarter // 2
     inner = summed(top // 2 * quarter, half) + summed(top // 2 * quarter + half, half)
     inner = jnp.concatenate([inner[:, :width], inner[:, width:]], axis=0)
-    inner_ref[...] = jnp.transpose(inner).astype(jnp.bfloat16)
+    inner = jnp.transpose(inner).astype(jnp.bfloat16)
 
     def one_group(step, carry):
-        group = lax.rem(place_ref[0] + groups - step, groups)
+        group = jnp.bitwise_xor(place_ref[0], step)
         dense = []
         for pair in range(experts // 2):
             base = group * experts + 2 * pair
@@ -171,28 +212,28 @@
         ).astype(jnp.bfloat16)
         share_width = result.shape[1] // shares
         for share in range(shares):
-            payload_ref[group * shares + share] = result[:, share * share_width : (share + 1) * share_width]
+            piece = result[:, share * share_width : (share + 1) * share_width]
+            payload_ref[group * shares + share, :quarter, :] = piece
+            payload_ref[group * shares + share, quarter:, :] = inner
         return carry
 
     lax.fori_loop(0, groups, one_group, 0, unroll=groups <= 4)
 
 
-def condition(place, parts, quarter_routes, weights, shares, width):
+def condition(place, own, near, far, quarter_routes, weights, shares, width):
     quarter, top = quarter_routes.shape
     groups = weights.shape[0]
     return pl.pallas_call(
         functools.partial(condition_kernel, top=top, width=width),
-        in_specs=[SMEM, VMEM, VMEM, VMEM],
-        out_shape=[
-            jax.ShapeDtypeStruct((groups * shares, quarter, LANES), jnp.bfloat16),
-            jax.ShapeDtypeStruct((width, quarter), jnp.bfloat16),
-        ],
+        in_specs=[SMEM] + [VMEM] * 5,
+        out_shape=jax.ShapeDtypeStruct((groups * shares, quarter + width, LANES), jnp.bfloat16),
         scratch_shapes=[
             pltpu.VMEM((top, quarter, LANES), jnp.float32),
             pltpu.VMEM((top, quarter, LANES), jnp.int32),
         ],
         compiler_params=pltpu.CompilerParams(vmem_limit_bytes=40 * MIB),
-    )(place, parts, quarter_routes, weights)
+        cost_estimate=cost(2),
+    )(place, own, near, far, quarter_routes, weights)
 
 
 def query_kernel(query_ref, inverse_ref, out_ref, factor_ref, spread_ref, wide_ref):
@@ -249,23 +290,20 @@
             pltpu.VMEM((count * experts, LANES), jnp.float32),
             pltpu.VMEM((count // LANES, rows, LANES), jnp.float32),
         ],
-        compiler_params=pltpu.CompilerParams(vmem_limit_bytes=40 * MIB),
+        compiler_params=pltpu.CompilerParams(vmem_limit_bytes=57 * MIB),
+        cost_estimate=cost(10),
     )(query_grads, inverse_in)
 
 
-def score_kernel(place_ref, arrived_ref, docs_ref, *refs, width, doc_count, shares):
-    *inner_refs, queries_ref, out_ref, grads_ref = refs
-    owners = arrived_ref.shape[0] // shares
-    outer, inner, docs = [], [], []
-    for turn in range(shares):
-        share = lax.rem(place_ref[1] + shares - turn, shares)
-        for step in range(owners):
-            owner = lax.rem(place_ref[0] + owners - step, owners)
-            outer.append(arrived_ref[owner * shares + share])
-            docs.append(docs_ref[owner, pl.ds(share, 1), :])
-            inner.append(inner_refs[turn][step])
-    outer = jnp.concatenate(outer, axis=0)
-    inner = jnp.concatenate(inner, axis=1)
+def score_kernel(arrived_ref, docs_ref, far_ref, out_ref, grads_ref, queries_ref, sem, *, width, doc_count, shares):
+    fetch = pltpu.make_async_copy(far_ref, queries_ref, sem)
+    fetch.start()
+    sources, rows, lanes = arrived_ref.shape
+    owners = sources // shares
+    quarter = rows - width
+    outer = arrived_ref[:, :quarter, :].reshape(sources * quarter, lanes)
+    inner = jnp.concatenate([arrived_ref[s, quarter:, :] for s in range(sources)], axis=1)
+    docs = [docs_ref[s // shares, s % shares : s % shares + 1, :] for s in range(sources)]
     docs = jnp.broadcast_to(jnp.concatenate(docs, axis=1), inner.shape)
     doc_group = 8
 
@@ -286,6 +324,7 @@
         high.append(parts[0])
         low.append(parts[1])
     flat = jnp.concatenate([jnp.concatenate(high, axis=1), jnp.concatenate(low, axis=1)], axis=0)
+    fetch.wait()
     result = jnp.dot(flat, queries_ref[...], preferred_element_type=jnp.float32)
     result = result[:doc_count] + result[doc_count:]
     columns = result.shape[1] // shares
@@ -296,16 +335,21 @@
             out_ref[owner * shares + share] = jnp.concatenate([piece, fill], axis=1)
 
 
-def score(place, arrived, docs, inner, queries, width, shares):
+def score(arrived, docs, queries, width, shares):
     sources = arrived.shape[0]
     doc_count = DOC_DEV * sources // shares
     return pl.pallas_call(
         functools.partial(score_kernel, width=width, doc_count=doc_count, shares=shares),
-        in_specs=[SMEM, VMEM, VMEM] + [VMEM] * len(inner) + [VMEM],
+        in_specs=[VMEM, VMEM, pl.BlockSpec(memory_space=pl.ANY)],
         out_shape=jax.ShapeDtypeStruct((sources, DOC_DEV, LANES), jnp.float32),
-        scratch_shapes=[pltpu.VMEM((doc_count * width, arrived.shape[2]), jnp.float32)],
-        compiler_params=pltpu.CompilerParams(vmem_limit_bytes=40 * MIB),
-    )(place, arrived, docs, *inner, queries)
+        scratch_shapes=[
+            pltpu.VMEM((doc_count * width, arrived.shape[2]), jnp.float32),
+            pltpu.VMEM(queries.shape, jnp.bfloat16),
+            pltpu.SemaphoreType.DMA,
+        ],
+        compiler_params=pltpu.CompilerParams(vmem_limit_bytes=57 * MIB),
+        cost_estimate=cost(5),
+    )(arrived, docs, queries)
 
 
 def sum_kernel(pieces_ref, out_ref):
@@ -323,11 +367,13 @@
     )(pieces)
 
 
-def gather_turned(block, axis, size):
-    arrived = [block]
-    for step in range(1, size):
-        arrived.append(lax.ppermute(block, axis, [(i, (i + step) % size) for i in range(size)]))
-    return arrived
+def exchange(block, axis, size, turn):
+    return lax.ppermute(block, axis, [(i, i ^ turn) for i in range(size)])
+
+
+def double(blocks, turns, axis, size, turn):
+    blocks = jnp.concatenate([blocks, exchange(blocks, axis, size, turn)], axis=0)
+    return blocks, turns + tuple(t ^ turn for t in turns)
 
 
 def local(
@@ -347,28 +393,30 @@
     shares = lax.axis_size("proj")
     quarter = tokens // shares
     assert quarter == LANES and 2 * width == LANES and experts * width // shares == LANES
+    assert shares == 4 and owners & (owners - 1) == 0
     assert DOC_DEV * owners <= 256
     place = jnp.stack([lax.axis_index("expert"), lax.axis_index("proj")]).astype(jnp.int32)
 
     flat_hidden = grad_hidden.reshape(tokens * top, grad_hidden.shape[2])
-    wire, shared = project(
-        activations,
-        flat_hidden,
-        in_projection,
-        out_projection,
-        inverse_out,
-        doc_ids.reshape(shares, quarter),
-        shares,
-        top,
+    factors = (activations, flat_hidden, in_projection, out_projection, shares, top)
+    leaving, shared = project(
+        place, *factors, lambda g: 2 * g + 1, (inverse_out, doc_ids.reshape(shares, quarter))
     )
-    parts = lax.all_to_all(wire, "proj", 0, 0, tiled=True)
-    weights, all_docs = expand(place, gather_turned(shared, "expert", owners), width, experts, shares)
+    near = exchange(leaving, "proj", shares, 1)
+    first = exchange(shared, "expert", owners, owners // 2)
+    (own,) = project(place, *factors, lambda g: 2 - 2 * g)
+    first, own = lax.optimization_barrier((first, own))
+    shared, turns = jnp.stack([shared, first]), (0, owners // 2)
+    for bit in reversed(range((owners // 2).bit_length() - 1)):
+        shared, turns = double(shared, turns, "expert", owners, 1 << bit)
+    far = exchange(combine(own, near, top // 2 * quarter), "proj", shares, 2)
+    weights, all_docs = expand(place, shared, turns, width, experts, shares)
     quarter_routes = lax.dynamic_slice_in_dim(routes, lax.axis_index("proj") * quarter, quarter, 0)
-    payload, inner = condition(place, parts, quarter_routes, weights, shares, width)
+    payload = condition(place, own, near, far, quarter_routes, weights, shares, width)
+    payload, query_grads = lax.optimization_barrier((payload, query_grads))
     arrived = lax.all_to_all(payload, ("expert", "proj"), 0, 0, tiled=True)
-    inner = gather_turned(jnp.stack(gather_turned(inner, "expert", owners)), "proj", shares)
     queries = condition_queries(query_grads, inverse_in)
-    partial_scores = score(place, arrived, all_docs, inner, queries, width, shares)
+    partial_scores = score(arrived, all_docs, queries, width, shares)
     pieces = lax.all_to_all(partial_scores, ("expert", "proj"), 0, 0, tiled=True)
     return sum_pieces(pieces, query_grads.shape[0] // shares).T
 

time: 83 us -> 71.4 us (0.86)
  waiting for transfers between devices: 18.3 us -> 9.49 us
  starting transfers between devices: 20.7 us -> 12.1 us
  Pallas kernels: 25.5 us -> 32.2 us
  local copies, waits for them, and re-layouts: 7.3 us -> 3.58 us
  blocking collectives: 10.5 us -> 12.5 us
    ppermute x9 -> x4, waiting for transfers between devices: 18.3 us -> 2.92 us  [exchange(): return lax.ppermute(block, axis, [(i, i ^ turn) for i in range(size)])]
    all_to_all x1, waiting for transfers between devices: 0.01 us -> 6.57 us  [local(): arrived = lax.all_to_all(payload, ('expert', 'proj'), 0, 0, tiled=True)]
    ppermute x9 -> x4, starting transfers between devices: 12 us -> 6.85 us  [exchange(): return lax.ppermute(block, axis, [(i, i ^ turn) for i in range(size)])]
    all_to_all x1 -> x0, starting transfers between devices: 4.35 us -> none  [local(): parts = lax.all_to_all(wire, 'proj', 0, 0, tiled=True)]
    unnamed x13 -> x15, local copies, waits for them, and re-layouts: 7.3 us -> 3.58 us
    pallas_call x1 -> x3, Pallas kernels: 5.66 us -> 8.23 us  [the longest x2 8.19 us: project(): pl.pallas_call(functools.partial(project_kernel, top=top), grid_spec=pltp...]
    pallas_call x1, Pallas kernels: 10.1 us -> 12.1 us  [condition_queries(): pl.pallas_call(query_kernel, grid=(flat // LANES,), in_specs=[pl.BlockSpe...]
    all_to_all x1, blocking collectives: 10.5 us -> 12.5 us  [local(): lax.all_to_all(partial_scores, ('expert', 'proj'), 0, 0, tiled=True)]
  transfers between devices with their start and end apart: 11 -> 5, of which waited for: 4 -> 4; matrix products, arithmetic and copies ran while one was open for 0% -> 0% of each run, Pallas kernels for 14% -> 25%
where the time goes in v4:
time: 71.4 us; the launch traced here: 70.7 us
  Pallas kernels  32.2 us (45%)
  blocking collectives  12.5 us (18%)
  starting transfers between devices  12.1 us (17%)
  waiting for transfers between devices  9.49 us (13%)
  local copies, waits for them, and re-layouts  3.58 us (5%)
    all_to_all x1, blocking collectives, local(): lax.all_to_all(partial_scores, ('expert', 'proj'), 0, 0, tiled=True)  12.5 us
    pallas_call x1, Pallas kernels, condition_queries(): pl.pallas_call(query_kernel, grid=(flat // LANES,), in_specs=[pl.BlockSpe...  12.1 us
    pallas_call x2, Pallas kernels, project(): pl.pallas_call(functools.partial(project_kernel, top=top), grid_spec=pltp...  8.19 us
    ppermute x4, starting transfers between devices, exchange(): return lax.ppermute(block, axis, [(i, i ^ turn) for i in range(size)])  6.85 us
    pallas_call x1, Pallas kernels, score(): pl.pallas_call(functools.partial(score_kernel, width=width, doc_count=doc...  6.75 us
    all_to_all x1, waiting for transfers between devices, local(): arrived = lax.all_to_all(payload, ('expert', 'proj'), 0, 0, tiled=True)  6.57 us
    all_to_all x1, starting transfers between devices, local(): arrived = lax.all_to_all(payload, ('expert', 'proj'), 0, 0, tiled=True)  5.27 us
    unnamed x15, local copies, waits for them, and re-layouts  3.58 us
  transfers between devices with their start and end apart: 5, of which 4 were waited for; matrix products, arithmetic and copies ran while one was open for 0% of the time, Pallas kernels for 25%

profile of v4, /device:TPU:0, one launch (start us, length us, event | category | flops | bytes accessed | tf_op | source)
XLA Modules:
  0.0 70.7 jit_solution(16019841688212367983)
XLA Ops:
  0.0 0.0 copy-start
  0.0 0.6 pad_add_fusion.place_ref
  0.7 4.2 %shard_map.91 = (bf16[2,640,128]{2,1,0:T(8,128)(2,1)}, bf16[272,128]{1,0:T(8,128)(2,1)}) custom-call(s32[2]{0:T(128)} %pad_add_fusion.place_ref, bf16[512,1792]{1,0:T(8,128)(2,1)} %act_ref.3, bf16[4096,512]{1,0:T(8,128)(2,1)} %bitcast.7, bf16[64,1792]{1,0:T(8,128)(2,1)} %in_proj_ref.3, bf16[64,512]{1,0:T(8,128)(2,1)} %out_proj_ref.3, f32[8,64,64]{2,1,0:T(8,128)} %refs_0_.1, ...), custom_call_target="tpu_custom_call" | custom-call | bytes 9900000 | tf_op jit(solution)/shard_map/pallas_call | solution.py:92
  4.8 0.0 copy-start.6
  4.9 0.5 collective-permute-start.1
  5.3 0.0 copy-start.4
  5.3 3.7 %collective-permute-start = (bf16[272,128]{1,0:T(8,128)(2,1)}, bf16[272,128]{1,0:T(8,128)(2,1)S(1)}, u32[]{:S(2)}, u32[]{:S(2)}) collective-permute-start(bf16[272,128]{1,0:T(8,128)(2,1)} %get-tuple-element.13), channel_id=1, source_target_pairs={{0,8},{4,12},{8,0},{12,4},{1,9},{5,13},{9,1},{13,5},{2,10},{6,14},... | collective-permute-start | bytes 208904 | tf_op jit(solution)/shard_map/ppermute | solution.py:371
  9.0 4.0 %shard_map.92.own_ref = bf16[2,640,128]{2,1,0:T(8,128)(2,1)} custom-call(s32[2]{0:T(128)} %pad_add_fusion.place_ref, bf16[512,1792]{1,0:T(8,128)(2,1)} %act_ref.3, bf16[4096,512]{1,0:T(8,128)(2,1)} %bitcast.8, bf16[64,1792]{1,0:T(8,128)(2,1)} %in_proj_ref.3, bf16[64,512]{1,0:T(8,128)(2,1)} %out_proj_ref.3), custom_call_target="tpu_custom_call" | custom-call | bytes 9900000 | tf_op jit(solution)/shard_map/pallas_call | solution.py:92
  13.0 0.5 collective-permute-done
  13.5 0.0 copy-done.6
  13.5 1.2 %collective-permute-start.3 = (bf16[2,272,128]{2,1,0:T(8,128)(2,1)S(1)}, bf16[2,272,128]{2,1,0:T(8,128)(2,1)S(1)}, u32[]{:S(2)}, u32[]{:S(2)}) collective-permute-start(bf16[2,272,128]{2,1,0:T(8,128)(2,1)S(1)} %pad_maximum_fusion.1), channel_id=1, source_target_pairs={{0,4},{4,0},{8,12},{12,8},{1,5},{5,1},{9,13},{13,9},{2,6},{6,2},{1... | collective-permute-start | bytes 417800 | tf_op jit(solution)/shard_map/ppermute | solution.py:371
  14.6 0.0 collective-permute-done.1.other_ref.near_ref
  14.6 0.0 copy-start.1
  14.6 1.0 %copy-done.1 = bf16[2,640,128]{2,1,0:T(8,128)(2,1)S(1)} copy-done((bf16[2,640,128]{2,1,0:T(8,128)(2,1)S(1)}, bf16[2,640,128]{2,1,0:T(8,128)(2,1)}, u32[]{:S(2)}) %copy-start.1) | copy-done | bytes 327704
  15.7 1.6 %collective-permute-start.2 = (bf16[640,128]{1,0:T(8,128)(2,1)S(1)}, bf16[640,128]{1,0:T(8,128)(2,1)S(1)}, u32[]{:S(2)}, u32[]{:S(2)}) collective-permute-start(bf16[640,128]{1,0:T(8,128)(2,1)S(1)} %shard_map.93), channel_id=1, source_target_pairs={{0,2},{1,3},{2,0},{3,1},{4,6},{5,7},{6,4},{7,5},{8,10},{9,11},{10,... | collective-permute-start | bytes 491528 | tf_op jit(solution)/shard_map/ppermute | solution.py:371
  17.2 0.0 copy-done
  17.2 0.1 copy.11.routes_ref
  17.3 1.6 %collective-permute-done.3 = bf16[2,272,128]{2,1,0:T(8,128)(2,1)S(1)} collective-permute-done((bf16[2,272,128]{2,1,0:T(8,128)(2,1)S(1)}, bf16[2,272,128]{2,1,0:T(8,128)(2,1)S(1)}, u32[]{:S(2)}, u32[]{:S(2)}) %collective-permute-start.3) | collective-permute-done | bytes 139296 | tf_op jit(solution)/shard_map/ppermute | solution.py:371
  19.0 0.0 copy-done.4
  19.0 1.3 %shard_map.94 = (bf16[4,512,512]{2,1,0:T(8,128)(2,1)S(1)}, s32[4,16,128]{2,1,0:T(8,128)S(1)}) custom-call(s32[2]{0:T(128)S(1)} %copy-done.4, bf16[4,272,128]{2,1,0:T(8,128)(2,1)S(1)} %pad_maximum_fusion.shared_ref), custom_call_target="tpu_custom_call" | custom-call | bytes 4290000 | tf_op jit(solution)/shard_map/pallas_call | solution.py:162
  20.3 0.0 copy-start.3
  20.3 0.6 copy-done.3
  20.9 0.8 %collective-permute-done.2.far_ref = bf16[640,128]{1,0:T(8,128)(2,1)S(1)} collective-permute-done((bf16[640,128]{1,0:T(8,128)(2,1)S(1)}, bf16[640,128]{1,0:T(8,128)(2,1)S(1)}, u32[]{:S(2)}, u32[]{:S(2)}) %collective-permute-start.2) | collective-permute-done | bytes 163872 | tf_op jit(solution)/shard_map/ppermute | solution.py:371
  21.7 0.0 copy-start.2
  21.7 1.0 %copy-done.2 = bf16[2,640,128]{2,1,0:T(8,128)(2,1)S(1)} copy-done((bf16[2,640,128]{2,1,0:T(8,128)(2,1)S(1)}, bf16[2,640,128]{2,1,0:T(8,128)(2,1)}, u32[]{:S(2)}) %copy-start.2) | copy-done | bytes 327704
  22.7 2.4 %shard_map.95 = bf16[16,192,128]{2,1,0:T(8,128)(2,1)} custom-call(s32[2]{0:T(128)S(1)} %copy-done.4, bf16[2,640,128]{2,1,0:T(8,128)(2,1)S(1)} %copy-done.2, bf16[2,640,128]{2,1,0:T(8,128)(2,1)S(1)} %collective-permute-done.1.other_ref.near_ref, bf16[640,128]{1,0:T(8,128)(2,1)S(1)} %collective-permute-done.2.far_ref, s32[128,8]{1,0:T(8,128)S(1)} %copy.11.routes_ref, ...), custom_call_target="tpu_custom_call" | custom-call | bytes 6600000 | tf_op jit(solution)/shard_map/pallas_call | solution.py:226
  25.1 5.3 %all-to-all-start = ((bf16[16,192,128]{2,1,0:T(8,128)(2,1)}), bf16[16,192,128]{2,1,0:T(8,128)(2,1)S(1)}, u32[]{:S(2)}, u32[]{:S(2)}) async-start(bf16[16,192,128]{2,1,0:T(8,128)(2,1)} %shard_map.95), calls=%async_computation | async-start | bytes 1572864 | tf_op jit(solution)/shard_map/all_to_all | solution.py:417
  30.4 12.1 %shard_map.96.far_ref = bf16[8192,256]{1,0:T(8,128)(2,1)} custom-call(bf16[256,8,1024]{2,1,0:T(8,128)(2,1)} %query_ref, f32[8,64,64]{2,1,0:T(8,128)} %inverse_ref.1), custom_call_target="tpu_custom_call" | custom-call | bytes 33000000 | tf_op jit(solution)/shard_map/pallas_call | solution.py:279
  42.5 6.6 %all-to-all-done.arrived_ref = bf16[16,192,128]{2,1,0:T(8,128)(2,1)S(1)} async-done(((bf16[16,192,128]{2,1,0:T(8,128)(2,1)}), bf16[16,192,128]{2,1,0:T(8,128)(2,1)S(1)}, u32[]{:S(2)}, u32[]{:S(2)}) %all-to-all-start) | async-done | bytes 786464 | tf_op jit(solution)/shard_map/all_to_all | solution.py:417
  49.1 0.0 copy-start.5
  49.1 0.9 %copy-done.5 = bf16[16,192,128]{2,1,0:T(8,128)(2,1)} copy-done((bf16[16,192,128]{2,1,0:T(8,128)(2,1)}, bf16[16,192,128]{2,1,0:T(8,128)(2,1)S(1)}, u32[]{:S(2)}) %copy-start.5) | copy-done | bytes 786456
  50.0 6.8 %shard_map.97 = f32[16,8,128]{2,1,0:T(8,128)} custom-call(bf16[16,192,128]{2,1,0:T(8,128)(2,1)} %copy-done.5, s32[4,16,128]{2,1,0:T(8,128)} %copy-done.3, bf16[8192,256]{1,0:T(8,128)(2,1)} %shard_map.96.far_ref), custom_call_target="tpu_custom_call" | custom-call | bytes 16500000 | tf_op jit(solution)/shard_map/pallas_call | solution.py:341
  56.7 12.5 %all_to_all.10.pieces_ref = f32[16,8,128]{2,1,0:T(8,128)} all-to-all(f32[16,8,128]{2,1,0:T(8,128)} %shard_map.97), channel_id=1, replica_groups=mesh['groups'=2,'expert'=4,'proj'=4] {'expert','proj'}, dimensions={0} | all-to-all | bytes 131072 | tf_op jit(solution)/shard_map/all_to_all | solution.py:420
  69.2 1.4 %shard_map.98 = f32[8,64]{1,0:T(8,128)} custom-call(f32[16,8,128]{2,1,0:T(8,128)} %all_to_all.10.pieces_ref), custom_call_target="tpu_custom_call" | custom-call | tf_op jit(solution)/shard_map/pallas_call | solution.py:363
  (4 shorter events, 0.1 us)
Async XLA Ops:
  0.0 17.2 %copy-start = (s32[512,8]{0,1:T(8,128)S(1)}, s32[512,8]{0,1:T(8,128)}, u32[]{:S(2)}) copy-start(s32[512,8]{0,1:T(8,128)} %param.11) | copy-start | bytes 49156
  4.8 8.6 %copy-start.6 = (bf16[272,128]{1,0:T(8,128)(2,1)S(1)}, bf16[272,128]{1,0:T(8,128)(2,1)}, u32[]{:S(2)}) copy-start(bf16[272,128]{1,0:T(8,128)(2,1)} %get-tuple-element.13) | copy-start | bytes 208900
  4.9 9.8 %collective-permute-start.1 = (bf16[2,640,128]{2,1,0:T(8,128)(2,1)}, bf16[2,640,128]{2,1,0:T(8,128)(2,1)S(1)}, u32[]{:S(2)}, u32[]{:S(2)}) collective-permute-start(bf16[2,640,128]{2,1,0:T(8,128)(2,1)} %get-tuple-element.15), channel_id=1, source_target_pairs={{0,1},{1,0},{2,3},{3,2},{4,5},{5,4},{6,7},{7,6},{8,9},{9,8},{10,11... | collective-permute-start | bytes 983048 | tf_op jit(solution)/shard_map/ppermute | solution.py:371
  5.3 13.7 %copy-start.4 = (s32[2]{0:T(128)S(1)}, s32[2]{0:T(128)}, u32[]{:S(2)}) copy-start(s32[2]{0:T(128)} %pad_add_fusion.place_ref) | copy-start | bytes 28
  5.3 8.1 %collective-permute-start = (bf16[272,128]{1,0:T(8,128)(2,1)}, bf16[272,128]{1,0:T(8,128)(2,1)S(1)}, u32[]{:S(2)}, u32[]{:S(2)}) collective-permute-start(bf16[272,128]{1,0:T(8,128)(2,1)} %get-tuple-element.13), channel_id=1, source_target_pairs={{0,8},{4,12},{8,0},{12,4},{1,9},{5,13},{9,1},{13,5},{2,10},{6,14},... | collective-permute-start | bytes 208904 | tf_op jit(solution)/shard_map/ppermute | solution.py:371
  13.5 5.5 %collective-permute-start.3 = (bf16[2,272,128]{2,1,0:T(8,128)(2,1)S(1)}, bf16[2,272,128]{2,1,0:T(8,128)(2,1)S(1)}, u32[]{:S(2)}, u32[]{:S(2)}) collective-permute-start(bf16[2,272,128]{2,1,0:T(8,128)(2,1)S(1)} %pad_maximum_fusion.1), channel_id=1, source_target_pairs={{0,4},{4,0},{8,12},{12,8},{1,5},{5,1},{9,13},{13,9},{2,6},{6,2},{1... | collective-permute-start | bytes 417800 | tf_op jit(solution)/shard_map/ppermute | solution.py:371
  14.6 1.0 %copy-start.1 = (bf16[2,640,128]{2,1,0:T(8,128)(2,1)S(1)}, bf16[2,640,128]{2,1,0:T(8,128)(2,1)}, u32[]{:S(2)}) copy-start(bf16[2,640,128]{2,1,0:T(8,128)(2,1)} %shard_map.92.own_ref) | copy-start | bytes 983044
  15.7 6.1 %collective-permute-start.2 = (bf16[640,128]{1,0:T(8,128)(2,1)S(1)}, bf16[640,128]{1,0:T(8,128)(2,1)S(1)}, u32[]{:S(2)}, u32[]{:S(2)}) collective-permute-start(bf16[640,128]{1,0:T(8,128)(2,1)S(1)} %shard_map.93), channel_id=1, source_target_pairs={{0,2},{1,3},{2,0},{3,1},{4,6},{5,7},{6,4},{7,5},{8,10},{9,11},{10,... | collective-permute-start | bytes 491528 | tf_op jit(solution)/shard_map/ppermute | solution.py:371
  20.3 0.6 copy-start.3
  21.7 1.0 %copy-start.2 = (bf16[2,640,128]{2,1,0:T(8,128)(2,1)S(1)}, bf16[2,640,128]{2,1,0:T(8,128)(2,1)}, u32[]{:S(2)}) copy-start(bf16[2,640,128]{2,1,0:T(8,128)(2,1)} %shard_map.92.own_ref) | copy-start | bytes 983044
  25.1 24.0 %all-to-all-start = ((bf16[16,192,128]{2,1,0:T(8,128)(2,1)}), bf16[16,192,128]{2,1,0:T(8,128)(2,1)S(1)}, u32[]{:S(2)}, u32[]{:S(2)}) async-start(bf16[16,192,128]{2,1,0:T(8,128)(2,1)} %shard_map.95), calls=%async_computation | async-start | bytes 1572864 | tf_op jit(solution)/shard_map/all_to_all | solution.py:417
  49.1 0.9 %copy-start.5 = (bf16[16,192,128]{2,1,0:T(8,128)(2,1)}, bf16[16,192,128]{2,1,0:T(8,128)(2,1)S(1)}, u32[]{:S(2)}) copy-start(bf16[16,192,128]{2,1,0:T(8,128)(2,1)S(1)} %all-to-all-done.arrived_ref) | copy-start | bytes 2359300

commit v5 on v4

--- a/solution.py
+++ b/solution.py
@@ -12,11 +12,15 @@
 DOC_ROWS = 16
 MIB = 1024 * 1024
 VMEM = pl.BlockSpec(memory_space=pltpu.VMEM)
-SMEM = pl.BlockSpec(memory_space=pltpu.SMEM)
+HBM = pl.BlockSpec(memory_space=pltpu.HBM)
 
 
 def low_lanes(rows, width):
     return lax.broadcasted_iota(jnp.int32, (rows, LANES), 1) < width
+
+
+def stay(array):
+    return pltpu.with_memory_space_constraint(array, pltpu.HBM)
 
 
 def split(value):
@@ -39,75 +43,95 @@
     shared_ref[half * width :, :] = docs.astype(jnp.bfloat16)
 
 
-def project_kernel(place_ref, act_ref, hidden_ref, in_proj_ref, out_proj_ref, *refs, top):
-    *pack_refs, rows_ref = refs
-    if len(pack_refs) == 1:
-        wire_ref = pack_refs[0]
-    else:
-        inverse_ref, docs_ref, wire_ref, shared_ref = pack_refs
-
-        @pl.when(pl.program_id(0) == 0)
-        def _():
+def project_kernel(
+    act_hbm, hidden_hbm, in_proj_hbm, out_proj_hbm, inverse_hbm, docs_hbm, leaving_ref, own_ref, shared_ref, *refs, top
+):
+    act_ref, hidden_ref, in_proj_ref, out_proj_ref, inverse_ref, docs_ref, rows_ref, quarter_sems, sems = refs
+    turns = (1, 3, 2, 0)
+    quarter = act_ref.shape[1]
+    width = in_proj_ref.shape[0]
+    place = lax.axis_index("proj")
+    fixed = [
+        pltpu.make_async_copy(source, target, sems.at[i])
+        for i, (source, target) in enumerate(
+            [(out_proj_hbm, out_proj_ref), (in_proj_hbm, in_proj_ref), (inverse_hbm, inverse_ref), (docs_hbm, docs_ref)]
+        )
+    ]
+    fixed[0].start()
+    moving = []
+    for g, turn in enumerate(turns):
+        start = jnp.bitwise_xor(place, turn) * quarter
+        hidden_rows = pl.ds(pl.multiple_of(start * top, quarter * top), quarter * top)
+        act_rows = pl.ds(pl.multiple_of(start, quarter), quarter)
+        moving.append(
+            (
+                pltpu.make_async_copy(hidden_hbm.at[hidden_rows], hidden_ref.at[g], quarter_sems.at[g, 0]),
+                pltpu.make_async_copy(act_hbm.at[act_rows], act_ref.at[g], quarter_sems.at[g, 1]),
+            )
+        )
+        moving[g][0].start()
+        if g == 0:
+            fixed[1].start()
+        moving[g][1].start()
+        if g == 0:
+            fixed[2].start()
+            fixed[3].start()
+    half = quarter // 2
+    first = low_lanes(quarter, width)
+    fixed[0].wait()
+    twice = jnp.concatenate([out_proj_ref[...], out_proj_ref[...]], axis=0)
+    for g in range(len(turns)):
+        wire_ref = leaving_ref.at[g] if g < 2 else own_ref.at[g - 2]
+        moving[g][0].wait()
+        rows_ref[g % 2] = lax.dot_general(
+            hidden_ref[g], twice, (((1,), (1,)), ((), ())), preferred_element_type=jnp.float32
+        )
+        for pair in range(top // 2):
+            even = rows_ref[g % 2, pl.ds(2 * pair, quarter, stride=top), :]
+            odd = rows_ref[g % 2, pl.ds(2 * pair + 1, quarter, stride=top), :]
+            wire_ref[pair * quarter : (pair + 1) * quarter, :] = jnp.where(first, even, odd).astype(jnp.bfloat16)
+        if g == 0:
+            fixed[1].wait()
+        twice_in = jnp.concatenate([in_proj_ref[...], in_proj_ref[...]], axis=0)
+        moving[g][1].wait()
+        inner = lax.dot_general(
+            act_ref[g], twice_in, (((1,), (1,)), ((), ())), preferred_element_type=jnp.float32
+        )
+        high, low = split(jnp.where(low_lanes(half, width), inner[:half], inner[half:]))
+        start = top // 2 * quarter
+        wire_ref[start : start + half, :] = high
+        wire_ref[start + half :, :] = low
+        if g == 0:
+            fixed[2].wait()
+            fixed[3].wait()
             pack_shared(inverse_ref, docs_ref, shared_ref)
 
-    quarter = act_ref.shape[0]
-    width = in_proj_ref.shape[0]
-    twice = jnp.concatenate([out_proj_ref[...], out_proj_ref[...]], axis=0)
-    rows_ref[...] = lax.dot_general(
-        hidden_ref[...], twice, (((1,), (1,)), ((), ())), preferred_element_type=jnp.float32
-    )
-    first = low_lanes(quarter, width)
-    for pair in range(top // 2):
-        even = rows_ref[pl.ds(2 * pair, quarter, stride=top), :]
-        odd = rows_ref[pl.ds(2 * pair + 1, quarter, stride=top), :]
-        wire_ref[0, pair * quarter : (pair + 1) * quarter, :] = jnp.where(first, even, odd).astype(jnp.bfloat16)
-    twice_in = jnp.concatenate([in_proj_ref[...], in_proj_ref[...]], axis=0)
-    inner = lax.dot_general(
-        act_ref[...], twice_in, (((1,), (1,)), ((), ())), preferred_element_type=jnp.float32
-    )
-    half = quarter // 2
-    high, low = split(jnp.where(low_lanes(half, width), inner[:half], inner[half:]))
-    start = top // 2 * quarter
-    wire_ref[0, start : start + half, :] = high
-    wire_ref[0, start + half :, :] = low
-
-
-def project(place, activations, flat_hidden, in_projection, out_projection, quarters, top, turn, packed=()):
+
+def project(activations, flat_hidden, in_projection, out_projection, inverse_out, doc_rows, quarters, top):
     tokens, model = activations.shape
     quarter = tokens // quarters
     wire_rows = top // 2 * quarter + quarter
-
-    def rows(g, place_ref):
-        return jnp.bitwise_xor(place_ref[1], turn(g)), 0
-
-    def fixed(array):
-        return pl.BlockSpec(array.shape, lambda g, place_ref: (0,) * array.ndim)
-
-    out_specs = [pl.BlockSpec((1, wire_rows, LANES), lambda g, place_ref: (g, 0, 0))]
-    out_shape = [jax.ShapeDtypeStruct((quarters // 2, wire_rows, LANES), jnp.bfloat16)]
-    if packed:
-        experts, width, _ = packed[0].shape
-        out_shape.append(jax.ShapeDtypeStruct((experts // 2 * width + DOC_ROWS, LANES), jnp.bfloat16))
-        out_specs.append(fixed(out_shape[1]))
+    experts, width, _ = inverse_out.shape
+    wire = jax.ShapeDtypeStruct((quarters // 2, wire_rows, LANES), jnp.bfloat16)
+    fixed = (in_projection, out_projection, inverse_out, doc_rows)
     return pl.pallas_call(
         functools.partial(project_kernel, top=top),
-        grid_spec=pltpu.PrefetchScalarGridSpec(
-            num_scalar_prefetch=1,
-            grid=(quarters // 2,),
-            in_specs=[
-                pl.BlockSpec((quarter, model), rows),
-                pl.BlockSpec((quarter * top, flat_hidden.shape[1]), rows),
-                fixed(in_projection),
-                fixed(out_projection),
-            ]
-            + [fixed(array) for array in packed],
-            out_specs=out_specs,
-            scratch_shapes=[pltpu.VMEM((quarter * top, LANES), jnp.float32)],
-        ),
-        out_shape=out_shape,
-        compiler_params=pltpu.CompilerParams(vmem_limit_bytes=57 * MIB),
-        cost_estimate=cost(3),
-    )(place, activations, flat_hidden, in_projection, out_projection, *packed)
+        in_specs=[HBM] * 6,
+        out_specs=[VMEM] * 3,
+        out_shape=[wire, wire, jax.ShapeDtypeStruct((experts // 2 * width + DOC_ROWS, LANES), jnp.bfloat16)],
+        scratch_shapes=[
+            pltpu.VMEM((quarters, quarter, model), jnp.bfloat16),
+            pltpu.VMEM((quarters, quarter * top, flat_hidden.shape[1]), jnp.bfloat16),
+        ]
+        + [pltpu.VMEM(array.shape, array.dtype) for array in fixed]
+        + [
+            pltpu.VMEM((2, quarter * top, LANES), jnp.float32),
+            pltpu.SemaphoreType.DMA((quarters, 2)),
+            pltpu.SemaphoreType.DMA((len(fixed),)),
+        ],
+        compiler_params=pltpu.CompilerParams(vmem_limit_bytes=40 * MIB),
+        cost_estimate=cost(5),
+    )(*[stay(array) for array in (activations, flat_hidden, *fixed)])
 
 
 def combine_kernel(own_ref, other_ref, out_ref, *, value_rows):
@@ -133,7 +157,7 @@
     )(own, other)
 
 
-def expand_kernel(place_ref, shared_ref, weights_ref, docs_ref, *, width, experts, shares, turns):
+def expand_kernel(shared_ref, weights_ref, docs_ref, *, width, experts, shares, turns):
     columns = experts * width
     share_rows = width // shares
     half = experts // 2
@@ -153,26 +177,26 @@
                 own, placed, 0.0
             ).astype(jnp.bfloat16)
     for entry, turn in enumerate(turns):
-        owner = jnp.bitwise_xor(place_ref[0], turn)
+        owner = jnp.bitwise_xor(lax.axis_index("expert"), turn)
         docs_ref[owner] = shared_ref[entry, half * width :, :].astype(jnp.float32).astype(jnp.int32)
 
 
-def expand(place, shared, turns, width, experts, shares):
+def expand(shared, turns, width, experts, shares):
     owners = shared.shape[0]
     return pl.pallas_call(
         functools.partial(expand_kernel, width=width, experts=experts, shares=shares, turns=turns),
-        in_specs=[SMEM, VMEM],
+        in_specs=[VMEM],
         out_shape=[
             jax.ShapeDtypeStruct((owners, experts * width, experts * width), jnp.bfloat16),
             jax.ShapeDtypeStruct((owners, DOC_ROWS, LANES), jnp.int32),
         ],
         compiler_params=pltpu.CompilerParams(vmem_limit_bytes=40 * MIB),
         cost_estimate=cost(1.3),
-    )(place, shared)
+    )(shared)
 
 
 def condition_kernel(
-    place_ref, own_ref, near_ref, far_ref, routes_ref, weights_ref, payload_ref, value_ref, name_ref, *, top, width
+    own_ref, near_ref, far_ref, routes_ref, weights_ref, payload_ref, value_ref, name_ref, *, top, width
 ):
     quarter = routes_ref.shape[0]
     groups, dense_width, _ = weights_ref.shape
@@ -199,7 +223,7 @@
     inner = jnp.transpose(inner).astype(jnp.bfloat16)
 
     def one_group(step, carry):
-        group = jnp.bitwise_xor(place_ref[0], step)
+        group = jnp.bitwise_xor(lax.axis_index("expert"), step)
         dense = []
         for pair in range(experts // 2):
             base = group * experts + 2 * pair
@@ -220,12 +244,12 @@
     lax.fori_loop(0, groups, one_group, 0, unroll=groups <= 4)
 
 
-def condition(place, own, near, far, quarter_routes, weights, shares, width):
+def condition(own, near, far, quarter_routes, weights, shares, width):
     quarter, top = quarter_routes.shape
     groups = weights.shape[0]
     return pl.pallas_call(
         functools.partial(condition_kernel, top=top, width=width),
-        in_specs=[SMEM] + [VMEM] * 5,
+        in_specs=[VMEM] * 5,
         out_shape=jax.ShapeDtypeStruct((groups * shares, quarter + width, LANES), jnp.bfloat16),
         scratch_shapes=[
             pltpu.VMEM((top, quarter, LANES), jnp.float32),
@@ -233,7 +257,7 @@
         ],
         compiler_params=pltpu.CompilerParams(vmem_limit_bytes=40 * MIB),
         cost_estimate=cost(2),
-    )(place, own, near, far, quarter_routes, weights)
+    )(own, near, far, quarter_routes, weights)
 
 
 def query_kernel(query_ref, inverse_ref, out_ref, factor_ref, spread_ref, wide_ref):
@@ -290,9 +314,9 @@
             pltpu.VMEM((count * experts, LANES), jnp.float32),
             pltpu.VMEM((count // LANES, rows, LANES), jnp.float32),
         ],
-        compiler_params=pltpu.CompilerParams(vmem_limit_bytes=57 * MIB),
+        compiler_params=pltpu.CompilerParams(vmem_limit_bytes=40 * MIB),
         cost_estimate=cost(10),
-    )(query_grads, inverse_in)
+    )(stay(query_grads), inverse_in)
 
 
 def score_kernel(arrived_ref, docs_ref, far_ref, out_ref, grads_ref, queries_ref, sem, *, width, doc_count, shares):
@@ -340,16 +364,16 @@
     doc_count = DOC_DEV * sources // shares
     return pl.pallas_call(
         functools.partial(score_kernel, width=width, doc_count=doc_count, shares=shares),
-        in_specs=[VMEM, VMEM, pl.BlockSpec(memory_space=pl.ANY)],
+        in_specs=[VMEM, VMEM, HBM],
         out_shape=jax.ShapeDtypeStruct((sources, DOC_DEV, LANES), jnp.float32),
         scratch_shapes=[
             pltpu.VMEM((doc_count * width, arrived.shape[2]), jnp.float32),
             pltpu.VMEM(queries.shape, jnp.bfloat16),
             pltpu.SemaphoreType.DMA,
         ],
-        compiler_params=pltpu.CompilerParams(vmem_limit_bytes=57 * MIB),
+        compiler_params=pltpu.CompilerParams(vmem_limit_bytes=40 * MIB),
         cost_estimate=cost(5),
-    )(arrived, docs, queries)
+    )(arrived, docs, stay(queries))
 
 
 def sum_kernel(pieces_ref, out_ref):
@@ -395,24 +419,21 @@
     assert quarter == LANES and 2 * width == LANES and experts * width // shares == LANES
     assert shares == 4 and owners & (owners - 1) == 0
     assert DOC_DEV * owners <= 256
-    place = jnp.stack([lax.axis_index("expert"), lax.axis_index("proj")]).astype(jnp.int32)
 
     flat_hidden = grad_hidden.reshape(tokens * top, grad_hidden.shape[2])
-    factors = (activations, flat_hidden, in_projection, out_projection, shares, top)
-    leaving, shared = project(
-        place, *factors, lambda g: 2 * g + 1, (inverse_out, doc_ids.reshape(shares, quarter))
+    doc_rows = doc_ids.reshape(shares, quarter)
+    leaving, own, shared = project(
+        activations, flat_hidden, in_projection, out_projection, inverse_out, doc_rows, shares, top
     )
     near = exchange(leaving, "proj", shares, 1)
     first = exchange(shared, "expert", owners, owners // 2)
-    (own,) = project(place, *factors, lambda g: 2 - 2 * g)
-    first, own = lax.optimization_barrier((first, own))
     shared, turns = jnp.stack([shared, first]), (0, owners // 2)
     for bit in reversed(range((owners // 2).bit_length() - 1)):
         shared, turns = double(shared, turns, "expert", owners, 1 << bit)
     far = exchange(combine(own, near, top // 2 * quarter), "proj", shares, 2)
-    weights, all_docs = expand(place, shared, turns, width, experts, shares)
+    weights, all_docs = expand(shared, turns, width, experts, shares)
     quarter_routes = lax.dynamic_slice_in_dim(routes, lax.axis_index("proj") * quarter, quarter, 0)
-    payload = condition(place, own, near, far, quarter_routes, weights, shares, width)
+    payload = condition(own, near, far, quarter_routes, weights, shares, width)
     payload, query_grads = lax.optimization_barrier((payload, query_grads))
     arrived = lax.all_to_all(payload, ("expert", "proj"), 0, 0, tiled=True)
     queries = condition_queries(query_grads, inverse_in)

time: 71.4 us -> 68.6 us (0.961)
  Pallas kernels: 32.2 us -> 26.9 us
  waiting for transfers between devices: 9.49 us -> 14.4 us
  local copies, waits for them, and re-layouts: 3.58 us -> 2.06 us
    ppermute x4, waiting for transfers between devices: 2.92 us -> 7.77 us  [exchange(): return lax.ppermute(block, axis, [(i, i ^ turn) for i in range(size)])]
    pallas_call x1, Pallas kernels: 12.1 us -> 10.1 us  [condition_queries(): pl.pallas_call(query_kernel, grid=(flat // LANES,), in_specs=[pl.BlockSpe...]
    pallas_call x2 -> x1, Pallas kernels: 8.19 us -> 6.18 us  [project(): pl.pallas_call(functools.partial(project_kernel, top=top), in_specs=[HBM]...]
    unnamed x15 -> x7, local copies, waits for them, and re-layouts: 3.58 us -> 2.06 us
  transfers between devices with their start and end apart: 5 -> 5, of which waited for: 4 -> 4; matrix products, arithmetic and copies ran while one was open for 0% -> 0% of each run, Pallas kernels for 25% -> 16%
where the time goes in v5:
time: 68.6 us; the launch traced here: 68 us
  Pallas kernels  26.9 us (39%)
  waiting for transfers between devices  14.4 us (21%)
  blocking collectives  12.3 us (18%)
  starting transfers between devices  12.2 us (18%)
  local copies, waits for them, and re-layouts  2.06 us (3%)
    all_to_all x1, blocking collectives, local(): lax.all_to_all(partial_scores, ('expert', 'proj'), 0, 0, tiled=True)  12.3 us
    pallas_call x1, Pallas kernels, condition_queries(): pl.pallas_call(query_kernel, grid=(flat // LANES,), in_specs=[pl.BlockSpe...  10.1 us
    ppermute x4, waiting for transfers between devices, exchange(): return lax.ppermute(block, axis, [(i, i ^ turn) for i in range(size)])  7.77 us
    all_to_all x1, waiting for transfers between devices, local(): arrived = lax.all_to_all(payload, ('expert', 'proj'), 0, 0, tiled=True)  6.64 us
    pallas_call x1, Pallas kernels, score(): pl.pallas_call(functools.partial(score_kernel, width=width, doc_count=doc...  6.59 us
    ppermute x4, starting transfers between devices, exchange(): return lax.ppermute(block, axis, [(i, i ^ turn) for i in range(size)])  6.55 us
    pallas_call x1, Pallas kernels, project(): pl.pallas_call(functools.partial(project_kernel, top=top), in_specs=[HBM]...  6.18 us
    all_to_all x1, starting transfers between devices, local(): arrived = lax.all_to_all(payload, ('expert', 'proj'), 0, 0, tiled=True)  5.68 us
  transfers between devices with their start and end apart: 5, of which 4 were waited for; matrix products, arithmetic and copies ran while one was open for 0% of the time, Pallas kernels for 16%

profile of v5, /device:TPU:0, one launch (start us, length us, event | category | flops | bytes accessed | tf_op | source)
XLA Modules:
  0.0 68.0 jit_solution(16379017552980798816)
XLA Ops:
  0.0 0.0 copy-start
  0.0 6.2 %shard_map.91 = (bf16[2,640,128]{2,1,0:T(8,128)(2,1)S(1)}, bf16[2,640,128]{2,1,0:T(8,128)(2,1)S(1)}, bf16[272,128]{1,0:T(8,128)(2,1)S(1)}) custom-call(bf16[512,1792]{1,0:T(8,128)(2,1)} %act_hbm.1, bf16[4096,512]{1,0:T(8,128)(2,1)} %bitcast.7, bf16[64,1792]{1,0:T(8,128)(2,1)} %in_proj_hbm.1, bf16[64,512]{1,0:T(8,128)(2,1)} %out_proj_hbm.1, ...), custom_call_target="tpu_custom_call" | custom-call | bytes 16500000 | tf_op jit(solution)/shard_map/pallas_call | solution.py:117
  6.2 0.0 copy-start.2
  6.2 0.5 collective-permute-start
  6.7 3.7 %collective-permute-start.2 = (bf16[272,128]{1,0:T(8,128)(2,1)S(1)}, bf16[272,128]{1,0:T(8,128)(2,1)S(1)}, u32[]{:S(2)}, u32[]{:S(2)}) collective-permute-start(bf16[272,128]{1,0:T(8,128)(2,1)S(1)} %get-tuple-element.14), channel_id=1, source_target_pairs={{0,8},{4,12},{8,0},{12,4},{1,9},{5,13},{9,1},{13,5},{2,10},{6,14},... | collective-permute-start | bytes 208904 | tf_op jit(solution)/shard_map/ppermute | solution.py:395
  10.4 4.3 %collective-permute-done.2 = bf16[272,128]{1,0:T(8,128)(2,1)S(1)} collective-permute-done((bf16[272,128]{1,0:T(8,128)(2,1)S(1)}, bf16[272,128]{1,0:T(8,128)(2,1)S(1)}, u32[]{:S(2)}, u32[]{:S(2)}) %collective-permute-start.2) | collective-permute-done | bytes 69664 | tf_op jit(solution)/shard_map/ppermute | solution.py:395
  14.7 0.8 %collective-permute-start.3 = (bf16[2,272,128]{2,1,0:T(8,128)(2,1)S(1)}, bf16[2,272,128]{2,1,0:T(8,128)(2,1)S(1)}, u32[]{:S(2)}, u32[]{:S(2)}) collective-permute-start(bf16[2,272,128]{2,1,0:T(8,128)(2,1)S(1)} %pad_maximum_fusion.1), channel_id=1, source_target_pairs={{0,4},{4,0},{8,12},{12,8},{1,5},{5,1},{9,13},{13,9},{2,6},{6,2},{1... | collective-permute-start | bytes 417800 | tf_op jit(solution)/shard_map/ppermute | solution.py:395
  15.5 0.0 collective-permute-done.other_ref.near_ref
  15.5 1.6 %collective-permute-start.1 = (bf16[640,128]{1,0:T(8,128)(2,1)S(1)}, bf16[640,128]{1,0:T(8,128)(2,1)S(1)}, u32[]{:S(2)}, u32[]{:S(2)}) collective-permute-start(bf16[640,128]{1,0:T(8,128)(2,1)S(1)} %shard_map.92), channel_id=1, source_target_pairs={{0,2},{1,3},{2,0},{3,1},{4,6},{5,7},{6,4},{7,5},{8,10},{9,11},{10,... | collective-permute-start | bytes 491528 | tf_op jit(solution)/shard_map/ppermute | solution.py:395
  17.1 0.0 copy-done
  17.1 0.1 copy.11.routes_ref
  17.2 3.0 %collective-permute-done.3 = bf16[2,272,128]{2,1,0:T(8,128)(2,1)S(1)} collective-permute-done((bf16[2,272,128]{2,1,0:T(8,128)(2,1)S(1)}, bf16[2,272,128]{2,1,0:T(8,128)(2,1)S(1)}, u32[]{:S(2)}, u32[]{:S(2)}) %collective-permute-start.3) | collective-permute-done | bytes 139296 | tf_op jit(solution)/shard_map/ppermute | solution.py:395
  20.2 0.7 %shard_map.93 = (bf16[4,512,512]{2,1,0:T(8,128)(2,1)S(1)}, s32[4,16,128]{2,1,0:T(8,128)S(1)}) custom-call(bf16[4,272,128]{2,1,0:T(8,128)(2,1)S(1)} %pad_maximum_fusion.shared_ref), custom_call_target="tpu_custom_call" | custom-call | bytes 4290000 | tf_op jit(solution)/shard_map/pallas_call | solution.py:186
  20.9 0.5 collective-permute-done.1.far_ref
  21.5 1.8 %shard_map.94 = bf16[16,192,128]{2,1,0:T(8,128)(2,1)} custom-call(bf16[2,640,128]{2,1,0:T(8,128)(2,1)S(1)} %get-tuple-element.12.own_ref, bf16[2,640,128]{2,1,0:T(8,128)(2,1)S(1)} %collective-permute-done.other_ref.near_ref, bf16[640,128]{1,0:T(8,128)(2,1)S(1)} %collective-permute-done.1.far_ref, s32[128,8]{1,0:T(8,128)S(1)} %copy.11.routes_ref, ...), custom_call_target="tpu_custom_call" | custom-call | bytes 6600000 | tf_op jit(solution)/shard_map/pallas_call | solution.py:250
  23.3 5.7 %all-to-all-start = ((bf16[16,192,128]{2,1,0:T(8,128)(2,1)}), bf16[16,192,128]{2,1,0:T(8,128)(2,1)S(1)}, u32[]{:S(2)}, u32[]{:S(2)}) async-start(bf16[16,192,128]{2,1,0:T(8,128)(2,1)} %shard_map.94), calls=%async_computation | async-start | bytes 1572864 | tf_op jit(solution)/shard_map/all_to_all | solution.py:438
  29.0 0.0 copy-done.2
  29.0 10.1 %shard_map.95.far_ref = bf16[8192,256]{1,0:T(8,128)(2,1)S(1)} custom-call(bf16[256,8,1024]{2,1,0:T(8,128)(2,1)} %query_ref, f32[8,64,64]{2,1,0:T(8,128)S(1)} %copy-done.2), custom_call_target="tpu_custom_call" | custom-call | bytes 33000000 | tf_op jit(solution)/shard_map/pallas_call | solution.py:303
  39.1 0.0 copy-start.1
  39.1 1.9 %copy-done.1 = bf16[8192,256]{1,0:T(8,128)(2,1)} copy-done((bf16[8192,256]{1,0:T(8,128)(2,1)}, bf16[8192,256]{1,0:T(8,128)(2,1)S(1)}, u32[]{:S(2)}) %copy-start.1) | copy-done | bytes 4194328
  41.1 6.6 %all-to-all-done.arrived_ref = bf16[16,192,128]{2,1,0:T(8,128)(2,1)S(1)} async-done(((bf16[16,192,128]{2,1,0:T(8,128)(2,1)}), bf16[16,192,128]{2,1,0:T(8,128)(2,1)S(1)}, u32[]{:S(2)}, u32[]{:S(2)}) %all-to-all-start) | async-done | bytes 786464 | tf_op jit(solution)/shard_map/all_to_all | solution.py:438
  47.7 6.6 %shard_map.96 = f32[16,8,128]{2,1,0:T(8,128)S(1)} custom-call(bf16[16,192,128]{2,1,0:T(8,128)(2,1)S(1)} %all-to-all-done.arrived_ref, s32[4,16,128]{2,1,0:T(8,128)S(1)} %get-tuple-element.17.docs_ref, bf16[8192,256]{1,0:T(8,128)(2,1)} %copy-done.1), custom_call_target="tpu_custom_call" | custom-call | bytes 16500000 | tf_op jit(solution)/shard_map/pallas_call | solution.py:365
  54.3 12.3 %all_to_all.10.pieces_ref = f32[16,8,128]{2,1,0:T(8,128)} all-to-all(f32[16,8,128]{2,1,0:T(8,128)S(1)} %shard_map.96), channel_id=1, replica_groups=mesh['groups'=2,'expert'=4,'proj'=4] {'expert','proj'}, dimensions={0} | all-to-all | bytes 131072 | tf_op jit(solution)/shard_map/all_to_all | solution.py:441
  66.6 1.4 %shard_map.97 = f32[8,64]{1,0:T(8,128)} custom-call(f32[16,8,128]{2,1,0:T(8,128)} %all_to_all.10.pieces_ref), custom_call_target="tpu_custom_call" | custom-call | tf_op jit(solution)/shard_map/pallas_call | solution.py:387
  (4 shorter events, 0.1 us)
Async XLA Ops:
  0.0 17.1 %copy-start = (s32[512,8]{0,1:T(8,128)S(1)}, s32[512,8]{0,1:T(8,128)}, u32[]{:S(2)}) copy-start(s32[512,8]{0,1:T(8,128)} %param.11) | copy-start | bytes 49156
  6.2 22.8 %copy-start.2 = (f32[8,64,64]{2,1,0:T(8,128)S(1)}, f32[8,64,64]{2,1,0:T(8,128)}, u32[]{:S(2)}) copy-start(f32[8,64,64]{2,1,0:T(8,128)} %inverse_ref.1) | copy-start | bytes 393220
  6.2 9.3 %collective-permute-start = (bf16[2,640,128]{2,1,0:T(8,128)(2,1)S(1)}, bf16[2,640,128]{2,1,0:T(8,128)(2,1)S(1)}, u32[]{:S(2)}, u32[]{:S(2)}) collective-permute-start(bf16[2,640,128]{2,1,0:T(8,128)(2,1)S(1)} %get-tuple-element.13), channel_id=1, source_target_pairs={{0,1},{1,0},{2,3},{3,2},{4,5},{5,4},{6,7},{7,6},{8,9},{9,8},{10,11... | collective-permute-start | bytes 983048 | tf_op jit(solution)/shard_map/ppermute | solution.py:395
  6.7 7.9 %collective-permute-start.2 = (bf16[272,128]{1,0:T(8,128)(2,1)S(1)}, bf16[272,128]{1,0:T(8,128)(2,1)S(1)}, u32[]{:S(2)}, u32[]{:S(2)}) collective-permute-start(bf16[272,128]{1,0:T(8,128)(2,1)S(1)} %get-tuple-element.14), channel_id=1, source_target_pairs={{0,8},{4,12},{8,0},{12,4},{1,9},{5,13},{9,1},{13,5},{2,10},{6,14},... | collective-permute-start | bytes 208904 | tf_op jit(solution)/shard_map/ppermute | solution.py:395
  14.7 5.5 %collective-permute-start.3 = (bf16[2,272,128]{2,1,0:T(8,128)(2,1)S(1)}, bf16[2,272,128]{2,1,0:T(8,128)(2,1)S(1)}, u32[]{:S(2)}, u32[]{:S(2)}) collective-permute-start(bf16[2,272,128]{2,1,0:T(8,128)(2,1)S(1)} %pad_maximum_fusion.1), channel_id=1, source_target_pairs={{0,4},{4,0},{8,12},{12,8},{1,5},{5,1},{9,13},{13,9},{2,6},{6,2},{1... | collective-permute-start | bytes 417800 | tf_op jit(solution)/shard_map/ppermute | solution.py:395
  15.5 5.9 %collective-permute-start.1 = (bf16[640,128]{1,0:T(8,128)(2,1)S(1)}, bf16[640,128]{1,0:T(8,128)(2,1)S(1)}, u32[]{:S(2)}, u32[]{:S(2)}) collective-permute-start(bf16[640,128]{1,0:T(8,128)(2,1)S(1)} %shard_map.92), channel_id=1, source_target_pairs={{0,2},{1,3},{2,0},{3,1},{4,6},{5,7},{6,4},{7,5},{8,10},{9,11},{10,... | collective-permute-start | bytes 491528 | tf_op jit(solution)/shard_map/ppermute | solution.py:395
  23.3 24.4 %all-to-all-start = ((bf16[16,192,128]{2,1,0:T(8,128)(2,1)}), bf16[16,192,128]{2,1,0:T(8,128)(2,1)S(1)}, u32[]{:S(2)}, u32[]{:S(2)}) async-start(bf16[16,192,128]{2,1,0:T(8,128)(2,1)} %shard_map.94), calls=%async_computation | async-start | bytes 1572864 | tf_op jit(solution)/shard_map/all_to_all | solution.py:438
  39.1 1.9 %copy-start.1 = (bf16[8192,256]{1,0:T(8,128)(2,1)}, bf16[8192,256]{1,0:T(8,128)(2,1)S(1)}, u32[]{:S(2)}) copy-start(bf16[8192,256]{1,0:T(8,128)(2,1)S(1)} %shard_map.95.far_ref) | copy-start | bytes 12582916

commit v6 on v5

--- a/solution.py
+++ b/solution.py
@@ -32,7 +32,15 @@
     return pl.CostEstimate(flops=0, bytes_accessed=int(microseconds * 3.3e6), transcendentals=0)
 
 
-def pack_shared(inverse_ref, docs_ref, shared_ref):
+def pack_kernel(inverse_hbm, docs_hbm, shared_ref, inverse_ref, docs_ref, sems):
+    copies = [
+        pltpu.make_async_copy(inverse_hbm, inverse_ref, sems.at[0]),
+        pltpu.make_async_copy(docs_hbm, docs_ref, sems.at[1]),
+    ]
+    for copy in copies:
+        copy.start()
+    for copy in copies:
+        copy.wait()
     width = inverse_ref.shape[1]
     half = inverse_ref.shape[0] // 2
     for e in range(half):
@@ -43,91 +51,102 @@
     shared_ref[half * width :, :] = docs.astype(jnp.bfloat16)
 
 
-def project_kernel(
-    act_hbm, hidden_hbm, in_proj_hbm, out_proj_hbm, inverse_hbm, docs_hbm, leaving_ref, own_ref, shared_ref, *refs, top
-):
-    act_ref, hidden_ref, in_proj_ref, out_proj_ref, inverse_ref, docs_ref, rows_ref, quarter_sems, sems = refs
+def pack(inverse_out, doc_rows):
+    experts, width, _ = inverse_out.shape
+    return pl.pallas_call(
+        pack_kernel,
+        in_specs=[HBM, HBM],
+        out_specs=VMEM,
+        out_shape=jax.ShapeDtypeStruct((experts // 2 * width + DOC_ROWS, LANES), jnp.bfloat16),
+        scratch_shapes=[
+            pltpu.VMEM(inverse_out.shape, inverse_out.dtype),
+            pltpu.VMEM(doc_rows.shape, doc_rows.dtype),
+            pltpu.SemaphoreType.DMA((2,)),
+        ],
+        cost_estimate=cost(1),
+    )(stay(inverse_out), stay(doc_rows))
+
+
+def project_kernel(act_hbm, hidden_hbm, in_proj_hbm, out_proj_hbm, leaving_ref, own_ref, *refs, top):
+    act_ref, hidden_ref, in_proj_ref, out_proj_ref, rows_ref, sems = refs
     turns = (1, 3, 2, 0)
     quarter = act_ref.shape[1]
     width = in_proj_ref.shape[0]
+    half = quarter // 2
     place = lax.axis_index("proj")
-    fixed = [
-        pltpu.make_async_copy(source, target, sems.at[i])
-        for i, (source, target) in enumerate(
-            [(out_proj_hbm, out_proj_ref), (in_proj_hbm, in_proj_ref), (inverse_hbm, inverse_ref), (docs_hbm, docs_ref)]
-        )
-    ]
-    fixed[0].start()
-    moving = []
+    pairs = []
     for g, turn in enumerate(turns):
         start = jnp.bitwise_xor(place, turn) * quarter
-        hidden_rows = pl.ds(pl.multiple_of(start * top, quarter * top), quarter * top)
-        act_rows = pl.ds(pl.multiple_of(start, quarter), quarter)
-        moving.append(
-            (
-                pltpu.make_async_copy(hidden_hbm.at[hidden_rows], hidden_ref.at[g], quarter_sems.at[g, 0]),
-                pltpu.make_async_copy(act_hbm.at[act_rows], act_ref.at[g], quarter_sems.at[g, 1]),
-            )
-        )
-        moving[g][0].start()
+        for part in range(2):
+            rows = pl.ds(pl.multiple_of((start + part * half) * top, half * top), half * top)
+            pairs.append((hidden_hbm.at[rows], hidden_ref.at[g, part]))
+            if g == 0 and part == 0:
+                pairs.append((out_proj_hbm, out_proj_ref))
+        rows = pl.ds(pl.multiple_of(start, quarter), quarter)
         if g == 0:
-            fixed[1].start()
-        moving[g][1].start()
-        if g == 0:
-            fixed[2].start()
-            fixed[3].start()
-    half = quarter // 2
-    first = low_lanes(quarter, width)
-    fixed[0].wait()
-    twice = jnp.concatenate([out_proj_ref[...], out_proj_ref[...]], axis=0)
+            pairs.append((in_proj_hbm, in_proj_ref))
+        pairs.append((act_hbm.at[rows], act_ref.at[g]))
+    copies = [pltpu.make_async_copy(source, target, sems.at[i]) for i, (source, target) in enumerate(pairs)]
+    ahead = 4
+    for copy in copies[:ahead]:
+        copy.start()
+    arrived = 0
+
+    def take():
+        nonlocal arrived
+        copies[arrived].wait()
+        if arrived + ahead < len(copies):
+            copies[arrived + ahead].start()
+        arrived += 1
+
+    first = low_lanes(half, width)
     for g in range(len(turns)):
         wire_ref = leaving_ref.at[g] if g < 2 else own_ref.at[g - 2]
-        moving[g][0].wait()
-        rows_ref[g % 2] = lax.dot_general(
-            hidden_ref[g], twice, (((1,), (1,)), ((), ())), preferred_element_type=jnp.float32
-        )
-        for pair in range(top // 2):
-            even = rows_ref[g % 2, pl.ds(2 * pair, quarter, stride=top), :]
-            odd = rows_ref[g % 2, pl.ds(2 * pair + 1, quarter, stride=top), :]
-            wire_ref[pair * quarter : (pair + 1) * quarter, :] = jnp.where(first, even, odd).astype(jnp.bfloat16)
+        for part in range(2):
+            take()
+            if g == 0 and part == 0:
+                take()
+            twice = jnp.concatenate([out_proj_ref[...], out_proj_ref[...]], axis=0)
+            rows_ref[part] = lax.dot_general(
+                hidden_ref[g, part], twice, (((1,), (1,)), ((), ())), preferred_element_type=jnp.float32
+            )
+            for pair in range(top // 2):
+                even = rows_ref[part, pl.ds(2 * pair, half, stride=top), :]
+                odd = rows_ref[part, pl.ds(2 * pair + 1, half, stride=top), :]
+                start = pair * quarter + part * half
+                wire_ref[start : start + half, :] = jnp.where(first, even, odd).astype(jnp.bfloat16)
         if g == 0:
-            fixed[1].wait()
+            take()
+        take()
         twice_in = jnp.concatenate([in_proj_ref[...], in_proj_ref[...]], axis=0)
-        moving[g][1].wait()
         inner = lax.dot_general(
             act_ref[g], twice_in, (((1,), (1,)), ((), ())), preferred_element_type=jnp.float32
         )
-        high, low = split(jnp.where(low_lanes(half, width), inner[:half], inner[half:]))
+        high, low = split(jnp.where(first, inner[:half], inner[half:]))
         start = top // 2 * quarter
         wire_ref[start : start + half, :] = high
         wire_ref[start + half :, :] = low
-        if g == 0:
-            fixed[2].wait()
-            fixed[3].wait()
-            pack_shared(inverse_ref, docs_ref, shared_ref)
-
-
-def project(activations, flat_hidden, in_projection, out_projection, inverse_out, doc_rows, quarters, top):
+
+
+def project(activations, flat_hidden, in_projection, out_projection, quarters, top):
     tokens, model = activations.shape
     quarter = tokens // quarters
     wire_rows = top // 2 * quarter + quarter
-    experts, width, _ = inverse_out.shape
     wire = jax.ShapeDtypeStruct((quarters // 2, wire_rows, LANES), jnp.bfloat16)
-    fixed = (in_projection, out_projection, inverse_out, doc_rows)
+    fixed = (in_projection, out_projection)
     return pl.pallas_call(
         functools.partial(project_kernel, top=top),
-        in_specs=[HBM] * 6,
-        out_specs=[VMEM] * 3,
-        out_shape=[wire, wire, jax.ShapeDtypeStruct((experts // 2 * width + DOC_ROWS, LANES), jnp.bfloat16)],
+        in_specs=[HBM] * 4,
+        out_specs=[VMEM] * 2,
+        out_shape=[wire, wire],
         scratch_shapes=[
             pltpu.VMEM((quarters, quarter, model), jnp.bfloat16),
-            pltpu.VMEM((quarters, quarter * top, flat_hidden.shape[1]), jnp.bfloat16),
+            pltpu.VMEM((quarters, 2, quarter // 2 * top, flat_hidden.shape[1]), jnp.bfloat16),
         ]
         + [pltpu.VMEM(array.shape, array.dtype) for array in fixed]
         + [
-            pltpu.VMEM((2, quarter * top, LANES), jnp.float32),
-            pltpu.SemaphoreType.DMA((quarters, 2)),
-            pltpu.SemaphoreType.DMA((len(fixed),)),
+            pltpu.VMEM((2, quarter // 2 * top, LANES), jnp.float32),
+            pltpu.SemaphoreType.DMA((3 * quarters + len(fixed),)),
         ],
         compiler_params=pltpu.CompilerParams(vmem_limit_bytes=40 * MIB),
         cost_estimate=cost(5),
@@ -356,7 +375,9 @@
     for owner in range(owners):
         for share in range(shares):
             piece = result[owner * DOC_DEV : (owner + 1) * DOC_DEV, share * columns : (share + 1) * columns]
-            out_ref[owner * shares + share] = jnp.concatenate([piece, fill], axis=1)
+            share_turn = jnp.bitwise_xor(lax.axis_index("proj"), share)
+            owner_turn = jnp.bitwise_xor(lax.axis_index("expert"), owner)
+            out_ref[share_turn, owner_turn] = jnp.concatenate([piece, fill], axis=1)
 
 
 def score(arrived, docs, queries, width, shares):
@@ -365,7 +386,7 @@
     return pl.pallas_call(
         functools.partial(score_kernel, width=width, doc_count=doc_count, shares=shares),
         in_specs=[VMEM, VMEM, HBM],
-        out_shape=jax.ShapeDtypeStruct((sources, DOC_DEV, LANES), jnp.float32),
+        out_shape=jax.ShapeDtypeStruct((shares, sources // shares, DOC_DEV, LANES), jnp.float32),
         scratch_shapes=[
             pltpu.VMEM((doc_count * width, arrived.shape[2]), jnp.float32),
             pltpu.VMEM(queries.shape, jnp.bfloat16),
@@ -374,21 +395,6 @@
         compiler_params=pltpu.CompilerParams(vmem_limit_bytes=40 * MIB),
         cost_estimate=cost(5),
     )(arrived, docs, stay(queries))
-
-
-def sum_kernel(pieces_ref, out_ref):
-    total = pieces_ref[0]
-    for source in range(1, pieces_ref.shape[0]):
-        total = total + pieces_ref[source]
-    out_ref[...] = total[:, : out_ref.shape[1]]
-
-
-def sum_pieces(pieces, columns):
-    return pl.pallas_call(
-        sum_kernel,
-        in_specs=[VMEM],
-        out_shape=jax.ShapeDtypeStruct((pieces.shape[1], columns), jnp.float32),
-    )(pieces)
 
 
 def exchange(block, axis, size, turn):
@@ -422,11 +428,12 @@
 
     flat_hidden = grad_hidden.reshape(tokens * top, grad_hidden.shape[2])
     doc_rows = doc_ids.reshape(shares, quarter)
-    leaving, own, shared = project(
-        activations, flat_hidden, in_projection, out_projection, inverse_out, doc_rows, shares, top
-    )
+    shared = pack(inverse_out, doc_rows)
+    first = exchange(shared, "expert", owners, owners // 2)
+    shared, activations = lax.optimization_barrier((shared, activations))
+    leaving, own = project(activations, flat_hidden, in_projection, out_projection, shares, top)
+    first, leaving = lax.optimization_barrier((first, leaving))
     near = exchange(leaving, "proj", shares, 1)
-    first = exchange(shared, "expert", owners, owners // 2)
     shared, turns = jnp.stack([shared, first]), (0, owners // 2)
     for bit in reversed(range((owners // 2).bit_length() - 1)):
         shared, turns = double(shared, turns, "expert", owners, 1 << bit)
@@ -437,9 +444,15 @@
     payload, query_grads = lax.optimization_barrier((payload, query_grads))
     arrived = lax.all_to_all(payload, ("expert", "proj"), 0, 0, tiled=True)
     queries = condition_queries(query_grads, inverse_in)
-    partial_scores = score(arrived, all_docs, queries, width, shares)
-    pieces = lax.all_to_all(partial_scores, ("expert", "proj"), 0, 0, tiled=True)
-    return sum_pieces(pieces, query_grads.shape[0] // shares).T
+    pieces = score(arrived, all_docs, queries, width, shares)
+    leaving, staying = pieces[1::2], pieces[0::2]
+    pieces = staying + exchange(leaving, "proj", shares, 1)
+    pieces = pieces[0] + exchange(pieces[1], "proj", shares, 2)
+    turn = owners // 2
+    while turn:
+        pieces = pieces[:turn] + exchange(pieces[turn:], "expert", owners, turn)
+        turn //= 2
+    return pieces[0, :, : query_grads.shape[0] // shares].T
 
 
 def solution(mesh):

time: 68.6 us -> 66.6 us (0.971)
  blocking collectives: 12.3 us -> 0 us
  starting transfers between devices: 12.2 us -> 18.5 us
  waiting for transfers between devices: 14.4 us -> 17.2 us
    all_to_all x1 -> x0, blocking collectives: 12.3 us -> none  [local(): lax.all_to_all(partial_scores, ('expert', 'proj'), 0, 0, tiled=True)]
    ppermute x4 -> x8, starting transfers between devices: 6.55 us -> 14.8 us  [exchange(): return lax.ppermute(block, axis, [(i, i ^ turn) for i in range(size)])]
    ppermute x4 -> x8, waiting for transfers between devices: 7.77 us -> 10.5 us  [exchange(): return lax.ppermute(block, axis, [(i, i ^ turn) for i in range(size)])]
    all_to_all x1, starting transfers between devices: 5.68 us -> 3.76 us  [local(): arrived = lax.all_to_all(payload, ('expert', 'proj'), 0, 0, tiled=True)]
    unnamed x7 -> x9, local copies, waits for them, and re-layouts: 2.06 us -> 2.07 us
  transfers between devices with their start and end apart: 5 -> 9, of which waited for: 4 -> 7; matrix products, arithmetic and copies ran while one was open for 0% -> 0% of each run, Pallas kernels for 16% -> 26%
where the time goes in v6:
time: 66.6 us; the launch traced here: 66 us
  Pallas kernels  27.5 us (41%)
  starting transfers between devices  18.5 us (28%)
  waiting for transfers between devices  17.2 us (26%)
  local copies, waits for them, and re-layouts  2.68 us (4%)
    ppermute x8, starting transfers between devices, exchange(): return lax.ppermute(block, axis, [(i, i ^ turn) for i in range(size)])  14.8 us
    ppermute x8, waiting for transfers between devices, exchange(): return lax.ppermute(block, axis, [(i, i ^ turn) for i in range(size)])  10.5 us
    pallas_call x1, Pallas kernels, condition_queries(): pl.pallas_call(query_kernel, grid=(flat // LANES,), in_specs=[pl.BlockSpe...  10.1 us
    all_to_all x1, waiting for transfers between devices, local(): arrived = lax.all_to_all(payload, ('expert', 'proj'), 0, 0, tiled=True)  6.64 us
    pallas_call x1, Pallas kernels, score(): pl.pallas_call(functools.partial(score_kernel, width=width, doc_count=doc...  6.59 us
    pallas_call x1, Pallas kernels, project(): pl.pallas_call(functools.partial(project_kernel, top=top), in_specs=[HBM]...  6.47 us
    all_to_all x1, starting transfers between devices, local(): arrived = lax.all_to_all(payload, ('expert', 'proj'), 0, 0, tiled=True)  3.76 us
    unnamed x9, local copies, waits for them, and re-layouts  2.07 us
  transfers between devices with their start and end apart: 9, of which 7 were waited for; matrix products, arithmetic and copies ran while one was open for 0% of the time, Pallas kernels for 26%

profile of v6, /device:TPU:0, one launch (start us, length us, event | category | flops | bytes accessed | tf_op | source)
XLA Modules:
  0.0 66.0 jit_solution(16346015781634081789)
XLA Ops:
  0.0 0.0 copy-start
  0.0 1.7 %shard_map.91 = bf16[272,128]{1,0:T(8,128)(2,1)} custom-call(f32[8,64,64]{2,1,0:T(8,128)} %inverse_hbm.1, s32[4,128]{1,0:T(4,128)} %bitcast.19), custom_call_target="tpu_custom_call" | custom-call | bytes 3300000 | tf_op jit(solution)/shard_map/pallas_call | solution.py:56
  1.7 0.0 copy-start.3
  1.7 4.1 %collective-permute-start = (bf16[272,128]{1,0:T(8,128)(2,1)}, bf16[272,128]{1,0:T(8,128)(2,1)S(1)}, u32[]{:S(2)}, u32[]{:S(2)}) collective-permute-start(bf16[272,128]{1,0:T(8,128)(2,1)} %shard_map.91), channel_id=1, source_target_pairs={{0,8},{4,12},{8,0},{12,4},{1,9},{5,13},{9,1},{13,5},{2,10},{6,14},... | collective-permute-start | bytes 208904 | tf_op jit(solution)/shard_map/ppermute | solution.py:401
  5.8 6.5 %shard_map.92 = (bf16[2,640,128]{2,1,0:T(8,128)(2,1)S(1)}, bf16[2,640,128]{2,1,0:T(8,128)(2,1)S(1)}) custom-call(bf16[512,1792]{1,0:T(8,128)(2,1)} %act_hbm, bf16[4096,512]{1,0:T(8,128)(2,1)} %bitcast.14, bf16[64,1792]{1,0:T(8,128)(2,1)} %in_proj_hbm.1, bf16[64,512]{1,0:T(8,128)(2,1)} %out_proj_hbm.1), custom_call_target="tpu_custom_call" | custom-call | bytes 16500000 | tf_op jit(solution)/shard_map/pallas_call | solution.py:137
  12.3 0.0 copy-start.2
  12.3 0.0 collective-permute-done
  12.3 0.1 collective-permute-start.1
  12.4 0.0 copy-done.3
  12.4 1.6 %collective-permute-start.3 = (bf16[2,272,128]{2,1,0:T(8,128)(2,1)S(1)}, bf16[2,272,128]{2,1,0:T(8,128)(2,1)S(1)}, u32[]{:S(2)}, u32[]{:S(2)}) collective-permute-start(bf16[2,272,128]{2,1,0:T(8,128)(2,1)S(1)} %pad_maximum_fusion.1), channel_id=1, source_target_pairs={{0,4},{4,0},{8,12},{12,8},{1,5},{5,1},{9,13},{13,9},{2,6},{6,2},{1... | collective-permute-start | bytes 417800 | tf_op jit(solution)/shard_map/ppermute | solution.py:401
  14.1 0.0 collective-permute-done.1.other_ref.near_ref
  14.1 1.6 %collective-permute-start.2 = (bf16[640,128]{1,0:T(8,128)(2,1)S(1)}, bf16[640,128]{1,0:T(8,128)(2,1)S(1)}, u32[]{:S(2)}, u32[]{:S(2)}) collective-permute-start(bf16[640,128]{1,0:T(8,128)(2,1)S(1)} %shard_map.93), channel_id=1, source_target_pairs={{0,2},{1,3},{2,0},{3,1},{4,6},{5,7},{6,4},{7,5},{8,10},{9,11},{10,... | collective-permute-start | bytes 491528 | tf_op jit(solution)/shard_map/ppermute | solution.py:401
  15.7 0.0 copy-done
  15.7 0.1 copy.11.routes_ref
  15.8 2.8 %collective-permute-done.3 = bf16[2,272,128]{2,1,0:T(8,128)(2,1)S(1)} collective-permute-done((bf16[2,272,128]{2,1,0:T(8,128)(2,1)S(1)}, bf16[2,272,128]{2,1,0:T(8,128)(2,1)S(1)}, u32[]{:S(2)}, u32[]{:S(2)}) %collective-permute-start.3) | collective-permute-done | bytes 139296 | tf_op jit(solution)/shard_map/ppermute | solution.py:401
  18.6 0.7 %shard_map.94 = (bf16[4,512,512]{2,1,0:T(8,128)(2,1)S(1)}, s32[4,16,128]{2,1,0:T(8,128)S(1)}) custom-call(bf16[4,272,128]{2,1,0:T(8,128)(2,1)S(1)} %pad_maximum_fusion.shared_ref), custom_call_target="tpu_custom_call" | custom-call | bytes 4290000 | tf_op jit(solution)/shard_map/pallas_call | solution.py:205
  19.3 1.2 %collective-permute-done.2.far_ref = bf16[640,128]{1,0:T(8,128)(2,1)S(1)} collective-permute-done((bf16[640,128]{1,0:T(8,128)(2,1)S(1)}, bf16[640,128]{1,0:T(8,128)(2,1)S(1)}, u32[]{:S(2)}, u32[]{:S(2)}) %collective-permute-start.2) | collective-permute-done | bytes 163872 | tf_op jit(solution)/shard_map/ppermute | solution.py:401
  20.5 1.8 %shard_map.95 = bf16[16,192,128]{2,1,0:T(8,128)(2,1)} custom-call(bf16[2,640,128]{2,1,0:T(8,128)(2,1)S(1)} %get-tuple-element.16.own_ref, bf16[2,640,128]{2,1,0:T(8,128)(2,1)S(1)} %collective-permute-done.1.other_ref.near_ref, bf16[640,128]{1,0:T(8,128)(2,1)S(1)} %collective-permute-done.2.far_ref, s32[128,8]{1,0:T(8,128)S(1)} %copy.11.routes_ref, ...), custom_call_target="tpu_custom_call" | custom-call | bytes 6600000 | tf_op jit(solution)/shard_map/pallas_call | solution.py:269
  22.3 3.8 %all-to-all-start = ((bf16[16,192,128]{2,1,0:T(8,128)(2,1)}), bf16[16,192,128]{2,1,0:T(8,128)(2,1)S(1)}, u32[]{:S(2)}, u32[]{:S(2)}) async-start(bf16[16,192,128]{2,1,0:T(8,128)(2,1)} %shard_map.95), calls=%async_computation | async-start | bytes 1572864 | tf_op jit(solution)/shard_map/all_to_all | solution.py:445
  26.1 0.0 copy-done.2
  26.1 10.1 %shard_map.96.far_ref = bf16[8192,256]{1,0:T(8,128)(2,1)S(1)} custom-call(bf16[256,8,1024]{2,1,0:T(8,128)(2,1)} %query_ref, f32[8,64,64]{2,1,0:T(8,128)S(1)} %copy-done.2), custom_call_target="tpu_custom_call" | custom-call | bytes 33000000 | tf_op jit(solution)/shard_map/pallas_call | solution.py:322
  36.2 0.0 copy-start.1
  36.2 1.9 %copy-done.1 = bf16[8192,256]{1,0:T(8,128)(2,1)} copy-done((bf16[8192,256]{1,0:T(8,128)(2,1)}, bf16[8192,256]{1,0:T(8,128)(2,1)S(1)}, u32[]{:S(2)}) %copy-start.1) | copy-done | bytes 4194328
  38.2 6.6 %all-to-all-done.arrived_ref = bf16[16,192,128]{2,1,0:T(8,128)(2,1)S(1)} async-done(((bf16[16,192,128]{2,1,0:T(8,128)(2,1)}), bf16[16,192,128]{2,1,0:T(8,128)(2,1)S(1)}, u32[]{:S(2)}, u32[]{:S(2)}) %all-to-all-start) | async-done | bytes 786464 | tf_op jit(solution)/shard_map/all_to_all | solution.py:445
  44.8 6.6 %shard_map.97 = f32[4,4,8,128]{3,2,1,0:T(8,128)S(1)} custom-call(bf16[16,192,128]{2,1,0:T(8,128)(2,1)S(1)} %all-to-all-done.arrived_ref, s32[4,16,128]{2,1,0:T(8,128)S(1)} %get-tuple-element.23.docs_ref, bf16[8192,256]{1,0:T(8,128)(2,1)} %copy-done.1), custom_call_target="tpu_custom_call" | custom-call | bytes 16500000 | tf_op jit(solution)/shard_map/pallas_call | solution.py:386
  51.4 0.3 collective-permute-start.4
  51.7 1.0 %collective-permute-done.4 = f32[2,4,8,128]{3,2,1,0:T(8,128)S(1)} collective-permute-done((f32[2,4,8,128]{3,2,1,0:T(8,128)S(1)}, f32[2,4,8,128]{3,2,1,0:T(8,128)S(1)}, u32[]{:S(2)}, u32[]{:S(2)}) %collective-permute-start.4) | collective-permute-done | bytes 32800 | tf_op jit(solution)/shard_map/ppermute | solution.py:401
  52.7 1.6 %collective-permute-start.5 = (f32[4,8,128]{2,1,0:T(8,128)S(1)}, f32[4,8,128]{2,1,0:T(8,128)S(1)}, u32[]{:S(2)}, u32[]{:S(2)}) collective-permute-start(f32[4,8,128]{2,1,0:T(8,128)S(1)} %slice_bitcast_fusion), channel_id=1, source_target_pairs={{0,2},{1,3},{2,0},{3,1},{4,6},{5,7},{6,4},{7,5},{8,10},{9,11},{10,... | collective-permute-start | bytes 49160 | tf_op jit(solution)/shard_map/ppermute | solution.py:401
  54.3 2.2 %collective-permute-done.5 = f32[4,8,128]{2,1,0:T(8,128)S(1)} collective-permute-done((f32[4,8,128]{2,1,0:T(8,128)S(1)}, f32[4,8,128]{2,1,0:T(8,128)S(1)}, u32[]{:S(2)}, u32[]{:S(2)}) %collective-permute-start.5) | collective-permute-done | bytes 16416 | tf_op jit(solution)/shard_map/ppermute | solution.py:401
  56.5 3.7 %collective-permute-start.6 = (f32[2,8,128]{2,1,0:T(8,128)S(1)}, f32[2,8,128]{2,1,0:T(8,128)S(1)}, u32[]{:S(2)}, u32[]{:S(2)}) collective-permute-start(f32[2,8,128]{2,1,0:T(8,128)S(1)} %slice.39), channel_id=1, source_target_pairs={{0,8},{4,12},{8,0},{12,4},{1,9},{5,13},{9,1},{13,5},{2,10},{6,14},... | collective-permute-start | bytes 24584 | tf_op jit(solution)/shard_map/ppermute | solution.py:401
  60.2 1.6 %collective-permute-done.6 = f32[2,8,128]{2,1,0:T(8,128)S(1)} collective-permute-done((f32[2,8,128]{2,1,0:T(8,128)S(1)}, f32[2,8,128]{2,1,0:T(8,128)S(1)}, u32[]{:S(2)}, u32[]{:S(2)}) %collective-permute-start.6) | collective-permute-done | bytes 8224 | tf_op jit(solution)/shard_map/ppermute | solution.py:401
  61.8 1.8 %collective-permute-start.7 = (f32[1,8,128]{2,1,0:T(8,128)S(1)}, f32[1,8,128]{2,1,0:T(8,128)S(1)}, u32[]{:S(2)}, u32[]{:S(2)}) collective-permute-start(f32[1,8,128]{2,1,0:T(8,128)S(1)} %slice.41), channel_id=1, source_target_pairs={{0,4},{4,0},{8,12},{12,8},{1,5},{5,1},{9,13},{13,9},{2,6},{6,2},{1... | collective-permute-start | bytes 12296 | tf_op jit(solution)/shard_map/ppermute | solution.py:401
  63.7 1.8 %collective-permute-done.7 = f32[1,8,128]{2,1,0:T(8,128)S(1)} collective-permute-done((f32[1,8,128]{2,1,0:T(8,128)S(1)}, f32[1,8,128]{2,1,0:T(8,128)S(1)}, u32[]{:S(2)}, u32[]{:S(2)}) %collective-permute-start.7) | collective-permute-done | bytes 4128 | tf_op jit(solution)/shard_map/ppermute | solution.py:401
  65.4 0.6 slice_bitcast_fusion.2
  (12 shorter events, 0.1 us)
Async XLA Ops:
  0.0 15.7 %copy-start = (s32[512,8]{0,1:T(8,128)S(1)}, s32[512,8]{0,1:T(8,128)}, u32[]{:S(2)}) copy-start(s32[512,8]{0,1:T(8,128)} %param.11) | copy-start | bytes 49156
  1.7 10.7 %copy-start.3 = (bf16[272,128]{1,0:T(8,128)(2,1)S(1)}, bf16[272,128]{1,0:T(8,128)(2,1)}, u32[]{:S(2)}) copy-start(bf16[272,128]{1,0:T(8,128)(2,1)} %shard_map.91) | copy-start | bytes 208900
  1.7 10.6 %collective-permute-start = (bf16[272,128]{1,0:T(8,128)(2,1)}, bf16[272,128]{1,0:T(8,128)(2,1)S(1)}, u32[]{:S(2)}, u32[]{:S(2)}) collective-permute-start(bf16[272,128]{1,0:T(8,128)(2,1)} %shard_map.91), channel_id=1, source_target_pairs={{0,8},{4,12},{8,0},{12,4},{1,9},{5,13},{9,1},{13,5},{2,10},{6,14},... | collective-permute-start | bytes 208904 | tf_op jit(solution)/shard_map/ppermute | solution.py:401
  12.3 13.8 %copy-start.2 = (f32[8,64,64]{2,1,0:T(8,128)S(1)}, f32[8,64,64]{2,1,0:T(8,128)}, u32[]{:S(2)}) copy-start(f32[8,64,64]{2,1,0:T(8,128)} %inverse_ref.1) | copy-start | bytes 393220
  12.3 1.8 %collective-permute-start.1 = (bf16[2,640,128]{2,1,0:T(8,128)(2,1)S(1)}, bf16[2,640,128]{2,1,0:T(8,128)(2,1)S(1)}, u32[]{:S(2)}, u32[]{:S(2)}) collective-permute-start(bf16[2,640,128]{2,1,0:T(8,128)(2,1)S(1)} %get-tuple-element.18), channel_id=1, source_target_pairs={{0,1},{1,0},{2,3},{3,2},{4,5},{5,4},{6,7},{7,6},{8,9},{9,8},{10,11... | collective-permute-start | bytes 983048 | tf_op jit(solution)/shard_map/ppermute | solution.py:401
  12.4 6.1 %collective-permute-start.3 = (bf16[2,272,128]{2,1,0:T(8,128)(2,1)S(1)}, bf16[2,272,128]{2,1,0:T(8,128)(2,1)S(1)}, u32[]{:S(2)}, u32[]{:S(2)}) collective-permute-start(bf16[2,272,128]{2,1,0:T(8,128)(2,1)S(1)} %pad_maximum_fusion.1), channel_id=1, source_target_pairs={{0,4},{4,0},{8,12},{12,8},{1,5},{5,1},{9,13},{13,9},{2,6},{6,2},{1... | collective-permute-start | bytes 417800 | tf_op jit(solution)/shard_map/ppermute | solution.py:401
  14.1 6.4 %collective-permute-start.2 = (bf16[640,128]{1,0:T(8,128)(2,1)S(1)}, bf16[640,128]{1,0:T(8,128)(2,1)S(1)}, u32[]{:S(2)}, u32[]{:S(2)}) collective-permute-start(bf16[640,128]{1,0:T(8,128)(2,1)S(1)} %shard_map.93), channel_id=1, source_target_pairs={{0,2},{1,3},{2,0},{3,1},{4,6},{5,7},{6,4},{7,5},{8,10},{9,11},{10,... | collective-permute-start | bytes 491528 | tf_op jit(solution)/shard_map/ppermute | solution.py:401
  22.3 22.5 %all-to-all-start = ((bf16[16,192,128]{2,1,0:T(8,128)(2,1)}), bf16[16,192,128]{2,1,0:T(8,128)(2,1)S(1)}, u32[]{:S(2)}, u32[]{:S(2)}) async-start(bf16[16,192,128]{2,1,0:T(8,128)(2,1)} %shard_map.95), calls=%async_computation | async-start | bytes 1572864 | tf_op jit(solution)/shard_map/all_to_all | solution.py:445
  36.2 2.0 %copy-start.1 = (bf16[8192,256]{1,0:T(8,128)(2,1)}, bf16[8192,256]{1,0:T(8,128)(2,1)S(1)}, u32[]{:S(2)}) copy-start(bf16[8192,256]{1,0:T(8,128)(2,1)S(1)} %shard_map.96.far_ref) | copy-start | bytes 12582916
  51.4 1.3 %collective-permute-start.4 = (f32[2,4,8,128]{3,2,1,0:T(8,128)S(1)}, f32[2,4,8,128]{3,2,1,0:T(8,128)S(1)}, u32[]{:S(2)}, u32[]{:S(2)}) collective-permute-start(f32[2,4,8,128]{3,2,1,0:T(8,128)S(1)} %slice.28), channel_id=1, source_target_pairs={{0,1},{1,0},{2,3},{3,2},{4,5},{5,4},{6,7},{7,6},{8,9},{9,8},{10,11... | collective-permute-start | bytes 98312 | tf_op jit(solution)/shard_map/ppermute | solution.py:401
  52.7 3.8 %collective-permute-start.5 = (f32[4,8,128]{2,1,0:T(8,128)S(1)}, f32[4,8,128]{2,1,0:T(8,128)S(1)}, u32[]{:S(2)}, u32[]{:S(2)}) collective-permute-start(f32[4,8,128]{2,1,0:T(8,128)S(1)} %slice_bitcast_fusion), channel_id=1, source_target_pairs={{0,2},{1,3},{2,0},{3,1},{4,6},{5,7},{6,4},{7,5},{8,10},{9,11},{10,... | collective-permute-start | bytes 49160 | tf_op jit(solution)/shard_map/ppermute | solution.py:401
  56.5 5.3 %collective-permute-start.6 = (f32[2,8,128]{2,1,0:T(8,128)S(1)}, f32[2,8,128]{2,1,0:T(8,128)S(1)}, u32[]{:S(2)}, u32[]{:S(2)}) collective-permute-start(f32[2,8,128]{2,1,0:T(8,128)S(1)} %slice.39), channel_id=1, source_target_pairs={{0,8},{4,12},{8,0},{12,4},{1,9},{5,13},{9,1},{13,5},{2,10},{6,14},... | collective-permute-start | bytes 24584 | tf_op jit(solution)/shard_map/ppermute | solution.py:401
  61.8 3.6 %collective-permute-start.7 = (f32[1,8,128]{2,1,0:T(8,128)S(1)}, f32[1,8,128]{2,1,0:T(8,128)S(1)}, u32[]{:S(2)}, u32[]{:S(2)}) collective-permute-start(f32[1,8,128]{2,1,0:T(8,128)S(1)} %slice.41), channel_id=1, source_target_pairs={{0,4},{4,0},{8,12},{12,8},{1,5},{5,1},{9,13},{13,9},{2,6},{6,2},{1... | collective-permute-start | bytes 12296 | tf_op jit(solution)/shard_map/ppermute | solution.py:401

commit v7 on v5

--- a/solution.py
+++ b/solution.py
@@ -32,129 +32,173 @@
     return pl.CostEstimate(flops=0, bytes_accessed=int(microseconds * 3.3e6), transcendentals=0)
 
 
-def pack_shared(inverse_ref, docs_ref, shared_ref):
-    width = inverse_ref.shape[1]
-    half = inverse_ref.shape[0] // 2
-    for e in range(half):
-        pair = jnp.concatenate([inverse_ref[e], inverse_ref[half + e]], axis=1)
-        shared_ref[e * width : (e + 1) * width, :] = pair.astype(jnp.bfloat16)
-    docs = docs_ref[...].astype(jnp.float32)
-    docs = jnp.concatenate([docs, jnp.zeros((DOC_ROWS - docs.shape[0], LANES), jnp.float32)], axis=0)
-    shared_ref[half * width :, :] = docs.astype(jnp.bfloat16)
-
-
-def project_kernel(
-    act_hbm, hidden_hbm, in_proj_hbm, out_proj_hbm, inverse_hbm, docs_hbm, leaving_ref, own_ref, shared_ref, *refs, top
+def in_order(copies, ahead):
+    for copy in copies[:ahead]:
+        copy.start()
+    state = [0]
+
+    def take():
+        copies[state[0]].wait()
+        if state[0] + ahead < len(copies):
+            copies[state[0] + ahead].start()
+        state[0] += 1
+
+    return take
+
+
+def inner_kernel(
+    act_hbm, in_proj_hbm, inverse_hbm, docs_hbm, leaving_ref, own_ref, shared_ref, act_ref, in_proj_ref, inverse_ref, docs_ref, sems
 ):
-    act_ref, hidden_ref, in_proj_ref, out_proj_ref, inverse_ref, docs_ref, rows_ref, quarter_sems, sems = refs
     turns = (1, 3, 2, 0)
     quarter = act_ref.shape[1]
     width = in_proj_ref.shape[0]
+    half = quarter // 2
     place = lax.axis_index("proj")
-    fixed = [
-        pltpu.make_async_copy(source, target, sems.at[i])
-        for i, (source, target) in enumerate(
-            [(out_proj_hbm, out_proj_ref), (in_proj_hbm, in_proj_ref), (inverse_hbm, inverse_ref), (docs_hbm, docs_ref)]
-        )
-    ]
-    fixed[0].start()
-    moving = []
+    pairs = [(in_proj_hbm, in_proj_ref)]
     for g, turn in enumerate(turns):
-        start = jnp.bitwise_xor(place, turn) * quarter
-        hidden_rows = pl.ds(pl.multiple_of(start * top, quarter * top), quarter * top)
-        act_rows = pl.ds(pl.multiple_of(start, quarter), quarter)
-        moving.append(
-            (
-                pltpu.make_async_copy(hidden_hbm.at[hidden_rows], hidden_ref.at[g], quarter_sems.at[g, 0]),
-                pltpu.make_async_copy(act_hbm.at[act_rows], act_ref.at[g], quarter_sems.at[g, 1]),
-            )
-        )
-        moving[g][0].start()
+        rows = pl.ds(pl.multiple_of(jnp.bitwise_xor(place, turn) * quarter, quarter), quarter)
+        pairs.append((act_hbm.at[rows], act_ref.at[g]))
         if g == 0:
-            fixed[1].start()
-        moving[g][1].start()
-        if g == 0:
-            fixed[2].start()
-            fixed[3].start()
-    half = quarter // 2
-    first = low_lanes(quarter, width)
-    fixed[0].wait()
-    twice = jnp.concatenate([out_proj_ref[...], out_proj_ref[...]], axis=0)
+            pairs += [(inverse_hbm, inverse_ref), (docs_hbm, docs_ref)]
+    take = in_order([pltpu.make_async_copy(*pair, sems.at[i]) for i, pair in enumerate(pairs)], 5)
+    take()
+    first = low_lanes(half, width)
     for g in range(len(turns)):
         wire_ref = leaving_ref.at[g] if g < 2 else own_ref.at[g - 2]
-        moving[g][0].wait()
-        rows_ref[g % 2] = lax.dot_general(
-            hidden_ref[g], twice, (((1,), (1,)), ((), ())), preferred_element_type=jnp.float32
+        take()
+        if g == 0:
+            take()
+            take()
+            experts = inverse_ref.shape[0] // 2
+            for e in range(experts):
+                pair = jnp.concatenate([inverse_ref[e], inverse_ref[experts + e]], axis=1)
+                shared_ref[e * width : (e + 1) * width, :] = pair.astype(jnp.bfloat16)
+            docs = docs_ref[...].astype(jnp.float32)
+            docs = jnp.concatenate([docs, jnp.zeros((DOC_ROWS - docs.shape[0], LANES), jnp.float32)], axis=0)
+            shared_ref[experts * width :, :] = docs.astype(jnp.bfloat16)
+        twice = jnp.concatenate([in_proj_ref[...], in_proj_ref[...]], axis=0)
+        inner = lax.dot_general(
+            act_ref[g], twice, (((1,), (1,)), ((), ())), preferred_element_type=jnp.float32
         )
-        for pair in range(top // 2):
-            even = rows_ref[g % 2, pl.ds(2 * pair, quarter, stride=top), :]
-            odd = rows_ref[g % 2, pl.ds(2 * pair + 1, quarter, stride=top), :]
-            wire_ref[pair * quarter : (pair + 1) * quarter, :] = jnp.where(first, even, odd).astype(jnp.bfloat16)
-        if g == 0:
-            fixed[1].wait()
-        twice_in = jnp.concatenate([in_proj_ref[...], in_proj_ref[...]], axis=0)
-        moving[g][1].wait()
-        inner = lax.dot_general(
-            act_ref[g], twice_in, (((1,), (1,)), ((), ())), preferred_element_type=jnp.float32
-        )
-        high, low = split(jnp.where(low_lanes(half, width), inner[:half], inner[half:]))
-        start = top // 2 * quarter
-        wire_ref[start : start + half, :] = high
-        wire_ref[start + half :, :] = low
-        if g == 0:
-            fixed[2].wait()
-            fixed[3].wait()
-            pack_shared(inverse_ref, docs_ref, shared_ref)
-
-
-def project(activations, flat_hidden, in_projection, out_projection, inverse_out, doc_rows, quarters, top):
+        high, low = split(jnp.where(first, inner[:half], inner[half:]))
+        wire_ref[:half, :] = high
+        wire_ref[half:, :] = low
+
+
+def project_inner(activations, in_projection, inverse_out, doc_rows, quarters):
     tokens, model = activations.shape
     quarter = tokens // quarters
-    wire_rows = top // 2 * quarter + quarter
     experts, width, _ = inverse_out.shape
-    wire = jax.ShapeDtypeStruct((quarters // 2, wire_rows, LANES), jnp.bfloat16)
-    fixed = (in_projection, out_projection, inverse_out, doc_rows)
-    return pl.pallas_call(
-        functools.partial(project_kernel, top=top),
-        in_specs=[HBM] * 6,
+    wire = jax.ShapeDtypeStruct((quarters // 2, quarter, LANES), jnp.bfloat16)
+    fixed = (in_projection, inverse_out, doc_rows)
+    return pl.pallas_call(
+        inner_kernel,
+        in_specs=[HBM] * 4,
         out_specs=[VMEM] * 3,
         out_shape=[wire, wire, jax.ShapeDtypeStruct((experts // 2 * width + DOC_ROWS, LANES), jnp.bfloat16)],
+        scratch_shapes=[pltpu.VMEM((quarters, quarter, model), jnp.bfloat16)]
+        + [pltpu.VMEM(array.shape, array.dtype) for array in fixed]
+        + [pltpu.SemaphoreType.DMA((quarters + len(fixed),))],
+        compiler_params=pltpu.CompilerParams(vmem_limit_bytes=40 * MIB),
+        cost_estimate=cost(2.5),
+    )(*[stay(array) for array in (activations, *fixed)])
+
+
+def outer_kernel(hidden_hbm, out_proj_hbm, leaving_ref, own_ref, hidden_ref, out_proj_ref, rows_ref, sems, *, top):
+    turns = (1, 3, 2, 0)
+    chunks, chunk_rows, _ = hidden_ref.shape
+    chunk = chunk_rows // top
+    split_by = chunks // len(turns)
+    quarter = chunk * split_by
+    width = out_proj_ref.shape[0]
+    place = lax.axis_index("proj")
+    pairs = [(out_proj_hbm, out_proj_ref)]
+    for i in range(chunks):
+        start = (jnp.bitwise_xor(place, turns[i // split_by]) * split_by + i % split_by) * chunk_rows
+        pairs.append((hidden_hbm.at[pl.ds(pl.multiple_of(start, chunk_rows), chunk_rows)], hidden_ref.at[i]))
+    take = in_order([pltpu.make_async_copy(*pair, sems.at[i]) for i, pair in enumerate(pairs)], 4)
+    take()
+    first = low_lanes(chunk, width)
+
+    def pack_rows(i):
+        g, part = i // split_by, i % split_by
+        wire_ref = leaving_ref.at[g] if g < 2 else own_ref.at[g - 2]
+        for pair in range(top // 2):
+            even = rows_ref[i % 2, pl.ds(2 * pair, chunk, stride=top), :]
+            odd = rows_ref[i % 2, pl.ds(2 * pair + 1, chunk, stride=top), :]
+            start = pair * quarter + part * chunk
+            wire_ref[start : start + chunk, :] = jnp.where(first, even, odd).astype(jnp.bfloat16)
+
+    for i in range(chunks):
+        take()
+        twice = jnp.concatenate([out_proj_ref[...], out_proj_ref[...]], axis=0)
+        rows_ref[i % 2] = lax.dot_general(
+            hidden_ref[i], twice, (((1,), (1,)), ((), ())), preferred_element_type=jnp.float32
+        )
+        if i:
+            pack_rows(i - 1)
+    pack_rows(chunks - 1)
+
+
+def project_outer(flat_hidden, out_projection, quarters, top):
+    rows, hidden = flat_hidden.shape
+    chunks = 2 * quarters
+    wire = jax.ShapeDtypeStruct((quarters // 2, rows // quarters // 2, LANES), jnp.bfloat16)
+    return pl.pallas_call(
+        functools.partial(outer_kernel, top=top),
+        in_specs=[HBM] * 2,
+        out_specs=[VMEM] * 2,
+        out_shape=[wire, wire],
         scratch_shapes=[
-            pltpu.VMEM((quarters, quarter, model), jnp.bfloat16),
-            pltpu.VMEM((quarters, quarter * top, flat_hidden.shape[1]), jnp.bfloat16),
-        ]
-        + [pltpu.VMEM(array.shape, array.dtype) for array in fixed]
-        + [
-            pltpu.VMEM((2, quarter * top, LANES), jnp.float32),
-            pltpu.SemaphoreType.DMA((quarters, 2)),
-            pltpu.SemaphoreType.DMA((len(fixed),)),
+            pltpu.VMEM((chunks, rows // chunks, hidden), jnp.bfloat16),
+            pltpu.VMEM(out_projection.shape, out_projection.dtype),
+            pltpu.VMEM((2, rows // chunks, LANES), jnp.float32),
+            pltpu.SemaphoreType.DMA((chunks + 1,)),
         ],
         compiler_params=pltpu.CompilerParams(vmem_limit_bytes=40 * MIB),
-        cost_estimate=cost(5),
-    )(*[stay(array) for array in (activations, flat_hidden, *fixed)])
-
-
-def combine_kernel(own_ref, other_ref, out_ref, *, value_rows):
-    total = own_ref[0, :value_rows, :].astype(jnp.float32) + other_ref[1, :value_rows, :].astype(jnp.float32)
-    out_ref[:value_rows, :] = total.astype(jnp.bfloat16)
-    half = (out_ref.shape[0] - value_rows) // 2
-    exact = jnp.zeros((half, LANES), jnp.float32)
-    for part in (own_ref[0], other_ref[1]):
-        exact = exact + part[value_rows : value_rows + half].astype(jnp.float32)
-        exact = exact + part[value_rows + half :].astype(jnp.float32)
-    high, low = split(exact)
-    out_ref[value_rows : value_rows + half, :] = high
-    out_ref[value_rows + half :, :] = low
-
-
-def combine(own, other, value_rows):
-    return pl.pallas_call(
-        functools.partial(combine_kernel, value_rows=value_rows),
+        cost_estimate=cost(4),
+    )(stay(flat_hidden), stay(out_projection))
+
+
+def exact_rows(rows):
+    half = rows.shape[0] // 2
+    return rows[:half].astype(jnp.float32) + rows[half:].astype(jnp.float32)
+
+
+def combine_inner_kernel(own_ref, near_ref, out_ref):
+    high, low = split(exact_rows(own_ref[0]) + exact_rows(near_ref[1]))
+    out_ref[: high.shape[0], :] = high
+    out_ref[high.shape[0] :, :] = low
+
+
+def combine_outer_kernel(own_ref, near_ref, out_ref):
+    out_ref[...] = (own_ref[0].astype(jnp.float32) + near_ref[1].astype(jnp.float32)).astype(jnp.bfloat16)
+
+
+def combine(kernel, own, near):
+    return pl.pallas_call(
+        kernel,
         in_specs=[VMEM, VMEM],
         out_shape=jax.ShapeDtypeStruct(own.shape[1:], jnp.bfloat16),
         compiler_params=pltpu.CompilerParams(vmem_limit_bytes=40 * MIB),
-        cost_estimate=cost(1),
-    )(own, other)
+        cost_estimate=cost(0.5),
+    )(own, near)
+
+
+def finish_inner_kernel(own_ref, near_ref, far_ref, out_ref):
+    total = exact_rows(own_ref[1]) + exact_rows(near_ref[0]) + exact_rows(far_ref[...])
+    width = out_ref.shape[0]
+    total = jnp.concatenate([total[:, :width], total[:, width:]], axis=0)
+    out_ref[...] = jnp.transpose(total).astype(jnp.bfloat16)
+
+
+def finish_inner(own, near, far, width):
+    return pl.pallas_call(
+        finish_inner_kernel,
+        in_specs=[VMEM] * 3,
+        out_shape=jax.ShapeDtypeStruct((width, own.shape[1]), jnp.bfloat16),
+        cost_estimate=cost(0.5),
+    )(own, near, far)
 
 
 def expand_kernel(shared_ref, weights_ref, docs_ref, *, width, experts, shares, turns):
@@ -217,11 +261,6 @@
         value_ref[2 * pair + 1] = jnp.where(first, swapped, both)
     for k in range(top):
         name_ref[k] = jnp.broadcast_to(routes_ref[:, k : k + 1], (quarter, LANES)) - second
-    half = quarter // 2
-    inner = summed(top // 2 * quarter, half) + summed(top // 2 * quarter + half, half)
-    inner = jnp.concatenate([inner[:, :width], inner[:, width:]], axis=0)
-    inner = jnp.transpose(inner).astype(jnp.bfloat16)
-
     def one_group(step, carry):
         group = jnp.bitwise_xor(lax.axis_index("expert"), step)
         dense = []
@@ -236,9 +275,7 @@
         ).astype(jnp.bfloat16)
         share_width = result.shape[1] // shares
         for share in range(shares):
-            piece = result[:, share * share_width : (share + 1) * share_width]
-            payload_ref[group * shares + share, :quarter, :] = piece
-            payload_ref[group * shares + share, quarter:, :] = inner
+            payload_ref[group * shares + share] = result[:, share * share_width : (share + 1) * share_width]
         return carry
 
     lax.fori_loop(0, groups, one_group, 0, unroll=groups <= 4)
@@ -250,7 +287,7 @@
     return pl.pallas_call(
         functools.partial(condition_kernel, top=top, width=width),
         in_specs=[VMEM] * 5,
-        out_shape=jax.ShapeDtypeStruct((groups * shares, quarter + width, LANES), jnp.bfloat16),
+        out_shape=jax.ShapeDtypeStruct((groups * shares, quarter, LANES), jnp.bfloat16),
         scratch_shapes=[
             pltpu.VMEM((top, quarter, LANES), jnp.float32),
             pltpu.VMEM((top, quarter, LANES), jnp.int32),
@@ -319,15 +356,23 @@
     )(stay(query_grads), inverse_in)
 
 
-def score_kernel(arrived_ref, docs_ref, far_ref, out_ref, grads_ref, queries_ref, sem, *, width, doc_count, shares):
+def score_kernel(
+    arrived_ref, inner_ref, docs_ref, far_ref, out_ref, grads_ref, queries_ref, sem, *, width, doc_count, turns
+):
     fetch = pltpu.make_async_copy(far_ref, queries_ref, sem)
     fetch.start()
-    sources, rows, lanes = arrived_ref.shape
+    sources, quarter, lanes = arrived_ref.shape
+    shares = lax.axis_size("proj")
     owners = sources // shares
-    quarter = rows - width
-    outer = arrived_ref[:, :quarter, :].reshape(sources * quarter, lanes)
-    inner = jnp.concatenate([arrived_ref[s, quarter:, :] for s in range(sources)], axis=1)
-    docs = [docs_ref[s // shares, s % shares : s % shares + 1, :] for s in range(sources)]
+    outer, inner, docs = [], [], []
+    for entry, (owner_turn, share_turn) in enumerate(turns):
+        owner = jnp.bitwise_xor(lax.axis_index("expert"), owner_turn)
+        share = jnp.bitwise_xor(lax.axis_index("proj"), share_turn)
+        outer.append(arrived_ref[owner * shares + share])
+        docs.append(docs_ref[owner, pl.ds(share, 1), :])
+        inner.append(inner_ref[entry])
+    outer = jnp.concatenate(outer, axis=0)
+    inner = jnp.concatenate(inner, axis=1)
     docs = jnp.broadcast_to(jnp.concatenate(docs, axis=1), inner.shape)
     doc_group = 8
 
@@ -359,12 +404,13 @@
             out_ref[owner * shares + share] = jnp.concatenate([piece, fill], axis=1)
 
 
-def score(arrived, docs, queries, width, shares):
+def score(arrived, inner, docs, queries, turns):
     sources = arrived.shape[0]
-    doc_count = DOC_DEV * sources // shares
-    return pl.pallas_call(
-        functools.partial(score_kernel, width=width, doc_count=doc_count, shares=shares),
-        in_specs=[VMEM, VMEM, HBM],
+    width = inner.shape[1]
+    doc_count = DOC_DEV * docs.shape[0]
+    return pl.pallas_call(
+        functools.partial(score_kernel, width=width, doc_count=doc_count, turns=turns),
+        in_specs=[VMEM, VMEM, VMEM, HBM],
         out_shape=jax.ShapeDtypeStruct((sources, DOC_DEV, LANES), jnp.float32),
         scratch_shapes=[
             pltpu.VMEM((doc_count * width, arrived.shape[2]), jnp.float32),
@@ -373,7 +419,7 @@
         ],
         compiler_params=pltpu.CompilerParams(vmem_limit_bytes=40 * MIB),
         cost_estimate=cost(5),
-    )(arrived, docs, stay(queries))
+    )(arrived, inner, docs, stay(queries))
 
 
 def sum_kernel(pieces_ref, out_ref):
@@ -421,24 +467,39 @@
     assert DOC_DEV * owners <= 256
 
     flat_hidden = grad_hidden.reshape(tokens * top, grad_hidden.shape[2])
-    doc_rows = doc_ids.reshape(shares, quarter)
-    leaving, own, shared = project(
-        activations, flat_hidden, in_projection, out_projection, inverse_out, doc_rows, shares, top
+    inner_leaving, inner_own, shared = project_inner(
+        activations, in_projection, inverse_out, doc_ids.reshape(shares, quarter), shares
     )
+    far_shared = exchange(shared, "expert", owners, owners // 2)
+    inner_near = exchange(inner_leaving, "proj", shares, 1)
+    inner_far = exchange(combine(combine_inner_kernel, inner_own, inner_near), "proj", shares, 2)
+    leaving, own = project_outer(flat_hidden, out_projection, shares, top)
+    far_shared, inner_far, leaving = lax.optimization_barrier((far_shared, inner_far, leaving))
     near = exchange(leaving, "proj", shares, 1)
-    first = exchange(shared, "expert", owners, owners // 2)
-    shared, turns = jnp.stack([shared, first]), (0, owners // 2)
+    shared, turns = jnp.stack([shared, far_shared]), (0, owners // 2)
     for bit in reversed(range((owners // 2).bit_length() - 1)):
         shared, turns = double(shared, turns, "expert", owners, 1 << bit)
-    far = exchange(combine(own, near, top // 2 * quarter), "proj", shares, 2)
+    sent = combine(combine_outer_kernel, own, near)
+    far = exchange(sent, "proj", shares, 2)
+    inner = finish_inner(inner_own, inner_near, inner_far, width)
+    inner, _ = lax.optimization_barrier((inner, sent))
+    inner, owner_turns = inner[None], (0,)
+    for bit in reversed(range(owners.bit_length() - 1)):
+        inner, owner_turns = double(inner, owner_turns, "expert", owners, 1 << bit)
     weights, all_docs = expand(shared, turns, width, experts, shares)
     quarter_routes = lax.dynamic_slice_in_dim(routes, lax.axis_index("proj") * quarter, quarter, 0)
     payload = condition(own, near, far, quarter_routes, weights, shares, width)
-    payload, query_grads = lax.optimization_barrier((payload, query_grads))
+    payload, inner = lax.optimization_barrier((payload, inner))
     arrived = lax.all_to_all(payload, ("expert", "proj"), 0, 0, tiled=True)
+    inner, share_turns = inner[None], (0,)
+    inner, share_turns = double(inner, share_turns, "proj", shares, 1)
+    inner, query_grads = lax.optimization_barrier((inner, query_grads))
+    inner, share_turns = double(inner, share_turns, "proj", shares, 2)
+    inner = inner.reshape(owners * shares, width, quarter)
+    all_turns = tuple((o, p) for p in share_turns for o in owner_turns)
     queries = condition_queries(query_grads, inverse_in)
-    partial_scores = score(arrived, all_docs, queries, width, shares)
-    pieces = lax.all_to_all(partial_scores, ("expert", "proj"), 0, 0, tiled=True)
+    pieces = score(arrived, inner, all_docs, queries, all_turns)
+    pieces = lax.all_to_all(pieces, ("expert", "proj"), 0, 0, tiled=True)
     return sum_pieces(pieces, query_grads.shape[0] // shares).T
 
 

time: 68.6 us -> 68.2 us (level)
  waiting for transfers between devices: 14.4 us -> 6.68 us
  starting transfers between devices: 12.2 us -> 15.5 us
  Pallas kernels: 26.9 us -> 29.9 us
  other arithmetic: 0.04 us -> 1.53 us
  blocking collectives: 12.3 us -> 11.5 us
    all_to_all x1, waiting for transfers between devices: 6.64 us -> 0.01 us  [local(): arrived = lax.all_to_all(payload, ('expert', 'proj'), 0, 0, tiled=True)]
    ppermute x4 -> x10, starting transfers between devices: 6.55 us -> 11.9 us  [exchange(): return lax.ppermute(block, axis, [(i, i ^ turn) for i in range(size)])]
    pallas_call x2 -> x5, Pallas kernels: 6.22 us -> 9.34 us  [the longest x1 4.79 us: project_outer(): pl.pallas_call(functools.partial(outer_kernel, top=top), in_specs=[HBM] *...]
    all_to_all x1, starting transfers between devices: 5.68 us -> 3.57 us  [local(): arrived = lax.all_to_all(payload, ('expert', 'proj'), 0, 0, tiled=True)]
    concatenate x1 -> x5, other arithmetic: 0.03 us -> 1.52 us  [double(): jnp.concatenate([blocks, exchange(blocks, axis, size, turn)], axis=0)]
    ppermute x4 -> x10, waiting for transfers between devices: 7.77 us -> 6.68 us  [exchange(): return lax.ppermute(block, axis, [(i, i ^ turn) for i in range(size)])]
    all_to_all x1, blocking collectives: 12.3 us -> 11.5 us  [local(): pieces = lax.all_to_all(pieces, ('expert', 'proj'), 0, 0, tiled=True)]
    unnamed x7 -> x13, local copies, waits for them, and re-layouts: 2.06 us -> 2.07 us
  transfers between devices with their start and end apart: 5 -> 11, of which waited for: 4 -> 3; matrix products, arithmetic and copies ran while one was open for 0% -> 2% of each run, Pallas kernels for 16% -> 26%
where the time goes in v7:
time: 68.2 us; the launch traced here: 67.4 us
  Pallas kernels  29.9 us (44%)
  starting transfers between devices  15.5 us (23%)
  blocking collectives  11.5 us (17%)
  waiting for transfers between devices  6.68 us (10%)
  local copies, waits for them, and re-layouts  2.07 us (3%)
  other arithmetic  1.53 us (2%)
    ppermute x10, starting transfers between devices, exchange(): return lax.ppermute(block, axis, [(i, i ^ turn) for i in range(size)])  11.9 us
    all_to_all x1, blocking collectives, local(): pieces = lax.all_to_all(pieces, ('expert', 'proj'), 0, 0, tiled=True)  11.5 us
    pallas_call x1, Pallas kernels, condition_queries(): pl.pallas_call(query_kernel, grid=(flat // LANES,), in_specs=[pl.BlockSpe...  10.1 us
    ppermute x10, waiting for transfers between devices, exchange(): return lax.ppermute(block, axis, [(i, i ^ turn) for i in range(size)])  6.68 us
    pallas_call x1, Pallas kernels, score(): pl.pallas_call(functools.partial(score_kernel, width=width, doc_count=doc...  6.61 us
    pallas_call x1, Pallas kernels, project_outer(): pl.pallas_call(functools.partial(outer_kernel, top=top), in_specs=[HBM] *...  4.79 us
    all_to_all x1, starting transfers between devices, local(): arrived = lax.all_to_all(payload, ('expert', 'proj'), 0, 0, tiled=True)  3.57 us
    pallas_call x1, Pallas kernels, project_inner(): pl.pallas_call(inner_kernel, in_specs=[HBM] * 4, out_specs=[VMEM] * 3, ou...  2.89 us
  transfers between devices with their start and end apart: 11, of which 3 were waited for; matrix products, arithmetic and copies ran while one was open for 2% of the time, Pallas kernels for 26%

profile of v7, /device:TPU:0, one launch (start us, length us, event | category | flops | bytes accessed | tf_op | source)
XLA Modules:
  0.0 67.4 jit_solution(2604977371641724903)
XLA Ops:
  0.0 0.0 copy-start
  0.0 2.9 %shard_map.92 = (bf16[2,128,128]{2,1,0:T(8,128)(2,1)S(1)}, bf16[2,128,128]{2,1,0:T(8,128)(2,1)S(1)}, bf16[272,128]{1,0:T(8,128)(2,1)S(1)}) custom-call(bf16[512,1792]{1,0:T(8,128)(2,1)} %act_hbm.1, bf16[64,1792]{1,0:T(8,128)(2,1)} %in_proj_hbm.1, f32[8,64,64]{2,1,0:T(8,128)} %inverse_hbm.1, s32[4,128]{1,0:T(4,128)} %bitcast.19), custom_call_target="tpu_custom_call" | custom-call | bytes 8250000 | tf_op jit(solution)/shard_map/pallas_call | solution.py:94
  2.9 0.0 copy-start.3
  2.9 0.5 collective-permute-start.1
  3.4 3.7 %collective-permute-start = (bf16[272,128]{1,0:T(8,128)(2,1)S(1)}, bf16[272,128]{1,0:T(8,128)(2,1)S(1)}, u32[]{:S(2)}, u32[]{:S(2)}) collective-permute-start(bf16[272,128]{1,0:T(8,128)(2,1)S(1)} %get-tuple-element.21), channel_id=1, source_target_pairs={{0,8},{4,12},{8,0},{12,4},{1,9},{5,13},{9,1},{13,5},{2,10},{6,14},... | collective-permute-start | bytes 208904 | tf_op jit(solution)/shard_map/ppermute | solution.py:441
  7.1 0.0 collective-permute-done.1.near_ref
  7.1 0.0 copy-start.4
  7.1 1.6 %collective-permute-start.2 = (bf16[128,128]{1,0:T(8,128)(2,1)S(1)}, bf16[128,128]{1,0:T(8,128)(2,1)S(1)}, u32[]{:S(2)}, u32[]{:S(2)}) collective-permute-start(bf16[128,128]{1,0:T(8,128)(2,1)S(1)} %shard_map.93), channel_id=1, source_target_pairs={{0,2},{1,3},{2,0},{3,1},{4,6},{5,7},{6,4},{7,5},{8,10},{9,11},{10,... | collective-permute-start | bytes 98312 | tf_op jit(solution)/shard_map/ppermute | solution.py:441
  8.7 4.8 %shard_map.91 = (bf16[2,512,128]{2,1,0:T(8,128)(2,1)S(1)}, bf16[2,512,128]{2,1,0:T(8,128)(2,1)S(1)}) custom-call(bf16[4096,512]{1,0:T(8,128)(2,1)} %bitcast.11, bf16[64,512]{1,0:T(8,128)(2,1)} %out_proj_hbm.1), custom_call_target="tpu_custom_call" | custom-call | bytes 13200000 | tf_op jit(solution)/shard_map/pallas_call | solution.py:147
  13.5 0.0 copy-start.2
  13.5 0.0 collective-permute-done
  13.5 0.0 collective-permute-done.2.far_ref
  13.5 0.0 copy-start.5
  13.5 0.1 collective-permute-start.3
  13.6 1.6 %collective-permute-start.5 = (bf16[2,272,128]{2,1,0:T(8,128)(2,1)S(1)}, bf16[2,272,128]{2,1,0:T(8,128)(2,1)S(1)}, u32[]{:S(2)}, u32[]{:S(2)}) collective-permute-start(bf16[2,272,128]{2,1,0:T(8,128)(2,1)S(1)} %pad_maximum_fusion.2), channel_id=1, source_target_pairs={{0,4},{4,0},{8,12},{12,8},{1,5},{5,1},{9,13},{13,9},{2,6},{6,2},{1... | collective-permute-start | bytes 417800 | tf_op jit(solution)/shard_map/ppermute | solution.py:441
  15.3 0.0 copy-done.3
  15.3 0.0 copy-done.4
  15.3 0.0 copy-done.5
  15.3 1.6 %shard_map.97 = bf16[64,128]{1,0:T(8,128)(2,1)} custom-call(bf16[2,128,128]{2,1,0:T(8,128)(2,1)} %copy-done.3, bf16[2,128,128]{2,1,0:T(8,128)(2,1)} %copy-done.4, bf16[128,128]{1,0:T(8,128)(2,1)} %copy-done.5), custom_call_target="tpu_custom_call" | custom-call | bytes 1650000 | tf_op jit(solution)/shard_map/pallas_call | solution.py:196
  16.9 0.0 collective-permute-done.3.near_ref
  16.9 1.2 %collective-permute-start.6 = (bf16[1,64,128]{2,1,0:T(8,128)(2,1)}, bf16[1,64,128]{2,1,0:T(8,128)(2,1)S(1)}, u32[]{:S(2)}, u32[]{:S(2)}) collective-permute-start(bf16[1,64,128]{2,1,0:T(8,128)(2,1)} %bitcast.16), channel_id=1, source_target_pairs={{0,8},{4,12},{8,0},{12,4},{1,9},{5,13},{9,1},{13,5},{2,10},{6,14},... | collective-permute-start | bytes 49160 | tf_op jit(solution)/shard_map/ppermute | solution.py:441
  18.2 0.0 copy-done
  18.2 0.1 copy.11.routes_ref
  18.3 0.8 %collective-permute-start.4 = (bf16[512,128]{1,0:T(8,128)(2,1)S(1)}, bf16[512,128]{1,0:T(8,128)(2,1)S(1)}, u32[]{:S(2)}, u32[]{:S(2)}) collective-permute-start(bf16[512,128]{1,0:T(8,128)(2,1)S(1)} %shard_map.94), channel_id=1, source_target_pairs={{0,2},{1,3},{2,0},{3,1},{4,6},{5,7},{6,4},{7,5},{8,10},{9,11},{10,... | collective-permute-start | bytes 393224 | tf_op jit(solution)/shard_map/ppermute | solution.py:441
  19.0 2.9 %collective-permute-done.6 = bf16[1,64,128]{2,1,0:T(8,128)(2,1)S(1)} collective-permute-done((bf16[1,64,128]{2,1,0:T(8,128)(2,1)}, bf16[1,64,128]{2,1,0:T(8,128)(2,1)S(1)}, u32[]{:S(2)}, u32[]{:S(2)}) %collective-permute-start.6) | collective-permute-done | bytes 16416 | tf_op jit(solution)/shard_map/ppermute | solution.py:441
  21.9 0.7 %pad_maximum_fusion.5 = bf16[2,64,128]{2,1,0:T(8,128)(2,1)S(1)} fusion(bf16[1,64,128]{2,1,0:T(8,128)(2,1)S(1)} %collective-permute-done.6, bf16[1,64,128]{2,1,0:T(8,128)(2,1)} %bitcast.17), kind=kLoop, calls=%fused_computation.5 | loop fusion | flops 16384 | bytes 65536 | tf_op jit(solution)/shard_map/concatenate | solution.py:445
  22.6 0.4 collective-permute-start.7
  23.0 0.0 collective-permute-done.5
  23.0 0.7 %shard_map.95 = (bf16[4,512,512]{2,1,0:T(8,128)(2,1)S(1)}, s32[4,16,128]{2,1,0:T(8,128)S(1)}) custom-call(bf16[4,272,128]{2,1,0:T(8,128)(2,1)S(1)} %pad_maximum_fusion.shared_ref), custom_call_target="tpu_custom_call" | custom-call | bytes 4290000 | tf_op jit(solution)/shard_map/pallas_call | solution.py:230
  23.8 2.7 %collective-permute-done.7 = bf16[2,64,128]{2,1,0:T(8,128)(2,1)S(1)} collective-permute-done((bf16[2,64,128]{2,1,0:T(8,128)(2,1)S(1)}, bf16[2,64,128]{2,1,0:T(8,128)(2,1)S(1)}, u32[]{:S(2)}, u32[]{:S(2)}) %collective-permute-start.7) | collective-permute-done | bytes 32800 | tf_op jit(solution)/shard_map/ppermute | solution.py:441
  26.5 0.7 %pad_maximum_fusion.4 = bf16[4,64,128]{2,1,0:T(8,128)(2,1)S(1)} fusion(bf16[2,64,128]{2,1,0:T(8,128)(2,1)S(1)} %collective-permute-done.7, bf16[1,64,128]{2,1,0:T(8,128)(2,1)S(1)} %collective-permute-done.6, bf16[1,64,128]{2,1,0:T(8,128)(2,1)} %bitcast.18), kind=kLoop, calls=%fused_computation.4 | loop fusion | flops 65536 | bytes 131072 | tf_op jit(solution)/shard_map/concatenate | solution.py:445
  27.3 0.0 collective-permute-done.4.far_ref
  27.3 1.7 %shard_map.96 = bf16[16,128,128]{2,1,0:T(8,128)(2,1)} custom-call(bf16[2,512,128]{2,1,0:T(8,128)(2,1)S(1)} %get-tuple-element.20.own_ref, bf16[2,512,128]{2,1,0:T(8,128)(2,1)S(1)} %collective-permute-done.3.near_ref, bf16[512,128]{1,0:T(8,128)(2,1)S(1)} %collective-permute-done.4.far_ref, s32[128,8]{1,0:T(8,128)S(1)} %copy.11.routes_ref, ...), custom_call_target="tpu_custom_call" | custom-call | bytes 6600000 | tf_op jit(solution)/shard_map/pallas_call | solution.py:287
  29.0 3.6 %all-to-all-start = ((bf16[16,128,128]{2,1,0:T(8,128)(2,1)}), bf16[16,128,128]{2,1,0:T(8,128)(2,1)S(1)}, u32[]{:S(2)}, u32[]{:S(2)}) async-start(bf16[16,128,128]{2,1,0:T(8,128)(2,1)} %shard_map.96), calls=%async_computation | async-start | bytes 1048576 | tf_op jit(solution)/shard_map/all_to_all | solution.py:493
  32.6 0.3 collective-permute-start.8
  32.9 1.0 %collective-permute-done.8 = bf16[1,4,64,128]{3,2,1,0:T(8,128)(2,1)S(1)} collective-permute-done((bf16[1,4,64,128]{3,2,1,0:T(8,128)(2,1)S(1)}, bf16[1,4,64,128]{3,2,1,0:T(8,128)(2,1)S(1)}, u32[]{:S(2)}, u32[]{:S(2)}) %collective-permute-start.8) | collective-permute-done | bytes 65568 | tf_op jit(solution)/shard_map/ppermute | solution.py:441
  33.9 1.8 %collective-permute-start.9 = (bf16[2,4,64,128]{3,2,1,0:T(8,128)(2,1)S(1)}, bf16[2,4,64,128]{3,2,1,0:T(8,128)(2,1)S(1)}, u32[]{:S(2)}, u32[]{:S(2)}) collective-permute-start(bf16[2,4,64,128]{3,2,1,0:T(8,128)(2,1)S(1)} %pad_maximum_fusion.3), channel_id=1, source_target_pairs={{0,2},{1,3},{2,0},{3,1},{4,6},{5,7},{6,4},{7,5},{8,10},{9,11},{10,... | collective-permute-start | bytes 393224 | tf_op jit(solution)/shard_map/ppermute | solution.py:441
  35.7 0.0 copy-done.2
  35.7 10.1 %shard_map.98.far_ref = bf16[8192,256]{1,0:T(8,128)(2,1)S(1)} custom-call(bf16[256,8,1024]{2,1,0:T(8,128)(2,1)} %query_ref, f32[8,64,64]{2,1,0:T(8,128)S(1)} %copy-done.2), custom_call_target="tpu_custom_call" | custom-call | bytes 33000000 | tf_op jit(solution)/shard_map/pallas_call | solution.py:340
  45.8 0.0 copy-start.1
  45.8 1.9 %copy-done.1 = bf16[8192,256]{1,0:T(8,128)(2,1)} copy-done((bf16[8192,256]{1,0:T(8,128)(2,1)}, bf16[8192,256]{1,0:T(8,128)(2,1)S(1)}, u32[]{:S(2)}) %copy-start.1) | copy-done | bytes 4194328
  47.8 0.0 collective-permute-done.9
  47.8 0.0 all-to-all-done.arrived_ref
  47.8 6.6 %shard_map.99 = f32[16,8,128]{2,1,0:T(8,128)S(1)} custom-call(bf16[16,128,128]{2,1,0:T(8,128)(2,1)S(1)} %all-to-all-done.arrived_ref, bf16[16,64,128]{2,1,0:T(8,128)(2,1)S(1)} %bitcast.8, s32[4,16,128]{2,1,0:T(8,128)S(1)} %get-tuple-element.33.docs_ref, bf16[8192,256]{1,0:T(8,128)(2,1)} %copy-done.1), custom_call_target="tpu_custom_call" | custom-call | bytes 16500000 | tf_op jit(solution)/shard_map/pallas_call | solution.py:411
  54.4 11.5 %all_to_all.10.pieces_ref = f32[16,8,128]{2,1,0:T(8,128)} all-to-all(f32[16,8,128]{2,1,0:T(8,128)S(1)} %shard_map.99), channel_id=1, replica_groups=mesh['groups'=2,'expert'=4,'proj'=4] {'expert','proj'}, dimensions={0} | all-to-all | bytes 131072 | tf_op jit(solution)/shard_map/all_to_all | solution.py:502
  66.0 1.4 %shard_map.100 = f32[8,64]{1,0:T(8,128)} custom-call(f32[16,8,128]{2,1,0:T(8,128)} %all_to_all.10.pieces_ref), custom_call_target="tpu_custom_call" | custom-call | tf_op jit(solution)/shard_map/pallas_call | solution.py:433
  (7 shorter events, 0.1 us)
Async XLA Ops:
  0.0 18.2 %copy-start = (s32[512,8]{0,1:T(8,128)S(1)}, s32[512,8]{0,1:T(8,128)}, u32[]{:S(2)}) copy-start(s32[512,8]{0,1:T(8,128)} %param.11) | copy-start | bytes 49156
  2.9 12.4 %copy-start.3 = (bf16[2,128,128]{2,1,0:T(8,128)(2,1)}, bf16[2,128,128]{2,1,0:T(8,128)(2,1)S(1)}, u32[]{:S(2)}) copy-start(bf16[2,128,128]{2,1,0:T(8,128)(2,1)S(1)} %get-tuple-element.22.own_ref) | copy-start | bytes 196612
  2.9 4.2 %collective-permute-start.1 = (bf16[2,128,128]{2,1,0:T(8,128)(2,1)S(1)}, bf16[2,128,128]{2,1,0:T(8,128)(2,1)S(1)}, u32[]{:S(2)}, u32[]{:S(2)}) collective-permute-start(bf16[2,128,128]{2,1,0:T(8,128)(2,1)S(1)} %get-tuple-element.23), channel_id=1, source_target_pairs={{0,1},{1,0},{2,3},{3,2},{4,5},{5,4},{6,7},{7,6},{8,9},{9,8},{10,11... | collective-permute-start | bytes 196616 | tf_op jit(solution)/shard_map/ppermute | solution.py:441
  3.4 10.1 %collective-permute-start = (bf16[272,128]{1,0:T(8,128)(2,1)S(1)}, bf16[272,128]{1,0:T(8,128)(2,1)S(1)}, u32[]{:S(2)}, u32[]{:S(2)}) collective-permute-start(bf16[272,128]{1,0:T(8,128)(2,1)S(1)} %get-tuple-element.21), channel_id=1, source_target_pairs={{0,8},{4,12},{8,0},{12,4},{1,9},{5,13},{9,1},{13,5},{2,10},{6,14},... | collective-permute-start | bytes 208904 | tf_op jit(solution)/shard_map/ppermute | solution.py:441
  7.1 8.2 %copy-start.4 = (bf16[2,128,128]{2,1,0:T(8,128)(2,1)}, bf16[2,128,128]{2,1,0:T(8,128)(2,1)S(1)}, u32[]{:S(2)}) copy-start(bf16[2,128,128]{2,1,0:T(8,128)(2,1)S(1)} %collective-permute-done.1.near_ref) | copy-start | bytes 196612
  7.1 6.4 %collective-permute-start.2 = (bf16[128,128]{1,0:T(8,128)(2,1)S(1)}, bf16[128,128]{1,0:T(8,128)(2,1)S(1)}, u32[]{:S(2)}, u32[]{:S(2)}) collective-permute-start(bf16[128,128]{1,0:T(8,128)(2,1)S(1)} %shard_map.93), channel_id=1, source_target_pairs={{0,2},{1,3},{2,0},{3,1},{4,6},{5,7},{6,4},{7,5},{8,10},{9,11},{10,... | collective-permute-start | bytes 98312 | tf_op jit(solution)/shard_map/ppermute | solution.py:441
  13.5 22.3 %copy-start.2 = (f32[8,64,64]{2,1,0:T(8,128)S(1)}, f32[8,64,64]{2,1,0:T(8,128)}, u32[]{:S(2)}) copy-start(f32[8,64,64]{2,1,0:T(8,128)} %inverse_ref.1) | copy-start | bytes 393220
  13.5 1.8 %copy-start.5 = (bf16[128,128]{1,0:T(8,128)(2,1)}, bf16[128,128]{1,0:T(8,128)(2,1)S(1)}, u32[]{:S(2)}) copy-start(bf16[128,128]{1,0:T(8,128)(2,1)S(1)} %collective-permute-done.2.far_ref) | copy-start | bytes 98308
  13.5 3.4 %collective-permute-start.3 = (bf16[2,512,128]{2,1,0:T(8,128)(2,1)S(1)}, bf16[2,512,128]{2,1,0:T(8,128)(2,1)S(1)}, u32[]{:S(2)}, u32[]{:S(2)}) collective-permute-start(bf16[2,512,128]{2,1,0:T(8,128)(2,1)S(1)} %get-tuple-element.25), channel_id=1, source_target_pairs={{0,1},{1,0},{2,3},{3,2},{4,5},{5,4},{6,7},{7,6},{8,9},{9,8},{10,11... | collective-permute-start | bytes 786440 | tf_op jit(solution)/shard_map/ppermute | solution.py:441
  13.6 9.4 %collective-permute-start.5 = (bf16[2,272,128]{2,1,0:T(8,128)(2,1)S(1)}, bf16[2,272,128]{2,1,0:T(8,128)(2,1)S(1)}, u32[]{:S(2)}, u32[]{:S(2)}) collective-permute-start(bf16[2,272,128]{2,1,0:T(8,128)(2,1)S(1)} %pad_maximum_fusion.2), channel_id=1, source_target_pairs={{0,4},{4,0},{8,12},{12,8},{1,5},{5,1},{9,13},{13,9},{2,6},{6,2},{1... | collective-permute-start | bytes 417800 | tf_op jit(solution)/shard_map/ppermute | solution.py:441
  16.9 5.0 %collective-permute-start.6 = (bf16[1,64,128]{2,1,0:T(8,128)(2,1)}, bf16[1,64,128]{2,1,0:T(8,128)(2,1)S(1)}, u32[]{:S(2)}, u32[]{:S(2)}) collective-permute-start(bf16[1,64,128]{2,1,0:T(8,128)(2,1)} %bitcast.16), channel_id=1, source_target_pairs={{0,8},{4,12},{8,0},{12,4},{1,9},{5,13},{9,1},{13,5},{2,10},{6,14},... | collective-permute-start | bytes 49160 | tf_op jit(solution)/shard_map/ppermute | solution.py:441
  18.3 9.0 %collective-permute-start.4 = (bf16[512,128]{1,0:T(8,128)(2,1)S(1)}, bf16[512,128]{1,0:T(8,128)(2,1)S(1)}, u32[]{:S(2)}, u32[]{:S(2)}) collective-permute-start(bf16[512,128]{1,0:T(8,128)(2,1)S(1)} %shard_map.94), channel_id=1, source_target_pairs={{0,2},{1,3},{2,0},{3,1},{4,6},{5,7},{6,4},{7,5},{8,10},{9,11},{10,... | collective-permute-start | bytes 393224 | tf_op jit(solution)/shard_map/ppermute | solution.py:441
  22.6 3.9 %collective-permute-start.7 = (bf16[2,64,128]{2,1,0:T(8,128)(2,1)S(1)}, bf16[2,64,128]{2,1,0:T(8,128)(2,1)S(1)}, u32[]{:S(2)}, u32[]{:S(2)}) collective-permute-start(bf16[2,64,128]{2,1,0:T(8,128)(2,1)S(1)} %pad_maximum_fusion.5), channel_id=1, source_target_pairs={{0,4},{4,0},{8,12},{12,8},{1,5},{5,1},{9,13},{13,9},{2,6},{6,2},{1... | collective-permute-start | bytes 98312 | tf_op jit(solution)/shard_map/ppermute | solution.py:441
  29.0 18.8 %all-to-all-start = ((bf16[16,128,128]{2,1,0:T(8,128)(2,1)}), bf16[16,128,128]{2,1,0:T(8,128)(2,1)S(1)}, u32[]{:S(2)}, u32[]{:S(2)}) async-start(bf16[16,128,128]{2,1,0:T(8,128)(2,1)} %shard_map.96), calls=%async_computation | async-start | bytes 1048576 | tf_op jit(solution)/shard_map/all_to_all | solution.py:493
  32.6 1.3 %collective-permute-start.8 = (bf16[1,4,64,128]{3,2,1,0:T(8,128)(2,1)S(1)}, bf16[1,4,64,128]{3,2,1,0:T(8,128)(2,1)S(1)}, u32[]{:S(2)}, u32[]{:S(2)}) collective-permute-start(bf16[1,4,64,128]{3,2,1,0:T(8,128)(2,1)S(1)} %bitcast.14), channel_id=1, source_target_pairs={{0,1},{1,0},{2,3},{3,2},{4,5},{5,4},{6,7},{7,6},{8,9},{9,8},{10,11... | collective-permute-start | bytes 196616 | tf_op jit(solution)/shard_map/ppermute | solution.py:441
  33.9 13.9 %collective-permute-start.9 = (bf16[2,4,64,128]{3,2,1,0:T(8,128)(2,1)S(1)}, bf16[2,4,64,128]{3,2,1,0:T(8,128)(2,1)S(1)}, u32[]{:S(2)}, u32[]{:S(2)}) collective-permute-start(bf16[2,4,64,128]{3,2,1,0:T(8,128)(2,1)S(1)} %pad_maximum_fusion.3), channel_id=1, source_target_pairs={{0,2},{1,3},{2,0},{3,1},{4,6},{5,7},{6,4},{7,5},{8,10},{9,11},{10,... | collective-permute-start | bytes 393224 | tf_op jit(solution)/shard_map/ppermute | solution.py:441
  45.8 1.9 %copy-start.1 = (bf16[8192,256]{1,0:T(8,128)(2,1)}, bf16[8192,256]{1,0:T(8,128)(2,1)S(1)}, u32[]{:S(2)}) copy-start(bf16[8192,256]{1,0:T(8,128)(2,1)S(1)} %shard_map.98.far_ref) | copy-start | bytes 12582916

commit v8 on v7

--- a/solution.py
+++ b/solution.py
@@ -197,6 +197,7 @@
         finish_inner_kernel,
         in_specs=[VMEM] * 3,
         out_shape=jax.ShapeDtypeStruct((width, own.shape[1]), jnp.bfloat16),
+        compiler_params=pltpu.CompilerParams(vmem_limit_bytes=40 * MIB),
         cost_estimate=cost(0.5),
     )(own, near, far)
 
@@ -308,19 +309,17 @@
         zeros = jnp.zeros((width, width), jnp.bfloat16)
         for e in range(experts):
             high, low = split(inverse_ref[e])
-            upper = jnp.concatenate([high, zeros, low, zeros], axis=1)
-            lower = jnp.concatenate([zeros, high, zeros, low], axis=1)
-            factor_ref[e] = jnp.concatenate([upper, lower], axis=0)
+            left = jnp.concatenate([high, zeros, low, zeros], axis=0)
+            right = jnp.concatenate([zeros, high, zeros, low], axis=0)
+            factor_ref[e] = jnp.concatenate([left, right], axis=1)
 
     spread_ref[...] = query_ref[...].astype(jnp.float32).reshape(count * experts, LANES)
     for e in range(experts):
         query = spread_ref[pl.ds(e, count, stride=experts), :].astype(jnp.bfloat16)
         result = lax.dot_general(
-            factor_ref[e],
-            jnp.concatenate([query, query], axis=1),
-            (((1,), (1,)), ((), ())),
-            preferred_element_type=jnp.float32,
+            factor_ref[e], query, (((1,), (1,)), ((), ())), preferred_element_type=jnp.float32
         )
+        result = result[: 2 * width] + result[2 * width :]
         start = e * (rows // experts) + 2 * step
         for tile in range(wide_ref.shape[0]):
             part = result[:, tile * LANES : (tile + 1) * LANES]
@@ -347,7 +346,7 @@
         out_specs=pl.BlockSpec((rows, count), lambda c: (0, 0)),
         out_shape=jax.ShapeDtypeStruct((rows, count), jnp.bfloat16),
         scratch_shapes=[
-            pltpu.VMEM((experts, 2 * width, 4 * width), jnp.bfloat16),
+            pltpu.VMEM((experts, 4 * width, 2 * width), jnp.bfloat16),
             pltpu.VMEM((count * experts, LANES), jnp.float32),
             pltpu.VMEM((count // LANES, rows, LANES), jnp.float32),
         ],
@@ -434,6 +433,7 @@
         sum_kernel,
         in_specs=[VMEM],
         out_shape=jax.ShapeDtypeStruct((pieces.shape[1], columns), jnp.float32),
+        compiler_params=pltpu.CompilerParams(vmem_limit_bytes=40 * MIB),
     )(pieces)
 
 
@@ -483,14 +483,15 @@
     far = exchange(sent, "proj", shares, 2)
     inner = finish_inner(inner_own, inner_near, inner_far, width)
     inner, _ = lax.optimization_barrier((inner, sent))
-    inner, owner_turns = inner[None], (0,)
-    for bit in reversed(range(owners.bit_length() - 1)):
+    inner, owner_turns = double(inner[None], (0,), "expert", owners, owners // 2)
+    inner, far, shared = lax.optimization_barrier((inner, far, shared))
+    for bit in reversed(range((owners // 2).bit_length() - 1)):
         inner, owner_turns = double(inner, owner_turns, "expert", owners, 1 << bit)
     weights, all_docs = expand(shared, turns, width, experts, shares)
     quarter_routes = lax.dynamic_slice_in_dim(routes, lax.axis_index("proj") * quarter, quarter, 0)
     payload = condition(own, near, far, quarter_routes, weights, shares, width)
-    payload, inner = lax.optimization_barrier((payload, inner))
     arrived = lax.all_to_all(payload, ("expert", "proj"), 0, 0, tiled=True)
+    inner, _ = lax.optimization_barrier((inner, payload))
     inner, share_turns = inner[None], (0,)
     inner, share_turns = double(inner, share_turns, "proj", shares, 1)
     inner, query_grads = lax.optimization_barrier((inner, query_grads))

time: 68.2 us -> 73.1 us (1.072)
  waiting for transfers between devices: 6.68 us -> 13.7 us
  Pallas kernels: 29.9 us -> 27.7 us
  other arithmetic: 1.53 us -> 0.1 us
  blocking collectives: 11.5 us -> 12.4 us
  starting transfers between devices: 15.5 us -> 16.3 us
    ppermute x10, waiting for transfers between devices: 6.68 us -> 13.7 us  [exchange(): return lax.ppermute(block, axis, [(i, i ^ turn) for i in range(size)])]
    pallas_call x1, Pallas kernels: 1.61 us -> 0.11 us  [finish_inner(): pl.pallas_call(finish_inner_kernel, in_specs=[VMEM] * 3, out_shape=jax.Sh...]
    concatenate x5, other arithmetic: 1.52 us -> 0.08 us  [double(): jnp.concatenate([blocks, exchange(blocks, axis, size, turn)], axis=0)]
    all_to_all x1, blocking collectives: 11.5 us -> 12.4 us  [local(): pieces = lax.all_to_all(pieces, ('expert', 'proj'), 0, 0, tiled=True)]
    pallas_call x1, Pallas kernels: 1.45 us -> 0.61 us  [sum_pieces(): pl.pallas_call(sum_kernel, in_specs=[VMEM], out_shape=jax.ShapeDtypeStruc...]
    ppermute x10, starting transfers between devices: 11.9 us -> 12.7 us  [exchange(): return lax.ppermute(block, axis, [(i, i ^ turn) for i in range(size)])]
    unnamed x13 -> x7, local copies, waits for them, and re-layouts: 2.07 us -> 2.07 us
  transfers between devices with their start and end apart: 11 -> 11, of which waited for: 3 -> 5; matrix products, arithmetic and copies ran while one was open for 2% -> 0% of each run, Pallas kernels for 26% -> 21%
where the time goes in v8:
time: 73.1 us; the launch traced here: 72.5 us
  Pallas kernels  27.7 us (38%)
  starting transfers between devices  16.3 us (22%)
  waiting for transfers between devices  13.7 us (19%)
  blocking collectives  12.4 us (17%)
  local copies, waits for them, and re-layouts  2.07 us (3%)
    ppermute x10, waiting for transfers between devices, exchange(): return lax.ppermute(block, axis, [(i, i ^ turn) for i in range(size)])  13.7 us
    ppermute x10, starting transfers between devices, exchange(): return lax.ppermute(block, axis, [(i, i ^ turn) for i in range(size)])  12.7 us
    all_to_all x1, blocking collectives, local(): pieces = lax.all_to_all(pieces, ('expert', 'proj'), 0, 0, tiled=True)  12.4 us
    pallas_call x1, Pallas kernels, condition_queries(): pl.pallas_call(query_kernel, grid=(flat // LANES,), in_specs=[pl.BlockSpe...  10.2 us
    pallas_call x1, Pallas kernels, score(): pl.pallas_call(functools.partial(score_kernel, width=width, doc_count=doc...  6.61 us
    pallas_call x1, Pallas kernels, project_outer(): pl.pallas_call(functools.partial(outer_kernel, top=top), in_specs=[HBM] *...  4.79 us
    all_to_all x1, starting transfers between devices, local(): arrived = lax.all_to_all(payload, ('expert', 'proj'), 0, 0, tiled=True)  3.67 us
    pallas_call x1, Pallas kernels, project_inner(): pl.pallas_call(inner_kernel, in_specs=[HBM] * 4, out_specs=[VMEM] * 3, ou...  2.89 us
  transfers between devices with their start and end apart: 11, of which 5 were waited for; matrix products, arithmetic and copies ran while one was open for 0% of the time, Pallas kernels for 21%

profile of v8, /device:TPU:0, one launch (start us, length us, event | category | flops | bytes accessed | tf_op | source)
XLA Modules:
  0.0 72.5 jit_solution(16505251245572357391)
XLA Ops:
  0.0 0.0 copy-start
  0.0 2.9 %shard_map.92 = (bf16[2,128,128]{2,1,0:T(8,128)(2,1)S(1)}, bf16[2,128,128]{2,1,0:T(8,128)(2,1)S(1)}, bf16[272,128]{1,0:T(8,128)(2,1)S(1)}) custom-call(bf16[512,1792]{1,0:T(8,128)(2,1)} %act_hbm.1, bf16[64,1792]{1,0:T(8,128)(2,1)} %in_proj_hbm.1, f32[8,64,64]{2,1,0:T(8,128)} %inverse_hbm.1, s32[4,128]{1,0:T(4,128)} %bitcast.18), custom_call_target="tpu_custom_call" | custom-call | bytes 8250000 | tf_op jit(solution)/shard_map/pallas_call | solution.py:94
  2.9 0.5 collective-permute-start.1
  3.4 3.7 %collective-permute-start = (bf16[272,128]{1,0:T(8,128)(2,1)S(1)}, bf16[272,128]{1,0:T(8,128)(2,1)S(1)}, u32[]{:S(2)}, u32[]{:S(2)}) collective-permute-start(bf16[272,128]{1,0:T(8,128)(2,1)S(1)} %get-tuple-element.23), channel_id=1, source_target_pairs={{0,8},{4,12},{8,0},{12,4},{1,9},{5,13},{9,1},{13,5},{2,10},{6,14},... | collective-permute-start | bytes 208904 | tf_op jit(solution)/shard_map/ppermute | solution.py:441
  7.1 0.0 collective-permute-done.1.near_ref
  7.1 1.6 %collective-permute-start.2 = (bf16[128,128]{1,0:T(8,128)(2,1)S(1)}, bf16[128,128]{1,0:T(8,128)(2,1)S(1)}, u32[]{:S(2)}, u32[]{:S(2)}) collective-permute-start(bf16[128,128]{1,0:T(8,128)(2,1)S(1)} %shard_map.93), channel_id=1, source_target_pairs={{0,2},{1,3},{2,0},{3,1},{4,6},{5,7},{6,4},{7,5},{8,10},{9,11},{10,... | collective-permute-start | bytes 98312 | tf_op jit(solution)/shard_map/ppermute | solution.py:441
  8.7 4.8 %shard_map.91 = (bf16[2,512,128]{2,1,0:T(8,128)(2,1)S(1)}, bf16[2,512,128]{2,1,0:T(8,128)(2,1)S(1)}) custom-call(bf16[4096,512]{1,0:T(8,128)(2,1)} %bitcast.13, bf16[64,512]{1,0:T(8,128)(2,1)} %out_proj_hbm.1), custom_call_target="tpu_custom_call" | custom-call | bytes 13200000 | tf_op jit(solution)/shard_map/pallas_call | solution.py:147
  13.5 0.0 copy-start.2
  13.5 0.0 collective-permute-done
  13.5 0.0 collective-permute-done.2.far_ref
  13.5 0.1 collective-permute-start.3
  13.6 1.6 %collective-permute-start.6 = (bf16[2,272,128]{2,1,0:T(8,128)(2,1)S(1)}, bf16[2,272,128]{2,1,0:T(8,128)(2,1)S(1)}, u32[]{:S(2)}, u32[]{:S(2)}) collective-permute-start(bf16[2,272,128]{2,1,0:T(8,128)(2,1)S(1)} %pad_maximum_fusion.2), channel_id=1, source_target_pairs={{0,4},{4,0},{8,12},{12,8},{1,5},{5,1},{9,13},{13,9},{2,6},{6,2},{1... | collective-permute-start | bytes 417800 | tf_op jit(solution)/shard_map/ppermute | solution.py:441
  15.2 0.0 copy-done
  15.2 0.1 copy.11.routes_ref
  15.3 0.1 shard_map.94
  15.5 0.0 collective-permute-done.3.near_ref
  15.5 0.6 collective-permute-start.5
  16.1 1.3 %collective-permute-start.4 = (bf16[1,64,128]{2,1,0:T(8,128)(2,1)S(1)}, bf16[1,64,128]{2,1,0:T(8,128)(2,1)S(1)}, u32[]{:S(2)}, u32[]{:S(2)}) collective-permute-start(bf16[1,64,128]{2,1,0:T(8,128)(2,1)S(1)} %bitcast.11), channel_id=1, source_target_pairs={{0,8},{4,12},{8,0},{12,4},{1,9},{5,13},{9,1},{13,5},{2,10},{6,14},... | collective-permute-start | bytes 49160 | tf_op jit(solution)/shard_map/ppermute | solution.py:441
  17.5 2.4 %collective-permute-done.6 = bf16[2,272,128]{2,1,0:T(8,128)(2,1)S(1)} collective-permute-done((bf16[2,272,128]{2,1,0:T(8,128)(2,1)S(1)}, bf16[2,272,128]{2,1,0:T(8,128)(2,1)S(1)}, u32[]{:S(2)}, u32[]{:S(2)}) %collective-permute-start.6) | collective-permute-done | bytes 139296 | tf_op jit(solution)/shard_map/ppermute | solution.py:441
  19.9 0.8 %collective-permute-done.4 = bf16[1,64,128]{2,1,0:T(8,128)(2,1)S(1)} collective-permute-done((bf16[1,64,128]{2,1,0:T(8,128)(2,1)S(1)}, bf16[1,64,128]{2,1,0:T(8,128)(2,1)S(1)}, u32[]{:S(2)}, u32[]{:S(2)}) %collective-permute-start.4) | collective-permute-done | bytes 16416 | tf_op jit(solution)/shard_map/ppermute | solution.py:441
  20.8 0.4 collective-permute-done.5.far_ref
  21.2 0.7 %shard_map.96 = (bf16[4,512,512]{2,1,0:T(8,128)(2,1)S(1)}, s32[4,16,128]{2,1,0:T(8,128)S(1)}) custom-call(bf16[4,272,128]{2,1,0:T(8,128)(2,1)S(1)} %pad_maximum_fusion.shared_ref), custom_call_target="tpu_custom_call" | custom-call | bytes 4290000 | tf_op jit(solution)/shard_map/pallas_call | solution.py:231
  21.9 1.7 %shard_map.97 = bf16[16,128,128]{2,1,0:T(8,128)(2,1)} custom-call(bf16[2,512,128]{2,1,0:T(8,128)(2,1)S(1)} %get-tuple-element.22.own_ref, bf16[2,512,128]{2,1,0:T(8,128)(2,1)S(1)} %collective-permute-done.3.near_ref, bf16[512,128]{1,0:T(8,128)(2,1)S(1)} %collective-permute-done.5.far_ref, s32[128,8]{1,0:T(8,128)S(1)} %copy.11.routes_ref, ...), custom_call_target="tpu_custom_call" | custom-call | bytes 6600000 | tf_op jit(solution)/shard_map/pallas_call | solution.py:288
  23.7 3.7 %all-to-all-start = ((bf16[16,128,128]{2,1,0:T(8,128)(2,1)}), bf16[16,128,128]{2,1,0:T(8,128)(2,1)S(1)}, u32[]{:S(2)}, u32[]{:S(2)}) async-start(bf16[16,128,128]{2,1,0:T(8,128)(2,1)} %shard_map.97), calls=%async_computation | async-start | bytes 1048576 | tf_op jit(solution)/shard_map/all_to_all | solution.py:493
  27.4 1.9 %collective-permute-start.7 = (bf16[2,64,128]{2,1,0:T(8,128)(2,1)S(1)}, bf16[2,64,128]{2,1,0:T(8,128)(2,1)S(1)}, u32[]{:S(2)}, u32[]{:S(2)}) collective-permute-start(bf16[2,64,128]{2,1,0:T(8,128)(2,1)S(1)} %pad_maximum_fusion.5), channel_id=1, source_target_pairs={{0,4},{4,0},{8,12},{12,8},{1,5},{5,1},{9,13},{13,9},{2,6},{6,2},{1... | collective-permute-start | bytes 98312 | tf_op jit(solution)/shard_map/ppermute | solution.py:441
  29.3 8.7 %collective-permute-done.7 = bf16[2,64,128]{2,1,0:T(8,128)(2,1)S(1)} collective-permute-done((bf16[2,64,128]{2,1,0:T(8,128)(2,1)S(1)}, bf16[2,64,128]{2,1,0:T(8,128)(2,1)S(1)}, u32[]{:S(2)}, u32[]{:S(2)}) %collective-permute-start.7) | collective-permute-done | bytes 32800 | tf_op jit(solution)/shard_map/ppermute | solution.py:441
  38.0 0.1 collective-permute-start.8
  38.1 1.2 %collective-permute-done.8 = bf16[1,4,64,128]{3,2,1,0:T(8,128)(2,1)S(1)} collective-permute-done((bf16[1,4,64,128]{3,2,1,0:T(8,128)(2,1)S(1)}, bf16[1,4,64,128]{3,2,1,0:T(8,128)(2,1)S(1)}, u32[]{:S(2)}, u32[]{:S(2)}) %collective-permute-start.8) | collective-permute-done | bytes 65568 | tf_op jit(solution)/shard_map/ppermute | solution.py:441
  39.3 1.3 %collective-permute-start.9 = (bf16[2,4,64,128]{3,2,1,0:T(8,128)(2,1)S(1)}, bf16[2,4,64,128]{3,2,1,0:T(8,128)(2,1)S(1)}, u32[]{:S(2)}, u32[]{:S(2)}) collective-permute-start(bf16[2,4,64,128]{3,2,1,0:T(8,128)(2,1)S(1)} %pad_maximum_fusion.3), channel_id=1, source_target_pairs={{0,2},{1,3},{2,0},{3,1},{4,6},{5,7},{6,4},{7,5},{8,10},{9,11},{10,... | collective-permute-start | bytes 393224 | tf_op jit(solution)/shard_map/ppermute | solution.py:441
  40.6 0.0 copy-done.2
  40.6 10.2 %shard_map.98.far_ref = bf16[8192,256]{1,0:T(8,128)(2,1)S(1)} custom-call(bf16[256,8,1024]{2,1,0:T(8,128)(2,1)} %query_ref, f32[8,64,64]{2,1,0:T(8,128)S(1)} %copy-done.2), custom_call_target="tpu_custom_call" | custom-call | bytes 33000000 | tf_op jit(solution)/shard_map/pallas_call | solution.py:339
  50.8 0.0 copy-start.1
  50.9 2.0 %copy-done.1 = bf16[8192,256]{1,0:T(8,128)(2,1)} copy-done((bf16[8192,256]{1,0:T(8,128)(2,1)}, bf16[8192,256]{1,0:T(8,128)(2,1)S(1)}, u32[]{:S(2)}) %copy-start.1) | copy-done | bytes 4194328
  52.8 0.0 collective-permute-done.9
  52.8 0.0 all-to-all-done.arrived_ref
  52.9 6.6 %shard_map.99 = f32[16,8,128]{2,1,0:T(8,128)S(1)} custom-call(bf16[16,128,128]{2,1,0:T(8,128)(2,1)S(1)} %all-to-all-done.arrived_ref, bf16[16,64,128]{2,1,0:T(8,128)(2,1)S(1)} %bitcast.8, s32[4,16,128]{2,1,0:T(8,128)S(1)} %get-tuple-element.37.docs_ref, bf16[8192,256]{1,0:T(8,128)(2,1)} %copy-done.1), custom_call_target="tpu_custom_call" | custom-call | bytes 16500000 | tf_op jit(solution)/shard_map/pallas_call | solution.py:410
  59.5 12.4 %all_to_all.10.pieces_ref = f32[16,8,128]{2,1,0:T(8,128)S(1)} all-to-all(f32[16,8,128]{2,1,0:T(8,128)S(1)} %shard_map.99), channel_id=1, replica_groups=mesh['groups'=2,'expert'=4,'proj'=4] {'expert','proj'}, dimensions={0} | all-to-all | bytes 131072 | tf_op jit(solution)/shard_map/all_to_all | solution.py:503
  71.9 0.6 shard_map.100
  (9 shorter events, 0.1 us)
Async XLA Ops:
  0.0 15.2 %copy-start = (s32[512,8]{0,1:T(8,128)S(1)}, s32[512,8]{0,1:T(8,128)}, u32[]{:S(2)}) copy-start(s32[512,8]{0,1:T(8,128)} %param.11) | copy-start | bytes 49156
  2.9 4.2 %collective-permute-start.1 = (bf16[2,128,128]{2,1,0:T(8,128)(2,1)S(1)}, bf16[2,128,128]{2,1,0:T(8,128)(2,1)S(1)}, u32[]{:S(2)}, u32[]{:S(2)}) collective-permute-start(bf16[2,128,128]{2,1,0:T(8,128)(2,1)S(1)} %get-tuple-element.25), channel_id=1, source_target_pairs={{0,1},{1,0},{2,3},{3,2},{4,5},{5,4},{6,7},{7,6},{8,9},{9,8},{10,11... | collective-permute-start | bytes 196616 | tf_op jit(solution)/shard_map/ppermute | solution.py:441
  3.4 10.1 %collective-permute-start = (bf16[272,128]{1,0:T(8,128)(2,1)S(1)}, bf16[272,128]{1,0:T(8,128)(2,1)S(1)}, u32[]{:S(2)}, u32[]{:S(2)}) collective-permute-start(bf16[272,128]{1,0:T(8,128)(2,1)S(1)} %get-tuple-element.23), channel_id=1, source_target_pairs={{0,8},{4,12},{8,0},{12,4},{1,9},{5,13},{9,1},{13,5},{2,10},{6,14},... | collective-permute-start | bytes 208904 | tf_op jit(solution)/shard_map/ppermute | solution.py:441
  7.1 6.4 %collective-permute-start.2 = (bf16[128,128]{1,0:T(8,128)(2,1)S(1)}, bf16[128,128]{1,0:T(8,128)(2,1)S(1)}, u32[]{:S(2)}, u32[]{:S(2)}) collective-permute-start(bf16[128,128]{1,0:T(8,128)(2,1)S(1)} %shard_map.93), channel_id=1, source_target_pairs={{0,2},{1,3},{2,0},{3,1},{4,6},{5,7},{6,4},{7,5},{8,10},{9,11},{10,... | collective-permute-start | bytes 98312 | tf_op jit(solution)/shard_map/ppermute | solution.py:441
  13.5 27.2 %copy-start.2 = (f32[8,64,64]{2,1,0:T(8,128)S(1)}, f32[8,64,64]{2,1,0:T(8,128)}, u32[]{:S(2)}) copy-start(f32[8,64,64]{2,1,0:T(8,128)} %inverse_ref.1) | copy-start | bytes 393220
  13.5 2.0 %collective-permute-start.3 = (bf16[2,512,128]{2,1,0:T(8,128)(2,1)S(1)}, bf16[2,512,128]{2,1,0:T(8,128)(2,1)S(1)}, u32[]{:S(2)}, u32[]{:S(2)}) collective-permute-start(bf16[2,512,128]{2,1,0:T(8,128)(2,1)S(1)} %get-tuple-element.27), channel_id=1, source_target_pairs={{0,1},{1,0},{2,3},{3,2},{4,5},{5,4},{6,7},{7,6},{8,9},{9,8},{10,11... | collective-permute-start | bytes 786440 | tf_op jit(solution)/shard_map/ppermute | solution.py:441
  13.6 6.3 %collective-permute-start.6 = (bf16[2,272,128]{2,1,0:T(8,128)(2,1)S(1)}, bf16[2,272,128]{2,1,0:T(8,128)(2,1)S(1)}, u32[]{:S(2)}, u32[]{:S(2)}) collective-permute-start(bf16[2,272,128]{2,1,0:T(8,128)(2,1)S(1)} %pad_maximum_fusion.2), channel_id=1, source_target_pairs={{0,4},{4,0},{8,12},{12,8},{1,5},{5,1},{9,13},{13,9},{2,6},{6,2},{1... | collective-permute-start | bytes 417800 | tf_op jit(solution)/shard_map/ppermute | solution.py:441
  15.5 5.7 %collective-permute-start.5 = (bf16[512,128]{1,0:T(8,128)(2,1)S(1)}, bf16[512,128]{1,0:T(8,128)(2,1)S(1)}, u32[]{:S(2)}, u32[]{:S(2)}) collective-permute-start(bf16[512,128]{1,0:T(8,128)(2,1)S(1)} %shard_map.95), channel_id=1, source_target_pairs={{0,2},{1,3},{2,0},{3,1},{4,6},{5,7},{6,4},{7,5},{8,10},{9,11},{10,... | collective-permute-start | bytes 393224 | tf_op jit(solution)/shard_map/ppermute | solution.py:441
  16.1 4.6 %collective-permute-start.4 = (bf16[1,64,128]{2,1,0:T(8,128)(2,1)S(1)}, bf16[1,64,128]{2,1,0:T(8,128)(2,1)S(1)}, u32[]{:S(2)}, u32[]{:S(2)}) collective-permute-start(bf16[1,64,128]{2,1,0:T(8,128)(2,1)S(1)} %bitcast.11), channel_id=1, source_target_pairs={{0,8},{4,12},{8,0},{12,4},{1,9},{5,13},{9,1},{13,5},{2,10},{6,14},... | collective-permute-start | bytes 49160 | tf_op jit(solution)/shard_map/ppermute | solution.py:441
  23.7 29.2 %all-to-all-start = ((bf16[16,128,128]{2,1,0:T(8,128)(2,1)}), bf16[16,128,128]{2,1,0:T(8,128)(2,1)S(1)}, u32[]{:S(2)}, u32[]{:S(2)}) async-start(bf16[16,128,128]{2,1,0:T(8,128)(2,1)} %shard_map.97), calls=%async_computation | async-start | bytes 1048576 | tf_op jit(solution)/shard_map/all_to_all | solution.py:493
  27.4 10.6 %collective-permute-start.7 = (bf16[2,64,128]{2,1,0:T(8,128)(2,1)S(1)}, bf16[2,64,128]{2,1,0:T(8,128)(2,1)S(1)}, u32[]{:S(2)}, u32[]{:S(2)}) collective-permute-start(bf16[2,64,128]{2,1,0:T(8,128)(2,1)S(1)} %pad_maximum_fusion.5), channel_id=1, source_target_pairs={{0,4},{4,0},{8,12},{12,8},{1,5},{5,1},{9,13},{13,9},{2,6},{6,2},{1... | collective-permute-start | bytes 98312 | tf_op jit(solution)/shard_map/ppermute | solution.py:441
  38.0 1.3 %collective-permute-start.8 = (bf16[1,4,64,128]{3,2,1,0:T(8,128)(2,1)S(1)}, bf16[1,4,64,128]{3,2,1,0:T(8,128)(2,1)S(1)}, u32[]{:S(2)}, u32[]{:S(2)}) collective-permute-start(bf16[1,4,64,128]{3,2,1,0:T(8,128)(2,1)S(1)} %bitcast.16), channel_id=1, source_target_pairs={{0,1},{1,0},{2,3},{3,2},{4,5},{5,4},{6,7},{7,6},{8,9},{9,8},{10,11... | collective-permute-start | bytes 196616 | tf_op jit(solution)/shard_map/ppermute | solution.py:441
  39.3 13.5 %collective-permute-start.9 = (bf16[2,4,64,128]{3,2,1,0:T(8,128)(2,1)S(1)}, bf16[2,4,64,128]{3,2,1,0:T(8,128)(2,1)S(1)}, u32[]{:S(2)}, u32[]{:S(2)}) collective-permute-start(bf16[2,4,64,128]{3,2,1,0:T(8,128)(2,1)S(1)} %pad_maximum_fusion.3), channel_id=1, source_target_pairs={{0,2},{1,3},{2,0},{3,1},{4,6},{5,7},{6,4},{7,5},{8,10},{9,11},{10,... | collective-permute-start | bytes 393224 | tf_op jit(solution)/shard_map/ppermute | solution.py:441
  50.8 2.0 %copy-start.1 = (bf16[8192,256]{1,0:T(8,128)(2,1)}, bf16[8192,256]{1,0:T(8,128)(2,1)S(1)}, u32[]{:S(2)}) copy-start(bf16[8192,256]{1,0:T(8,128)(2,1)S(1)} %shard_map.98.far_ref) | copy-start | bytes 12582916

commit v9 on v8

--- a/solution.py
+++ b/solution.py
@@ -298,11 +298,12 @@
     )(own, near, far, quarter_routes, weights)
 
 
-def query_kernel(query_ref, inverse_ref, out_ref, factor_ref, spread_ref, wide_ref):
+def query_kernel(query_ref, inverse_ref, out_hbm, factor_ref, spread_ref, wide_ref, out_ref, sems):
     count, experts, _ = query_ref.shape
     width = inverse_ref.shape[1]
     step = pl.program_id(0)
     rows = out_ref.shape[0] // width
+    pitch = wide_ref.shape[1] // width
 
     @pl.when(step == 0)
     def _():
@@ -323,13 +324,24 @@
         start = e * (rows // experts) + 2 * step
         for tile in range(wide_ref.shape[0]):
             part = result[:, tile * LANES : (tile + 1) * LANES]
-            wide_ref[tile, pl.ds(start, width, stride=rows), :] = part[:width]
-            wide_ref[tile, pl.ds(start + 1, width, stride=rows), :] = part[width:]
+            wide_ref[tile, pl.ds(start, width, stride=pitch), :] = part[:width]
+            wide_ref[tile, pl.ds(start + 1, width, stride=pitch), :] = part[width:]
 
     @pl.when(step == pl.num_programs(0) - 1)
     def _():
-        for tile in range(wide_ref.shape[0]):
-            out_ref[:, tile * LANES : (tile + 1) * LANES] = wide_ref[tile].astype(jnp.bfloat16)
+        copies = []
+        for part in range(sems.shape[0]):
+            first = part * (width // sems.shape[0])
+            for j in range(first, first + width // sems.shape[0]):
+                for tile in range(wide_ref.shape[0]):
+                    out_ref[j * rows : (j + 1) * rows, tile * LANES : (tile + 1) * LANES] = wide_ref[
+                        tile, j * pitch : j * pitch + rows, :
+                    ].astype(jnp.bfloat16)
+            block = pl.ds(first * rows, width // sems.shape[0] * rows)
+            copies.append(pltpu.make_async_copy(out_ref.at[block], out_hbm.at[block], sems.at[part]))
+            copies[-1].start()
+        for copy in copies:
+            copy.wait()
 
 
 def condition_queries(query_grads, inverse_in):
@@ -343,12 +355,14 @@
             pl.BlockSpec((count, experts, LANES), lambda c: (0, 0, c)),
             pl.BlockSpec(inverse_in.shape, lambda c: (0, 0, 0)),
         ],
-        out_specs=pl.BlockSpec((rows, count), lambda c: (0, 0)),
-        out_shape=jax.ShapeDtypeStruct((rows, count), jnp.bfloat16),
+        out_specs=HBM,
+        out_shape=pltpu.HBM((rows, count), jnp.bfloat16),
         scratch_shapes=[
             pltpu.VMEM((experts, 4 * width, 2 * width), jnp.bfloat16),
             pltpu.VMEM((count * experts, LANES), jnp.float32),
-            pltpu.VMEM((count // LANES, rows, LANES), jnp.float32),
+            pltpu.VMEM((count // LANES, rows + 8 * width, LANES), jnp.float32),
+            pltpu.VMEM((rows, count), jnp.bfloat16),
+            pltpu.SemaphoreType.DMA((4,)),
         ],
         compiler_params=pltpu.CompilerParams(vmem_limit_bytes=40 * MIB),
         cost_estimate=cost(10),
@@ -374,21 +388,22 @@
     inner = jnp.concatenate(inner, axis=1)
     docs = jnp.broadcast_to(jnp.concatenate(docs, axis=1), inner.shape)
     doc_group = 8
+    pitch = grads_ref.shape[0] // doc_count
 
     def one_group(group, carry):
         masked = [
             jnp.where(docs == group * doc_group + d, inner, jnp.zeros_like(inner)) for d in range(doc_group)
         ]
-        start = pl.multiple_of(group * doc_group * width, doc_group * width)
-        grads_ref[pl.ds(start, doc_group * width), :] = jnp.dot(
-            jnp.concatenate(masked, axis=0), outer, preferred_element_type=jnp.float32
-        )
+        sums = jnp.dot(jnp.concatenate(masked, axis=0), outer, preferred_element_type=jnp.float32)
+        for d in range(doc_group):
+            start = pl.multiple_of((group * doc_group + d) * pitch, 8)
+            grads_ref[pl.ds(start, width), :] = sums[d * width : (d + 1) * width]
         return carry
 
     lax.fori_loop(0, doc_count // doc_group, one_group, 0, unroll=doc_count <= 32)
     high, low = [], []
     for j in range(width):
-        parts = split(grads_ref[pl.ds(j, doc_count, stride=width), :])
+        parts = split(grads_ref[pl.ds(j, doc_count, stride=pitch), :])
         high.append(parts[0])
         low.append(parts[1])
     flat = jnp.concatenate([jnp.concatenate(high, axis=1), jnp.concatenate(low, axis=1)], axis=0)
@@ -412,7 +427,7 @@
         in_specs=[VMEM, VMEM, VMEM, HBM],
         out_shape=jax.ShapeDtypeStruct((sources, DOC_DEV, LANES), jnp.float32),
         scratch_shapes=[
-            pltpu.VMEM((doc_count * width, arrived.shape[2]), jnp.float32),
+            pltpu.VMEM((doc_count * (width + 8), arrived.shape[2]), jnp.float32),
             pltpu.VMEM(queries.shape, jnp.bfloat16),
             pltpu.SemaphoreType.DMA,
         ],
@@ -486,12 +501,16 @@
     inner, owner_turns = double(inner[None], (0,), "expert", owners, owners // 2)
     inner, far, shared = lax.optimization_barrier((inner, far, shared))
     for bit in reversed(range((owners // 2).bit_length() - 1)):
-        inner, owner_turns = double(inner, owner_turns, "expert", owners, 1 << bit)
+        arriving = exchange(inner, "expert", owners, 1 << bit)
+        owner_turns = owner_turns + tuple(t ^ (1 << bit) for t in owner_turns)
+        if bit:
+            inner = jnp.concatenate([inner, arriving], axis=0)
     weights, all_docs = expand(shared, turns, width, experts, shares)
     quarter_routes = lax.dynamic_slice_in_dim(routes, lax.axis_index("proj") * quarter, quarter, 0)
     payload = condition(own, near, far, quarter_routes, weights, shares, width)
+    payload, arriving = lax.optimization_barrier((payload, arriving))
     arrived = lax.all_to_all(payload, ("expert", "proj"), 0, 0, tiled=True)
-    inner, _ = lax.optimization_barrier((inner, payload))
+    inner = jnp.concatenate([inner, arriving], axis=0)
     inner, share_turns = inner[None], (0,)
     inner, share_turns = double(inner, share_turns, "proj", shares, 1)
     inner, query_grads = lax.optimization_barrier((inner, query_grads))

time: 73.1 us -> 61.5 us (0.84)
  waiting for transfers between devices: 13.7 us -> 6.29 us
  local copies, waits for them, and re-layouts: 2.07 us -> 0.12 us
  blocking collectives: 12.4 us -> 10.8 us
  Pallas kernels: 27.7 us -> 26.7 us
    ppermute x10, waiting for transfers between devices: 13.7 us -> 4.75 us  [exchange(): return lax.ppermute(block, axis, [(i, i ^ turn) for i in range(size)])]
    unnamed x7 -> x5, local copies, waits for them, and re-layouts: 2.07 us -> 0.11 us
    all_to_all x1, blocking collectives: 12.4 us -> 10.8 us  [local(): pieces = lax.all_to_all(pieces, ('expert', 'proj'), 0, 0, tiled=True)]
    all_to_all x1, waiting for transfers between devices: 0.01 us -> 1.54 us  [local(): arrived = lax.all_to_all(payload, ('expert', 'proj'), 0, 0, tiled=True)]
  transfers between devices with their start and end apart: 11 -> 11, of which waited for: 5 -> 6; matrix products, arithmetic and copies ran while one was open for 0% -> 0% of each run, Pallas kernels for 21% -> 28%
where the time goes in v9:
time: 61.5 us; the launch traced here: 61 us
  Pallas kernels  26.7 us (43%)
  starting transfers between devices  16.9 us (27%)
  blocking collectives  10.8 us (18%)
  waiting for transfers between devices  6.29 us (10%)
    ppermute x10, starting transfers between devices, exchange(): return lax.ppermute(block, axis, [(i, i ^ turn) for i in range(size)])  13 us
    all_to_all x1, blocking collectives, local(): pieces = lax.all_to_all(pieces, ('expert', 'proj'), 0, 0, tiled=True)  10.8 us
    pallas_call x1, Pallas kernels, condition_queries(): pl.pallas_call(query_kernel, grid=(flat // LANES,), in_specs=[pl.BlockSpe...  9.53 us
    pallas_call x1, Pallas kernels, score(): pl.pallas_call(functools.partial(score_kernel, width=width, doc_count=doc...  6.27 us
    pallas_call x1, Pallas kernels, project_outer(): pl.pallas_call(functools.partial(outer_kernel, top=top), in_specs=[HBM] *...  4.79 us
    ppermute x10, waiting for transfers between devices, exchange(): return lax.ppermute(block, axis, [(i, i ^ turn) for i in range(size)])  4.75 us
    all_to_all x1, starting transfers between devices, local(): arrived = lax.all_to_all(payload, ('expert', 'proj'), 0, 0, tiled=True)  3.84 us
    pallas_call x1, Pallas kernels, project_inner(): pl.pallas_call(inner_kernel, in_specs=[HBM] * 4, out_specs=[VMEM] * 3, ou...  2.89 us
  transfers between devices with their start and end apart: 11, of which 6 were waited for; matrix products, arithmetic and copies ran while one was open for 0% of the time, Pallas kernels for 28%

profile of v9, /device:TPU:0, one launch (start us, length us, event | category | flops | bytes accessed | tf_op | source)
XLA Modules:
  0.0 61.0 jit_solution(18337881981770445102)
XLA Ops:
  0.0 0.0 copy-start
  0.0 2.9 %shard_map.92 = (bf16[2,128,128]{2,1,0:T(8,128)(2,1)S(1)}, bf16[2,128,128]{2,1,0:T(8,128)(2,1)S(1)}, bf16[272,128]{1,0:T(8,128)(2,1)S(1)}) custom-call(bf16[512,1792]{1,0:T(8,128)(2,1)} %act_hbm.1, bf16[64,1792]{1,0:T(8,128)(2,1)} %in_proj_hbm.1, f32[8,64,64]{2,1,0:T(8,128)} %inverse_hbm.1, s32[4,128]{1,0:T(4,128)} %bitcast.17), custom_call_target="tpu_custom_call" | custom-call | bytes 8250000 | tf_op jit(solution)/shard_map/pallas_call | solution.py:94
  2.9 0.5 collective-permute-start.1
  3.4 3.7 %collective-permute-start = (bf16[272,128]{1,0:T(8,128)(2,1)S(1)}, bf16[272,128]{1,0:T(8,128)(2,1)S(1)}, u32[]{:S(2)}, u32[]{:S(2)}) collective-permute-start(bf16[272,128]{1,0:T(8,128)(2,1)S(1)} %get-tuple-element.24), channel_id=1, source_target_pairs={{0,8},{4,12},{8,0},{12,4},{1,9},{5,13},{9,1},{13,5},{2,10},{6,14},... | collective-permute-start | bytes 208904 | tf_op jit(solution)/shard_map/ppermute | solution.py:456
  7.1 0.0 collective-permute-done.1.near_ref
  7.1 1.6 %collective-permute-start.2 = (bf16[128,128]{1,0:T(8,128)(2,1)S(1)}, bf16[128,128]{1,0:T(8,128)(2,1)S(1)}, u32[]{:S(2)}, u32[]{:S(2)}) collective-permute-start(bf16[128,128]{1,0:T(8,128)(2,1)S(1)} %shard_map.93), channel_id=1, source_target_pairs={{0,2},{1,3},{2,0},{3,1},{4,6},{5,7},{6,4},{7,5},{8,10},{9,11},{10,... | collective-permute-start | bytes 98312 | tf_op jit(solution)/shard_map/ppermute | solution.py:456
  8.7 4.8 %shard_map.91 = (bf16[2,512,128]{2,1,0:T(8,128)(2,1)S(1)}, bf16[2,512,128]{2,1,0:T(8,128)(2,1)S(1)}) custom-call(bf16[4096,512]{1,0:T(8,128)(2,1)} %bitcast.14, bf16[64,512]{1,0:T(8,128)(2,1)} %out_proj_hbm.1), custom_call_target="tpu_custom_call" | custom-call | bytes 13200000 | tf_op jit(solution)/shard_map/pallas_call | solution.py:147
  13.5 0.0 copy-start.1
  13.5 0.0 collective-permute-done
  13.5 0.0 collective-permute-done.2.far_ref
  13.5 0.1 collective-permute-start.3
  13.6 1.6 %collective-permute-start.6 = (bf16[2,272,128]{2,1,0:T(8,128)(2,1)S(1)}, bf16[2,272,128]{2,1,0:T(8,128)(2,1)S(1)}, u32[]{:S(2)}, u32[]{:S(2)}) collective-permute-start(bf16[2,272,128]{2,1,0:T(8,128)(2,1)S(1)} %pad_maximum_fusion.2), channel_id=1, source_target_pairs={{0,4},{4,0},{8,12},{12,8},{1,5},{5,1},{9,13},{13,9},{2,6},{6,2},{1... | collective-permute-start | bytes 417800 | tf_op jit(solution)/shard_map/ppermute | solution.py:456
  15.2 0.1 shard_map.94
  15.3 0.0 collective-permute-done.3.near_ref
  15.4 0.6 collective-permute-start.5
  16.0 1.3 %collective-permute-start.4 = (bf16[1,64,128]{2,1,0:T(8,128)(2,1)S(1)}, bf16[1,64,128]{2,1,0:T(8,128)(2,1)S(1)}, u32[]{:S(2)}, u32[]{:S(2)}) collective-permute-start(bf16[1,64,128]{2,1,0:T(8,128)(2,1)S(1)} %bitcast.12), channel_id=1, source_target_pairs={{0,8},{4,12},{8,0},{12,4},{1,9},{5,13},{9,1},{13,5},{2,10},{6,14},... | collective-permute-start | bytes 49160 | tf_op jit(solution)/shard_map/ppermute | solution.py:456
  17.4 2.5 %collective-permute-done.6 = bf16[2,272,128]{2,1,0:T(8,128)(2,1)S(1)} collective-permute-done((bf16[2,272,128]{2,1,0:T(8,128)(2,1)S(1)}, bf16[2,272,128]{2,1,0:T(8,128)(2,1)S(1)}, u32[]{:S(2)}, u32[]{:S(2)}) %collective-permute-start.6) | collective-permute-done | bytes 139296 | tf_op jit(solution)/shard_map/ppermute | solution.py:456
  19.9 0.7 %collective-permute-done.4 = bf16[1,64,128]{2,1,0:T(8,128)(2,1)S(1)} collective-permute-done((bf16[1,64,128]{2,1,0:T(8,128)(2,1)S(1)}, bf16[1,64,128]{2,1,0:T(8,128)(2,1)S(1)}, u32[]{:S(2)}, u32[]{:S(2)}) %collective-permute-start.4) | collective-permute-done | bytes 16416 | tf_op jit(solution)/shard_map/ppermute | solution.py:456
  20.7 0.4 collective-permute-done.5.far_ref
  21.1 1.2 %collective-permute-start.7 = (bf16[2,64,128]{2,1,0:T(8,128)(2,1)S(1)}, bf16[2,64,128]{2,1,0:T(8,128)(2,1)S(1)}, u32[]{:S(2)}, u32[]{:S(2)}) collective-permute-start(bf16[2,64,128]{2,1,0:T(8,128)(2,1)S(1)} %pad_maximum_fusion.4), channel_id=1, source_target_pairs={{0,4},{4,0},{8,12},{12,8},{1,5},{5,1},{9,13},{13,9},{2,6},{6,2},{1... | collective-permute-start | bytes 98312 | tf_op jit(solution)/shard_map/ppermute | solution.py:456
  22.3 0.0 copy-done
  22.3 0.1 copy.11.routes_ref
  22.4 0.7 %shard_map.96 = (bf16[4,512,512]{2,1,0:T(8,128)(2,1)S(1)}, s32[4,16,128]{2,1,0:T(8,128)S(1)}) custom-call(bf16[4,272,128]{2,1,0:T(8,128)(2,1)S(1)} %pad_maximum_fusion.shared_ref), custom_call_target="tpu_custom_call" | custom-call | bytes 4290000 | tf_op jit(solution)/shard_map/pallas_call | solution.py:231
  23.2 1.7 %shard_map.97 = bf16[16,128,128]{2,1,0:T(8,128)(2,1)} custom-call(bf16[2,512,128]{2,1,0:T(8,128)(2,1)S(1)} %get-tuple-element.23.own_ref, bf16[2,512,128]{2,1,0:T(8,128)(2,1)S(1)} %collective-permute-done.3.near_ref, bf16[512,128]{1,0:T(8,128)(2,1)S(1)} %collective-permute-done.5.far_ref, s32[128,8]{1,0:T(8,128)S(1)} %copy.11.routes_ref, ...), custom_call_target="tpu_custom_call" | custom-call | bytes 6600000 | tf_op jit(solution)/shard_map/pallas_call | solution.py:288
  24.9 0.1 collective-permute-done.7
  25.0 3.8 %all-to-all-start = ((bf16[16,128,128]{2,1,0:T(8,128)(2,1)}), bf16[16,128,128]{2,1,0:T(8,128)(2,1)S(1)}, u32[]{:S(2)}, u32[]{:S(2)}) async-start(bf16[16,128,128]{2,1,0:T(8,128)(2,1)} %shard_map.97), calls=%async_computation | async-start | bytes 1048576 | tf_op jit(solution)/shard_map/all_to_all | solution.py:512
  28.9 0.5 collective-permute-start.8
  29.4 0.9 %collective-permute-done.8 = bf16[1,4,64,128]{3,2,1,0:T(8,128)(2,1)S(1)} collective-permute-done((bf16[1,4,64,128]{3,2,1,0:T(8,128)(2,1)S(1)}, bf16[1,4,64,128]{3,2,1,0:T(8,128)(2,1)S(1)}, u32[]{:S(2)}, u32[]{:S(2)}) %collective-permute-start.8) | collective-permute-done | bytes 65568 | tf_op jit(solution)/shard_map/ppermute | solution.py:456
  30.3 1.9 %collective-permute-start.9 = (bf16[2,4,64,128]{3,2,1,0:T(8,128)(2,1)S(1)}, bf16[2,4,64,128]{3,2,1,0:T(8,128)(2,1)S(1)}, u32[]{:S(2)}, u32[]{:S(2)}) collective-permute-start(bf16[2,4,64,128]{3,2,1,0:T(8,128)(2,1)S(1)} %pad_maximum_fusion.3), channel_id=1, source_target_pairs={{0,2},{1,3},{2,0},{3,1},{4,6},{5,7},{6,4},{7,5},{8,10},{9,11},{10,... | collective-permute-start | bytes 393224 | tf_op jit(solution)/shard_map/ppermute | solution.py:456
  32.2 0.0 copy-done.1
  32.2 9.5 %shard_map.98.far_ref = bf16[8192,256]{1,0:T(8,128)(2,1)} custom-call(bf16[256,8,1024]{2,1,0:T(8,128)(2,1)} %query_ref, f32[8,64,64]{2,1,0:T(8,128)S(1)} %copy-done.1), custom_call_target="tpu_custom_call" | custom-call | bytes 33000000 | tf_op jit(solution)/shard_map/pallas_call | solution.py:351
  41.7 0.0 collective-permute-done.9
  41.8 1.5 %all-to-all-done.arrived_ref = bf16[16,128,128]{2,1,0:T(8,128)(2,1)S(1)} async-done(((bf16[16,128,128]{2,1,0:T(8,128)(2,1)}), bf16[16,128,128]{2,1,0:T(8,128)(2,1)S(1)}, u32[]{:S(2)}, u32[]{:S(2)}) %all-to-all-start) | async-done | bytes 524320 | tf_op jit(solution)/shard_map/all_to_all | solution.py:512
  43.3 6.3 %shard_map.99 = f32[16,8,128]{2,1,0:T(8,128)S(1)} custom-call(bf16[16,128,128]{2,1,0:T(8,128)(2,1)S(1)} %all-to-all-done.arrived_ref, bf16[16,64,128]{2,1,0:T(8,128)(2,1)S(1)} %bitcast.9, s32[4,16,128]{2,1,0:T(8,128)S(1)} %get-tuple-element.39.docs_ref, bf16[8192,256]{1,0:T(8,128)(2,1)} %shard_map.98.far_ref), custom_call_target="tpu_custom_call" | custom-call | bytes 16500000 | tf_op jit(solution)/shard_map/pallas_call | solution.py:425
  49.6 10.8 %all_to_all.10.pieces_ref = f32[16,8,128]{2,1,0:T(8,128)S(1)} all-to-all(f32[16,8,128]{2,1,0:T(8,128)S(1)} %shard_map.99), channel_id=1, replica_groups=mesh['groups'=2,'expert'=4,'proj'=4] {'expert','proj'}, dimensions={0} | all-to-all | bytes 131072 | tf_op jit(solution)/shard_map/all_to_all | solution.py:522
  60.4 0.6 shard_map.100
  (9 shorter events, 0.2 us)
Async XLA Ops:
  0.0 22.3 %copy-start = (s32[512,8]{0,1:T(8,128)S(1)}, s32[512,8]{0,1:T(8,128)}, u32[]{:S(2)}) copy-start(s32[512,8]{0,1:T(8,128)} %param.11) | copy-start | bytes 49156
  2.9 4.2 %collective-permute-start.1 = (bf16[2,128,128]{2,1,0:T(8,128)(2,1)S(1)}, bf16[2,128,128]{2,1,0:T(8,128)(2,1)S(1)}, u32[]{:S(2)}, u32[]{:S(2)}) collective-permute-start(bf16[2,128,128]{2,1,0:T(8,128)(2,1)S(1)} %get-tuple-element.26), channel_id=1, source_target_pairs={{0,1},{1,0},{2,3},{3,2},{4,5},{5,4},{6,7},{7,6},{8,9},{9,8},{10,11... | collective-permute-start | bytes 196616 | tf_op jit(solution)/shard_map/ppermute | solution.py:456
  3.4 10.1 %collective-permute-start = (bf16[272,128]{1,0:T(8,128)(2,1)S(1)}, bf16[272,128]{1,0:T(8,128)(2,1)S(1)}, u32[]{:S(2)}, u32[]{:S(2)}) collective-permute-start(bf16[272,128]{1,0:T(8,128)(2,1)S(1)} %get-tuple-element.24), channel_id=1, source_target_pairs={{0,8},{4,12},{8,0},{12,4},{1,9},{5,13},{9,1},{13,5},{2,10},{6,14},... | collective-permute-start | bytes 208904 | tf_op jit(solution)/shard_map/ppermute | solution.py:456
  7.1 6.4 %collective-permute-start.2 = (bf16[128,128]{1,0:T(8,128)(2,1)S(1)}, bf16[128,128]{1,0:T(8,128)(2,1)S(1)}, u32[]{:S(2)}, u32[]{:S(2)}) collective-permute-start(bf16[128,128]{1,0:T(8,128)(2,1)S(1)} %shard_map.93), channel_id=1, source_target_pairs={{0,2},{1,3},{2,0},{3,1},{4,6},{5,7},{6,4},{7,5},{8,10},{9,11},{10,... | collective-permute-start | bytes 98312 | tf_op jit(solution)/shard_map/ppermute | solution.py:456
  13.5 18.8 %copy-start.1 = (f32[8,64,64]{2,1,0:T(8,128)S(1)}, f32[8,64,64]{2,1,0:T(8,128)}, u32[]{:S(2)}) copy-start(f32[8,64,64]{2,1,0:T(8,128)} %inverse_ref.1) | copy-start | bytes 393220
  13.5 1.9 %collective-permute-start.3 = (bf16[2,512,128]{2,1,0:T(8,128)(2,1)S(1)}, bf16[2,512,128]{2,1,0:T(8,128)(2,1)S(1)}, u32[]{:S(2)}, u32[]{:S(2)}) collective-permute-start(bf16[2,512,128]{2,1,0:T(8,128)(2,1)S(1)} %get-tuple-element.28), channel_id=1, source_target_pairs={{0,1},{1,0},{2,3},{3,2},{4,5},{5,4},{6,7},{7,6},{8,9},{9,8},{10,11... | collective-permute-start | bytes 786440 | tf_op jit(solution)/shard_map/ppermute | solution.py:456
  13.6 6.3 %collective-permute-start.6 = (bf16[2,272,128]{2,1,0:T(8,128)(2,1)S(1)}, bf16[2,272,128]{2,1,0:T(8,128)(2,1)S(1)}, u32[]{:S(2)}, u32[]{:S(2)}) collective-permute-start(bf16[2,272,128]{2,1,0:T(8,128)(2,1)S(1)} %pad_maximum_fusion.2), channel_id=1, source_target_pairs={{0,4},{4,0},{8,12},{12,8},{1,5},{5,1},{9,13},{13,9},{2,6},{6,2},{1... | collective-permute-start | bytes 417800 | tf_op jit(solution)/shard_map/ppermute | solution.py:456
  15.4 5.7 %collective-permute-start.5 = (bf16[512,128]{1,0:T(8,128)(2,1)S(1)}, bf16[512,128]{1,0:T(8,128)(2,1)S(1)}, u32[]{:S(2)}, u32[]{:S(2)}) collective-permute-start(bf16[512,128]{1,0:T(8,128)(2,1)S(1)} %shard_map.95), channel_id=1, source_target_pairs={{0,2},{1,3},{2,0},{3,1},{4,6},{5,7},{6,4},{7,5},{8,10},{9,11},{10,... | collective-permute-start | bytes 393224 | tf_op jit(solution)/shard_map/ppermute | solution.py:456
  16.0 4.7 %collective-permute-start.4 = (bf16[1,64,128]{2,1,0:T(8,128)(2,1)S(1)}, bf16[1,64,128]{2,1,0:T(8,128)(2,1)S(1)}, u32[]{:S(2)}, u32[]{:S(2)}) collective-permute-start(bf16[1,64,128]{2,1,0:T(8,128)(2,1)S(1)} %bitcast.12), channel_id=1, source_target_pairs={{0,8},{4,12},{8,0},{12,4},{1,9},{5,13},{9,1},{13,5},{2,10},{6,14},... | collective-permute-start | bytes 49160 | tf_op jit(solution)/shard_map/ppermute | solution.py:456
  21.1 3.9 %collective-permute-start.7 = (bf16[2,64,128]{2,1,0:T(8,128)(2,1)S(1)}, bf16[2,64,128]{2,1,0:T(8,128)(2,1)S(1)}, u32[]{:S(2)}, u32[]{:S(2)}) collective-permute-start(bf16[2,64,128]{2,1,0:T(8,128)(2,1)S(1)} %pad_maximum_fusion.4), channel_id=1, source_target_pairs={{0,4},{4,0},{8,12},{12,8},{1,5},{5,1},{9,13},{13,9},{2,6},{6,2},{1... | collective-permute-start | bytes 98312 | tf_op jit(solution)/shard_map/ppermute | solution.py:456
  25.0 18.3 %all-to-all-start = ((bf16[16,128,128]{2,1,0:T(8,128)(2,1)}), bf16[16,128,128]{2,1,0:T(8,128)(2,1)S(1)}, u32[]{:S(2)}, u32[]{:S(2)}) async-start(bf16[16,128,128]{2,1,0:T(8,128)(2,1)} %shard_map.97), calls=%async_computation | async-start | bytes 1048576 | tf_op jit(solution)/shard_map/all_to_all | solution.py:512
  28.9 1.4 %collective-permute-start.8 = (bf16[1,4,64,128]{3,2,1,0:T(8,128)(2,1)S(1)}, bf16[1,4,64,128]{3,2,1,0:T(8,128)(2,1)S(1)}, u32[]{:S(2)}, u32[]{:S(2)}) collective-permute-start(bf16[1,4,64,128]{3,2,1,0:T(8,128)(2,1)S(1)} %maximum_bitcast_fusion), channel_id=1, source_target_pairs={{0,1},{1,0},{2,3},{3,2},{4,5},{5,4},{6,7},{7,6},{8,9},{9,8},{10,11... | collective-permute-start | bytes 196616 | tf_op jit(solution)/shard_map/ppermute | solution.py:456
  30.3 11.5 %collective-permute-start.9 = (bf16[2,4,64,128]{3,2,1,0:T(8,128)(2,1)S(1)}, bf16[2,4,64,128]{3,2,1,0:T(8,128)(2,1)S(1)}, u32[]{:S(2)}, u32[]{:S(2)}) collective-permute-start(bf16[2,4,64,128]{3,2,1,0:T(8,128)(2,1)S(1)} %pad_maximum_fusion.3), channel_id=1, source_target_pairs={{0,2},{1,3},{2,0},{3,1},{4,6},{5,7},{6,4},{7,5},{8,10},{9,11},{10,... | collective-permute-start | bytes 393224 | tf_op jit(solution)/shard_map/ppermute | solution.py:456

commit v10 on v9

--- a/solution.py
+++ b/solution.py
@@ -63,10 +63,9 @@
     take = in_order([pltpu.make_async_copy(*pair, sems.at[i]) for i, pair in enumerate(pairs)], 5)
     take()
     first = low_lanes(half, width)
-    for g in range(len(turns)):
-        wire_ref = leaving_ref.at[g] if g < 2 else own_ref.at[g - 2]
+    for wire_ref in (leaving_ref, own_ref):
         take()
-        if g == 0:
+        if wire_ref is leaving_ref:
             take()
             take()
             experts = inverse_ref.shape[0] // 2
@@ -76,13 +75,16 @@
             docs = docs_ref[...].astype(jnp.float32)
             docs = jnp.concatenate([docs, jnp.zeros((DOC_ROWS - docs.shape[0], LANES), jnp.float32)], axis=0)
             shared_ref[experts * width :, :] = docs.astype(jnp.bfloat16)
+        take()
         twice = jnp.concatenate([in_proj_ref[...], in_proj_ref[...]], axis=0)
-        inner = lax.dot_general(
-            act_ref[g], twice, (((1,), (1,)), ((), ())), preferred_element_type=jnp.float32
-        )
-        high, low = split(jnp.where(first, inner[:half], inner[half:]))
-        wire_ref[:half, :] = high
-        wire_ref[half:, :] = low
+        g = 0 if wire_ref is leaving_ref else 2
+        rows = act_ref[g : g + 2].reshape(2 * quarter, act_ref.shape[2])
+        inner = lax.dot_general(rows, twice, (((1,), (1,)), ((), ())), preferred_element_type=jnp.float32)
+        for i in range(2):
+            start = i * quarter
+            high, low = split(jnp.where(first, inner[start : start + half], inner[start + half : start + quarter]))
+            wire_ref[i, :half, :] = high
+            wire_ref[i, half:, :] = low
 
 
 def project_inner(activations, in_projection, inverse_out, doc_rows, quarters):
@@ -116,7 +118,7 @@
     for i in range(chunks):
         start = (jnp.bitwise_xor(place, turns[i // split_by]) * split_by + i % split_by) * chunk_rows
         pairs.append((hidden_hbm.at[pl.ds(pl.multiple_of(start, chunk_rows), chunk_rows)], hidden_ref.at[i]))
-    take = in_order([pltpu.make_async_copy(*pair, sems.at[i]) for i, pair in enumerate(pairs)], 4)
+    take = in_order([pltpu.make_async_copy(*pair, sems.at[i]) for i, pair in enumerate(pairs)], 3)
     take()
     first = low_lanes(chunk, width)
 
@@ -142,7 +144,7 @@
 
 def project_outer(flat_hidden, out_projection, quarters, top):
     rows, hidden = flat_hidden.shape
-    chunks = 2 * quarters
+    chunks = quarters
     wire = jax.ShapeDtypeStruct((quarters // 2, rows // quarters // 2, LANES), jnp.bfloat16)
     return pl.pallas_call(
         functools.partial(outer_kernel, top=top),
@@ -387,7 +389,7 @@
     outer = jnp.concatenate(outer, axis=0)
     inner = jnp.concatenate(inner, axis=1)
     docs = jnp.broadcast_to(jnp.concatenate(docs, axis=1), inner.shape)
-    doc_group = 8
+    doc_group = 16
     pitch = grads_ref.shape[0] // doc_count
 
     def one_group(group, carry):
@@ -400,7 +402,7 @@
             grads_ref[pl.ds(start, width), :] = sums[d * width : (d + 1) * width]
         return carry
 
-    lax.fori_loop(0, doc_count // doc_group, one_group, 0, unroll=doc_count <= 32)
+    lax.fori_loop(0, doc_count // doc_group, one_group, 0, unroll=doc_count <= 2 * doc_group)
     high, low = [], []
     for j in range(width):
         parts = split(grads_ref[pl.ds(j, doc_count, stride=pitch), :])
@@ -499,13 +501,13 @@
     inner = finish_inner(inner_own, inner_near, inner_far, width)
     inner, _ = lax.optimization_barrier((inner, sent))
     inner, owner_turns = double(inner[None], (0,), "expert", owners, owners // 2)
-    inner, far, shared = lax.optimization_barrier((inner, far, shared))
+    weights, all_docs = expand(shared, turns, width, experts, shares)
+    inner, far, weights = lax.optimization_barrier((inner, far, weights))
     for bit in reversed(range((owners // 2).bit_length() - 1)):
         arriving = exchange(inner, "expert", owners, 1 << bit)
         owner_turns = owner_turns + tuple(t ^ (1 << bit) for t in owner_turns)
         if bit:
             inner = jnp.concatenate([inner, arriving], axis=0)
-    weights, all_docs = expand(shared, turns, width, experts, shares)
     quarter_routes = lax.dynamic_slice_in_dim(routes, lax.axis_index("proj") * quarter, quarter, 0)
     payload = condition(own, near, far, quarter_routes, weights, shares, width)
     payload, arriving = lax.optimization_barrier((payload, arriving))

time: 61.5 us -> 60.9 us (level)
  transfers between devices with their start and end apart: 11 -> 11, of which waited for: 6 -> 5; matrix products, arithmetic and copies ran while one was open for 0% -> 0% of each run, Pallas kernels for 28% -> 27%
where the time goes in v10:
time: 60.9 us; the launch traced here: 60.4 us
  Pallas kernels  26.1 us (43%)
  starting transfers between devices  17.3 us (28%)
  blocking collectives  10.8 us (18%)
  waiting for transfers between devices  5.78 us (9%)
    ppermute x10, starting transfers between devices, exchange(): return lax.ppermute(block, axis, [(i, i ^ turn) for i in range(size)])  13.5 us
    all_to_all x1, blocking collectives, local(): pieces = lax.all_to_all(pieces, ('expert', 'proj'), 0, 0, tiled=True)  10.8 us
    pallas_call x1, Pallas kernels, condition_queries(): pl.pallas_call(query_kernel, grid=(flat // LANES,), in_specs=[pl.BlockSpe...  9.53 us
    pallas_call x1, Pallas kernels, score(): pl.pallas_call(functools.partial(score_kernel, width=width, doc_count=doc...  6.1 us
    pallas_call x1, Pallas kernels, project_outer(): pl.pallas_call(functools.partial(outer_kernel, top=top), in_specs=[HBM] *...  4.33 us
    ppermute x10, waiting for transfers between devices, exchange(): return lax.ppermute(block, axis, [(i, i ^ turn) for i in range(size)])  4.24 us
    all_to_all x1, starting transfers between devices, local(): arrived = lax.all_to_all(payload, ('expert', 'proj'), 0, 0, tiled=True)  3.84 us
    pallas_call x1, Pallas kernels, project_inner(): pl.pallas_call(inner_kernel, in_specs=[HBM] * 4, out_specs=[VMEM] * 3, ou...  2.93 us
  transfers between devices with their start and end apart: 11, of which 5 were waited for; matrix products, arithmetic and copies ran while one was open for 0% of the time, Pallas kernels for 27%

profile of v10, /device:TPU:0, one launch (start us, length us, event | category | flops | bytes accessed | tf_op | source)
XLA Modules:
  0.0 60.4 jit_solution(16885792244646425144)
XLA Ops:
  0.0 0.0 copy-start
  0.0 2.9 %shard_map.92 = (bf16[2,128,128]{2,1,0:T(8,128)(2,1)S(1)}, bf16[2,128,128]{2,1,0:T(8,128)(2,1)S(1)}, bf16[272,128]{1,0:T(8,128)(2,1)S(1)}) custom-call(bf16[512,1792]{1,0:T(8,128)(2,1)} %act_hbm.1, bf16[64,1792]{1,0:T(8,128)(2,1)} %in_proj_hbm.1, f32[8,64,64]{2,1,0:T(8,128)} %inverse_hbm.1, s32[4,128]{1,0:T(4,128)} %bitcast.17), custom_call_target="tpu_custom_call" | custom-call | bytes 8250000 | tf_op jit(solution)/shard_map/pallas_call | solution.py:96
  2.9 0.5 collective-permute-start.1
  3.5 3.7 %collective-permute-start = (bf16[272,128]{1,0:T(8,128)(2,1)S(1)}, bf16[272,128]{1,0:T(8,128)(2,1)S(1)}, u32[]{:S(2)}, u32[]{:S(2)}) collective-permute-start(bf16[272,128]{1,0:T(8,128)(2,1)S(1)} %get-tuple-element.24), channel_id=1, source_target_pairs={{0,8},{4,12},{8,0},{12,4},{1,9},{5,13},{9,1},{13,5},{2,10},{6,14},... | collective-permute-start | bytes 208904 | tf_op jit(solution)/shard_map/ppermute | solution.py:458
  7.1 0.0 collective-permute-done.1.near_ref
  7.1 1.6 %collective-permute-start.2 = (bf16[128,128]{1,0:T(8,128)(2,1)S(1)}, bf16[128,128]{1,0:T(8,128)(2,1)S(1)}, u32[]{:S(2)}, u32[]{:S(2)}) collective-permute-start(bf16[128,128]{1,0:T(8,128)(2,1)S(1)} %shard_map.93), channel_id=1, source_target_pairs={{0,2},{1,3},{2,0},{3,1},{4,6},{5,7},{6,4},{7,5},{8,10},{9,11},{10,... | collective-permute-start | bytes 98312 | tf_op jit(solution)/shard_map/ppermute | solution.py:458
  8.7 4.3 %shard_map.91 = (bf16[2,512,128]{2,1,0:T(8,128)(2,1)S(1)}, bf16[2,512,128]{2,1,0:T(8,128)(2,1)S(1)}) custom-call(bf16[4096,512]{1,0:T(8,128)(2,1)} %bitcast.14, bf16[64,512]{1,0:T(8,128)(2,1)} %out_proj_hbm.1), custom_call_target="tpu_custom_call" | custom-call | bytes 13200000 | tf_op jit(solution)/shard_map/pallas_call | solution.py:149
  13.0 0.0 copy-start.1
  13.0 0.0 collective-permute-done
  13.1 0.0 collective-permute-done.2.far_ref
  13.1 0.1 collective-permute-start.3
  13.2 1.6 %collective-permute-start.6 = (bf16[2,272,128]{2,1,0:T(8,128)(2,1)S(1)}, bf16[2,272,128]{2,1,0:T(8,128)(2,1)S(1)}, u32[]{:S(2)}, u32[]{:S(2)}) collective-permute-start(bf16[2,272,128]{2,1,0:T(8,128)(2,1)S(1)} %pad_maximum_fusion.2), channel_id=1, source_target_pairs={{0,4},{4,0},{8,12},{12,8},{1,5},{5,1},{9,13},{13,9},{2,6},{6,2},{1... | collective-permute-start | bytes 417800 | tf_op jit(solution)/shard_map/ppermute | solution.py:458
  14.8 0.1 shard_map.94
  14.9 0.0 collective-permute-done.3.near_ref
  15.0 0.6 collective-permute-start.5
  15.6 1.8 %collective-permute-start.4 = (bf16[1,64,128]{2,1,0:T(8,128)(2,1)S(1)}, bf16[1,64,128]{2,1,0:T(8,128)(2,1)S(1)}, u32[]{:S(2)}, u32[]{:S(2)}) collective-permute-start(bf16[1,64,128]{2,1,0:T(8,128)(2,1)S(1)} %bitcast.12), channel_id=1, source_target_pairs={{0,8},{4,12},{8,0},{12,4},{1,9},{5,13},{9,1},{13,5},{2,10},{6,14},... | collective-permute-start | bytes 49160 | tf_op jit(solution)/shard_map/ppermute | solution.py:458
  17.4 2.1 %collective-permute-done.6 = bf16[2,272,128]{2,1,0:T(8,128)(2,1)S(1)} collective-permute-done((bf16[2,272,128]{2,1,0:T(8,128)(2,1)S(1)}, bf16[2,272,128]{2,1,0:T(8,128)(2,1)S(1)}, u32[]{:S(2)}, u32[]{:S(2)}) %collective-permute-start.6) | collective-permute-done | bytes 139296 | tf_op jit(solution)/shard_map/ppermute | solution.py:458
  19.5 0.7 %shard_map.96 = (bf16[4,512,512]{2,1,0:T(8,128)(2,1)S(1)}, s32[4,16,128]{2,1,0:T(8,128)S(1)}) custom-call(bf16[4,272,128]{2,1,0:T(8,128)(2,1)S(1)} %pad_maximum_fusion.shared_ref), custom_call_target="tpu_custom_call" | custom-call | bytes 4290000 | tf_op jit(solution)/shard_map/pallas_call | solution.py:233
  20.3 0.0 collective-permute-done.4
  20.3 0.4 collective-permute-done.5.far_ref
  20.7 1.3 %collective-permute-start.7 = (bf16[2,64,128]{2,1,0:T(8,128)(2,1)S(1)}, bf16[2,64,128]{2,1,0:T(8,128)(2,1)S(1)}, u32[]{:S(2)}, u32[]{:S(2)}) collective-permute-start(bf16[2,64,128]{2,1,0:T(8,128)(2,1)S(1)} %pad_maximum_fusion.4), channel_id=1, source_target_pairs={{0,4},{4,0},{8,12},{12,8},{1,5},{5,1},{9,13},{13,9},{2,6},{6,2},{1... | collective-permute-start | bytes 98312 | tf_op jit(solution)/shard_map/ppermute | solution.py:458
  21.9 0.0 copy-done
  21.9 0.1 copy.11.routes_ref
  22.0 1.7 %shard_map.97 = bf16[16,128,128]{2,1,0:T(8,128)(2,1)} custom-call(bf16[2,512,128]{2,1,0:T(8,128)(2,1)S(1)} %get-tuple-element.23.own_ref, bf16[2,512,128]{2,1,0:T(8,128)(2,1)S(1)} %collective-permute-done.3.near_ref, bf16[512,128]{1,0:T(8,128)(2,1)S(1)} %collective-permute-done.5.far_ref, s32[128,8]{1,0:T(8,128)S(1)} %copy.11.routes_ref, ...), custom_call_target="tpu_custom_call" | custom-call | bytes 6600000 | tf_op jit(solution)/shard_map/pallas_call | solution.py:290
  23.8 0.8 %collective-permute-done.7 = bf16[2,64,128]{2,1,0:T(8,128)(2,1)S(1)} collective-permute-done((bf16[2,64,128]{2,1,0:T(8,128)(2,1)S(1)}, bf16[2,64,128]{2,1,0:T(8,128)(2,1)S(1)}, u32[]{:S(2)}, u32[]{:S(2)}) %collective-permute-start.7) | collective-permute-done | bytes 32800 | tf_op jit(solution)/shard_map/ppermute | solution.py:458
  24.6 3.8 %all-to-all-start = ((bf16[16,128,128]{2,1,0:T(8,128)(2,1)}), bf16[16,128,128]{2,1,0:T(8,128)(2,1)S(1)}, u32[]{:S(2)}, u32[]{:S(2)}) async-start(bf16[16,128,128]{2,1,0:T(8,128)(2,1)} %shard_map.97), calls=%async_computation | async-start | bytes 1048576 | tf_op jit(solution)/shard_map/all_to_all | solution.py:514
  28.5 0.5 collective-permute-start.8
  28.9 0.9 %collective-permute-done.8 = bf16[1,4,64,128]{3,2,1,0:T(8,128)(2,1)S(1)} collective-permute-done((bf16[1,4,64,128]{3,2,1,0:T(8,128)(2,1)S(1)}, bf16[1,4,64,128]{3,2,1,0:T(8,128)(2,1)S(1)}, u32[]{:S(2)}, u32[]{:S(2)}) %collective-permute-start.8) | collective-permute-done | bytes 65568 | tf_op jit(solution)/shard_map/ppermute | solution.py:458
  29.8 1.9 %collective-permute-start.9 = (bf16[2,4,64,128]{3,2,1,0:T(8,128)(2,1)S(1)}, bf16[2,4,64,128]{3,2,1,0:T(8,128)(2,1)S(1)}, u32[]{:S(2)}, u32[]{:S(2)}) collective-permute-start(bf16[2,4,64,128]{3,2,1,0:T(8,128)(2,1)S(1)} %pad_maximum_fusion.3), channel_id=1, source_target_pairs={{0,2},{1,3},{2,0},{3,1},{4,6},{5,7},{6,4},{7,5},{8,10},{9,11},{10,... | collective-permute-start | bytes 393224 | tf_op jit(solution)/shard_map/ppermute | solution.py:458
  31.8 0.0 copy-done.1
  31.8 9.5 %shard_map.98.far_ref = bf16[8192,256]{1,0:T(8,128)(2,1)} custom-call(bf16[256,8,1024]{2,1,0:T(8,128)(2,1)} %query_ref, f32[8,64,64]{2,1,0:T(8,128)S(1)} %copy-done.1), custom_call_target="tpu_custom_call" | custom-call | bytes 33000000 | tf_op jit(solution)/shard_map/pallas_call | solution.py:353
  41.3 0.0 collective-permute-done.9
  41.4 1.5 %all-to-all-done.arrived_ref = bf16[16,128,128]{2,1,0:T(8,128)(2,1)S(1)} async-done(((bf16[16,128,128]{2,1,0:T(8,128)(2,1)}), bf16[16,128,128]{2,1,0:T(8,128)(2,1)S(1)}, u32[]{:S(2)}, u32[]{:S(2)}) %all-to-all-start) | async-done | bytes 524320 | tf_op jit(solution)/shard_map/all_to_all | solution.py:514
  42.9 6.1 %shard_map.99 = f32[16,8,128]{2,1,0:T(8,128)S(1)} custom-call(bf16[16,128,128]{2,1,0:T(8,128)(2,1)S(1)} %all-to-all-done.arrived_ref, bf16[16,64,128]{2,1,0:T(8,128)(2,1)S(1)} %bitcast.9, s32[4,16,128]{2,1,0:T(8,128)S(1)} %get-tuple-element.39.docs_ref, bf16[8192,256]{1,0:T(8,128)(2,1)} %shard_map.98.far_ref), custom_call_target="tpu_custom_call" | custom-call | bytes 16500000 | tf_op jit(solution)/shard_map/pallas_call | solution.py:427
  49.0 10.8 %all_to_all.10.pieces_ref = f32[16,8,128]{2,1,0:T(8,128)S(1)} all-to-all(f32[16,8,128]{2,1,0:T(8,128)S(1)} %shard_map.99), channel_id=1, replica_groups=mesh['groups'=2,'expert'=4,'proj'=4] {'expert','proj'}, dimensions={0} | all-to-all | bytes 131072 | tf_op jit(solution)/shard_map/all_to_all | solution.py:524
  59.8 0.6 %shard_map.100 = f32[8,64]{1,0:T(8,128)} custom-call(f32[16,8,128]{2,1,0:T(8,128)S(1)} %all_to_all.10.pieces_ref), custom_call_target="tpu_custom_call" | custom-call | tf_op jit(solution)/shard_map/pallas_call | solution.py:449
  (9 shorter events, 0.2 us)
Async XLA Ops:
  0.0 21.9 %copy-start = (s32[512,8]{0,1:T(8,128)S(1)}, s32[512,8]{0,1:T(8,128)}, u32[]{:S(2)}) copy-start(s32[512,8]{0,1:T(8,128)} %param.11) | copy-start | bytes 49156
  2.9 4.2 %collective-permute-start.1 = (bf16[2,128,128]{2,1,0:T(8,128)(2,1)S(1)}, bf16[2,128,128]{2,1,0:T(8,128)(2,1)S(1)}, u32[]{:S(2)}, u32[]{:S(2)}) collective-permute-start(bf16[2,128,128]{2,1,0:T(8,128)(2,1)S(1)} %get-tuple-element.26), channel_id=1, source_target_pairs={{0,1},{1,0},{2,3},{3,2},{4,5},{5,4},{6,7},{7,6},{8,9},{9,8},{10,11... | collective-permute-start | bytes 196616 | tf_op jit(solution)/shard_map/ppermute | solution.py:458
  3.5 9.6 %collective-permute-start = (bf16[272,128]{1,0:T(8,128)(2,1)S(1)}, bf16[272,128]{1,0:T(8,128)(2,1)S(1)}, u32[]{:S(2)}, u32[]{:S(2)}) collective-permute-start(bf16[272,128]{1,0:T(8,128)(2,1)S(1)} %get-tuple-element.24), channel_id=1, source_target_pairs={{0,8},{4,12},{8,0},{12,4},{1,9},{5,13},{9,1},{13,5},{2,10},{6,14},... | collective-permute-start | bytes 208904 | tf_op jit(solution)/shard_map/ppermute | solution.py:458
  7.1 5.9 %collective-permute-start.2 = (bf16[128,128]{1,0:T(8,128)(2,1)S(1)}, bf16[128,128]{1,0:T(8,128)(2,1)S(1)}, u32[]{:S(2)}, u32[]{:S(2)}) collective-permute-start(bf16[128,128]{1,0:T(8,128)(2,1)S(1)} %shard_map.93), channel_id=1, source_target_pairs={{0,2},{1,3},{2,0},{3,1},{4,6},{5,7},{6,4},{7,5},{8,10},{9,11},{10,... | collective-permute-start | bytes 98312 | tf_op jit(solution)/shard_map/ppermute | solution.py:458
  13.0 18.7 %copy-start.1 = (f32[8,64,64]{2,1,0:T(8,128)S(1)}, f32[8,64,64]{2,1,0:T(8,128)}, u32[]{:S(2)}) copy-start(f32[8,64,64]{2,1,0:T(8,128)} %inverse_ref.1) | copy-start | bytes 393220
  13.1 1.9 %collective-permute-start.3 = (bf16[2,512,128]{2,1,0:T(8,128)(2,1)S(1)}, bf16[2,512,128]{2,1,0:T(8,128)(2,1)S(1)}, u32[]{:S(2)}, u32[]{:S(2)}) collective-permute-start(bf16[2,512,128]{2,1,0:T(8,128)(2,1)S(1)} %get-tuple-element.28), channel_id=1, source_target_pairs={{0,1},{1,0},{2,3},{3,2},{4,5},{5,4},{6,7},{7,6},{8,9},{9,8},{10,11... | collective-permute-start | bytes 786440 | tf_op jit(solution)/shard_map/ppermute | solution.py:458
  13.2 6.3 %collective-permute-start.6 = (bf16[2,272,128]{2,1,0:T(8,128)(2,1)S(1)}, bf16[2,272,128]{2,1,0:T(8,128)(2,1)S(1)}, u32[]{:S(2)}, u32[]{:S(2)}) collective-permute-start(bf16[2,272,128]{2,1,0:T(8,128)(2,1)S(1)} %pad_maximum_fusion.2), channel_id=1, source_target_pairs={{0,4},{4,0},{8,12},{12,8},{1,5},{5,1},{9,13},{13,9},{2,6},{6,2},{1... | collective-permute-start | bytes 417800 | tf_op jit(solution)/shard_map/ppermute | solution.py:458
  15.0 5.7 %collective-permute-start.5 = (bf16[512,128]{1,0:T(8,128)(2,1)S(1)}, bf16[512,128]{1,0:T(8,128)(2,1)S(1)}, u32[]{:S(2)}, u32[]{:S(2)}) collective-permute-start(bf16[512,128]{1,0:T(8,128)(2,1)S(1)} %shard_map.95), channel_id=1, source_target_pairs={{0,2},{1,3},{2,0},{3,1},{4,6},{5,7},{6,4},{7,5},{8,10},{9,11},{10,... | collective-permute-start | bytes 393224 | tf_op jit(solution)/shard_map/ppermute | solution.py:458
  15.6 4.7 %collective-permute-start.4 = (bf16[1,64,128]{2,1,0:T(8,128)(2,1)S(1)}, bf16[1,64,128]{2,1,0:T(8,128)(2,1)S(1)}, u32[]{:S(2)}, u32[]{:S(2)}) collective-permute-start(bf16[1,64,128]{2,1,0:T(8,128)(2,1)S(1)} %bitcast.12), channel_id=1, source_target_pairs={{0,8},{4,12},{8,0},{12,4},{1,9},{5,13},{9,1},{13,5},{2,10},{6,14},... | collective-permute-start | bytes 49160 | tf_op jit(solution)/shard_map/ppermute | solution.py:458
  20.7 3.9 %collective-permute-start.7 = (bf16[2,64,128]{2,1,0:T(8,128)(2,1)S(1)}, bf16[2,64,128]{2,1,0:T(8,128)(2,1)S(1)}, u32[]{:S(2)}, u32[]{:S(2)}) collective-permute-start(bf16[2,64,128]{2,1,0:T(8,128)(2,1)S(1)} %pad_maximum_fusion.4), channel_id=1, source_target_pairs={{0,4},{4,0},{8,12},{12,8},{1,5},{5,1},{9,13},{13,9},{2,6},{6,2},{1... | collective-permute-start | bytes 98312 | tf_op jit(solution)/shard_map/ppermute | solution.py:458
  24.6 18.3 %all-to-all-start = ((bf16[16,128,128]{2,1,0:T(8,128)(2,1)}), bf16[16,128,128]{2,1,0:T(8,128)(2,1)S(1)}, u32[]{:S(2)}, u32[]{:S(2)}) async-start(bf16[16,128,128]{2,1,0:T(8,128)(2,1)} %shard_map.97), calls=%async_computation | async-start | bytes 1048576 | tf_op jit(solution)/shard_map/all_to_all | solution.py:514
  28.5 1.4 %collective-permute-start.8 = (bf16[1,4,64,128]{3,2,1,0:T(8,128)(2,1)S(1)}, bf16[1,4,64,128]{3,2,1,0:T(8,128)(2,1)S(1)}, u32[]{:S(2)}, u32[]{:S(2)}) collective-permute-start(bf16[1,4,64,128]{3,2,1,0:T(8,128)(2,1)S(1)} %maximum_bitcast_fusion), channel_id=1, source_target_pairs={{0,1},{1,0},{2,3},{3,2},{4,5},{5,4},{6,7},{7,6},{8,9},{9,8},{10,11... | collective-permute-start | bytes 196616 | tf_op jit(solution)/shard_map/ppermute | solution.py:458
  29.8 11.5 %collective-permute-start.9 = (bf16[2,4,64,128]{3,2,1,0:T(8,128)(2,1)S(1)}, bf16[2,4,64,128]{3,2,1,0:T(8,128)(2,1)S(1)}, u32[]{:S(2)}, u32[]{:S(2)}) collective-permute-start(bf16[2,4,64,128]{3,2,1,0:T(8,128)(2,1)S(1)} %pad_maximum_fusion.3), channel_id=1, source_target_pairs={{0,2},{1,3},{2,0},{3,1},{4,6},{5,7},{6,4},{7,5},{8,10},{9,11},{10,... | collective-permute-start | bytes 393224 | tf_op jit(solution)/shard_map/ppermute | solution.py:458

commit v11 on v10

--- a/solution.py
+++ b/solution.py
@@ -49,7 +49,7 @@
 def inner_kernel(
     act_hbm, in_proj_hbm, inverse_hbm, docs_hbm, leaving_ref, own_ref, shared_ref, act_ref, in_proj_ref, inverse_ref, docs_ref, sems
 ):
-    turns = (1, 3, 2, 0)
+    turns = (2, 3, 1, 0)
     quarter = act_ref.shape[1]
     width = in_proj_ref.shape[0]
     half = quarter // 2
@@ -487,32 +487,28 @@
     inner_leaving, inner_own, shared = project_inner(
         activations, in_projection, inverse_out, doc_ids.reshape(shares, quarter), shares
     )
+    inner_first = exchange(inner_leaving, "proj", shares, 2)
     far_shared = exchange(shared, "expert", owners, owners // 2)
-    inner_near = exchange(inner_leaving, "proj", shares, 1)
-    inner_far = exchange(combine(combine_inner_kernel, inner_own, inner_near), "proj", shares, 2)
     leaving, own = project_outer(flat_hidden, out_projection, shares, top)
-    far_shared, inner_far, leaving = lax.optimization_barrier((far_shared, inner_far, leaving))
+    far_shared, inner_first, leaving = lax.optimization_barrier((far_shared, inner_first, leaving))
     near = exchange(leaving, "proj", shares, 1)
     shared, turns = jnp.stack([shared, far_shared]), (0, owners // 2)
     for bit in reversed(range((owners // 2).bit_length() - 1)):
         shared, turns = double(shared, turns, "expert", owners, 1 << bit)
+    inner_second = exchange(combine(combine_inner_kernel, inner_own, inner_first), "proj", shares, 1)
     sent = combine(combine_outer_kernel, own, near)
     far = exchange(sent, "proj", shares, 2)
-    inner = finish_inner(inner_own, inner_near, inner_far, width)
+    inner = finish_inner(inner_own, inner_first, inner_second, width)
     inner, _ = lax.optimization_barrier((inner, sent))
-    inner, owner_turns = double(inner[None], (0,), "expert", owners, owners // 2)
+    owner_turns = tuple(reversed(range(owners)))
+    arriving = [exchange(inner, "expert", owners, turn) for turn in owner_turns if turn]
     weights, all_docs = expand(shared, turns, width, experts, shares)
-    inner, far, weights = lax.optimization_barrier((inner, far, weights))
-    for bit in reversed(range((owners // 2).bit_length() - 1)):
-        arriving = exchange(inner, "expert", owners, 1 << bit)
-        owner_turns = owner_turns + tuple(t ^ (1 << bit) for t in owner_turns)
-        if bit:
-            inner = jnp.concatenate([inner, arriving], axis=0)
+    far, weights = lax.optimization_barrier((far, weights))
     quarter_routes = lax.dynamic_slice_in_dim(routes, lax.axis_index("proj") * quarter, quarter, 0)
     payload = condition(own, near, far, quarter_routes, weights, shares, width)
     payload, arriving = lax.optimization_barrier((payload, arriving))
     arrived = lax.all_to_all(payload, ("expert", "proj"), 0, 0, tiled=True)
-    inner = jnp.concatenate([inner, arriving], axis=0)
+    inner = jnp.stack(arriving + [inner])
     inner, share_turns = inner[None], (0,)
     inner, share_turns = double(inner, share_turns, "proj", shares, 1)
     inner, query_grads = lax.optimization_barrier((inner, query_grads))

time: 60.9 us -> 60.6 us (level)
  waiting for transfers between devices: 5.78 us -> 3.45 us
  starting transfers between devices: 17.3 us -> 19.4 us
    ppermute x10 -> x11, waiting for transfers between devices: 4.24 us -> 1.91 us  [exchange(): return lax.ppermute(block, axis, [(i, i ^ turn) for i in range(size)])]
    ppermute x10 -> x11, starting transfers between devices: 13.5 us -> 15 us  [exchange(): return lax.ppermute(block, axis, [(i, i ^ turn) for i in range(size)])]
  transfers between devices with their start and end apart: 11 -> 12, of which waited for: 5 -> 4; matrix products, arithmetic and copies ran while one was open for 0% -> 0% of each run, Pallas kernels for 27% -> 27%
where the time goes in v11:
time: 60.6 us; the launch traced here: 60.1 us
  Pallas kernels  26.1 us (43%)
  starting transfers between devices  19.4 us (32%)
  blocking collectives  10.8 us (18%)
  waiting for transfers between devices  3.45 us (6%)
    ppermute x11, starting transfers between devices, exchange(): return lax.ppermute(block, axis, [(i, i ^ turn) for i in range(size)])  15 us
    all_to_all x1, blocking collectives, local(): pieces = lax.all_to_all(pieces, ('expert', 'proj'), 0, 0, tiled=True)  10.8 us
    pallas_call x1, Pallas kernels, condition_queries(): pl.pallas_call(query_kernel, grid=(flat // LANES,), in_specs=[pl.BlockSpe...  9.52 us
    pallas_call x1, Pallas kernels, score(): pl.pallas_call(functools.partial(score_kernel, width=width, doc_count=doc...  6.1 us
    all_to_all x1, starting transfers between devices, local(): arrived = lax.all_to_all(payload, ('expert', 'proj'), 0, 0, tiled=True)  4.33 us
    pallas_call x1, Pallas kernels, project_outer(): pl.pallas_call(functools.partial(outer_kernel, top=top), in_specs=[HBM] *...  4.33 us
    pallas_call x1, Pallas kernels, project_inner(): pl.pallas_call(inner_kernel, in_specs=[HBM] * 4, out_specs=[VMEM] * 3, ou...  2.93 us
    ppermute x11, waiting for transfers between devices, exchange(): return lax.ppermute(block, axis, [(i, i ^ turn) for i in range(size)])  1.91 us
  transfers between devices with their start and end apart: 12, of which 4 were waited for; matrix products, arithmetic and copies ran while one was open for 0% of the time, Pallas kernels for 27%

profile of v11, /device:TPU:0, one launch (start us, length us, event | category | flops | bytes accessed | tf_op | source)
XLA Modules:
  0.0 60.1 jit_solution(11646437952534822393)
XLA Ops:
  0.0 0.0 copy-start
  0.0 2.9 %shard_map.92 = (bf16[2,128,128]{2,1,0:T(8,128)(2,1)S(1)}, bf16[2,128,128]{2,1,0:T(8,128)(2,1)S(1)}, bf16[272,128]{1,0:T(8,128)(2,1)S(1)}) custom-call(bf16[512,1792]{1,0:T(8,128)(2,1)} %act_hbm.1, bf16[64,1792]{1,0:T(8,128)(2,1)} %in_proj_hbm.1, f32[8,64,64]{2,1,0:T(8,128)} %inverse_hbm.1, s32[4,128]{1,0:T(4,128)} %bitcast.22), custom_call_target="tpu_custom_call" | custom-call | bytes 8250000 | tf_op jit(solution)/shard_map/pallas_call | solution.py:96
  2.9 4.1 %collective-permute-start = (bf16[272,128]{1,0:T(8,128)(2,1)S(1)}, bf16[272,128]{1,0:T(8,128)(2,1)S(1)}, u32[]{:S(2)}, u32[]{:S(2)}) collective-permute-start(bf16[272,128]{1,0:T(8,128)(2,1)S(1)} %get-tuple-element.25), channel_id=1, source_target_pairs={{0,8},{4,12},{8,0},{12,4},{1,9},{5,13},{9,1},{13,5},{2,10},{6,14},... | collective-permute-start | bytes 208904 | tf_op jit(solution)/shard_map/ppermute | solution.py:458
  7.0 1.5 %collective-permute-start.1 = (bf16[2,128,128]{2,1,0:T(8,128)(2,1)S(1)}, bf16[2,128,128]{2,1,0:T(8,128)(2,1)S(1)}, u32[]{:S(2)}, u32[]{:S(2)}) collective-permute-start(bf16[2,128,128]{2,1,0:T(8,128)(2,1)S(1)} %get-tuple-element.26), channel_id=1, source_target_pairs={{0,2},{1,3},{2,0},{3,1},{4,6},{5,7},{6,4},{7,5},{8,10},{9,11},{10,... | collective-permute-start | bytes 196616 | tf_op jit(solution)/shard_map/ppermute | solution.py:458
  8.5 4.3 %shard_map.91 = (bf16[2,512,128]{2,1,0:T(8,128)(2,1)S(1)}, bf16[2,512,128]{2,1,0:T(8,128)(2,1)S(1)}) custom-call(bf16[4096,512]{1,0:T(8,128)(2,1)} %bitcast.16, bf16[64,512]{1,0:T(8,128)(2,1)} %out_proj_hbm.1), custom_call_target="tpu_custom_call" | custom-call | bytes 13200000 | tf_op jit(solution)/shard_map/pallas_call | solution.py:149
  12.9 0.0 copy-start.1
  12.9 0.0 collective-permute-done.1.near_ref
  12.9 0.0 collective-permute-done
  12.9 0.1 collective-permute-start.2
  13.0 1.6 %collective-permute-start.4 = (bf16[2,272,128]{2,1,0:T(8,128)(2,1)S(1)}, bf16[2,272,128]{2,1,0:T(8,128)(2,1)S(1)}, u32[]{:S(2)}, u32[]{:S(2)}) collective-permute-start(bf16[2,272,128]{2,1,0:T(8,128)(2,1)S(1)} %pad_maximum_fusion.2), channel_id=1, source_target_pairs={{0,4},{4,0},{8,12},{12,8},{1,5},{5,1},{9,13},{13,9},{2,6},{6,2},{1... | collective-permute-start | bytes 417800 | tf_op jit(solution)/shard_map/ppermute | solution.py:458
  14.7 0.3 collective-permute-start.5
  14.9 0.0 collective-permute-done.2.near_ref
  15.0 0.6 %collective-permute-start.3 = (bf16[512,128]{1,0:T(8,128)(2,1)S(1)}, bf16[512,128]{1,0:T(8,128)(2,1)S(1)}, u32[]{:S(2)}, u32[]{:S(2)}) collective-permute-start(bf16[512,128]{1,0:T(8,128)(2,1)S(1)} %shard_map.93), channel_id=1, source_target_pairs={{0,2},{1,3},{2,0},{3,1},{4,6},{5,7},{6,4},{7,5},{8,10},{9,11},{10,... | collective-permute-start | bytes 393224 | tf_op jit(solution)/shard_map/ppermute | solution.py:458
  15.6 0.0 copy-done
  15.6 0.1 copy.11.routes_ref
  15.7 0.2 collective-permute-done.5.far_ref
  15.9 0.1 shard_map.97
  16.0 1.0 %collective-permute-start.8 = (bf16[64,128]{1,0:T(8,128)(2,1)S(1)}, bf16[64,128]{1,0:T(8,128)(2,1)S(1)}, u32[]{:S(2)}, u32[]{:S(2)}) collective-permute-start(bf16[64,128]{1,0:T(8,128)(2,1)S(1)} %shard_map.97), channel_id=1, source_target_pairs={{0,4},{4,0},{8,12},{12,8},{1,5},{5,1},{9,13},{13,9},{2,6},{6,2},{1... | collective-permute-start | bytes 49160 | tf_op jit(solution)/shard_map/ppermute | solution.py:458
  17.0 1.2 %collective-permute-start.7 = (bf16[64,128]{1,0:T(8,128)(2,1)S(1)}, bf16[64,128]{1,0:T(8,128)(2,1)S(1)}, u32[]{:S(2)}, u32[]{:S(2)}) collective-permute-start(bf16[64,128]{1,0:T(8,128)(2,1)S(1)} %shard_map.97), channel_id=1, source_target_pairs={{0,8},{4,12},{8,0},{12,4},{1,9},{5,13},{9,1},{13,5},{2,10},{6,14},... | collective-permute-start | bytes 49160 | tf_op jit(solution)/shard_map/ppermute | solution.py:458
  18.2 2.3 %collective-permute-start.6 = (bf16[64,128]{1,0:T(8,128)(2,1)S(1)}, bf16[64,128]{1,0:T(8,128)(2,1)S(1)}, u32[]{:S(2)}, u32[]{:S(2)}) collective-permute-start(bf16[64,128]{1,0:T(8,128)(2,1)S(1)} %shard_map.97), channel_id=1, source_target_pairs={{0,12},{4,8},{8,4},{12,0},{1,13},{5,9},{9,5},{13,1},{2,14},{6,10},... | collective-permute-start | bytes 49160 | tf_op jit(solution)/shard_map/ppermute | solution.py:458
  20.5 0.0 collective-permute-done.4
  20.5 0.7 %shard_map.94 = (bf16[4,512,512]{2,1,0:T(8,128)(2,1)S(1)}, s32[4,16,128]{2,1,0:T(8,128)S(1)}) custom-call(bf16[4,272,128]{2,1,0:T(8,128)(2,1)S(1)} %pad_maximum_fusion.shared_ref), custom_call_target="tpu_custom_call" | custom-call | bytes 4290000 | tf_op jit(solution)/shard_map/pallas_call | solution.py:233
  21.3 0.0 collective-permute-done.3.far_ref
  21.3 1.7 %shard_map.95 = bf16[16,128,128]{2,1,0:T(8,128)(2,1)} custom-call(bf16[2,512,128]{2,1,0:T(8,128)(2,1)S(1)} %get-tuple-element.24.own_ref, bf16[2,512,128]{2,1,0:T(8,128)(2,1)S(1)} %collective-permute-done.2.near_ref, bf16[512,128]{1,0:T(8,128)(2,1)S(1)} %collective-permute-done.3.far_ref, s32[128,8]{1,0:T(8,128)S(1)} %copy.11.routes_ref, ...), custom_call_target="tpu_custom_call" | custom-call | bytes 6600000 | tf_op jit(solution)/shard_map/pallas_call | solution.py:290
  23.0 0.0 collective-permute-done.8
  23.0 0.0 collective-permute-done.7
  23.0 0.7 %collective-permute-done.6 = bf16[64,128]{1,0:T(8,128)(2,1)S(1)} collective-permute-done((bf16[64,128]{1,0:T(8,128)(2,1)S(1)}, bf16[64,128]{1,0:T(8,128)(2,1)S(1)}, u32[]{:S(2)}, u32[]{:S(2)}) %collective-permute-start.6) | collective-permute-done | bytes 16416 | tf_op jit(solution)/shard_map/ppermute | solution.py:458
  23.8 4.3 %all-to-all-start = ((bf16[16,128,128]{2,1,0:T(8,128)(2,1)}), bf16[16,128,128]{2,1,0:T(8,128)(2,1)S(1)}, u32[]{:S(2)}, u32[]{:S(2)}) async-start(bf16[16,128,128]{2,1,0:T(8,128)(2,1)} %shard_map.95), calls=%async_computation | async-start | bytes 1048576 | tf_op jit(solution)/shard_map/all_to_all | solution.py:510
  28.1 0.5 collective-permute-start.9
  28.6 0.9 %collective-permute-done.9 = bf16[1,4,64,128]{3,2,1,0:T(8,128)(2,1)S(1)} collective-permute-done((bf16[1,4,64,128]{3,2,1,0:T(8,128)(2,1)S(1)}, bf16[1,4,64,128]{3,2,1,0:T(8,128)(2,1)S(1)}, u32[]{:S(2)}, u32[]{:S(2)}) %collective-permute-start.9) | collective-permute-done | bytes 65568 | tf_op jit(solution)/shard_map/ppermute | solution.py:458
  29.5 1.9 %collective-permute-start.10 = (bf16[2,4,64,128]{3,2,1,0:T(8,128)(2,1)S(1)}, bf16[2,4,64,128]{3,2,1,0:T(8,128)(2,1)S(1)}, u32[]{:S(2)}, u32[]{:S(2)}) collective-permute-start(bf16[2,4,64,128]{3,2,1,0:T(8,128)(2,1)S(1)} %pad_maximum_fusion.3), channel_id=1, source_target_pairs={{0,2},{1,3},{2,0},{3,1},{4,6},{5,7},{6,4},{7,5},{8,10},{9,11},{10,... | collective-permute-start | bytes 393224 | tf_op jit(solution)/shard_map/ppermute | solution.py:458
  31.5 0.0 copy-done.1
  31.5 9.5 %shard_map.98.far_ref = bf16[8192,256]{1,0:T(8,128)(2,1)} custom-call(bf16[256,8,1024]{2,1,0:T(8,128)(2,1)} %query_ref, f32[8,64,64]{2,1,0:T(8,128)S(1)} %copy-done.1), custom_call_target="tpu_custom_call" | custom-call | bytes 33000000 | tf_op jit(solution)/shard_map/pallas_call | solution.py:353
  41.0 0.0 collective-permute-done.10
  41.0 1.5 %all-to-all-done.arrived_ref = bf16[16,128,128]{2,1,0:T(8,128)(2,1)S(1)} async-done(((bf16[16,128,128]{2,1,0:T(8,128)(2,1)}), bf16[16,128,128]{2,1,0:T(8,128)(2,1)S(1)}, u32[]{:S(2)}, u32[]{:S(2)}) %all-to-all-start) | async-done | bytes 524320 | tf_op jit(solution)/shard_map/all_to_all | solution.py:510
  42.6 6.1 %shard_map.99 = f32[16,8,128]{2,1,0:T(8,128)S(1)} custom-call(bf16[16,128,128]{2,1,0:T(8,128)(2,1)S(1)} %all-to-all-done.arrived_ref, bf16[16,64,128]{2,1,0:T(8,128)(2,1)S(1)} %bitcast.12, s32[4,16,128]{2,1,0:T(8,128)S(1)} %get-tuple-element.41.docs_ref, bf16[8192,256]{1,0:T(8,128)(2,1)} %shard_map.98.far_ref), custom_call_target="tpu_custom_call" | custom-call | bytes 16500000 | tf_op jit(solution)/shard_map/pallas_call | solution.py:427
  48.7 10.8 %all_to_all.10.pieces_ref = f32[16,8,128]{2,1,0:T(8,128)S(1)} all-to-all(f32[16,8,128]{2,1,0:T(8,128)S(1)} %shard_map.99), channel_id=1, replica_groups=mesh['groups'=2,'expert'=4,'proj'=4] {'expert','proj'}, dimensions={0} | all-to-all | bytes 131072 | tf_op jit(solution)/shard_map/all_to_all | solution.py:520
  59.5 0.6 %shard_map.100 = f32[8,64]{1,0:T(8,128)} custom-call(f32[16,8,128]{2,1,0:T(8,128)S(1)} %all_to_all.10.pieces_ref), custom_call_target="tpu_custom_call" | custom-call | tf_op jit(solution)/shard_map/pallas_call | solution.py:449
  (8 shorter events, 0.1 us)
Async XLA Ops:
  0.0 15.6 %copy-start = (s32[512,8]{0,1:T(8,128)S(1)}, s32[512,8]{0,1:T(8,128)}, u32[]{:S(2)}) copy-start(s32[512,8]{0,1:T(8,128)} %param.11) | copy-start | bytes 49156
  2.9 10.0 %collective-permute-start = (bf16[272,128]{1,0:T(8,128)(2,1)S(1)}, bf16[272,128]{1,0:T(8,128)(2,1)S(1)}, u32[]{:S(2)}, u32[]{:S(2)}) collective-permute-start(bf16[272,128]{1,0:T(8,128)(2,1)S(1)} %get-tuple-element.25), channel_id=1, source_target_pairs={{0,8},{4,12},{8,0},{12,4},{1,9},{5,13},{9,1},{13,5},{2,10},{6,14},... | collective-permute-start | bytes 208904 | tf_op jit(solution)/shard_map/ppermute | solution.py:458
  7.0 5.8 %collective-permute-start.1 = (bf16[2,128,128]{2,1,0:T(8,128)(2,1)S(1)}, bf16[2,128,128]{2,1,0:T(8,128)(2,1)S(1)}, u32[]{:S(2)}, u32[]{:S(2)}) collective-permute-start(bf16[2,128,128]{2,1,0:T(8,128)(2,1)S(1)} %get-tuple-element.26), channel_id=1, source_target_pairs={{0,2},{1,3},{2,0},{3,1},{4,6},{5,7},{6,4},{7,5},{8,10},{9,11},{10,... | collective-permute-start | bytes 196616 | tf_op jit(solution)/shard_map/ppermute | solution.py:458
  12.9 18.6 %copy-start.1 = (f32[8,64,64]{2,1,0:T(8,128)S(1)}, f32[8,64,64]{2,1,0:T(8,128)}, u32[]{:S(2)}) copy-start(f32[8,64,64]{2,1,0:T(8,128)} %inverse_ref.1) | copy-start | bytes 393220
  12.9 2.0 %collective-permute-start.2 = (bf16[2,512,128]{2,1,0:T(8,128)(2,1)S(1)}, bf16[2,512,128]{2,1,0:T(8,128)(2,1)S(1)}, u32[]{:S(2)}, u32[]{:S(2)}) collective-permute-start(bf16[2,512,128]{2,1,0:T(8,128)(2,1)S(1)} %get-tuple-element.28), channel_id=1, source_target_pairs={{0,1},{1,0},{2,3},{3,2},{4,5},{5,4},{6,7},{7,6},{8,9},{9,8},{10,11... | collective-permute-start | bytes 786440 | tf_op jit(solution)/shard_map/ppermute | solution.py:458
  13.0 7.5 %collective-permute-start.4 = (bf16[2,272,128]{2,1,0:T(8,128)(2,1)S(1)}, bf16[2,272,128]{2,1,0:T(8,128)(2,1)S(1)}, u32[]{:S(2)}, u32[]{:S(2)}) collective-permute-start(bf16[2,272,128]{2,1,0:T(8,128)(2,1)S(1)} %pad_maximum_fusion.2), channel_id=1, source_target_pairs={{0,4},{4,0},{8,12},{12,8},{1,5},{5,1},{9,13},{13,9},{2,6},{6,2},{1... | collective-permute-start | bytes 417800 | tf_op jit(solution)/shard_map/ppermute | solution.py:458
  14.7 1.3 %collective-permute-start.5 = (bf16[128,128]{1,0:T(8,128)(2,1)S(1)}, bf16[128,128]{1,0:T(8,128)(2,1)S(1)}, u32[]{:S(2)}, u32[]{:S(2)}) collective-permute-start(bf16[128,128]{1,0:T(8,128)(2,1)S(1)} %shard_map.96), channel_id=1, source_target_pairs={{0,1},{1,0},{2,3},{3,2},{4,5},{5,4},{6,7},{7,6},{8,9},{9,8},{10,11... | collective-permute-start | bytes 98312 | tf_op jit(solution)/shard_map/ppermute | solution.py:458
  15.0 6.3 %collective-permute-start.3 = (bf16[512,128]{1,0:T(8,128)(2,1)S(1)}, bf16[512,128]{1,0:T(8,128)(2,1)S(1)}, u32[]{:S(2)}, u32[]{:S(2)}) collective-permute-start(bf16[512,128]{1,0:T(8,128)(2,1)S(1)} %shard_map.93), channel_id=1, source_target_pairs={{0,2},{1,3},{2,0},{3,1},{4,6},{5,7},{6,4},{7,5},{8,10},{9,11},{10,... | collective-permute-start | bytes 393224 | tf_op jit(solution)/shard_map/ppermute | solution.py:458
  16.0 7.0 %collective-permute-start.8 = (bf16[64,128]{1,0:T(8,128)(2,1)S(1)}, bf16[64,128]{1,0:T(8,128)(2,1)S(1)}, u32[]{:S(2)}, u32[]{:S(2)}) collective-permute-start(bf16[64,128]{1,0:T(8,128)(2,1)S(1)} %shard_map.97), channel_id=1, source_target_pairs={{0,4},{4,0},{8,12},{12,8},{1,5},{5,1},{9,13},{13,9},{2,6},{6,2},{1... | collective-permute-start | bytes 49160 | tf_op jit(solution)/shard_map/ppermute | solution.py:458
  17.0 6.0 %collective-permute-start.7 = (bf16[64,128]{1,0:T(8,128)(2,1)S(1)}, bf16[64,128]{1,0:T(8,128)(2,1)S(1)}, u32[]{:S(2)}, u32[]{:S(2)}) collective-permute-start(bf16[64,128]{1,0:T(8,128)(2,1)S(1)} %shard_map.97), channel_id=1, source_target_pairs={{0,8},{4,12},{8,0},{12,4},{1,9},{5,13},{9,1},{13,5},{2,10},{6,14},... | collective-permute-start | bytes 49160 | tf_op jit(solution)/shard_map/ppermute | solution.py:458
  18.2 5.5 %collective-permute-start.6 = (bf16[64,128]{1,0:T(8,128)(2,1)S(1)}, bf16[64,128]{1,0:T(8,128)(2,1)S(1)}, u32[]{:S(2)}, u32[]{:S(2)}) collective-permute-start(bf16[64,128]{1,0:T(8,128)(2,1)S(1)} %shard_map.97), channel_id=1, source_target_pairs={{0,12},{4,8},{8,4},{12,0},{1,13},{5,9},{9,5},{13,1},{2,14},{6,10},... | collective-permute-start | bytes 49160 | tf_op jit(solution)/shard_map/ppermute | solution.py:458
  23.8 18.8 %all-to-all-start = ((bf16[16,128,128]{2,1,0:T(8,128)(2,1)}), bf16[16,128,128]{2,1,0:T(8,128)(2,1)S(1)}, u32[]{:S(2)}, u32[]{:S(2)}) async-start(bf16[16,128,128]{2,1,0:T(8,128)(2,1)} %shard_map.95), calls=%async_computation | async-start | bytes 1048576 | tf_op jit(solution)/shard_map/all_to_all | solution.py:510
  28.1 1.4 %collective-permute-start.9 = (bf16[1,4,64,128]{3,2,1,0:T(8,128)(2,1)S(1)}, bf16[1,4,64,128]{3,2,1,0:T(8,128)(2,1)S(1)}, u32[]{:S(2)}, u32[]{:S(2)}) collective-permute-start(bf16[1,4,64,128]{3,2,1,0:T(8,128)(2,1)S(1)} %maximum_bitcast_fusion), channel_id=1, source_target_pairs={{0,1},{1,0},{2,3},{3,2},{4,5},{5,4},{6,7},{7,6},{8,9},{9,8},{10,11... | collective-permute-start | bytes 196616 | tf_op jit(solution)/shard_map/ppermute | solution.py:458
  29.5 11.5 %collective-permute-start.10 = (bf16[2,4,64,128]{3,2,1,0:T(8,128)(2,1)S(1)}, bf16[2,4,64,128]{3,2,1,0:T(8,128)(2,1)S(1)}, u32[]{:S(2)}, u32[]{:S(2)}) collective-permute-start(bf16[2,4,64,128]{3,2,1,0:T(8,128)(2,1)S(1)} %pad_maximum_fusion.3), channel_id=1, source_target_pairs={{0,2},{1,3},{2,0},{3,1},{4,6},{5,7},{6,4},{7,5},{8,10},{9,11},{10,... | collective-permute-start | bytes 393224 | tf_op jit(solution)/shard_map/ppermute | solution.py:458

commit v12 on v11

--- a/solution.py
+++ b/solution.py
@@ -47,7 +47,7 @@
 
 
 def inner_kernel(
-    act_hbm, in_proj_hbm, inverse_hbm, docs_hbm, leaving_ref, own_ref, shared_ref, act_ref, in_proj_ref, inverse_ref, docs_ref, sems
+    act_hbm, in_proj_hbm, inverse_hbm, leaving_ref, own_ref, shared_ref, act_ref, in_proj_ref, inverse_ref, sems
 ):
     turns = (2, 3, 1, 0)
     quarter = act_ref.shape[1]
@@ -59,7 +59,7 @@
         rows = pl.ds(pl.multiple_of(jnp.bitwise_xor(place, turn) * quarter, quarter), quarter)
         pairs.append((act_hbm.at[rows], act_ref.at[g]))
         if g == 0:
-            pairs += [(inverse_hbm, inverse_ref), (docs_hbm, docs_ref)]
+            pairs.append((inverse_hbm, inverse_ref))
     take = in_order([pltpu.make_async_copy(*pair, sems.at[i]) for i, pair in enumerate(pairs)], 5)
     take()
     first = low_lanes(half, width)
@@ -67,14 +67,10 @@
         take()
         if wire_ref is leaving_ref:
             take()
-            take()
             experts = inverse_ref.shape[0] // 2
             for e in range(experts):
                 pair = jnp.concatenate([inverse_ref[e], inverse_ref[experts + e]], axis=1)
                 shared_ref[e * width : (e + 1) * width, :] = pair.astype(jnp.bfloat16)
-            docs = docs_ref[...].astype(jnp.float32)
-            docs = jnp.concatenate([docs, jnp.zeros((DOC_ROWS - docs.shape[0], LANES), jnp.float32)], axis=0)
-            shared_ref[experts * width :, :] = docs.astype(jnp.bfloat16)
         take()
         twice = jnp.concatenate([in_proj_ref[...], in_proj_ref[...]], axis=0)
         g = 0 if wire_ref is leaving_ref else 2
@@ -87,17 +83,17 @@
             wire_ref[i, half:, :] = low
 
 
-def project_inner(activations, in_projection, inverse_out, doc_rows, quarters):
+def project_inner(activations, in_projection, inverse_out, quarters):
     tokens, model = activations.shape
     quarter = tokens // quarters
     experts, width, _ = inverse_out.shape
     wire = jax.ShapeDtypeStruct((quarters // 2, quarter, LANES), jnp.bfloat16)
-    fixed = (in_projection, inverse_out, doc_rows)
+    fixed = (in_projection, inverse_out)
     return pl.pallas_call(
         inner_kernel,
-        in_specs=[HBM] * 4,
+        in_specs=[HBM] * 3,
         out_specs=[VMEM] * 3,
-        out_shape=[wire, wire, jax.ShapeDtypeStruct((experts // 2 * width + DOC_ROWS, LANES), jnp.bfloat16)],
+        out_shape=[wire, wire, jax.ShapeDtypeStruct((experts // 2 * width, LANES), jnp.bfloat16)],
         scratch_shapes=[pltpu.VMEM((quarters, quarter, model), jnp.bfloat16)]
         + [pltpu.VMEM(array.shape, array.dtype) for array in fixed]
         + [pltpu.SemaphoreType.DMA((quarters + len(fixed),))],
@@ -187,24 +183,26 @@
     )(own, near)
 
 
-def finish_inner_kernel(own_ref, near_ref, far_ref, out_ref):
-    total = exact_rows(own_ref[1]) + exact_rows(near_ref[0]) + exact_rows(far_ref[...])
-    width = out_ref.shape[0]
+def finish_inner_kernel(own_ref, first_ref, second_ref, docs_ref, out_ref):
+    total = exact_rows(own_ref[1]) + exact_rows(first_ref[0]) + exact_rows(second_ref[...])
+    width = out_ref.shape[0] - DOC_ROWS
     total = jnp.concatenate([total[:, :width], total[:, width:]], axis=0)
-    out_ref[...] = jnp.transpose(total).astype(jnp.bfloat16)
-
-
-def finish_inner(own, near, far, width):
+    out_ref[:width, :] = jnp.transpose(total).astype(jnp.bfloat16)
+    docs = docs_ref[pl.ds(lax.axis_index("proj"), 1), :].astype(jnp.float32)
+    out_ref[width:, :] = jnp.broadcast_to(docs, (DOC_ROWS, LANES)).astype(jnp.bfloat16)
+
+
+def finish_inner(own, first, second, doc_rows, width):
     return pl.pallas_call(
         finish_inner_kernel,
-        in_specs=[VMEM] * 3,
-        out_shape=jax.ShapeDtypeStruct((width, own.shape[1]), jnp.bfloat16),
+        in_specs=[VMEM] * 4,
+        out_shape=jax.ShapeDtypeStruct((width + DOC_ROWS, own.shape[1]), jnp.bfloat16),
         compiler_params=pltpu.CompilerParams(vmem_limit_bytes=40 * MIB),
         cost_estimate=cost(0.5),
-    )(own, near, far)
-
-
-def expand_kernel(shared_ref, weights_ref, docs_ref, *, width, experts, shares, turns):
+    )(own, first, second, doc_rows)
+
+
+def expand_kernel(shared_ref, weights_ref, *, width, experts, shares, turns):
     columns = experts * width
     share_rows = width // shares
     half = experts // 2
@@ -218,14 +216,11 @@
         own = expert_lane == expert_row + side * half
         for entry, turn in enumerate(turns):
             placed = jnp.dot(
-                shared_ref[entry, : half * width, :], spread, preferred_element_type=jnp.float32
+                shared_ref[entry], spread, preferred_element_type=jnp.float32
             )
             weights_ref[turn, side * half * width : (side + 1) * half * width, :] = jnp.where(
                 own, placed, 0.0
             ).astype(jnp.bfloat16)
-    for entry, turn in enumerate(turns):
-        owner = jnp.bitwise_xor(lax.axis_index("expert"), turn)
-        docs_ref[owner] = shared_ref[entry, half * width :, :].astype(jnp.float32).astype(jnp.int32)
 
 
 def expand(shared, turns, width, experts, shares):
@@ -233,10 +228,7 @@
     return pl.pallas_call(
         functools.partial(expand_kernel, width=width, experts=experts, shares=shares, turns=turns),
         in_specs=[VMEM],
-        out_shape=[
-            jax.ShapeDtypeStruct((owners, experts * width, experts * width), jnp.bfloat16),
-            jax.ShapeDtypeStruct((owners, DOC_ROWS, LANES), jnp.int32),
-        ],
+        out_shape=jax.ShapeDtypeStruct((owners, experts * width, experts * width), jnp.bfloat16),
         compiler_params=pltpu.CompilerParams(vmem_limit_bytes=40 * MIB),
         cost_estimate=cost(1.3),
     )(shared)
@@ -372,7 +364,7 @@
 
 
 def score_kernel(
-    arrived_ref, inner_ref, docs_ref, far_ref, out_ref, grads_ref, queries_ref, sem, *, width, doc_count, turns
+    arrived_ref, inner_ref, far_ref, out_ref, grads_ref, queries_ref, sem, *, width, doc_count, turns
 ):
     fetch = pltpu.make_async_copy(far_ref, queries_ref, sem)
     fetch.start()
@@ -384,8 +376,8 @@
         owner = jnp.bitwise_xor(lax.axis_index("expert"), owner_turn)
         share = jnp.bitwise_xor(lax.axis_index("proj"), share_turn)
         outer.append(arrived_ref[owner * shares + share])
-        docs.append(docs_ref[owner, pl.ds(share, 1), :])
-        inner.append(inner_ref[entry])
+        docs.append(inner_ref[entry, width : width + 1, :].astype(jnp.float32).astype(jnp.int32))
+        inner.append(inner_ref[entry, :width, :])
     outer = jnp.concatenate(outer, axis=0)
     inner = jnp.concatenate(inner, axis=1)
     docs = jnp.broadcast_to(jnp.concatenate(docs, axis=1), inner.shape)
@@ -420,13 +412,13 @@
             out_ref[owner * shares + share] = jnp.concatenate([piece, fill], axis=1)
 
 
-def score(arrived, inner, docs, queries, turns):
+def score(arrived, inner, queries, turns, owners):
     sources = arrived.shape[0]
-    width = inner.shape[1]
-    doc_count = DOC_DEV * docs.shape[0]
+    width = inner.shape[1] - DOC_ROWS
+    doc_count = DOC_DEV * owners
     return pl.pallas_call(
         functools.partial(score_kernel, width=width, doc_count=doc_count, turns=turns),
-        in_specs=[VMEM, VMEM, VMEM, HBM],
+        in_specs=[VMEM, VMEM, HBM],
         out_shape=jax.ShapeDtypeStruct((sources, DOC_DEV, LANES), jnp.float32),
         scratch_shapes=[
             pltpu.VMEM((doc_count * (width + 8), arrived.shape[2]), jnp.float32),
@@ -435,7 +427,7 @@
         ],
         compiler_params=pltpu.CompilerParams(vmem_limit_bytes=40 * MIB),
         cost_estimate=cost(5),
-    )(arrived, inner, docs, stay(queries))
+    )(arrived, inner, stay(queries))
 
 
 def sum_kernel(pieces_ref, out_ref):
@@ -484,9 +476,7 @@
     assert DOC_DEV * owners <= 256
 
     flat_hidden = grad_hidden.reshape(tokens * top, grad_hidden.shape[2])
-    inner_leaving, inner_own, shared = project_inner(
-        activations, in_projection, inverse_out, doc_ids.reshape(shares, quarter), shares
-    )
+    inner_leaving, inner_own, shared = project_inner(activations, in_projection, inverse_out, shares)
     inner_first = exchange(inner_leaving, "proj", shares, 2)
     far_shared = exchange(shared, "expert", owners, owners // 2)
     leaving, own = project_outer(flat_hidden, out_projection, shares, top)
@@ -498,11 +488,11 @@
     inner_second = exchange(combine(combine_inner_kernel, inner_own, inner_first), "proj", shares, 1)
     sent = combine(combine_outer_kernel, own, near)
     far = exchange(sent, "proj", shares, 2)
-    inner = finish_inner(inner_own, inner_first, inner_second, width)
+    inner = finish_inner(inner_own, inner_first, inner_second, doc_ids.reshape(shares, quarter), width)
     inner, _ = lax.optimization_barrier((inner, sent))
     owner_turns = tuple(reversed(range(owners)))
     arriving = [exchange(inner, "expert", owners, turn) for turn in owner_turns if turn]
-    weights, all_docs = expand(shared, turns, width, experts, shares)
+    weights = expand(shared, turns, width, experts, shares)
     far, weights = lax.optimization_barrier((far, weights))
     quarter_routes = lax.dynamic_slice_in_dim(routes, lax.axis_index("proj") * quarter, quarter, 0)
     payload = condition(own, near, far, quarter_routes, weights, shares, width)
@@ -513,10 +503,10 @@
     inner, share_turns = double(inner, share_turns, "proj", shares, 1)
     inner, query_grads = lax.optimization_barrier((inner, query_grads))
     inner, share_turns = double(inner, share_turns, "proj", shares, 2)
-    inner = inner.reshape(owners * shares, width, quarter)
+    inner = inner.reshape(owners * shares, width + DOC_ROWS, quarter)
     all_turns = tuple((o, p) for p in share_turns for o in owner_turns)
     queries = condition_queries(query_grads, inverse_in)
-    pieces = score(arrived, inner, all_docs, queries, all_turns)
+    pieces = score(arrived, inner, queries, all_turns, owners)
     pieces = lax.all_to_all(pieces, ("expert", "proj"), 0, 0, tiled=True)
     return sum_pieces(pieces, query_grads.shape[0] // shares).T
 

time: 60.6 us -> 60.5 us (level)
  no operation moved by 1% of the time
where the time goes in v12:
time: 60.5 us; the launch traced here: 60 us
  Pallas kernels  26 us (43%)
  starting transfers between devices  19.3 us (32%)
  blocking collectives  10.8 us (18%)
  waiting for transfers between devices  3.6 us (6%)
    ppermute x11, starting transfers between devices, exchange(): return lax.ppermute(block, axis, [(i, i ^ turn) for i in range(size)])  15 us
    all_to_all x1, blocking collectives, local(): pieces = lax.all_to_all(pieces, ('expert', 'proj'), 0, 0, tiled=True)  10.8 us
    pallas_call x1, Pallas kernels, condition_queries(): pl.pallas_call(query_kernel, grid=(flat // LANES,), in_specs=[pl.BlockSpe...  9.53 us
    pallas_call x1, Pallas kernels, score(): pl.pallas_call(functools.partial(score_kernel, width=width, doc_count=doc...  6.1 us
    pallas_call x1, Pallas kernels, project_outer(): pl.pallas_call(functools.partial(outer_kernel, top=top), in_specs=[HBM] *...  4.33 us
    all_to_all x1, starting transfers between devices, local(): arrived = lax.all_to_all(payload, ('expert', 'proj'), 0, 0, tiled=True)  4.23 us
    pallas_call x1, Pallas kernels, project_inner(): pl.pallas_call(inner_kernel, in_specs=[HBM] * 3, out_specs=[VMEM] * 3, ou...  2.78 us
    ppermute x11, waiting for transfers between devices, exchange(): return lax.ppermute(block, axis, [(i, i ^ turn) for i in range(size)])  2.09 us
  transfers between devices with their start and end apart: 12, of which 4 were waited for; matrix products, arithmetic and copies ran while one was open for 0% of the time, Pallas kernels for 27%

profile of v12, /device:TPU:0, one launch (start us, length us, event | category | flops | bytes accessed | tf_op | source)
XLA Modules:
  0.0 60.0 jit_solution(6499466893608512811)
XLA Ops:
  0.0 0.0 copy-start
  0.0 0.0 copy-start.2
  0.0 2.8 %shard_map.92 = (bf16[2,128,128]{2,1,0:T(8,128)(2,1)S(1)}, bf16[2,128,128]{2,1,0:T(8,128)(2,1)S(1)}, bf16[256,128]{1,0:T(8,128)(2,1)S(1)}) custom-call(bf16[512,1792]{1,0:T(8,128)(2,1)} %act_hbm.1, bf16[64,1792]{1,0:T(8,128)(2,1)} %in_proj_hbm.1, f32[8,64,64]{2,1,0:T(8,128)} %inverse_hbm.1), custom_call_target="tpu_custom_call" | custom-call | bytes 8250000 | tf_op jit(solution)/shard_map/pallas_call | solution.py:92
  2.8 3.0 %collective-permute-start.1 = (bf16[2,128,128]{2,1,0:T(8,128)(2,1)S(1)}, bf16[2,128,128]{2,1,0:T(8,128)(2,1)S(1)}, u32[]{:S(2)}, u32[]{:S(2)}) collective-permute-start(bf16[2,128,128]{2,1,0:T(8,128)(2,1)S(1)} %get-tuple-element.24), channel_id=1, source_target_pairs={{0,2},{1,3},{2,0},{3,1},{4,6},{5,7},{6,4},{7,5},{8,10},{9,11},{10,... | collective-permute-start | bytes 196616 | tf_op jit(solution)/shard_map/ppermute | solution.py:450
  5.8 2.6 %collective-permute-start = (bf16[256,128]{1,0:T(8,128)(2,1)S(1)}, bf16[256,128]{1,0:T(8,128)(2,1)S(1)}, u32[]{:S(2)}, u32[]{:S(2)}) collective-permute-start(bf16[256,128]{1,0:T(8,128)(2,1)S(1)} %get-tuple-element.23), channel_id=1, source_target_pairs={{0,8},{4,12},{8,0},{12,4},{1,9},{5,13},{9,1},{13,5},{2,10},{6,14},... | collective-permute-start | bytes 196616 | tf_op jit(solution)/shard_map/ppermute | solution.py:450
  8.4 4.3 %shard_map.91 = (bf16[2,512,128]{2,1,0:T(8,128)(2,1)S(1)}, bf16[2,512,128]{2,1,0:T(8,128)(2,1)S(1)}) custom-call(bf16[4096,512]{1,0:T(8,128)(2,1)} %bitcast.17, bf16[64,512]{1,0:T(8,128)(2,1)} %out_proj_hbm.1), custom_call_target="tpu_custom_call" | custom-call | bytes 13200000 | tf_op jit(solution)/shard_map/pallas_call | solution.py:145
  12.7 0.0 collective-permute-done.1.near_ref.first_ref
  12.7 0.0 collective-permute-done
  12.8 0.1 collective-permute-start.2
  12.9 1.6 %collective-permute-start.4 = (bf16[2,256,128]{2,1,0:T(8,128)(2,1)S(1)}, bf16[2,256,128]{2,1,0:T(8,128)(2,1)S(1)}, u32[]{:S(2)}, u32[]{:S(2)}) collective-permute-start(bf16[2,256,128]{2,1,0:T(8,128)(2,1)S(1)} %pad_maximum_fusion.3), channel_id=1, source_target_pairs={{0,4},{4,0},{8,12},{12,8},{1,5},{5,1},{9,13},{13,9},{2,6},{6,2},{1... | collective-permute-start | bytes 393224 | tf_op jit(solution)/shard_map/ppermute | solution.py:450
  14.5 0.3 collective-permute-start.5
  14.8 0.0 collective-permute-done.2.near_ref
  14.8 0.0 copy-start.1
  14.8 0.6 %collective-permute-start.3 = (bf16[512,128]{1,0:T(8,128)(2,1)S(1)}, bf16[512,128]{1,0:T(8,128)(2,1)S(1)}, u32[]{:S(2)}, u32[]{:S(2)}) collective-permute-start(bf16[512,128]{1,0:T(8,128)(2,1)S(1)} %shard_map.93), channel_id=1, source_target_pairs={{0,2},{1,3},{2,0},{3,1},{4,6},{5,7},{6,4},{7,5},{8,10},{9,11},{10,... | collective-permute-start | bytes 393224 | tf_op jit(solution)/shard_map/ppermute | solution.py:450
  15.4 0.0 copy-done
  15.4 0.1 copy.11.routes_ref
  15.5 0.2 collective-permute-done.5.second_ref
  15.8 0.0 copy-done.2
  15.8 0.1 shard_map.97
  15.9 1.0 %collective-permute-start.8 = (bf16[80,128]{1,0:T(8,128)(2,1)S(1)}, bf16[80,128]{1,0:T(8,128)(2,1)S(1)}, u32[]{:S(2)}, u32[]{:S(2)}) collective-permute-start(bf16[80,128]{1,0:T(8,128)(2,1)S(1)} %shard_map.97), channel_id=1, source_target_pairs={{0,4},{4,0},{8,12},{12,8},{1,5},{5,1},{9,13},{13,9},{2,6},{6,2},{1... | collective-permute-start | bytes 61448 | tf_op jit(solution)/shard_map/ppermute | solution.py:450
  16.9 1.3 %collective-permute-start.7 = (bf16[80,128]{1,0:T(8,128)(2,1)S(1)}, bf16[80,128]{1,0:T(8,128)(2,1)S(1)}, u32[]{:S(2)}, u32[]{:S(2)}) collective-permute-start(bf16[80,128]{1,0:T(8,128)(2,1)S(1)} %shard_map.97), channel_id=1, source_target_pairs={{0,8},{4,12},{8,0},{12,4},{1,9},{5,13},{9,1},{13,5},{2,10},{6,14},... | collective-permute-start | bytes 61448 | tf_op jit(solution)/shard_map/ppermute | solution.py:450
  18.2 2.2 %collective-permute-start.6 = (bf16[80,128]{1,0:T(8,128)(2,1)S(1)}, bf16[80,128]{1,0:T(8,128)(2,1)S(1)}, u32[]{:S(2)}, u32[]{:S(2)}) collective-permute-start(bf16[80,128]{1,0:T(8,128)(2,1)S(1)} %shard_map.97), channel_id=1, source_target_pairs={{0,12},{4,8},{8,4},{12,0},{1,13},{5,9},{9,5},{13,1},{2,14},{6,10},... | collective-permute-start | bytes 61448 | tf_op jit(solution)/shard_map/ppermute | solution.py:450
  20.4 0.0 collective-permute-done.4
  20.4 0.7 %shard_map.94.weights_ref = bf16[4,512,512]{2,1,0:T(8,128)(2,1)S(1)} custom-call(bf16[4,256,128]{2,1,0:T(8,128)(2,1)S(1)} %pad_maximum_fusion.1.shared_ref), custom_call_target="tpu_custom_call" | custom-call | bytes 4290000 | tf_op jit(solution)/shard_map/pallas_call | solution.py:228
  21.1 0.0 collective-permute-done.3.far_ref
  21.1 1.7 %shard_map.95 = bf16[16,128,128]{2,1,0:T(8,128)(2,1)} custom-call(bf16[2,512,128]{2,1,0:T(8,128)(2,1)S(1)} %get-tuple-element.22.own_ref, bf16[2,512,128]{2,1,0:T(8,128)(2,1)S(1)} %collective-permute-done.2.near_ref, bf16[512,128]{1,0:T(8,128)(2,1)S(1)} %collective-permute-done.3.far_ref, s32[128,8]{1,0:T(8,128)S(1)} %copy.11.routes_ref, ...), custom_call_target="tpu_custom_call" | custom-call | bytes 6600000 | tf_op jit(solution)/shard_map/pallas_call | solution.py:282
  22.9 0.0 collective-permute-done.8
  22.9 0.0 collective-permute-done.7
  22.9 0.9 %collective-permute-done.6 = bf16[80,128]{1,0:T(8,128)(2,1)S(1)} collective-permute-done((bf16[80,128]{1,0:T(8,128)(2,1)S(1)}, bf16[80,128]{1,0:T(8,128)(2,1)S(1)}, u32[]{:S(2)}, u32[]{:S(2)}) %collective-permute-start.6) | collective-permute-done | bytes 20512 | tf_op jit(solution)/shard_map/ppermute | solution.py:450
  23.8 4.2 %all-to-all-start = ((bf16[16,128,128]{2,1,0:T(8,128)(2,1)}), bf16[16,128,128]{2,1,0:T(8,128)(2,1)S(1)}, u32[]{:S(2)}, u32[]{:S(2)}) async-start(bf16[16,128,128]{2,1,0:T(8,128)(2,1)} %shard_map.95), calls=%async_computation | async-start | bytes 1048576 | tf_op jit(solution)/shard_map/all_to_all | solution.py:500
  28.0 0.5 collective-permute-start.9
  28.5 0.9 %collective-permute-done.9 = bf16[1,4,80,128]{3,2,1,0:T(8,128)(2,1)S(1)} collective-permute-done((bf16[1,4,80,128]{3,2,1,0:T(8,128)(2,1)S(1)}, bf16[1,4,80,128]{3,2,1,0:T(8,128)(2,1)S(1)}, u32[]{:S(2)}, u32[]{:S(2)}) %collective-permute-start.9) | collective-permute-done | bytes 81952 | tf_op jit(solution)/shard_map/ppermute | solution.py:450
  29.5 1.9 %collective-permute-start.10 = (bf16[2,4,80,128]{3,2,1,0:T(8,128)(2,1)S(1)}, bf16[2,4,80,128]{3,2,1,0:T(8,128)(2,1)S(1)}, u32[]{:S(2)}, u32[]{:S(2)}) collective-permute-start(bf16[2,4,80,128]{3,2,1,0:T(8,128)(2,1)S(1)} %pad_maximum_fusion.2), channel_id=1, source_target_pairs={{0,2},{1,3},{2,0},{3,1},{4,6},{5,7},{6,4},{7,5},{8,10},{9,11},{10,... | collective-permute-start | bytes 491528 | tf_op jit(solution)/shard_map/ppermute | solution.py:450
  31.4 0.0 copy-done.1
  31.4 9.5 %shard_map.98.far_ref = bf16[8192,256]{1,0:T(8,128)(2,1)} custom-call(bf16[256,8,1024]{2,1,0:T(8,128)(2,1)} %query_ref, f32[8,64,64]{2,1,0:T(8,128)S(1)} %copy-done.1), custom_call_target="tpu_custom_call" | custom-call | bytes 33000000 | tf_op jit(solution)/shard_map/pallas_call | solution.py:345
  40.9 0.0 collective-permute-done.10
  41.0 1.5 %all-to-all-done.arrived_ref = bf16[16,128,128]{2,1,0:T(8,128)(2,1)S(1)} async-done(((bf16[16,128,128]{2,1,0:T(8,128)(2,1)}), bf16[16,128,128]{2,1,0:T(8,128)(2,1)S(1)}, u32[]{:S(2)}, u32[]{:S(2)}) %all-to-all-start) | async-done | bytes 524320 | tf_op jit(solution)/shard_map/all_to_all | solution.py:500
  42.5 6.1 %shard_map.99 = f32[16,8,128]{2,1,0:T(8,128)S(1)} custom-call(bf16[16,128,128]{2,1,0:T(8,128)(2,1)S(1)} %all-to-all-done.arrived_ref, bf16[16,80,128]{2,1,0:T(8,128)(2,1)S(1)} %bitcast.12, bf16[8192,256]{1,0:T(8,128)(2,1)} %shard_map.98.far_ref), custom_call_target="tpu_custom_call" | custom-call | bytes 16500000 | tf_op jit(solution)/shard_map/pallas_call | solution.py:419
  48.6 10.8 %all_to_all.10.pieces_ref = f32[16,8,128]{2,1,0:T(8,128)S(1)} all-to-all(f32[16,8,128]{2,1,0:T(8,128)S(1)} %shard_map.99), channel_id=1, replica_groups=mesh['groups'=2,'expert'=4,'proj'=4] {'expert','proj'}, dimensions={0} | all-to-all | bytes 131072 | tf_op jit(solution)/shard_map/all_to_all | solution.py:510
  59.4 0.6 %shard_map.100 = f32[8,64]{1,0:T(8,128)} custom-call(f32[16,8,128]{2,1,0:T(8,128)S(1)} %all_to_all.10.pieces_ref), custom_call_target="tpu_custom_call" | custom-call | tf_op jit(solution)/shard_map/pallas_call | solution.py:441
  (8 shorter events, 0.2 us)
Async XLA Ops:
  0.0 15.4 %copy-start = (s32[512,8]{0,1:T(8,128)S(1)}, s32[512,8]{0,1:T(8,128)}, u32[]{:S(2)}) copy-start(s32[512,8]{0,1:T(8,128)} %param.11) | copy-start | bytes 49156
  0.0 15.8 %copy-start.2 = (s32[512]{0:T(512)S(1)}, s32[512]{0:T(512)}, u32[]{:S(2)}) copy-start(s32[512]{0:T(512)} %param.12) | copy-start | bytes 6148
  2.8 9.9 %collective-permute-start.1 = (bf16[2,128,128]{2,1,0:T(8,128)(2,1)S(1)}, bf16[2,128,128]{2,1,0:T(8,128)(2,1)S(1)}, u32[]{:S(2)}, u32[]{:S(2)}) collective-permute-start(bf16[2,128,128]{2,1,0:T(8,128)(2,1)S(1)} %get-tuple-element.24), channel_id=1, source_target_pairs={{0,2},{1,3},{2,0},{3,1},{4,6},{5,7},{6,4},{7,5},{8,10},{9,11},{10,... | collective-permute-start | bytes 196616 | tf_op jit(solution)/shard_map/ppermute | solution.py:450
  5.8 6.9 %collective-permute-start = (bf16[256,128]{1,0:T(8,128)(2,1)S(1)}, bf16[256,128]{1,0:T(8,128)(2,1)S(1)}, u32[]{:S(2)}, u32[]{:S(2)}) collective-permute-start(bf16[256,128]{1,0:T(8,128)(2,1)S(1)} %get-tuple-element.23), channel_id=1, source_target_pairs={{0,8},{4,12},{8,0},{12,4},{1,9},{5,13},{9,1},{13,5},{2,10},{6,14},... | collective-permute-start | bytes 196616 | tf_op jit(solution)/shard_map/ppermute | solution.py:450
  12.8 2.0 %collective-permute-start.2 = (bf16[2,512,128]{2,1,0:T(8,128)(2,1)S(1)}, bf16[2,512,128]{2,1,0:T(8,128)(2,1)S(1)}, u32[]{:S(2)}, u32[]{:S(2)}) collective-permute-start(bf16[2,512,128]{2,1,0:T(8,128)(2,1)S(1)} %get-tuple-element.26), channel_id=1, source_target_pairs={{0,1},{1,0},{2,3},{3,2},{4,5},{5,4},{6,7},{7,6},{8,9},{9,8},{10,11... | collective-permute-start | bytes 786440 | tf_op jit(solution)/shard_map/ppermute | solution.py:450
  12.9 7.5 %collective-permute-start.4 = (bf16[2,256,128]{2,1,0:T(8,128)(2,1)S(1)}, bf16[2,256,128]{2,1,0:T(8,128)(2,1)S(1)}, u32[]{:S(2)}, u32[]{:S(2)}) collective-permute-start(bf16[2,256,128]{2,1,0:T(8,128)(2,1)S(1)} %pad_maximum_fusion.3), channel_id=1, source_target_pairs={{0,4},{4,0},{8,12},{12,8},{1,5},{5,1},{9,13},{13,9},{2,6},{6,2},{1... | collective-permute-start | bytes 393224 | tf_op jit(solution)/shard_map/ppermute | solution.py:450
  14.5 1.3 %collective-permute-start.5 = (bf16[128,128]{1,0:T(8,128)(2,1)S(1)}, bf16[128,128]{1,0:T(8,128)(2,1)S(1)}, u32[]{:S(2)}, u32[]{:S(2)}) collective-permute-start(bf16[128,128]{1,0:T(8,128)(2,1)S(1)} %shard_map.96), channel_id=1, source_target_pairs={{0,1},{1,0},{2,3},{3,2},{4,5},{5,4},{6,7},{7,6},{8,9},{9,8},{10,11... | collective-permute-start | bytes 98312 | tf_op jit(solution)/shard_map/ppermute | solution.py:450
  14.8 16.6 %copy-start.1 = (f32[8,64,64]{2,1,0:T(8,128)S(1)}, f32[8,64,64]{2,1,0:T(8,128)}, u32[]{:S(2)}) copy-start(f32[8,64,64]{2,1,0:T(8,128)} %inverse_ref.1) | copy-start | bytes 393220
  14.8 6.3 %collective-permute-start.3 = (bf16[512,128]{1,0:T(8,128)(2,1)S(1)}, bf16[512,128]{1,0:T(8,128)(2,1)S(1)}, u32[]{:S(2)}, u32[]{:S(2)}) collective-permute-start(bf16[512,128]{1,0:T(8,128)(2,1)S(1)} %shard_map.93), channel_id=1, source_target_pairs={{0,2},{1,3},{2,0},{3,1},{4,6},{5,7},{6,4},{7,5},{8,10},{9,11},{10,... | collective-permute-start | bytes 393224 | tf_op jit(solution)/shard_map/ppermute | solution.py:450
  15.9 7.0 %collective-permute-start.8 = (bf16[80,128]{1,0:T(8,128)(2,1)S(1)}, bf16[80,128]{1,0:T(8,128)(2,1)S(1)}, u32[]{:S(2)}, u32[]{:S(2)}) collective-permute-start(bf16[80,128]{1,0:T(8,128)(2,1)S(1)} %shard_map.97), channel_id=1, source_target_pairs={{0,4},{4,0},{8,12},{12,8},{1,5},{5,1},{9,13},{13,9},{2,6},{6,2},{1... | collective-permute-start | bytes 61448 | tf_op jit(solution)/shard_map/ppermute | solution.py:450
  16.9 6.0 %collective-permute-start.7 = (bf16[80,128]{1,0:T(8,128)(2,1)S(1)}, bf16[80,128]{1,0:T(8,128)(2,1)S(1)}, u32[]{:S(2)}, u32[]{:S(2)}) collective-permute-start(bf16[80,128]{1,0:T(8,128)(2,1)S(1)} %shard_map.97), channel_id=1, source_target_pairs={{0,8},{4,12},{8,0},{12,4},{1,9},{5,13},{9,1},{13,5},{2,10},{6,14},... | collective-permute-start | bytes 61448 | tf_op jit(solution)/shard_map/ppermute | solution.py:450
  18.2 5.6 %collective-permute-start.6 = (bf16[80,128]{1,0:T(8,128)(2,1)S(1)}, bf16[80,128]{1,0:T(8,128)(2,1)S(1)}, u32[]{:S(2)}, u32[]{:S(2)}) collective-permute-start(bf16[80,128]{1,0:T(8,128)(2,1)S(1)} %shard_map.97), channel_id=1, source_target_pairs={{0,12},{4,8},{8,4},{12,0},{1,13},{5,9},{9,5},{13,1},{2,14},{6,10},... | collective-permute-start | bytes 61448 | tf_op jit(solution)/shard_map/ppermute | solution.py:450
  23.8 18.7 %all-to-all-start = ((bf16[16,128,128]{2,1,0:T(8,128)(2,1)}), bf16[16,128,128]{2,1,0:T(8,128)(2,1)S(1)}, u32[]{:S(2)}, u32[]{:S(2)}) async-start(bf16[16,128,128]{2,1,0:T(8,128)(2,1)} %shard_map.95), calls=%async_computation | async-start | bytes 1048576 | tf_op jit(solution)/shard_map/all_to_all | solution.py:500
  28.0 1.4 %collective-permute-start.9 = (bf16[1,4,80,128]{3,2,1,0:T(8,128)(2,1)S(1)}, bf16[1,4,80,128]{3,2,1,0:T(8,128)(2,1)S(1)}, u32[]{:S(2)}, u32[]{:S(2)}) collective-permute-start(bf16[1,4,80,128]{3,2,1,0:T(8,128)(2,1)S(1)} %maximum_bitcast_fusion), channel_id=1, source_target_pairs={{0,1},{1,0},{2,3},{3,2},{4,5},{5,4},{6,7},{7,6},{8,9},{9,8},{10,11... | collective-permute-start | bytes 245768 | tf_op jit(solution)/shard_map/ppermute | solution.py:450
  29.5 11.5 %collective-permute-start.10 = (bf16[2,4,80,128]{3,2,1,0:T(8,128)(2,1)S(1)}, bf16[2,4,80,128]{3,2,1,0:T(8,128)(2,1)S(1)}, u32[]{:S(2)}, u32[]{:S(2)}) collective-permute-start(bf16[2,4,80,128]{3,2,1,0:T(8,128)(2,1)S(1)} %pad_maximum_fusion.2), channel_id=1, source_target_pairs={{0,2},{1,3},{2,0},{3,1},{4,6},{5,7},{6,4},{7,5},{8,10},{9,11},{10,... | collective-permute-start | bytes 491528 | tf_op jit(solution)/shard_map/ppermute | solution.py:450

commit v13 on v12

--- a/solution.py
+++ b/solution.py
@@ -21,6 +21,15 @@
 
 def stay(array):
     return pltpu.with_memory_space_constraint(array, pltpu.HBM)
+
+
+def listed(owner, owners):
+    return (owner + owners // 2) % owners
+
+
+def send_to_all(blocks, owners, shares):
+    members = [(i + owners // 2 * shares) % (owners * shares) for i in range(owners * shares)]
+    return lax.all_to_all(blocks, ("expert", "proj"), 0, 0, tiled=True, axis_index_groups=[members])
 
 
 def split(value):
@@ -270,7 +279,7 @@
         ).astype(jnp.bfloat16)
         share_width = result.shape[1] // shares
         for share in range(shares):
-            payload_ref[group * shares + share] = result[:, share * share_width : (share + 1) * share_width]
+            payload_ref[listed(group, groups) * shares + share] = result[:, share * share_width : (share + 1) * share_width]
         return carry
 
     lax.fori_loop(0, groups, one_group, 0, unroll=groups <= 4)
@@ -375,7 +384,7 @@
     for entry, (owner_turn, share_turn) in enumerate(turns):
         owner = jnp.bitwise_xor(lax.axis_index("expert"), owner_turn)
         share = jnp.bitwise_xor(lax.axis_index("proj"), share_turn)
-        outer.append(arrived_ref[owner * shares + share])
+        outer.append(arrived_ref[listed(owner, owners) * shares + share])
         docs.append(inner_ref[entry, width : width + 1, :].astype(jnp.float32).astype(jnp.int32))
         inner.append(inner_ref[entry, :width, :])
     outer = jnp.concatenate(outer, axis=0)
@@ -409,7 +418,7 @@
     for owner in range(owners):
         for share in range(shares):
             piece = result[owner * DOC_DEV : (owner + 1) * DOC_DEV, share * columns : (share + 1) * columns]
-            out_ref[owner * shares + share] = jnp.concatenate([piece, fill], axis=1)
+            out_ref[listed(owner, owners) * shares + share] = jnp.concatenate([piece, fill], axis=1)
 
 
 def score(arrived, inner, queries, turns, owners):
@@ -497,7 +506,7 @@
     quarter_routes = lax.dynamic_slice_in_dim(routes, lax.axis_index("proj") * quarter, quarter, 0)
     payload = condition(own, near, far, quarter_routes, weights, shares, width)
     payload, arriving = lax.optimization_barrier((payload, arriving))
-    arrived = lax.all_to_all(payload, ("expert", "proj"), 0, 0, tiled=True)
+    arrived = send_to_all(payload, owners, shares)
     inner = jnp.stack(arriving + [inner])
     inner, share_turns = inner[None], (0,)
     inner, share_turns = double(inner, share_turns, "proj", shares, 1)
@@ -507,7 +516,7 @@
     all_turns = tuple((o, p) for p in share_turns for o in owner_turns)
     queries = condition_queries(query_grads, inverse_in)
     pieces = score(arrived, inner, queries, all_turns, owners)
-    pieces = lax.all_to_all(pieces, ("expert", "proj"), 0, 0, tiled=True)
+    pieces = send_to_all(pieces, owners, shares)
     return sum_pieces(pieces, query_grads.shape[0] // shares).T
 
 

time: 60.5 us -> 58.5 us (0.967)
  waiting for transfers between devices: 3.6 us -> 2.3 us
  blocking collectives: 10.8 us -> 9.91 us
    all_to_all x1, waiting for transfers between devices: 1.51 us -> 0.01 us  [send_to_all(): lax.all_to_all(blocks, ('expert', 'proj'), 0, 0, tiled=True, axis_index_g...]
    all_to_all x1, starting transfers between devices: 4.23 us -> 5.14 us  [send_to_all(): lax.all_to_all(blocks, ('expert', 'proj'), 0, 0, tiled=True, axis_index_g...]
    all_to_all x1, blocking collectives: 10.8 us -> 9.91 us  [send_to_all(): lax.all_to_all(blocks, ('expert', 'proj'), 0, 0, tiled=True, axis_index_g...]
    ppermute x11, starting transfers between devices: 15 us -> 14.4 us  [exchange(): return lax.ppermute(block, axis, [(i, i ^ turn) for i in range(size)])]
  transfers between devices with their start and end apart: 12 -> 12, of which waited for: 4 -> 3; matrix products, arithmetic and copies ran while one was open for 0% -> 0% of each run, Pallas kernels for 27% -> 28%
where the time goes in v13:
time: 58.5 us; the launch traced here: 58.1 us
  Pallas kernels  26 us (44%)
  starting transfers between devices  19.5 us (33%)
  blocking collectives  9.91 us (17%)
  waiting for transfers between devices  2.3 us (4%)
    ppermute x11, starting transfers between devices, exchange(): return lax.ppermute(block, axis, [(i, i ^ turn) for i in range(size)])  14.4 us
    all_to_all x1, blocking collectives, send_to_all(): lax.all_to_all(blocks, ('expert', 'proj'), 0, 0, tiled=True, axis_index_g...  9.91 us
    pallas_call x1, Pallas kernels, condition_queries(): pl.pallas_call(query_kernel, grid=(flat // LANES,), in_specs=[pl.BlockSpe...  9.53 us
    pallas_call x1, Pallas kernels, score(): pl.pallas_call(functools.partial(score_kernel, width=width, doc_count=doc...  6.11 us
    all_to_all x1, starting transfers between devices, send_to_all(): lax.all_to_all(blocks, ('expert', 'proj'), 0, 0, tiled=True, axis_index_g...  5.14 us
    pallas_call x1, Pallas kernels, project_outer(): pl.pallas_call(functools.partial(outer_kernel, top=top), in_specs=[HBM] *...  4.33 us
    pallas_call x1, Pallas kernels, project_inner(): pl.pallas_call(inner_kernel, in_specs=[HBM] * 3, out_specs=[VMEM] * 3, ou...  2.78 us
    ppermute x11, waiting for transfers between devices, exchange(): return lax.ppermute(block, axis, [(i, i ^ turn) for i in range(size)])  2.3 us
  transfers between devices with their start and end apart: 12, of which 3 were waited for; matrix products, arithmetic and copies ran while one was open for 0% of the time, Pallas kernels for 28%

profile of v13, /device:TPU:0, one launch (start us, length us, event | category | flops | bytes accessed | tf_op | source)
XLA Modules:
  0.0 58.1 jit_solution(14990728843722480768)
XLA Ops:
  0.0 0.0 copy-start
  0.0 0.0 copy-start.2
  0.0 2.8 %shard_map.92 = (bf16[2,128,128]{2,1,0:T(8,128)(2,1)S(1)}, bf16[2,128,128]{2,1,0:T(8,128)(2,1)S(1)}, bf16[256,128]{1,0:T(8,128)(2,1)S(1)}) custom-call(bf16[512,1792]{1,0:T(8,128)(2,1)} %act_hbm.1, bf16[64,1792]{1,0:T(8,128)(2,1)} %in_proj_hbm.1, f32[8,64,64]{2,1,0:T(8,128)} %inverse_hbm.1), custom_call_target="tpu_custom_call" | custom-call | bytes 8250000 | tf_op jit(solution)/shard_map/pallas_call | solution.py:101
  2.8 3.0 %collective-permute-start.1 = (bf16[2,128,128]{2,1,0:T(8,128)(2,1)S(1)}, bf16[2,128,128]{2,1,0:T(8,128)(2,1)S(1)}, u32[]{:S(2)}, u32[]{:S(2)}) collective-permute-start(bf16[2,128,128]{2,1,0:T(8,128)(2,1)S(1)} %get-tuple-element.24), channel_id=1, source_target_pairs={{0,2},{1,3},{2,0},{3,1},{4,6},{5,7},{6,4},{7,5},{8,10},{9,11},{10,... | collective-permute-start | bytes 196616 | tf_op jit(solution)/shard_map/ppermute | solution.py:459
  5.8 2.6 %collective-permute-start = (bf16[256,128]{1,0:T(8,128)(2,1)S(1)}, bf16[256,128]{1,0:T(8,128)(2,1)S(1)}, u32[]{:S(2)}, u32[]{:S(2)}) collective-permute-start(bf16[256,128]{1,0:T(8,128)(2,1)S(1)} %get-tuple-element.23), channel_id=1, source_target_pairs={{0,8},{4,12},{8,0},{12,4},{1,9},{5,13},{9,1},{13,5},{2,10},{6,14},... | collective-permute-start | bytes 196616 | tf_op jit(solution)/shard_map/ppermute | solution.py:459
  8.4 4.3 %shard_map.91 = (bf16[2,512,128]{2,1,0:T(8,128)(2,1)S(1)}, bf16[2,512,128]{2,1,0:T(8,128)(2,1)S(1)}) custom-call(bf16[4096,512]{1,0:T(8,128)(2,1)} %bitcast.17, bf16[64,512]{1,0:T(8,128)(2,1)} %out_proj_hbm.1), custom_call_target="tpu_custom_call" | custom-call | bytes 13200000 | tf_op jit(solution)/shard_map/pallas_call | solution.py:154
  12.7 0.0 collective-permute-done.1.near_ref.first_ref
  12.7 0.0 collective-permute-done
  12.8 0.1 collective-permute-start.2
  12.9 1.6 %collective-permute-start.4 = (bf16[2,256,128]{2,1,0:T(8,128)(2,1)S(1)}, bf16[2,256,128]{2,1,0:T(8,128)(2,1)S(1)}, u32[]{:S(2)}, u32[]{:S(2)}) collective-permute-start(bf16[2,256,128]{2,1,0:T(8,128)(2,1)S(1)} %pad_maximum_fusion.3), channel_id=1, source_target_pairs={{0,4},{4,0},{8,12},{12,8},{1,5},{5,1},{9,13},{13,9},{2,6},{6,2},{1... | collective-permute-start | bytes 393224 | tf_op jit(solution)/shard_map/ppermute | solution.py:459
  14.5 0.3 collective-permute-start.5
  14.8 0.0 collective-permute-done.2.near_ref
  14.8 0.0 copy-start.1
  14.8 0.6 %collective-permute-start.3 = (bf16[512,128]{1,0:T(8,128)(2,1)S(1)}, bf16[512,128]{1,0:T(8,128)(2,1)S(1)}, u32[]{:S(2)}, u32[]{:S(2)}) collective-permute-start(bf16[512,128]{1,0:T(8,128)(2,1)S(1)} %shard_map.93), channel_id=1, source_target_pairs={{0,2},{1,3},{2,0},{3,1},{4,6},{5,7},{6,4},{7,5},{8,10},{9,11},{10,... | collective-permute-start | bytes 393224 | tf_op jit(solution)/shard_map/ppermute | solution.py:459
  15.4 0.0 copy-done
  15.4 0.1 copy.11.routes_ref
  15.5 0.2 collective-permute-done.5.second_ref
  15.8 0.0 copy-done.2
  15.8 0.1 shard_map.97
  15.9 1.0 %collective-permute-start.8 = (bf16[80,128]{1,0:T(8,128)(2,1)S(1)}, bf16[80,128]{1,0:T(8,128)(2,1)S(1)}, u32[]{:S(2)}, u32[]{:S(2)}) collective-permute-start(bf16[80,128]{1,0:T(8,128)(2,1)S(1)} %shard_map.97), channel_id=1, source_target_pairs={{0,4},{4,0},{8,12},{12,8},{1,5},{5,1},{9,13},{13,9},{2,6},{6,2},{1... | collective-permute-start | bytes 61448 | tf_op jit(solution)/shard_map/ppermute | solution.py:459
  16.9 1.3 %collective-permute-start.7 = (bf16[80,128]{1,0:T(8,128)(2,1)S(1)}, bf16[80,128]{1,0:T(8,128)(2,1)S(1)}, u32[]{:S(2)}, u32[]{:S(2)}) collective-permute-start(bf16[80,128]{1,0:T(8,128)(2,1)S(1)} %shard_map.97), channel_id=1, source_target_pairs={{0,8},{4,12},{8,0},{12,4},{1,9},{5,13},{9,1},{13,5},{2,10},{6,14},... | collective-permute-start | bytes 61448 | tf_op jit(solution)/shard_map/ppermute | solution.py:459
  18.2 2.2 %collective-permute-start.6 = (bf16[80,128]{1,0:T(8,128)(2,1)S(1)}, bf16[80,128]{1,0:T(8,128)(2,1)S(1)}, u32[]{:S(2)}, u32[]{:S(2)}) collective-permute-start(bf16[80,128]{1,0:T(8,128)(2,1)S(1)} %shard_map.97), channel_id=1, source_target_pairs={{0,12},{4,8},{8,4},{12,0},{1,13},{5,9},{9,5},{13,1},{2,14},{6,10},... | collective-permute-start | bytes 61448 | tf_op jit(solution)/shard_map/ppermute | solution.py:459
  20.4 0.0 collective-permute-done.4
  20.4 0.7 %shard_map.94.weights_ref = bf16[4,512,512]{2,1,0:T(8,128)(2,1)S(1)} custom-call(bf16[4,256,128]{2,1,0:T(8,128)(2,1)S(1)} %pad_maximum_fusion.1.shared_ref), custom_call_target="tpu_custom_call" | custom-call | bytes 4290000 | tf_op jit(solution)/shard_map/pallas_call | solution.py:237
  21.1 0.0 collective-permute-done.3.far_ref
  21.1 1.7 %shard_map.95 = bf16[16,128,128]{2,1,0:T(8,128)(2,1)} custom-call(bf16[2,512,128]{2,1,0:T(8,128)(2,1)S(1)} %get-tuple-element.22.own_ref, bf16[2,512,128]{2,1,0:T(8,128)(2,1)S(1)} %collective-permute-done.2.near_ref, bf16[512,128]{1,0:T(8,128)(2,1)S(1)} %collective-permute-done.3.far_ref, s32[128,8]{1,0:T(8,128)S(1)} %copy.11.routes_ref, ...), custom_call_target="tpu_custom_call" | custom-call | bytes 6600000 | tf_op jit(solution)/shard_map/pallas_call | solution.py:291
  22.9 0.0 collective-permute-done.8
  22.9 0.0 collective-permute-done.7
  22.9 0.9 %collective-permute-done.6 = bf16[80,128]{1,0:T(8,128)(2,1)S(1)} collective-permute-done((bf16[80,128]{1,0:T(8,128)(2,1)S(1)}, bf16[80,128]{1,0:T(8,128)(2,1)S(1)}, u32[]{:S(2)}, u32[]{:S(2)}) %collective-permute-start.6) | collective-permute-done | bytes 20512 | tf_op jit(solution)/shard_map/ppermute | solution.py:459
  23.8 5.1 %all-to-all-start = ((bf16[16,128,128]{2,1,0:T(8,128)(2,1)}), bf16[16,128,128]{2,1,0:T(8,128)(2,1)S(1)}, u32[]{:S(2)}, u32[]{:S(2)}) async-start(bf16[16,128,128]{2,1,0:T(8,128)(2,1)} %shard_map.95), calls=%async_computation | async-start | bytes 1048576 | tf_op jit(solution)/shard_map/all_to_all | solution.py:32
  28.9 0.2 collective-permute-start.9
  29.2 1.1 %collective-permute-done.9 = bf16[1,4,80,128]{3,2,1,0:T(8,128)(2,1)S(1)} collective-permute-done((bf16[1,4,80,128]{3,2,1,0:T(8,128)(2,1)S(1)}, bf16[1,4,80,128]{3,2,1,0:T(8,128)(2,1)S(1)}, u32[]{:S(2)}, u32[]{:S(2)}) %collective-permute-start.9) | collective-permute-done | bytes 81952 | tf_op jit(solution)/shard_map/ppermute | solution.py:459
  30.3 1.5 %collective-permute-start.10 = (bf16[2,4,80,128]{3,2,1,0:T(8,128)(2,1)S(1)}, bf16[2,4,80,128]{3,2,1,0:T(8,128)(2,1)S(1)}, u32[]{:S(2)}, u32[]{:S(2)}) collective-permute-start(bf16[2,4,80,128]{3,2,1,0:T(8,128)(2,1)S(1)} %pad_maximum_fusion.2), channel_id=1, source_target_pairs={{0,2},{1,3},{2,0},{3,1},{4,6},{5,7},{6,4},{7,5},{8,10},{9,11},{10,... | collective-permute-start | bytes 491528 | tf_op jit(solution)/shard_map/ppermute | solution.py:459
  31.8 0.0 copy-done.1
  31.8 9.5 %shard_map.98.far_ref = bf16[8192,256]{1,0:T(8,128)(2,1)} custom-call(bf16[256,8,1024]{2,1,0:T(8,128)(2,1)} %query_ref, f32[8,64,64]{2,1,0:T(8,128)S(1)} %copy-done.1), custom_call_target="tpu_custom_call" | custom-call | bytes 33000000 | tf_op jit(solution)/shard_map/pallas_call | solution.py:354
  41.4 0.0 collective-permute-done.10
  41.4 0.0 all-to-all-done.arrived_ref
  41.4 6.1 %shard_map.99 = f32[16,8,128]{2,1,0:T(8,128)S(1)} custom-call(bf16[16,128,128]{2,1,0:T(8,128)(2,1)S(1)} %all-to-all-done.arrived_ref, bf16[16,80,128]{2,1,0:T(8,128)(2,1)S(1)} %bitcast.12, bf16[8192,256]{1,0:T(8,128)(2,1)} %shard_map.98.far_ref), custom_call_target="tpu_custom_call" | custom-call | bytes 16500000 | tf_op jit(solution)/shard_map/pallas_call | solution.py:428
  47.5 9.9 %all_to_all.10.pieces_ref = f32[16,8,128]{2,1,0:T(8,128)S(1)} all-to-all(f32[16,8,128]{2,1,0:T(8,128)S(1)} %shard_map.99), channel_id=1, replica_groups={{8,9,10,11,12,13,14,15,0,1,2,3,4,5,6,7},{24,25,26,27,28,29,30,31,16,17,..., dimensions={0} | all-to-all | bytes 131072 | tf_op jit(solution)/shard_map/all_to_all | solution.py:32
  57.5 0.6 %shard_map.100 = f32[8,64]{1,0:T(8,128)} custom-call(f32[16,8,128]{2,1,0:T(8,128)S(1)} %all_to_all.10.pieces_ref), custom_call_target="tpu_custom_call" | custom-call | tf_op jit(solution)/shard_map/pallas_call | solution.py:450
  (8 shorter events, 0.2 us)
Async XLA Ops:
  0.0 15.4 %copy-start = (s32[512,8]{0,1:T(8,128)S(1)}, s32[512,8]{0,1:T(8,128)}, u32[]{:S(2)}) copy-start(s32[512,8]{0,1:T(8,128)} %param.11) | copy-start | bytes 49156
  0.0 15.8 %copy-start.2 = (s32[512]{0:T(512)S(1)}, s32[512]{0:T(512)}, u32[]{:S(2)}) copy-start(s32[512]{0:T(512)} %param.12) | copy-start | bytes 6148
  2.8 9.9 %collective-permute-start.1 = (bf16[2,128,128]{2,1,0:T(8,128)(2,1)S(1)}, bf16[2,128,128]{2,1,0:T(8,128)(2,1)S(1)}, u32[]{:S(2)}, u32[]{:S(2)}) collective-permute-start(bf16[2,128,128]{2,1,0:T(8,128)(2,1)S(1)} %get-tuple-element.24), channel_id=1, source_target_pairs={{0,2},{1,3},{2,0},{3,1},{4,6},{5,7},{6,4},{7,5},{8,10},{9,11},{10,... | collective-permute-start | bytes 196616 | tf_op jit(solution)/shard_map/ppermute | solution.py:459
  5.8 6.9 %collective-permute-start = (bf16[256,128]{1,0:T(8,128)(2,1)S(1)}, bf16[256,128]{1,0:T(8,128)(2,1)S(1)}, u32[]{:S(2)}, u32[]{:S(2)}) collective-permute-start(bf16[256,128]{1,0:T(8,128)(2,1)S(1)} %get-tuple-element.23), channel_id=1, source_target_pairs={{0,8},{4,12},{8,0},{12,4},{1,9},{5,13},{9,1},{13,5},{2,10},{6,14},... | collective-permute-start | bytes 196616 | tf_op jit(solution)/shard_map/ppermute | solution.py:459
  12.8 2.0 %collective-permute-start.2 = (bf16[2,512,128]{2,1,0:T(8,128)(2,1)S(1)}, bf16[2,512,128]{2,1,0:T(8,128)(2,1)S(1)}, u32[]{:S(2)}, u32[]{:S(2)}) collective-permute-start(bf16[2,512,128]{2,1,0:T(8,128)(2,1)S(1)} %get-tuple-element.26), channel_id=1, source_target_pairs={{0,1},{1,0},{2,3},{3,2},{4,5},{5,4},{6,7},{7,6},{8,9},{9,8},{10,11... | collective-permute-start | bytes 786440 | tf_op jit(solution)/shard_map/ppermute | solution.py:459
  12.9 7.5 %collective-permute-start.4 = (bf16[2,256,128]{2,1,0:T(8,128)(2,1)S(1)}, bf16[2,256,128]{2,1,0:T(8,128)(2,1)S(1)}, u32[]{:S(2)}, u32[]{:S(2)}) collective-permute-start(bf16[2,256,128]{2,1,0:T(8,128)(2,1)S(1)} %pad_maximum_fusion.3), channel_id=1, source_target_pairs={{0,4},{4,0},{8,12},{12,8},{1,5},{5,1},{9,13},{13,9},{2,6},{6,2},{1... | collective-permute-start | bytes 393224 | tf_op jit(solution)/shard_map/ppermute | solution.py:459
  14.5 1.3 %collective-permute-start.5 = (bf16[128,128]{1,0:T(8,128)(2,1)S(1)}, bf16[128,128]{1,0:T(8,128)(2,1)S(1)}, u32[]{:S(2)}, u32[]{:S(2)}) collective-permute-start(bf16[128,128]{1,0:T(8,128)(2,1)S(1)} %shard_map.96), channel_id=1, source_target_pairs={{0,1},{1,0},{2,3},{3,2},{4,5},{5,4},{6,7},{7,6},{8,9},{9,8},{10,11... | collective-permute-start | bytes 98312 | tf_op jit(solution)/shard_map/ppermute | solution.py:459
  14.8 17.0 %copy-start.1 = (f32[8,64,64]{2,1,0:T(8,128)S(1)}, f32[8,64,64]{2,1,0:T(8,128)}, u32[]{:S(2)}) copy-start(f32[8,64,64]{2,1,0:T(8,128)} %inverse_ref.1) | copy-start | bytes 393220
  14.8 6.3 %collective-permute-start.3 = (bf16[512,128]{1,0:T(8,128)(2,1)S(1)}, bf16[512,128]{1,0:T(8,128)(2,1)S(1)}, u32[]{:S(2)}, u32[]{:S(2)}) collective-permute-start(bf16[512,128]{1,0:T(8,128)(2,1)S(1)} %shard_map.93), channel_id=1, source_target_pairs={{0,2},{1,3},{2,0},{3,1},{4,6},{5,7},{6,4},{7,5},{8,10},{9,11},{10,... | collective-permute-start | bytes 393224 | tf_op jit(solution)/shard_map/ppermute | solution.py:459
  15.9 7.0 %collective-permute-start.8 = (bf16[80,128]{1,0:T(8,128)(2,1)S(1)}, bf16[80,128]{1,0:T(8,128)(2,1)S(1)}, u32[]{:S(2)}, u32[]{:S(2)}) collective-permute-start(bf16[80,128]{1,0:T(8,128)(2,1)S(1)} %shard_map.97), channel_id=1, source_target_pairs={{0,4},{4,0},{8,12},{12,8},{1,5},{5,1},{9,13},{13,9},{2,6},{6,2},{1... | collective-permute-start | bytes 61448 | tf_op jit(solution)/shard_map/ppermute | solution.py:459
  16.9 6.0 %collective-permute-start.7 = (bf16[80,128]{1,0:T(8,128)(2,1)S(1)}, bf16[80,128]{1,0:T(8,128)(2,1)S(1)}, u32[]{:S(2)}, u32[]{:S(2)}) collective-permute-start(bf16[80,128]{1,0:T(8,128)(2,1)S(1)} %shard_map.97), channel_id=1, source_target_pairs={{0,8},{4,12},{8,0},{12,4},{1,9},{5,13},{9,1},{13,5},{2,10},{6,14},... | collective-permute-start | bytes 61448 | tf_op jit(solution)/shard_map/ppermute | solution.py:459
  18.2 5.6 %collective-permute-start.6 = (bf16[80,128]{1,0:T(8,128)(2,1)S(1)}, bf16[80,128]{1,0:T(8,128)(2,1)S(1)}, u32[]{:S(2)}, u32[]{:S(2)}) collective-permute-start(bf16[80,128]{1,0:T(8,128)(2,1)S(1)} %shard_map.97), channel_id=1, source_target_pairs={{0,12},{4,8},{8,4},{12,0},{1,13},{5,9},{9,5},{13,1},{2,14},{6,10},... | collective-permute-start | bytes 61448 | tf_op jit(solution)/shard_map/ppermute | solution.py:459
  23.8 17.6 %all-to-all-start = ((bf16[16,128,128]{2,1,0:T(8,128)(2,1)}), bf16[16,128,128]{2,1,0:T(8,128)(2,1)S(1)}, u32[]{:S(2)}, u32[]{:S(2)}) async-start(bf16[16,128,128]{2,1,0:T(8,128)(2,1)} %shard_map.95), calls=%async_computation | async-start | bytes 1048576 | tf_op jit(solution)/shard_map/all_to_all | solution.py:32
  28.9 1.3 %collective-permute-start.9 = (bf16[1,4,80,128]{3,2,1,0:T(8,128)(2,1)S(1)}, bf16[1,4,80,128]{3,2,1,0:T(8,128)(2,1)S(1)}, u32[]{:S(2)}, u32[]{:S(2)}) collective-permute-start(bf16[1,4,80,128]{3,2,1,0:T(8,128)(2,1)S(1)} %maximum_bitcast_fusion), channel_id=1, source_target_pairs={{0,1},{1,0},{2,3},{3,2},{4,5},{5,4},{6,7},{7,6},{8,9},{9,8},{10,11... | collective-permute-start | bytes 245768 | tf_op jit(solution)/shard_map/ppermute | solution.py:459
  30.3 11.1 %collective-permute-start.10 = (bf16[2,4,80,128]{3,2,1,0:T(8,128)(2,1)S(1)}, bf16[2,4,80,128]{3,2,1,0:T(8,128)(2,1)S(1)}, u32[]{:S(2)}, u32[]{:S(2)}) collective-permute-start(bf16[2,4,80,128]{3,2,1,0:T(8,128)(2,1)S(1)} %pad_maximum_fusion.2), channel_id=1, source_target_pairs={{0,2},{1,3},{2,0},{3,1},{4,6},{5,7},{6,4},{7,5},{8,10},{9,11},{10,... | collective-permute-start | bytes 491528 | tf_op jit(solution)/shard_map/ppermute | solution.py:459

commit v14 on v12

--- a/solution.py
+++ b/solution.py
@@ -21,6 +21,15 @@
 
 def stay(array):
     return pltpu.with_memory_space_constraint(array, pltpu.HBM)
+
+
+def listed(owner, owners, first):
+    return (owner + owners - first) % owners
+
+
+def send_to_all(blocks, owners, shares, first):
+    members = [(i + first * shares) % (owners * shares) for i in range(owners * shares)]
+    return lax.all_to_all(blocks, ("expert", "proj"), 0, 0, tiled=True, axis_index_groups=[members])
 
 
 def split(value):
@@ -104,43 +113,46 @@
 
 def outer_kernel(hidden_hbm, out_proj_hbm, leaving_ref, own_ref, hidden_ref, out_proj_ref, rows_ref, sems, *, top):
     turns = (1, 3, 2, 0)
-    chunks, chunk_rows, _ = hidden_ref.shape
-    chunk = chunk_rows // top
-    split_by = chunks // len(turns)
-    quarter = chunk * split_by
+    quarter_rows = hidden_ref.shape[1]
+    quarter = quarter_rows // top
+    half = quarter // 2
+    chunks = [(0, 0, half), (0, half, half), (1, 0, quarter), (2, 0, quarter), (3, 0, half), (3, half, half)]
     width = out_proj_ref.shape[0]
     place = lax.axis_index("proj")
     pairs = [(out_proj_hbm, out_proj_ref)]
-    for i in range(chunks):
-        start = (jnp.bitwise_xor(place, turns[i // split_by]) * split_by + i % split_by) * chunk_rows
-        pairs.append((hidden_hbm.at[pl.ds(pl.multiple_of(start, chunk_rows), chunk_rows)], hidden_ref.at[i]))
+    for g, token, size in chunks:
+        start = jnp.bitwise_xor(place, turns[g]) * quarter_rows + token * top
+        rows = pl.ds(pl.multiple_of(start, half * top), size * top)
+        pairs.append((hidden_hbm.at[rows], hidden_ref.at[g, pl.ds(token * top, size * top)]))
     take = in_order([pltpu.make_async_copy(*pair, sems.at[i]) for i, pair in enumerate(pairs)], 3)
     take()
-    first = low_lanes(chunk, width)
 
     def pack_rows(i):
-        g, part = i // split_by, i % split_by
+        g, token, size = chunks[i]
         wire_ref = leaving_ref.at[g] if g < 2 else own_ref.at[g - 2]
+        first = low_lanes(size, width)
         for pair in range(top // 2):
-            even = rows_ref[i % 2, pl.ds(2 * pair, chunk, stride=top), :]
-            odd = rows_ref[i % 2, pl.ds(2 * pair + 1, chunk, stride=top), :]
-            start = pair * quarter + part * chunk
-            wire_ref[start : start + chunk, :] = jnp.where(first, even, odd).astype(jnp.bfloat16)
-
-    for i in range(chunks):
+            even = rows_ref[i % 2, pl.ds(2 * pair, size, stride=top), :]
+            odd = rows_ref[i % 2, pl.ds(2 * pair + 1, size, stride=top), :]
+            start = pair * quarter + token
+            wire_ref[start : start + size, :] = jnp.where(first, even, odd).astype(jnp.bfloat16)
+
+    for i, (g, token, size) in enumerate(chunks):
         take()
         twice = jnp.concatenate([out_proj_ref[...], out_proj_ref[...]], axis=0)
-        rows_ref[i % 2] = lax.dot_general(
-            hidden_ref[i], twice, (((1,), (1,)), ((), ())), preferred_element_type=jnp.float32
+        rows_ref[i % 2, : size * top, :] = lax.dot_general(
+            hidden_ref[g, token * top : (token + size) * top, :],
+            twice,
+            (((1,), (1,)), ((), ())),
+            preferred_element_type=jnp.float32,
         )
         if i:
             pack_rows(i - 1)
-    pack_rows(chunks - 1)
+    pack_rows(len(chunks) - 1)
 
 
 def project_outer(flat_hidden, out_projection, quarters, top):
     rows, hidden = flat_hidden.shape
-    chunks = quarters
     wire = jax.ShapeDtypeStruct((quarters // 2, rows // quarters // 2, LANES), jnp.bfloat16)
     return pl.pallas_call(
         functools.partial(outer_kernel, top=top),
@@ -148,10 +160,10 @@
         out_specs=[VMEM] * 2,
         out_shape=[wire, wire],
         scratch_shapes=[
-            pltpu.VMEM((chunks, rows // chunks, hidden), jnp.bfloat16),
+            pltpu.VMEM((quarters, rows // quarters, hidden), jnp.bfloat16),
             pltpu.VMEM(out_projection.shape, out_projection.dtype),
-            pltpu.VMEM((2, rows // chunks, LANES), jnp.float32),
-            pltpu.SemaphoreType.DMA((chunks + 1,)),
+            pltpu.VMEM((2, rows // quarters, LANES), jnp.float32),
+            pltpu.SemaphoreType.DMA((quarters + 3,)),
         ],
         compiler_params=pltpu.CompilerParams(vmem_limit_bytes=40 * MIB),
         cost_estimate=cost(4),
@@ -270,7 +282,7 @@
         ).astype(jnp.bfloat16)
         share_width = result.shape[1] // shares
         for share in range(shares):
-            payload_ref[group * shares + share] = result[:, share * share_width : (share + 1) * share_width]
+            payload_ref[listed(group, groups, groups // 2) * shares + share] = result[:, share * share_width : (share + 1) * share_width]
         return carry
 
     lax.fori_loop(0, groups, one_group, 0, unroll=groups <= 4)
@@ -375,19 +387,22 @@
     for entry, (owner_turn, share_turn) in enumerate(turns):
         owner = jnp.bitwise_xor(lax.axis_index("expert"), owner_turn)
         share = jnp.bitwise_xor(lax.axis_index("proj"), share_turn)
-        outer.append(arrived_ref[owner * shares + share])
-        docs.append(inner_ref[entry, width : width + 1, :].astype(jnp.float32).astype(jnp.int32))
+        outer.append(arrived_ref[listed(owner, owners, owners // 2) * shares + share])
+        docs.append(inner_ref[entry, width:, :])
         inner.append(inner_ref[entry, :width, :])
     outer = jnp.concatenate(outer, axis=0)
     inner = jnp.concatenate(inner, axis=1)
-    docs = jnp.broadcast_to(jnp.concatenate(docs, axis=1), inner.shape)
-    doc_group = 16
+    docs = jnp.concatenate(docs, axis=1)
+    ones = jnp.ones_like(docs)
+    doc_group = min(doc_count, max(4, 8 * MIB // (2 * inner.size)))
     pitch = grads_ref.shape[0] // doc_count
 
     def one_group(group, carry):
-        masked = [
-            jnp.where(docs == group * doc_group + d, inner, jnp.zeros_like(inner)) for d in range(doc_group)
-        ]
+        masked = []
+        for d in range(doc_group):
+            named = jnp.full_like(docs, group * doc_group + d)
+            own = jnp.where(docs == named, ones, jnp.zeros_like(docs))
+            masked += [inner[r : r + DOC_ROWS] * own for r in range(0, width, DOC_ROWS)]
         sums = jnp.dot(jnp.concatenate(masked, axis=0), outer, preferred_element_type=jnp.float32)
         for d in range(doc_group):
             start = pl.multiple_of((group * doc_group + d) * pitch, 8)
@@ -409,7 +424,7 @@
     for owner in range(owners):
         for share in range(shares):
             piece = result[owner * DOC_DEV : (owner + 1) * DOC_DEV, share * columns : (share + 1) * columns]
-            out_ref[owner * shares + share] = jnp.concatenate([piece, fill], axis=1)
+            out_ref[listed(owner, owners, owners - 1) * shares + share] = jnp.concatenate([piece, fill], axis=1)
 
 
 def score(arrived, inner, queries, turns, owners):
@@ -497,7 +512,7 @@
     quarter_routes = lax.dynamic_slice_in_dim(routes, lax.axis_index("proj") * quarter, quarter, 0)
     payload = condition(own, near, far, quarter_routes, weights, shares, width)
     payload, arriving = lax.optimization_barrier((payload, arriving))
-    arrived = lax.all_to_all(payload, ("expert", "proj"), 0, 0, tiled=True)
+    arrived = send_to_all(payload, owners, shares, owners // 2)
     inner = jnp.stack(arriving + [inner])
     inner, share_turns = inner[None], (0,)
     inner, share_turns = double(inner, share_turns, "proj", shares, 1)
@@ -507,7 +522,7 @@
     all_turns = tuple((o, p) for p in share_turns for o in owner_turns)
     queries = condition_queries(query_grads, inverse_in)
     pieces = score(arrived, inner, queries, all_turns, owners)
-    pieces = lax.all_to_all(pieces, ("expert", "proj"), 0, 0, tiled=True)
+    pieces = send_to_all(pieces, owners, shares, owners - 1)
     return sum_pieces(pieces, query_grads.shape[0] // shares).T
 
 

time: 60.5 us -> 58 us (0.959)
  blocking collectives: 10.8 us -> 9.12 us
  waiting for transfers between devices: 3.6 us -> 1.97 us
    all_to_all x1, blocking collectives: 10.8 us -> 9.12 us  [send_to_all(): lax.all_to_all(blocks, ('expert', 'proj'), 0, 0, tiled=True, axis_index_g...]
    all_to_all x1, waiting for transfers between devices: 1.51 us -> 0.01 us  [send_to_all(): lax.all_to_all(blocks, ('expert', 'proj'), 0, 0, tiled=True, axis_index_g...]
    all_to_all x1, starting transfers between devices: 4.23 us -> 5.14 us  [send_to_all(): lax.all_to_all(blocks, ('expert', 'proj'), 0, 0, tiled=True, axis_index_g...]
    ppermute x11, starting transfers between devices: 15 us -> 14.4 us  [exchange(): return lax.ppermute(block, axis, [(i, i ^ turn) for i in range(size)])]
  transfers between devices with their start and end apart: 12 -> 12, of which waited for: 4 -> 3; matrix products, arithmetic and copies ran while one was open for 0% -> 0% of each run, Pallas kernels for 27% -> 29%
where the time goes in v14:
time: 58 us; the launch traced here: 57.5 us
  Pallas kernels  26.5 us (46%)
  starting transfers between devices  19.5 us (34%)
  blocking collectives  9.12 us (16%)
  waiting for transfers between devices  1.97 us (3%)
    ppermute x11, starting transfers between devices, exchange(): return lax.ppermute(block, axis, [(i, i ^ turn) for i in range(size)])  14.4 us
    pallas_call x1, Pallas kernels, condition_queries(): pl.pallas_call(query_kernel, grid=(flat // LANES,), in_specs=[pl.BlockSpe...  9.53 us
    all_to_all x1, blocking collectives, send_to_all(): lax.all_to_all(blocks, ('expert', 'proj'), 0, 0, tiled=True, axis_index_g...  9.12 us
    pallas_call x1, Pallas kernels, score(): pl.pallas_call(functools.partial(score_kernel, width=width, doc_count=doc...  6.32 us
    all_to_all x1, starting transfers between devices, send_to_all(): lax.all_to_all(blocks, ('expert', 'proj'), 0, 0, tiled=True, axis_index_g...  5.14 us
    pallas_call x1, Pallas kernels, project_outer(): pl.pallas_call(functools.partial(outer_kernel, top=top), in_specs=[HBM] *...  4.67 us
    pallas_call x1, Pallas kernels, project_inner(): pl.pallas_call(inner_kernel, in_specs=[HBM] * 3, out_specs=[VMEM] * 3, ou...  2.78 us
    ppermute x11, waiting for transfers between devices, exchange(): return lax.ppermute(block, axis, [(i, i ^ turn) for i in range(size)])  1.96 us
  transfers between devices with their start and end apart: 12, of which 3 were waited for; matrix products, arithmetic and copies ran while one was open for 0% of the time, Pallas kernels for 29%

profile of v14, /device:TPU:0, one launch (start us, length us, event | category | flops | bytes accessed | tf_op | source)
XLA Modules:
  0.0 57.5 jit_solution(1095085440547132615)
XLA Ops:
  0.0 0.0 copy-start
  0.0 0.0 copy-start.2
  0.0 2.8 %shard_map.92 = (bf16[2,128,128]{2,1,0:T(8,128)(2,1)S(1)}, bf16[2,128,128]{2,1,0:T(8,128)(2,1)S(1)}, bf16[256,128]{1,0:T(8,128)(2,1)S(1)}) custom-call(bf16[512,1792]{1,0:T(8,128)(2,1)} %act_hbm.1, bf16[64,1792]{1,0:T(8,128)(2,1)} %in_proj_hbm.1, f32[8,64,64]{2,1,0:T(8,128)} %inverse_hbm.1), custom_call_target="tpu_custom_call" | custom-call | bytes 8250000 | tf_op jit(solution)/shard_map/pallas_call | solution.py:101
  2.8 3.0 %collective-permute-start.1 = (bf16[2,128,128]{2,1,0:T(8,128)(2,1)S(1)}, bf16[2,128,128]{2,1,0:T(8,128)(2,1)S(1)}, u32[]{:S(2)}, u32[]{:S(2)}) collective-permute-start(bf16[2,128,128]{2,1,0:T(8,128)(2,1)S(1)} %get-tuple-element.24), channel_id=1, source_target_pairs={{0,2},{1,3},{2,0},{3,1},{4,6},{5,7},{6,4},{7,5},{8,10},{9,11},{10,... | collective-permute-start | bytes 196616 | tf_op jit(solution)/shard_map/ppermute | solution.py:465
  5.8 2.6 %collective-permute-start = (bf16[256,128]{1,0:T(8,128)(2,1)S(1)}, bf16[256,128]{1,0:T(8,128)(2,1)S(1)}, u32[]{:S(2)}, u32[]{:S(2)}) collective-permute-start(bf16[256,128]{1,0:T(8,128)(2,1)S(1)} %get-tuple-element.23), channel_id=1, source_target_pairs={{0,8},{4,12},{8,0},{12,4},{1,9},{5,13},{9,1},{13,5},{2,10},{6,14},... | collective-permute-start | bytes 196616 | tf_op jit(solution)/shard_map/ppermute | solution.py:465
  8.4 4.7 %shard_map.91 = (bf16[2,512,128]{2,1,0:T(8,128)(2,1)S(1)}, bf16[2,512,128]{2,1,0:T(8,128)(2,1)S(1)}) custom-call(bf16[4096,512]{1,0:T(8,128)(2,1)} %bitcast.17, bf16[64,512]{1,0:T(8,128)(2,1)} %out_proj_hbm.1), custom_call_target="tpu_custom_call" | custom-call | bytes 13200000 | tf_op jit(solution)/shard_map/pallas_call | solution.py:157
  13.1 0.0 collective-permute-done.1.near_ref.first_ref
  13.1 0.0 collective-permute-done
  13.1 0.1 collective-permute-start.2
  13.2 1.6 %collective-permute-start.4 = (bf16[2,256,128]{2,1,0:T(8,128)(2,1)S(1)}, bf16[2,256,128]{2,1,0:T(8,128)(2,1)S(1)}, u32[]{:S(2)}, u32[]{:S(2)}) collective-permute-start(bf16[2,256,128]{2,1,0:T(8,128)(2,1)S(1)} %pad_maximum_fusion.3), channel_id=1, source_target_pairs={{0,4},{4,0},{8,12},{12,8},{1,5},{5,1},{9,13},{13,9},{2,6},{6,2},{1... | collective-permute-start | bytes 393224 | tf_op jit(solution)/shard_map/ppermute | solution.py:465
  14.8 0.3 collective-permute-start.5
  15.1 0.0 collective-permute-done.2.near_ref
  15.1 0.0 copy-start.1
  15.2 0.6 %collective-permute-start.3 = (bf16[512,128]{1,0:T(8,128)(2,1)S(1)}, bf16[512,128]{1,0:T(8,128)(2,1)S(1)}, u32[]{:S(2)}, u32[]{:S(2)}) collective-permute-start(bf16[512,128]{1,0:T(8,128)(2,1)S(1)} %shard_map.93), channel_id=1, source_target_pairs={{0,2},{1,3},{2,0},{3,1},{4,6},{5,7},{6,4},{7,5},{8,10},{9,11},{10,... | collective-permute-start | bytes 393224 | tf_op jit(solution)/shard_map/ppermute | solution.py:465
  15.8 0.0 copy-done
  15.8 0.1 copy.11.routes_ref
  15.9 0.2 collective-permute-done.5.second_ref
  16.1 0.0 copy-done.2
  16.1 0.1 shard_map.97
  16.2 1.0 %collective-permute-start.8 = (bf16[80,128]{1,0:T(8,128)(2,1)S(1)}, bf16[80,128]{1,0:T(8,128)(2,1)S(1)}, u32[]{:S(2)}, u32[]{:S(2)}) collective-permute-start(bf16[80,128]{1,0:T(8,128)(2,1)S(1)} %shard_map.97), channel_id=1, source_target_pairs={{0,4},{4,0},{8,12},{12,8},{1,5},{5,1},{9,13},{13,9},{2,6},{6,2},{1... | collective-permute-start | bytes 61448 | tf_op jit(solution)/shard_map/ppermute | solution.py:465
  17.2 1.0 %collective-permute-start.7 = (bf16[80,128]{1,0:T(8,128)(2,1)S(1)}, bf16[80,128]{1,0:T(8,128)(2,1)S(1)}, u32[]{:S(2)}, u32[]{:S(2)}) collective-permute-start(bf16[80,128]{1,0:T(8,128)(2,1)S(1)} %shard_map.97), channel_id=1, source_target_pairs={{0,8},{4,12},{8,0},{12,4},{1,9},{5,13},{9,1},{13,5},{2,10},{6,14},... | collective-permute-start | bytes 61448 | tf_op jit(solution)/shard_map/ppermute | solution.py:465
  18.2 2.5 %collective-permute-start.6 = (bf16[80,128]{1,0:T(8,128)(2,1)S(1)}, bf16[80,128]{1,0:T(8,128)(2,1)S(1)}, u32[]{:S(2)}, u32[]{:S(2)}) collective-permute-start(bf16[80,128]{1,0:T(8,128)(2,1)S(1)} %shard_map.97), channel_id=1, source_target_pairs={{0,12},{4,8},{8,4},{12,0},{1,13},{5,9},{9,5},{13,1},{2,14},{6,10},... | collective-permute-start | bytes 61448 | tf_op jit(solution)/shard_map/ppermute | solution.py:465
  20.7 0.0 collective-permute-done.4
  20.7 0.7 %shard_map.94.weights_ref = bf16[4,512,512]{2,1,0:T(8,128)(2,1)S(1)} custom-call(bf16[4,256,128]{2,1,0:T(8,128)(2,1)S(1)} %pad_maximum_fusion.1.shared_ref), custom_call_target="tpu_custom_call" | custom-call | bytes 4290000 | tf_op jit(solution)/shard_map/pallas_call | solution.py:240
  21.5 0.0 collective-permute-done.3.far_ref
  21.5 1.7 %shard_map.95 = bf16[16,128,128]{2,1,0:T(8,128)(2,1)} custom-call(bf16[2,512,128]{2,1,0:T(8,128)(2,1)S(1)} %get-tuple-element.22.own_ref, bf16[2,512,128]{2,1,0:T(8,128)(2,1)S(1)} %collective-permute-done.2.near_ref, bf16[512,128]{1,0:T(8,128)(2,1)S(1)} %collective-permute-done.3.far_ref, s32[128,8]{1,0:T(8,128)S(1)} %copy.11.routes_ref, ...), custom_call_target="tpu_custom_call" | custom-call | bytes 6600000 | tf_op jit(solution)/shard_map/pallas_call | solution.py:294
  23.2 0.0 collective-permute-done.8
  23.2 0.0 collective-permute-done.7
  23.2 0.6 collective-permute-done.6
  23.8 5.1 %all-to-all-start = ((bf16[16,128,128]{2,1,0:T(8,128)(2,1)}), bf16[16,128,128]{2,1,0:T(8,128)(2,1)S(1)}, u32[]{:S(2)}, u32[]{:S(2)}) async-start(bf16[16,128,128]{2,1,0:T(8,128)(2,1)} %shard_map.95), calls=%async_computation | async-start | bytes 1048576 | tf_op jit(solution)/shard_map/all_to_all | solution.py:32
  28.9 0.2 collective-permute-start.9
  29.2 1.1 %collective-permute-done.9 = bf16[1,4,80,128]{3,2,1,0:T(8,128)(2,1)S(1)} collective-permute-done((bf16[1,4,80,128]{3,2,1,0:T(8,128)(2,1)S(1)}, bf16[1,4,80,128]{3,2,1,0:T(8,128)(2,1)S(1)}, u32[]{:S(2)}, u32[]{:S(2)}) %collective-permute-start.9) | collective-permute-done | bytes 81952 | tf_op jit(solution)/shard_map/ppermute | solution.py:465
  30.3 1.5 %collective-permute-start.10 = (bf16[2,4,80,128]{3,2,1,0:T(8,128)(2,1)S(1)}, bf16[2,4,80,128]{3,2,1,0:T(8,128)(2,1)S(1)}, u32[]{:S(2)}, u32[]{:S(2)}) collective-permute-start(bf16[2,4,80,128]{3,2,1,0:T(8,128)(2,1)S(1)} %pad_maximum_fusion.2), channel_id=1, source_target_pairs={{0,2},{1,3},{2,0},{3,1},{4,6},{5,7},{6,4},{7,5},{8,10},{9,11},{10,... | collective-permute-start | bytes 491528 | tf_op jit(solution)/shard_map/ppermute | solution.py:465
  31.8 0.0 copy-done.1
  31.8 9.5 %shard_map.98.far_ref = bf16[8192,256]{1,0:T(8,128)(2,1)} custom-call(bf16[256,8,1024]{2,1,0:T(8,128)(2,1)} %query_ref, f32[8,64,64]{2,1,0:T(8,128)S(1)} %copy-done.1), custom_call_target="tpu_custom_call" | custom-call | bytes 33000000 | tf_op jit(solution)/shard_map/pallas_call | solution.py:357
  41.4 0.0 collective-permute-done.10
  41.4 0.0 all-to-all-done.arrived_ref
  41.4 6.3 %shard_map.99 = f32[16,8,128]{2,1,0:T(8,128)S(1)} custom-call(bf16[16,128,128]{2,1,0:T(8,128)(2,1)S(1)} %all-to-all-done.arrived_ref, bf16[16,80,128]{2,1,0:T(8,128)(2,1)S(1)} %bitcast.12, bf16[8192,256]{1,0:T(8,128)(2,1)} %shard_map.98.far_ref), custom_call_target="tpu_custom_call" | custom-call | bytes 16500000 | tf_op jit(solution)/shard_map/pallas_call | solution.py:434
  47.8 9.1 %all_to_all.10.pieces_ref = f32[16,8,128]{2,1,0:T(8,128)S(1)} all-to-all(f32[16,8,128]{2,1,0:T(8,128)S(1)} %shard_map.99), channel_id=1, replica_groups={{12,13,14,15,0,1,2,3,4,5,6,7,8,9,10,11},{28,29,30,31,16,17,18,19,20,21,..., dimensions={0} | all-to-all | bytes 131072 | tf_op jit(solution)/shard_map/all_to_all | solution.py:32
  56.9 0.6 %shard_map.100 = f32[8,64]{1,0:T(8,128)} custom-call(f32[16,8,128]{2,1,0:T(8,128)S(1)} %all_to_all.10.pieces_ref), custom_call_target="tpu_custom_call" | custom-call | tf_op jit(solution)/shard_map/pallas_call | solution.py:456
  (8 shorter events, 0.2 us)
Async XLA Ops:
  0.0 15.8 %copy-start = (s32[512,8]{0,1:T(8,128)S(1)}, s32[512,8]{0,1:T(8,128)}, u32[]{:S(2)}) copy-start(s32[512,8]{0,1:T(8,128)} %param.11) | copy-start | bytes 49156
  0.0 16.1 %copy-start.2 = (s32[512]{0:T(512)S(1)}, s32[512]{0:T(512)}, u32[]{:S(2)}) copy-start(s32[512]{0:T(512)} %param.12) | copy-start | bytes 6148
  2.8 10.3 %collective-permute-start.1 = (bf16[2,128,128]{2,1,0:T(8,128)(2,1)S(1)}, bf16[2,128,128]{2,1,0:T(8,128)(2,1)S(1)}, u32[]{:S(2)}, u32[]{:S(2)}) collective-permute-start(bf16[2,128,128]{2,1,0:T(8,128)(2,1)S(1)} %get-tuple-element.24), channel_id=1, source_target_pairs={{0,2},{1,3},{2,0},{3,1},{4,6},{5,7},{6,4},{7,5},{8,10},{9,11},{10,... | collective-permute-start | bytes 196616 | tf_op jit(solution)/shard_map/ppermute | solution.py:465
  5.8 7.3 %collective-permute-start = (bf16[256,128]{1,0:T(8,128)(2,1)S(1)}, bf16[256,128]{1,0:T(8,128)(2,1)S(1)}, u32[]{:S(2)}, u32[]{:S(2)}) collective-permute-start(bf16[256,128]{1,0:T(8,128)(2,1)S(1)} %get-tuple-element.23), channel_id=1, source_target_pairs={{0,8},{4,12},{8,0},{12,4},{1,9},{5,13},{9,1},{13,5},{2,10},{6,14},... | collective-permute-start | bytes 196616 | tf_op jit(solution)/shard_map/ppermute | solution.py:465
  13.1 2.0 %collective-permute-start.2 = (bf16[2,512,128]{2,1,0:T(8,128)(2,1)S(1)}, bf16[2,512,128]{2,1,0:T(8,128)(2,1)S(1)}, u32[]{:S(2)}, u32[]{:S(2)}) collective-permute-start(bf16[2,512,128]{2,1,0:T(8,128)(2,1)S(1)} %get-tuple-element.26), channel_id=1, source_target_pairs={{0,1},{1,0},{2,3},{3,2},{4,5},{5,4},{6,7},{7,6},{8,9},{9,8},{10,11... | collective-permute-start | bytes 786440 | tf_op jit(solution)/shard_map/ppermute | solution.py:465
  13.2 7.5 %collective-permute-start.4 = (bf16[2,256,128]{2,1,0:T(8,128)(2,1)S(1)}, bf16[2,256,128]{2,1,0:T(8,128)(2,1)S(1)}, u32[]{:S(2)}, u32[]{:S(2)}) collective-permute-start(bf16[2,256,128]{2,1,0:T(8,128)(2,1)S(1)} %pad_maximum_fusion.3), channel_id=1, source_target_pairs={{0,4},{4,0},{8,12},{12,8},{1,5},{5,1},{9,13},{13,9},{2,6},{6,2},{1... | collective-permute-start | bytes 393224 | tf_op jit(solution)/shard_map/ppermute | solution.py:465
  14.8 1.3 %collective-permute-start.5 = (bf16[128,128]{1,0:T(8,128)(2,1)S(1)}, bf16[128,128]{1,0:T(8,128)(2,1)S(1)}, u32[]{:S(2)}, u32[]{:S(2)}) collective-permute-start(bf16[128,128]{1,0:T(8,128)(2,1)S(1)} %shard_map.96), channel_id=1, source_target_pairs={{0,1},{1,0},{2,3},{3,2},{4,5},{5,4},{6,7},{7,6},{8,9},{9,8},{10,11... | collective-permute-start | bytes 98312 | tf_op jit(solution)/shard_map/ppermute | solution.py:465
  15.1 16.7 %copy-start.1 = (f32[8,64,64]{2,1,0:T(8,128)S(1)}, f32[8,64,64]{2,1,0:T(8,128)}, u32[]{:S(2)}) copy-start(f32[8,64,64]{2,1,0:T(8,128)} %inverse_ref.1) | copy-start | bytes 393220
  15.2 6.3 %collective-permute-start.3 = (bf16[512,128]{1,0:T(8,128)(2,1)S(1)}, bf16[512,128]{1,0:T(8,128)(2,1)S(1)}, u32[]{:S(2)}, u32[]{:S(2)}) collective-permute-start(bf16[512,128]{1,0:T(8,128)(2,1)S(1)} %shard_map.93), channel_id=1, source_target_pairs={{0,2},{1,3},{2,0},{3,1},{4,6},{5,7},{6,4},{7,5},{8,10},{9,11},{10,... | collective-permute-start | bytes 393224 | tf_op jit(solution)/shard_map/ppermute | solution.py:465
  16.2 7.0 %collective-permute-start.8 = (bf16[80,128]{1,0:T(8,128)(2,1)S(1)}, bf16[80,128]{1,0:T(8,128)(2,1)S(1)}, u32[]{:S(2)}, u32[]{:S(2)}) collective-permute-start(bf16[80,128]{1,0:T(8,128)(2,1)S(1)} %shard_map.97), channel_id=1, source_target_pairs={{0,4},{4,0},{8,12},{12,8},{1,5},{5,1},{9,13},{13,9},{2,6},{6,2},{1... | collective-permute-start | bytes 61448 | tf_op jit(solution)/shard_map/ppermute | solution.py:465
  17.2 6.0 %collective-permute-start.7 = (bf16[80,128]{1,0:T(8,128)(2,1)S(1)}, bf16[80,128]{1,0:T(8,128)(2,1)S(1)}, u32[]{:S(2)}, u32[]{:S(2)}) collective-permute-start(bf16[80,128]{1,0:T(8,128)(2,1)S(1)} %shard_map.97), channel_id=1, source_target_pairs={{0,8},{4,12},{8,0},{12,4},{1,9},{5,13},{9,1},{13,5},{2,10},{6,14},... | collective-permute-start | bytes 61448 | tf_op jit(solution)/shard_map/ppermute | solution.py:465
  18.2 5.6 %collective-permute-start.6 = (bf16[80,128]{1,0:T(8,128)(2,1)S(1)}, bf16[80,128]{1,0:T(8,128)(2,1)S(1)}, u32[]{:S(2)}, u32[]{:S(2)}) collective-permute-start(bf16[80,128]{1,0:T(8,128)(2,1)S(1)} %shard_map.97), channel_id=1, source_target_pairs={{0,12},{4,8},{8,4},{12,0},{1,13},{5,9},{9,5},{13,1},{2,14},{6,10},... | collective-permute-start | bytes 61448 | tf_op jit(solution)/shard_map/ppermute | solution.py:465
  23.8 17.6 %all-to-all-start = ((bf16[16,128,128]{2,1,0:T(8,128)(2,1)}), bf16[16,128,128]{2,1,0:T(8,128)(2,1)S(1)}, u32[]{:S(2)}, u32[]{:S(2)}) async-start(bf16[16,128,128]{2,1,0:T(8,128)(2,1)} %shard_map.95), calls=%async_computation | async-start | bytes 1048576 | tf_op jit(solution)/shard_map/all_to_all | solution.py:32
  28.9 1.3 %collective-permute-start.9 = (bf16[1,4,80,128]{3,2,1,0:T(8,128)(2,1)S(1)}, bf16[1,4,80,128]{3,2,1,0:T(8,128)(2,1)S(1)}, u32[]{:S(2)}, u32[]{:S(2)}) collective-permute-start(bf16[1,4,80,128]{3,2,1,0:T(8,128)(2,1)S(1)} %maximum_bitcast_fusion), channel_id=1, source_target_pairs={{0,1},{1,0},{2,3},{3,2},{4,5},{5,4},{6,7},{7,6},{8,9},{9,8},{10,11... | collective-permute-start | bytes 245768 | tf_op jit(solution)/shard_map/ppermute | solution.py:465
  30.3 11.1 %collective-permute-start.10 = (bf16[2,4,80,128]{3,2,1,0:T(8,128)(2,1)S(1)}, bf16[2,4,80,128]{3,2,1,0:T(8,128)(2,1)S(1)}, u32[]{:S(2)}, u32[]{:S(2)}) collective-permute-start(bf16[2,4,80,128]{3,2,1,0:T(8,128)(2,1)S(1)} %pad_maximum_fusion.2), channel_id=1, source_target_pairs={{0,2},{1,3},{2,0},{3,1},{4,6},{5,7},{6,4},{7,5},{8,10},{9,11},{10,... | collective-permute-start | bytes 491528 | tf_op jit(solution)/shard_map/ppermute | solution.py:465

commit v15 on v12

--- a/solution.py
+++ b/solution.py
@@ -23,6 +23,15 @@
     return pltpu.with_memory_space_constraint(array, pltpu.HBM)
 
 
+def listed(owner, owners, first):
+    return (owner + owners - first) % owners
+
+
+def send_to_all(blocks, owners, shares, first):
+    members = [(i + first * shares) % (owners * shares) for i in range(owners * shares)]
+    return lax.all_to_all(blocks, ("expert", "proj"), 0, 0, tiled=True, axis_index_groups=[members])
+
+
 def split(value):
     high = value.astype(jnp.bfloat16)
     return high, (value - high.astype(jnp.float32)).astype(jnp.bfloat16)
@@ -44,6 +53,11 @@
         state[0] += 1
 
     return take
+
+
+def twice_transposed(projection):
+    once = jnp.transpose(projection.astype(jnp.float32))
+    return jnp.concatenate([once, once], axis=1).astype(jnp.bfloat16)
 
 
 def inner_kernel(
@@ -63,6 +77,7 @@
     take = in_order([pltpu.make_async_copy(*pair, sems.at[i]) for i, pair in enumerate(pairs)], 5)
     take()
     first = low_lanes(half, width)
+    weights = twice_transposed(in_proj_ref[...])
     for wire_ref in (leaving_ref, own_ref):
         take()
         if wire_ref is leaving_ref:
@@ -72,10 +87,9 @@
                 pair = jnp.concatenate([inverse_ref[e], inverse_ref[experts + e]], axis=1)
                 shared_ref[e * width : (e + 1) * width, :] = pair.astype(jnp.bfloat16)
         take()
-        twice = jnp.concatenate([in_proj_ref[...], in_proj_ref[...]], axis=0)
         g = 0 if wire_ref is leaving_ref else 2
         rows = act_ref[g : g + 2].reshape(2 * quarter, act_ref.shape[2])
-        inner = lax.dot_general(rows, twice, (((1,), (1,)), ((), ())), preferred_element_type=jnp.float32)
+        inner = jnp.dot(rows, weights, preferred_element_type=jnp.float32)
         for i in range(2):
             start = i * quarter
             high, low = split(jnp.where(first, inner[start : start + half], inner[start + half : start + quarter]))
@@ -117,6 +131,7 @@
     take = in_order([pltpu.make_async_copy(*pair, sems.at[i]) for i, pair in enumerate(pairs)], 3)
     take()
     first = low_lanes(chunk, width)
+    weights = twice_transposed(out_proj_ref[...])
 
     def pack_rows(i):
         g, part = i // split_by, i % split_by
@@ -129,10 +144,7 @@
 
     for i in range(chunks):
         take()
-        twice = jnp.concatenate([out_proj_ref[...], out_proj_ref[...]], axis=0)
-        rows_ref[i % 2] = lax.dot_general(
-            hidden_ref[i], twice, (((1,), (1,)), ((), ())), preferred_element_type=jnp.float32
-        )
+        rows_ref[i % 2] = jnp.dot(hidden_ref[i], weights, preferred_element_type=jnp.float32)
         if i:
             pack_rows(i - 1)
     pack_rows(chunks - 1)
@@ -270,7 +282,7 @@
         ).astype(jnp.bfloat16)
         share_width = result.shape[1] // shares
         for share in range(shares):
-            payload_ref[group * shares + share] = result[:, share * share_width : (share + 1) * share_width]
+            payload_ref[listed(group, groups, groups // 2) * shares + share] = result[:, share * share_width : (share + 1) * share_width]
         return carry
 
     lax.fori_loop(0, groups, one_group, 0, unroll=groups <= 4)
@@ -375,7 +387,7 @@
     for entry, (owner_turn, share_turn) in enumerate(turns):
         owner = jnp.bitwise_xor(lax.axis_index("expert"), owner_turn)
         share = jnp.bitwise_xor(lax.axis_index("proj"), share_turn)
-        outer.append(arrived_ref[owner * shares + share])
+        outer.append(arrived_ref[listed(owner, owners, owners // 2) * shares + share])
         docs.append(inner_ref[entry, width : width + 1, :].astype(jnp.float32).astype(jnp.int32))
         inner.append(inner_ref[entry, :width, :])
     outer = jnp.concatenate(outer, axis=0)
@@ -409,7 +421,7 @@
     for owner in range(owners):
         for share in range(shares):
             piece = result[owner * DOC_DEV : (owner + 1) * DOC_DEV, share * columns : (share + 1) * columns]
-            out_ref[owner * shares + share] = jnp.concatenate([piece, fill], axis=1)
+            out_ref[listed(owner, owners, owners - 1) * shares + share] = jnp.concatenate([piece, fill], axis=1)
 
 
 def score(arrived, inner, queries, turns, owners):
@@ -497,7 +509,7 @@
     quarter_routes = lax.dynamic_slice_in_dim(routes, lax.axis_index("proj") * quarter, quarter, 0)
     payload = condition(own, near, far, quarter_routes, weights, shares, width)
     payload, arriving = lax.optimization_barrier((payload, arriving))
-    arrived = lax.all_to_all(payload, ("expert", "proj"), 0, 0, tiled=True)
+    arrived = send_to_all(payload, owners, shares, owners // 2)
     inner = jnp.stack(arriving + [inner])
     inner, share_turns = inner[None], (0,)
     inner, share_turns = double(inner, share_turns, "proj", shares, 1)
@@ -507,7 +519,7 @@
     all_turns = tuple((o, p) for p in share_turns for o in owner_turns)
     queries = condition_queries(query_grads, inverse_in)
     pieces = score(arrived, inner, queries, all_turns, owners)
-    pieces = lax.all_to_all(pieces, ("expert", "proj"), 0, 0, tiled=True)
+    pieces = send_to_all(pieces, owners, shares, owners - 1)
     return sum_pieces(pieces, query_grads.shape[0] // shares).T
 
 

time: 60.5 us -> 57.5 us (0.950)
  blocking collectives: 10.8 us -> 9.13 us
  waiting for transfers between devices: 3.6 us -> 2.39 us
    all_to_all x1, blocking collectives: 10.8 us -> 9.13 us  [send_to_all(): lax.all_to_all(blocks, ('expert', 'proj'), 0, 0, tiled=True, axis_index_g...]
    all_to_all x1, waiting for transfers between devices: 1.51 us -> 0.01 us  [send_to_all(): lax.all_to_all(blocks, ('expert', 'proj'), 0, 0, tiled=True, axis_index_g...]
    all_to_all x1, starting transfers between devices: 4.23 us -> 5.14 us  [send_to_all(): lax.all_to_all(blocks, ('expert', 'proj'), 0, 0, tiled=True, axis_index_g...]
    ppermute x11, starting transfers between devices: 15 us -> 14.4 us  [exchange(): return lax.ppermute(block, axis, [(i, i ^ turn) for i in range(size)])]
  transfers between devices with their start and end apart: 12 -> 12, of which waited for: 4 -> 3; matrix products, arithmetic and copies ran while one was open for 0% -> 0% of each run, Pallas kernels for 27% -> 29%
where the time goes in v15:
time: 57.5 us; the launch traced here: 57.1 us
  Pallas kernels  25.7 us (45%)
  starting transfers between devices  19.5 us (34%)
  blocking collectives  9.13 us (16%)
  waiting for transfers between devices  2.39 us (4%)
    ppermute x11, starting transfers between devices, exchange(): return lax.ppermute(block, axis, [(i, i ^ turn) for i in range(size)])  14.4 us
    pallas_call x1, Pallas kernels, condition_queries(): pl.pallas_call(query_kernel, grid=(flat // LANES,), in_specs=[pl.BlockSpe...  9.52 us
    all_to_all x1, blocking collectives, send_to_all(): lax.all_to_all(blocks, ('expert', 'proj'), 0, 0, tiled=True, axis_index_g...  9.13 us
    pallas_call x1, Pallas kernels, score(): pl.pallas_call(functools.partial(score_kernel, width=width, doc_count=doc...  6.11 us
    all_to_all x1, starting transfers between devices, send_to_all(): lax.all_to_all(blocks, ('expert', 'proj'), 0, 0, tiled=True, axis_index_g...  5.14 us
    pallas_call x1, Pallas kernels, project_outer(): pl.pallas_call(functools.partial(outer_kernel, top=top), in_specs=[HBM] *...  4.25 us
    pallas_call x1, Pallas kernels, project_inner(): pl.pallas_call(inner_kernel, in_specs=[HBM] * 3, out_specs=[VMEM] * 3, ou...  2.58 us
    ppermute x11, waiting for transfers between devices, exchange(): return lax.ppermute(block, axis, [(i, i ^ turn) for i in range(size)])  2.39 us
  transfers between devices with their start and end apart: 12, of which 3 were waited for; matrix products, arithmetic and copies ran while one was open for 0% of the time, Pallas kernels for 29%

profile of v15, /device:TPU:0, one launch (start us, length us, event | category | flops | bytes accessed | tf_op | source)
XLA Modules:
  0.0 57.1 jit_solution(4700963342939384780)
XLA Ops:
  0.0 0.0 copy-start
  0.0 0.0 copy-start.2
  0.0 2.6 %shard_map.92 = (bf16[2,128,128]{2,1,0:T(8,128)(2,1)S(1)}, bf16[2,128,128]{2,1,0:T(8,128)(2,1)S(1)}, bf16[256,128]{1,0:T(8,128)(2,1)S(1)}) custom-call(bf16[512,1792]{1,0:T(8,128)(2,1)} %act_hbm.1, bf16[64,1792]{1,0:T(8,128)(2,1)} %in_proj_hbm.1, f32[8,64,64]{2,1,0:T(8,128)} %inverse_hbm.1), custom_call_target="tpu_custom_call" | custom-call | bytes 8250000 | tf_op jit(solution)/shard_map/pallas_call | solution.py:106
  2.6 3.0 %collective-permute-start.1 = (bf16[2,128,128]{2,1,0:T(8,128)(2,1)S(1)}, bf16[2,128,128]{2,1,0:T(8,128)(2,1)S(1)}, u32[]{:S(2)}, u32[]{:S(2)}) collective-permute-start(bf16[2,128,128]{2,1,0:T(8,128)(2,1)S(1)} %get-tuple-element.24), channel_id=1, source_target_pairs={{0,2},{1,3},{2,0},{3,1},{4,6},{5,7},{6,4},{7,5},{8,10},{9,11},{10,... | collective-permute-start | bytes 196616 | tf_op jit(solution)/shard_map/ppermute | solution.py:462
  5.6 2.6 %collective-permute-start = (bf16[256,128]{1,0:T(8,128)(2,1)S(1)}, bf16[256,128]{1,0:T(8,128)(2,1)S(1)}, u32[]{:S(2)}, u32[]{:S(2)}) collective-permute-start(bf16[256,128]{1,0:T(8,128)(2,1)S(1)} %get-tuple-element.23), channel_id=1, source_target_pairs={{0,8},{4,12},{8,0},{12,4},{1,9},{5,13},{9,1},{13,5},{2,10},{6,14},... | collective-permute-start | bytes 196616 | tf_op jit(solution)/shard_map/ppermute | solution.py:462
  8.2 4.2 %shard_map.91 = (bf16[2,512,128]{2,1,0:T(8,128)(2,1)S(1)}, bf16[2,512,128]{2,1,0:T(8,128)(2,1)S(1)}) custom-call(bf16[4096,512]{1,0:T(8,128)(2,1)} %bitcast.17, bf16[64,512]{1,0:T(8,128)(2,1)} %out_proj_hbm.1), custom_call_target="tpu_custom_call" | custom-call | bytes 13200000 | tf_op jit(solution)/shard_map/pallas_call | solution.py:157
  12.4 0.0 collective-permute-done.1.near_ref.first_ref
  12.5 0.0 collective-permute-done
  12.5 0.1 collective-permute-start.2
  12.6 1.6 %collective-permute-start.4 = (bf16[2,256,128]{2,1,0:T(8,128)(2,1)S(1)}, bf16[2,256,128]{2,1,0:T(8,128)(2,1)S(1)}, u32[]{:S(2)}, u32[]{:S(2)}) collective-permute-start(bf16[2,256,128]{2,1,0:T(8,128)(2,1)S(1)} %pad_maximum_fusion.3), channel_id=1, source_target_pairs={{0,4},{4,0},{8,12},{12,8},{1,5},{5,1},{9,13},{13,9},{2,6},{6,2},{1... | collective-permute-start | bytes 393224 | tf_op jit(solution)/shard_map/ppermute | solution.py:462
  14.2 0.3 collective-permute-start.5
  14.5 0.0 collective-permute-done.2.near_ref
  14.5 0.0 copy-start.1
  14.5 0.6 %collective-permute-start.3 = (bf16[512,128]{1,0:T(8,128)(2,1)S(1)}, bf16[512,128]{1,0:T(8,128)(2,1)S(1)}, u32[]{:S(2)}, u32[]{:S(2)}) collective-permute-start(bf16[512,128]{1,0:T(8,128)(2,1)S(1)} %shard_map.93), channel_id=1, source_target_pairs={{0,2},{1,3},{2,0},{3,1},{4,6},{5,7},{6,4},{7,5},{8,10},{9,11},{10,... | collective-permute-start | bytes 393224 | tf_op jit(solution)/shard_map/ppermute | solution.py:462
  15.1 0.0 copy-done
  15.2 0.1 copy.11.routes_ref
  15.3 0.2 collective-permute-done.5.second_ref
  15.5 0.0 copy-done.2
  15.5 0.1 shard_map.97
  15.6 1.0 %collective-permute-start.8 = (bf16[80,128]{1,0:T(8,128)(2,1)S(1)}, bf16[80,128]{1,0:T(8,128)(2,1)S(1)}, u32[]{:S(2)}, u32[]{:S(2)}) collective-permute-start(bf16[80,128]{1,0:T(8,128)(2,1)S(1)} %shard_map.97), channel_id=1, source_target_pairs={{0,4},{4,0},{8,12},{12,8},{1,5},{5,1},{9,13},{13,9},{2,6},{6,2},{1... | collective-permute-start | bytes 61448 | tf_op jit(solution)/shard_map/ppermute | solution.py:462
  16.6 1.4 %collective-permute-start.7 = (bf16[80,128]{1,0:T(8,128)(2,1)S(1)}, bf16[80,128]{1,0:T(8,128)(2,1)S(1)}, u32[]{:S(2)}, u32[]{:S(2)}) collective-permute-start(bf16[80,128]{1,0:T(8,128)(2,1)S(1)} %shard_map.97), channel_id=1, source_target_pairs={{0,8},{4,12},{8,0},{12,4},{1,9},{5,13},{9,1},{13,5},{2,10},{6,14},... | collective-permute-start | bytes 61448 | tf_op jit(solution)/shard_map/ppermute | solution.py:462
  18.0 2.1 %collective-permute-start.6 = (bf16[80,128]{1,0:T(8,128)(2,1)S(1)}, bf16[80,128]{1,0:T(8,128)(2,1)S(1)}, u32[]{:S(2)}, u32[]{:S(2)}) collective-permute-start(bf16[80,128]{1,0:T(8,128)(2,1)S(1)} %shard_map.97), channel_id=1, source_target_pairs={{0,12},{4,8},{8,4},{12,0},{1,13},{5,9},{9,5},{13,1},{2,14},{6,10},... | collective-permute-start | bytes 61448 | tf_op jit(solution)/shard_map/ppermute | solution.py:462
  20.1 0.0 collective-permute-done.4
  20.1 0.7 %shard_map.94.weights_ref = bf16[4,512,512]{2,1,0:T(8,128)(2,1)S(1)} custom-call(bf16[4,256,128]{2,1,0:T(8,128)(2,1)S(1)} %pad_maximum_fusion.1.shared_ref), custom_call_target="tpu_custom_call" | custom-call | bytes 4290000 | tf_op jit(solution)/shard_map/pallas_call | solution.py:240
  20.8 0.0 collective-permute-done.3.far_ref
  20.9 1.7 %shard_map.95 = bf16[16,128,128]{2,1,0:T(8,128)(2,1)} custom-call(bf16[2,512,128]{2,1,0:T(8,128)(2,1)S(1)} %get-tuple-element.22.own_ref, bf16[2,512,128]{2,1,0:T(8,128)(2,1)S(1)} %collective-permute-done.2.near_ref, bf16[512,128]{1,0:T(8,128)(2,1)S(1)} %collective-permute-done.3.far_ref, s32[128,8]{1,0:T(8,128)S(1)} %copy.11.routes_ref, ...), custom_call_target="tpu_custom_call" | custom-call | bytes 6600000 | tf_op jit(solution)/shard_map/pallas_call | solution.py:294
  22.6 0.0 collective-permute-done.8
  22.6 0.0 collective-permute-done.7
  22.6 1.0 %collective-permute-done.6 = bf16[80,128]{1,0:T(8,128)(2,1)S(1)} collective-permute-done((bf16[80,128]{1,0:T(8,128)(2,1)S(1)}, bf16[80,128]{1,0:T(8,128)(2,1)S(1)}, u32[]{:S(2)}, u32[]{:S(2)}) %collective-permute-start.6) | collective-permute-done | bytes 20512 | tf_op jit(solution)/shard_map/ppermute | solution.py:462
  23.6 5.1 %all-to-all-start = ((bf16[16,128,128]{2,1,0:T(8,128)(2,1)}), bf16[16,128,128]{2,1,0:T(8,128)(2,1)S(1)}, u32[]{:S(2)}, u32[]{:S(2)}) async-start(bf16[16,128,128]{2,1,0:T(8,128)(2,1)} %shard_map.95), calls=%async_computation | async-start | bytes 1048576 | tf_op jit(solution)/shard_map/all_to_all | solution.py:32
  28.7 0.2 collective-permute-start.9
  29.0 1.1 %collective-permute-done.9 = bf16[1,4,80,128]{3,2,1,0:T(8,128)(2,1)S(1)} collective-permute-done((bf16[1,4,80,128]{3,2,1,0:T(8,128)(2,1)S(1)}, bf16[1,4,80,128]{3,2,1,0:T(8,128)(2,1)S(1)}, u32[]{:S(2)}, u32[]{:S(2)}) %collective-permute-start.9) | collective-permute-done | bytes 81952 | tf_op jit(solution)/shard_map/ppermute | solution.py:462
  30.1 1.5 %collective-permute-start.10 = (bf16[2,4,80,128]{3,2,1,0:T(8,128)(2,1)S(1)}, bf16[2,4,80,128]{3,2,1,0:T(8,128)(2,1)S(1)}, u32[]{:S(2)}, u32[]{:S(2)}) collective-permute-start(bf16[2,4,80,128]{3,2,1,0:T(8,128)(2,1)S(1)} %pad_maximum_fusion.2), channel_id=1, source_target_pairs={{0,2},{1,3},{2,0},{3,1},{4,6},{5,7},{6,4},{7,5},{8,10},{9,11},{10,... | collective-permute-start | bytes 491528 | tf_op jit(solution)/shard_map/ppermute | solution.py:462
  31.6 0.0 copy-done.1
  31.6 9.5 %shard_map.98.far_ref = bf16[8192,256]{1,0:T(8,128)(2,1)} custom-call(bf16[256,8,1024]{2,1,0:T(8,128)(2,1)} %query_ref, f32[8,64,64]{2,1,0:T(8,128)S(1)} %copy-done.1), custom_call_target="tpu_custom_call" | custom-call | bytes 33000000 | tf_op jit(solution)/shard_map/pallas_call | solution.py:357
  41.2 0.0 collective-permute-done.10
  41.2 0.0 all-to-all-done.arrived_ref
  41.2 6.1 %shard_map.99 = f32[16,8,128]{2,1,0:T(8,128)S(1)} custom-call(bf16[16,128,128]{2,1,0:T(8,128)(2,1)S(1)} %all-to-all-done.arrived_ref, bf16[16,80,128]{2,1,0:T(8,128)(2,1)S(1)} %bitcast.12, bf16[8192,256]{1,0:T(8,128)(2,1)} %shard_map.98.far_ref), custom_call_target="tpu_custom_call" | custom-call | bytes 16500000 | tf_op jit(solution)/shard_map/pallas_call | solution.py:431
  47.3 9.1 %all_to_all.10.pieces_ref = f32[16,8,128]{2,1,0:T(8,128)S(1)} all-to-all(f32[16,8,128]{2,1,0:T(8,128)S(1)} %shard_map.99), channel_id=1, replica_groups={{12,13,14,15,0,1,2,3,4,5,6,7,8,9,10,11},{28,29,30,31,16,17,18,19,20,21,..., dimensions={0} | all-to-all | bytes 131072 | tf_op jit(solution)/shard_map/all_to_all | solution.py:32
  56.5 0.6 %shard_map.100 = f32[8,64]{1,0:T(8,128)} custom-call(f32[16,8,128]{2,1,0:T(8,128)S(1)} %all_to_all.10.pieces_ref), custom_call_target="tpu_custom_call" | custom-call | tf_op jit(solution)/shard_map/pallas_call | solution.py:453
  (8 shorter events, 0.2 us)
Async XLA Ops:
  0.0 15.1 %copy-start = (s32[512,8]{0,1:T(8,128)S(1)}, s32[512,8]{0,1:T(8,128)}, u32[]{:S(2)}) copy-start(s32[512,8]{0,1:T(8,128)} %param.11) | copy-start | bytes 49156
  0.0 15.5 %copy-start.2 = (s32[512]{0:T(512)S(1)}, s32[512]{0:T(512)}, u32[]{:S(2)}) copy-start(s32[512]{0:T(512)} %param.12) | copy-start | bytes 6148
  2.6 9.9 %collective-permute-start.1 = (bf16[2,128,128]{2,1,0:T(8,128)(2,1)S(1)}, bf16[2,128,128]{2,1,0:T(8,128)(2,1)S(1)}, u32[]{:S(2)}, u32[]{:S(2)}) collective-permute-start(bf16[2,128,128]{2,1,0:T(8,128)(2,1)S(1)} %get-tuple-element.24), channel_id=1, source_target_pairs={{0,2},{1,3},{2,0},{3,1},{4,6},{5,7},{6,4},{7,5},{8,10},{9,11},{10,... | collective-permute-start | bytes 196616 | tf_op jit(solution)/shard_map/ppermute | solution.py:462
  5.6 6.9 %collective-permute-start = (bf16[256,128]{1,0:T(8,128)(2,1)S(1)}, bf16[256,128]{1,0:T(8,128)(2,1)S(1)}, u32[]{:S(2)}, u32[]{:S(2)}) collective-permute-start(bf16[256,128]{1,0:T(8,128)(2,1)S(1)} %get-tuple-element.23), channel_id=1, source_target_pairs={{0,8},{4,12},{8,0},{12,4},{1,9},{5,13},{9,1},{13,5},{2,10},{6,14},... | collective-permute-start | bytes 196616 | tf_op jit(solution)/shard_map/ppermute | solution.py:462
  12.5 2.0 %collective-permute-start.2 = (bf16[2,512,128]{2,1,0:T(8,128)(2,1)S(1)}, bf16[2,512,128]{2,1,0:T(8,128)(2,1)S(1)}, u32[]{:S(2)}, u32[]{:S(2)}) collective-permute-start(bf16[2,512,128]{2,1,0:T(8,128)(2,1)S(1)} %get-tuple-element.26), channel_id=1, source_target_pairs={{0,1},{1,0},{2,3},{3,2},{4,5},{5,4},{6,7},{7,6},{8,9},{9,8},{10,11... | collective-permute-start | bytes 786440 | tf_op jit(solution)/shard_map/ppermute | solution.py:462
  12.6 7.5 %collective-permute-start.4 = (bf16[2,256,128]{2,1,0:T(8,128)(2,1)S(1)}, bf16[2,256,128]{2,1,0:T(8,128)(2,1)S(1)}, u32[]{:S(2)}, u32[]{:S(2)}) collective-permute-start(bf16[2,256,128]{2,1,0:T(8,128)(2,1)S(1)} %pad_maximum_fusion.3), channel_id=1, source_target_pairs={{0,4},{4,0},{8,12},{12,8},{1,5},{5,1},{9,13},{13,9},{2,6},{6,2},{1... | collective-permute-start | bytes 393224 | tf_op jit(solution)/shard_map/ppermute | solution.py:462
  14.2 1.3 %collective-permute-start.5 = (bf16[128,128]{1,0:T(8,128)(2,1)S(1)}, bf16[128,128]{1,0:T(8,128)(2,1)S(1)}, u32[]{:S(2)}, u32[]{:S(2)}) collective-permute-start(bf16[128,128]{1,0:T(8,128)(2,1)S(1)} %shard_map.96), channel_id=1, source_target_pairs={{0,1},{1,0},{2,3},{3,2},{4,5},{5,4},{6,7},{7,6},{8,9},{9,8},{10,11... | collective-permute-start | bytes 98312 | tf_op jit(solution)/shard_map/ppermute | solution.py:462
  14.5 17.1 %copy-start.1 = (f32[8,64,64]{2,1,0:T(8,128)S(1)}, f32[8,64,64]{2,1,0:T(8,128)}, u32[]{:S(2)}) copy-start(f32[8,64,64]{2,1,0:T(8,128)} %inverse_ref.1) | copy-start | bytes 393220
  14.5 6.3 %collective-permute-start.3 = (bf16[512,128]{1,0:T(8,128)(2,1)S(1)}, bf16[512,128]{1,0:T(8,128)(2,1)S(1)}, u32[]{:S(2)}, u32[]{:S(2)}) collective-permute-start(bf16[512,128]{1,0:T(8,128)(2,1)S(1)} %shard_map.93), channel_id=1, source_target_pairs={{0,2},{1,3},{2,0},{3,1},{4,6},{5,7},{6,4},{7,5},{8,10},{9,11},{10,... | collective-permute-start | bytes 393224 | tf_op jit(solution)/shard_map/ppermute | solution.py:462
  15.6 7.0 %collective-permute-start.8 = (bf16[80,128]{1,0:T(8,128)(2,1)S(1)}, bf16[80,128]{1,0:T(8,128)(2,1)S(1)}, u32[]{:S(2)}, u32[]{:S(2)}) collective-permute-start(bf16[80,128]{1,0:T(8,128)(2,1)S(1)} %shard_map.97), channel_id=1, source_target_pairs={{0,4},{4,0},{8,12},{12,8},{1,5},{5,1},{9,13},{13,9},{2,6},{6,2},{1... | collective-permute-start | bytes 61448 | tf_op jit(solution)/shard_map/ppermute | solution.py:462
  16.6 6.0 %collective-permute-start.7 = (bf16[80,128]{1,0:T(8,128)(2,1)S(1)}, bf16[80,128]{1,0:T(8,128)(2,1)S(1)}, u32[]{:S(2)}, u32[]{:S(2)}) collective-permute-start(bf16[80,128]{1,0:T(8,128)(2,1)S(1)} %shard_map.97), channel_id=1, source_target_pairs={{0,8},{4,12},{8,0},{12,4},{1,9},{5,13},{9,1},{13,5},{2,10},{6,14},... | collective-permute-start | bytes 61448 | tf_op jit(solution)/shard_map/ppermute | solution.py:462
  18.0 5.6 %collective-permute-start.6 = (bf16[80,128]{1,0:T(8,128)(2,1)S(1)}, bf16[80,128]{1,0:T(8,128)(2,1)S(1)}, u32[]{:S(2)}, u32[]{:S(2)}) collective-permute-start(bf16[80,128]{1,0:T(8,128)(2,1)S(1)} %shard_map.97), channel_id=1, source_target_pairs={{0,12},{4,8},{8,4},{12,0},{1,13},{5,9},{9,5},{13,1},{2,14},{6,10},... | collective-permute-start | bytes 61448 | tf_op jit(solution)/shard_map/ppermute | solution.py:462
  23.6 17.6 %all-to-all-start = ((bf16[16,128,128]{2,1,0:T(8,128)(2,1)}), bf16[16,128,128]{2,1,0:T(8,128)(2,1)S(1)}, u32[]{:S(2)}, u32[]{:S(2)}) async-start(bf16[16,128,128]{2,1,0:T(8,128)(2,1)} %shard_map.95), calls=%async_computation | async-start | bytes 1048576 | tf_op jit(solution)/shard_map/all_to_all | solution.py:32
  28.7 1.3 %collective-permute-start.9 = (bf16[1,4,80,128]{3,2,1,0:T(8,128)(2,1)S(1)}, bf16[1,4,80,128]{3,2,1,0:T(8,128)(2,1)S(1)}, u32[]{:S(2)}, u32[]{:S(2)}) collective-permute-start(bf16[1,4,80,128]{3,2,1,0:T(8,128)(2,1)S(1)} %maximum_bitcast_fusion), channel_id=1, source_target_pairs={{0,1},{1,0},{2,3},{3,2},{4,5},{5,4},{6,7},{7,6},{8,9},{9,8},{10,11... | collective-permute-start | bytes 245768 | tf_op jit(solution)/shard_map/ppermute | solution.py:462
  30.1 11.1 %collective-permute-start.10 = (bf16[2,4,80,128]{3,2,1,0:T(8,128)(2,1)S(1)}, bf16[2,4,80,128]{3,2,1,0:T(8,128)(2,1)S(1)}, u32[]{:S(2)}, u32[]{:S(2)}) collective-permute-start(bf16[2,4,80,128]{3,2,1,0:T(8,128)(2,1)S(1)} %pad_maximum_fusion.2), channel_id=1, source_target_pairs={{0,2},{1,3},{2,0},{3,1},{4,6},{5,7},{6,4},{7,5},{8,10},{9,11},{10,... | collective-permute-start | bytes 491528 | tf_op jit(solution)/shard_map/ppermute | solution.py:462

commit v16 on v15

--- a/solution.py
+++ b/solution.py
@@ -388,25 +388,38 @@
         owner = jnp.bitwise_xor(lax.axis_index("expert"), owner_turn)
         share = jnp.bitwise_xor(lax.axis_index("proj"), share_turn)
         outer.append(arrived_ref[listed(owner, owners, owners // 2) * shares + share])
-        docs.append(inner_ref[entry, width : width + 1, :].astype(jnp.float32).astype(jnp.int32))
+        docs.append(inner_ref[entry, width:, :].astype(jnp.float32).astype(jnp.int32))
         inner.append(inner_ref[entry, :width, :])
     outer = jnp.concatenate(outer, axis=0)
     inner = jnp.concatenate(inner, axis=1)
-    docs = jnp.broadcast_to(jnp.concatenate(docs, axis=1), inner.shape)
-    doc_group = 16
+    docs = jnp.concatenate(docs, axis=1)
+    odd = lax.dot_general(
+        (docs & 1).astype(jnp.float32).astype(jnp.bfloat16),
+        jnp.full((DOC_ROWS, lanes), 1 / DOC_ROWS, jnp.bfloat16),
+        (((0,), (0,)), ((), ())),
+        preferred_element_type=jnp.float32,
+    ).astype(jnp.bfloat16)
+    odd_outer = outer * odd
+    outer = jnp.concatenate([outer - odd_outer, odd_outer], axis=1)
+    pairs = jnp.broadcast_to(docs[:1] >> 1, inner.shape)
+    pair_group = min(16, doc_count // 2)
     pitch = grads_ref.shape[0] // doc_count
 
     def one_group(group, carry):
         masked = [
-            jnp.where(docs == group * doc_group + d, inner, jnp.zeros_like(inner)) for d in range(doc_group)
+            jnp.where(pairs == group * pair_group + p, inner, jnp.zeros_like(inner)) for p in range(pair_group)
         ]
         sums = jnp.dot(jnp.concatenate(masked, axis=0), outer, preferred_element_type=jnp.float32)
-        for d in range(doc_group):
-            start = pl.multiple_of((group * doc_group + d) * pitch, 8)
-            grads_ref[pl.ds(start, width), :] = sums[d * width : (d + 1) * width]
+        for p in range(pair_group):
+            for parity in range(2):
+                start = pl.multiple_of((2 * (group * pair_group + p) + parity) * pitch, 8)
+                grads_ref[pl.ds(start, width), :] = sums[
+                    p * width : (p + 1) * width, parity * lanes : (parity + 1) * lanes
+                ]
         return carry
 
-    lax.fori_loop(0, doc_count // doc_group, one_group, 0, unroll=doc_count <= 2 * doc_group)
+    groups = doc_count // (2 * pair_group)
+    lax.fori_loop(0, groups, one_group, 0, unroll=groups == 1)
     high, low = [], []
     for j in range(width):
         parts = split(grads_ref[pl.ds(j, doc_count, stride=pitch), :])

time: 57.5 us -> 57 us (level)
  Pallas kernels: 25.7 us -> 25.1 us
where the time goes in v16:
time: 57 us; the launch traced here: 56.5 us
  Pallas kernels  25.1 us (44%)
  starting transfers between devices  19.5 us (34%)
  blocking collectives  9.13 us (16%)
  waiting for transfers between devices  2.39 us (4%)
    ppermute x11, starting transfers between devices, exchange(): return lax.ppermute(block, axis, [(i, i ^ turn) for i in range(size)])  14.4 us
    pallas_call x1, Pallas kernels, condition_queries(): pl.pallas_call(query_kernel, grid=(flat // LANES,), in_specs=[pl.BlockSpe...  9.52 us
    all_to_all x1, blocking collectives, send_to_all(): lax.all_to_all(blocks, ('expert', 'proj'), 0, 0, tiled=True, axis_index_g...  9.13 us
    pallas_call x1, Pallas kernels, score(): pl.pallas_call(functools.partial(score_kernel, width=width, doc_count=doc...  5.55 us
    all_to_all x1, starting transfers between devices, send_to_all(): lax.all_to_all(blocks, ('expert', 'proj'), 0, 0, tiled=True, axis_index_g...  5.14 us
    pallas_call x1, Pallas kernels, project_outer(): pl.pallas_call(functools.partial(outer_kernel, top=top), in_specs=[HBM] *...  4.25 us
    pallas_call x1, Pallas kernels, project_inner(): pl.pallas_call(inner_kernel, in_specs=[HBM] * 3, out_specs=[VMEM] * 3, ou...  2.58 us
    ppermute x11, waiting for transfers between devices, exchange(): return lax.ppermute(block, axis, [(i, i ^ turn) for i in range(size)])  2.39 us
  transfers between devices with their start and end apart: 12, of which 3 were waited for; matrix products, arithmetic and copies ran while one was open for 0% of the time, Pallas kernels for 29%

profile of v16, /device:TPU:0, one launch (start us, length us, event | category | flops | bytes accessed | tf_op | source)
XLA Modules:
  0.0 56.5 jit_solution(11586642270139096162)
XLA Ops:
  0.0 0.0 copy-start
  0.0 0.0 copy-start.2
  0.0 2.6 %shard_map.92 = (bf16[2,128,128]{2,1,0:T(8,128)(2,1)S(1)}, bf16[2,128,128]{2,1,0:T(8,128)(2,1)S(1)}, bf16[256,128]{1,0:T(8,128)(2,1)S(1)}) custom-call(bf16[512,1792]{1,0:T(8,128)(2,1)} %act_hbm.1, bf16[64,1792]{1,0:T(8,128)(2,1)} %in_proj_hbm.1, f32[8,64,64]{2,1,0:T(8,128)} %inverse_hbm.1), custom_call_target="tpu_custom_call" | custom-call | bytes 8250000 | tf_op jit(solution)/shard_map/pallas_call | solution.py:106
  2.6 3.0 %collective-permute-start.1 = (bf16[2,128,128]{2,1,0:T(8,128)(2,1)S(1)}, bf16[2,128,128]{2,1,0:T(8,128)(2,1)S(1)}, u32[]{:S(2)}, u32[]{:S(2)}) collective-permute-start(bf16[2,128,128]{2,1,0:T(8,128)(2,1)S(1)} %get-tuple-element.24), channel_id=1, source_target_pairs={{0,2},{1,3},{2,0},{3,1},{4,6},{5,7},{6,4},{7,5},{8,10},{9,11},{10,... | collective-permute-start | bytes 196616 | tf_op jit(solution)/shard_map/ppermute | solution.py:475
  5.6 2.6 %collective-permute-start = (bf16[256,128]{1,0:T(8,128)(2,1)S(1)}, bf16[256,128]{1,0:T(8,128)(2,1)S(1)}, u32[]{:S(2)}, u32[]{:S(2)}) collective-permute-start(bf16[256,128]{1,0:T(8,128)(2,1)S(1)} %get-tuple-element.23), channel_id=1, source_target_pairs={{0,8},{4,12},{8,0},{12,4},{1,9},{5,13},{9,1},{13,5},{2,10},{6,14},... | collective-permute-start | bytes 196616 | tf_op jit(solution)/shard_map/ppermute | solution.py:475
  8.2 4.2 %shard_map.91 = (bf16[2,512,128]{2,1,0:T(8,128)(2,1)S(1)}, bf16[2,512,128]{2,1,0:T(8,128)(2,1)S(1)}) custom-call(bf16[4096,512]{1,0:T(8,128)(2,1)} %bitcast.17, bf16[64,512]{1,0:T(8,128)(2,1)} %out_proj_hbm.1), custom_call_target="tpu_custom_call" | custom-call | bytes 13200000 | tf_op jit(solution)/shard_map/pallas_call | solution.py:157
  12.4 0.0 collective-permute-done.1.near_ref.first_ref
  12.5 0.0 collective-permute-done
  12.5 0.1 collective-permute-start.2
  12.6 1.6 %collective-permute-start.4 = (bf16[2,256,128]{2,1,0:T(8,128)(2,1)S(1)}, bf16[2,256,128]{2,1,0:T(8,128)(2,1)S(1)}, u32[]{:S(2)}, u32[]{:S(2)}) collective-permute-start(bf16[2,256,128]{2,1,0:T(8,128)(2,1)S(1)} %pad_maximum_fusion.3), channel_id=1, source_target_pairs={{0,4},{4,0},{8,12},{12,8},{1,5},{5,1},{9,13},{13,9},{2,6},{6,2},{1... | collective-permute-start | bytes 393224 | tf_op jit(solution)/shard_map/ppermute | solution.py:475
  14.2 0.3 collective-permute-start.5
  14.5 0.0 collective-permute-done.2.near_ref
  14.5 0.0 copy-start.1
  14.5 0.6 %collective-permute-start.3 = (bf16[512,128]{1,0:T(8,128)(2,1)S(1)}, bf16[512,128]{1,0:T(8,128)(2,1)S(1)}, u32[]{:S(2)}, u32[]{:S(2)}) collective-permute-start(bf16[512,128]{1,0:T(8,128)(2,1)S(1)} %shard_map.93), channel_id=1, source_target_pairs={{0,2},{1,3},{2,0},{3,1},{4,6},{5,7},{6,4},{7,5},{8,10},{9,11},{10,... | collective-permute-start | bytes 393224 | tf_op jit(solution)/shard_map/ppermute | solution.py:475
  15.1 0.0 copy-done
  15.2 0.1 copy.11.routes_ref
  15.3 0.2 collective-permute-done.5.second_ref
  15.5 0.0 copy-done.2
  15.5 0.1 shard_map.97
  15.6 1.0 %collective-permute-start.8 = (bf16[80,128]{1,0:T(8,128)(2,1)S(1)}, bf16[80,128]{1,0:T(8,128)(2,1)S(1)}, u32[]{:S(2)}, u32[]{:S(2)}) collective-permute-start(bf16[80,128]{1,0:T(8,128)(2,1)S(1)} %shard_map.97), channel_id=1, source_target_pairs={{0,4},{4,0},{8,12},{12,8},{1,5},{5,1},{9,13},{13,9},{2,6},{6,2},{1... | collective-permute-start | bytes 61448 | tf_op jit(solution)/shard_map/ppermute | solution.py:475
  16.6 1.4 %collective-permute-start.7 = (bf16[80,128]{1,0:T(8,128)(2,1)S(1)}, bf16[80,128]{1,0:T(8,128)(2,1)S(1)}, u32[]{:S(2)}, u32[]{:S(2)}) collective-permute-start(bf16[80,128]{1,0:T(8,128)(2,1)S(1)} %shard_map.97), channel_id=1, source_target_pairs={{0,8},{4,12},{8,0},{12,4},{1,9},{5,13},{9,1},{13,5},{2,10},{6,14},... | collective-permute-start | bytes 61448 | tf_op jit(solution)/shard_map/ppermute | solution.py:475
  18.0 2.1 %collective-permute-start.6 = (bf16[80,128]{1,0:T(8,128)(2,1)S(1)}, bf16[80,128]{1,0:T(8,128)(2,1)S(1)}, u32[]{:S(2)}, u32[]{:S(2)}) collective-permute-start(bf16[80,128]{1,0:T(8,128)(2,1)S(1)} %shard_map.97), channel_id=1, source_target_pairs={{0,12},{4,8},{8,4},{12,0},{1,13},{5,9},{9,5},{13,1},{2,14},{6,10},... | collective-permute-start | bytes 61448 | tf_op jit(solution)/shard_map/ppermute | solution.py:475
  20.1 0.0 collective-permute-done.4
  20.1 0.7 %shard_map.94.weights_ref = bf16[4,512,512]{2,1,0:T(8,128)(2,1)S(1)} custom-call(bf16[4,256,128]{2,1,0:T(8,128)(2,1)S(1)} %pad_maximum_fusion.1.shared_ref), custom_call_target="tpu_custom_call" | custom-call | bytes 4290000 | tf_op jit(solution)/shard_map/pallas_call | solution.py:240
  20.8 0.0 collective-permute-done.3.far_ref
  20.9 1.7 %shard_map.95 = bf16[16,128,128]{2,1,0:T(8,128)(2,1)} custom-call(bf16[2,512,128]{2,1,0:T(8,128)(2,1)S(1)} %get-tuple-element.22.own_ref, bf16[2,512,128]{2,1,0:T(8,128)(2,1)S(1)} %collective-permute-done.2.near_ref, bf16[512,128]{1,0:T(8,128)(2,1)S(1)} %collective-permute-done.3.far_ref, s32[128,8]{1,0:T(8,128)S(1)} %copy.11.routes_ref, ...), custom_call_target="tpu_custom_call" | custom-call | bytes 6600000 | tf_op jit(solution)/shard_map/pallas_call | solution.py:294
  22.6 0.0 collective-permute-done.8
  22.6 0.0 collective-permute-done.7
  22.6 1.0 %collective-permute-done.6 = bf16[80,128]{1,0:T(8,128)(2,1)S(1)} collective-permute-done((bf16[80,128]{1,0:T(8,128)(2,1)S(1)}, bf16[80,128]{1,0:T(8,128)(2,1)S(1)}, u32[]{:S(2)}, u32[]{:S(2)}) %collective-permute-start.6) | collective-permute-done | bytes 20512 | tf_op jit(solution)/shard_map/ppermute | solution.py:475
  23.6 5.1 %all-to-all-start = ((bf16[16,128,128]{2,1,0:T(8,128)(2,1)}), bf16[16,128,128]{2,1,0:T(8,128)(2,1)S(1)}, u32[]{:S(2)}, u32[]{:S(2)}) async-start(bf16[16,128,128]{2,1,0:T(8,128)(2,1)} %shard_map.95), calls=%async_computation | async-start | bytes 1048576 | tf_op jit(solution)/shard_map/all_to_all | solution.py:32
  28.7 0.2 collective-permute-start.9
  29.0 1.1 %collective-permute-done.9 = bf16[1,4,80,128]{3,2,1,0:T(8,128)(2,1)S(1)} collective-permute-done((bf16[1,4,80,128]{3,2,1,0:T(8,128)(2,1)S(1)}, bf16[1,4,80,128]{3,2,1,0:T(8,128)(2,1)S(1)}, u32[]{:S(2)}, u32[]{:S(2)}) %collective-permute-start.9) | collective-permute-done | bytes 81952 | tf_op jit(solution)/shard_map/ppermute | solution.py:475
  30.1 1.5 %collective-permute-start.10 = (bf16[2,4,80,128]{3,2,1,0:T(8,128)(2,1)S(1)}, bf16[2,4,80,128]{3,2,1,0:T(8,128)(2,1)S(1)}, u32[]{:S(2)}, u32[]{:S(2)}) collective-permute-start(bf16[2,4,80,128]{3,2,1,0:T(8,128)(2,1)S(1)} %pad_maximum_fusion.2), channel_id=1, source_target_pairs={{0,2},{1,3},{2,0},{3,1},{4,6},{5,7},{6,4},{7,5},{8,10},{9,11},{10,... | collective-permute-start | bytes 491528 | tf_op jit(solution)/shard_map/ppermute | solution.py:475
  31.6 0.0 copy-done.1
  31.6 9.5 %shard_map.98.far_ref = bf16[8192,256]{1,0:T(8,128)(2,1)} custom-call(bf16[256,8,1024]{2,1,0:T(8,128)(2,1)} %query_ref, f32[8,64,64]{2,1,0:T(8,128)S(1)} %copy-done.1), custom_call_target="tpu_custom_call" | custom-call | bytes 33000000 | tf_op jit(solution)/shard_map/pallas_call | solution.py:357
  41.2 0.0 collective-permute-done.10
  41.2 0.0 all-to-all-done.arrived_ref
  41.2 5.5 %shard_map.99 = f32[16,8,128]{2,1,0:T(8,128)S(1)} custom-call(bf16[16,128,128]{2,1,0:T(8,128)(2,1)S(1)} %all-to-all-done.arrived_ref, bf16[16,80,128]{2,1,0:T(8,128)(2,1)S(1)} %bitcast.12, bf16[8192,256]{1,0:T(8,128)(2,1)} %shard_map.98.far_ref), custom_call_target="tpu_custom_call" | custom-call | bytes 16500000 | tf_op jit(solution)/shard_map/pallas_call | solution.py:444
  46.8 9.1 %all_to_all.10.pieces_ref = f32[16,8,128]{2,1,0:T(8,128)S(1)} all-to-all(f32[16,8,128]{2,1,0:T(8,128)S(1)} %shard_map.99), channel_id=1, replica_groups={{12,13,14,15,0,1,2,3,4,5,6,7,8,9,10,11},{28,29,30,31,16,17,18,19,20,21,..., dimensions={0} | all-to-all | bytes 131072 | tf_op jit(solution)/shard_map/all_to_all | solution.py:32
  55.9 0.6 %shard_map.100 = f32[8,64]{1,0:T(8,128)} custom-call(f32[16,8,128]{2,1,0:T(8,128)S(1)} %all_to_all.10.pieces_ref), custom_call_target="tpu_custom_call" | custom-call | tf_op jit(solution)/shard_map/pallas_call | solution.py:466
  (8 shorter events, 0.2 us)
Async XLA Ops:
  0.0 15.1 %copy-start = (s32[512,8]{0,1:T(8,128)S(1)}, s32[512,8]{0,1:T(8,128)}, u32[]{:S(2)}) copy-start(s32[512,8]{0,1:T(8,128)} %param.11) | copy-start | bytes 49156
  0.0 15.5 %copy-start.2 = (s32[512]{0:T(512)S(1)}, s32[512]{0:T(512)}, u32[]{:S(2)}) copy-start(s32[512]{0:T(512)} %param.12) | copy-start | bytes 6148
  2.6 9.9 %collective-permute-start.1 = (bf16[2,128,128]{2,1,0:T(8,128)(2,1)S(1)}, bf16[2,128,128]{2,1,0:T(8,128)(2,1)S(1)}, u32[]{:S(2)}, u32[]{:S(2)}) collective-permute-start(bf16[2,128,128]{2,1,0:T(8,128)(2,1)S(1)} %get-tuple-element.24), channel_id=1, source_target_pairs={{0,2},{1,3},{2,0},{3,1},{4,6},{5,7},{6,4},{7,5},{8,10},{9,11},{10,... | collective-permute-start | bytes 196616 | tf_op jit(solution)/shard_map/ppermute | solution.py:475
  5.6 6.9 %collective-permute-start = (bf16[256,128]{1,0:T(8,128)(2,1)S(1)}, bf16[256,128]{1,0:T(8,128)(2,1)S(1)}, u32[]{:S(2)}, u32[]{:S(2)}) collective-permute-start(bf16[256,128]{1,0:T(8,128)(2,1)S(1)} %get-tuple-element.23), channel_id=1, source_target_pairs={{0,8},{4,12},{8,0},{12,4},{1,9},{5,13},{9,1},{13,5},{2,10},{6,14},... | collective-permute-start | bytes 196616 | tf_op jit(solution)/shard_map/ppermute | solution.py:475
  12.5 2.0 %collective-permute-start.2 = (bf16[2,512,128]{2,1,0:T(8,128)(2,1)S(1)}, bf16[2,512,128]{2,1,0:T(8,128)(2,1)S(1)}, u32[]{:S(2)}, u32[]{:S(2)}) collective-permute-start(bf16[2,512,128]{2,1,0:T(8,128)(2,1)S(1)} %get-tuple-element.26), channel_id=1, source_target_pairs={{0,1},{1,0},{2,3},{3,2},{4,5},{5,4},{6,7},{7,6},{8,9},{9,8},{10,11... | collective-permute-start | bytes 786440 | tf_op jit(solution)/shard_map/ppermute | solution.py:475
  12.6 7.5 %collective-permute-start.4 = (bf16[2,256,128]{2,1,0:T(8,128)(2,1)S(1)}, bf16[2,256,128]{2,1,0:T(8,128)(2,1)S(1)}, u32[]{:S(2)}, u32[]{:S(2)}) collective-permute-start(bf16[2,256,128]{2,1,0:T(8,128)(2,1)S(1)} %pad_maximum_fusion.3), channel_id=1, source_target_pairs={{0,4},{4,0},{8,12},{12,8},{1,5},{5,1},{9,13},{13,9},{2,6},{6,2},{1... | collective-permute-start | bytes 393224 | tf_op jit(solution)/shard_map/ppermute | solution.py:475
  14.2 1.3 %collective-permute-start.5 = (bf16[128,128]{1,0:T(8,128)(2,1)S(1)}, bf16[128,128]{1,0:T(8,128)(2,1)S(1)}, u32[]{:S(2)}, u32[]{:S(2)}) collective-permute-start(bf16[128,128]{1,0:T(8,128)(2,1)S(1)} %shard_map.96), channel_id=1, source_target_pairs={{0,1},{1,0},{2,3},{3,2},{4,5},{5,4},{6,7},{7,6},{8,9},{9,8},{10,11... | collective-permute-start | bytes 98312 | tf_op jit(solution)/shard_map/ppermute | solution.py:475
  14.5 17.1 %copy-start.1 = (f32[8,64,64]{2,1,0:T(8,128)S(1)}, f32[8,64,64]{2,1,0:T(8,128)}, u32[]{:S(2)}) copy-start(f32[8,64,64]{2,1,0:T(8,128)} %inverse_ref.1) | copy-start | bytes 393220
  14.5 6.3 %collective-permute-start.3 = (bf16[512,128]{1,0:T(8,128)(2,1)S(1)}, bf16[512,128]{1,0:T(8,128)(2,1)S(1)}, u32[]{:S(2)}, u32[]{:S(2)}) collective-permute-start(bf16[512,128]{1,0:T(8,128)(2,1)S(1)} %shard_map.93), channel_id=1, source_target_pairs={{0,2},{1,3},{2,0},{3,1},{4,6},{5,7},{6,4},{7,5},{8,10},{9,11},{10,... | collective-permute-start | bytes 393224 | tf_op jit(solution)/shard_map/ppermute | solution.py:475
  15.6 7.0 %collective-permute-start.8 = (bf16[80,128]{1,0:T(8,128)(2,1)S(1)}, bf16[80,128]{1,0:T(8,128)(2,1)S(1)}, u32[]{:S(2)}, u32[]{:S(2)}) collective-permute-start(bf16[80,128]{1,0:T(8,128)(2,1)S(1)} %shard_map.97), channel_id=1, source_target_pairs={{0,4},{4,0},{8,12},{12,8},{1,5},{5,1},{9,13},{13,9},{2,6},{6,2},{1... | collective-permute-start | bytes 61448 | tf_op jit(solution)/shard_map/ppermute | solution.py:475
  16.6 6.0 %collective-permute-start.7 = (bf16[80,128]{1,0:T(8,128)(2,1)S(1)}, bf16[80,128]{1,0:T(8,128)(2,1)S(1)}, u32[]{:S(2)}, u32[]{:S(2)}) collective-permute-start(bf16[80,128]{1,0:T(8,128)(2,1)S(1)} %shard_map.97), channel_id=1, source_target_pairs={{0,8},{4,12},{8,0},{12,4},{1,9},{5,13},{9,1},{13,5},{2,10},{6,14},... | collective-permute-start | bytes 61448 | tf_op jit(solution)/shard_map/ppermute | solution.py:475
  18.0 5.6 %collective-permute-start.6 = (bf16[80,128]{1,0:T(8,128)(2,1)S(1)}, bf16[80,128]{1,0:T(8,128)(2,1)S(1)}, u32[]{:S(2)}, u32[]{:S(2)}) collective-permute-start(bf16[80,128]{1,0:T(8,128)(2,1)S(1)} %shard_map.97), channel_id=1, source_target_pairs={{0,12},{4,8},{8,4},{12,0},{1,13},{5,9},{9,5},{13,1},{2,14},{6,10},... | collective-permute-start | bytes 61448 | tf_op jit(solution)/shard_map/ppermute | solution.py:475
  23.6 17.6 %all-to-all-start = ((bf16[16,128,128]{2,1,0:T(8,128)(2,1)}), bf16[16,128,128]{2,1,0:T(8,128)(2,1)S(1)}, u32[]{:S(2)}, u32[]{:S(2)}) async-start(bf16[16,128,128]{2,1,0:T(8,128)(2,1)} %shard_map.95), calls=%async_computation | async-start | bytes 1048576 | tf_op jit(solution)/shard_map/all_to_all | solution.py:32
  28.7 1.3 %collective-permute-start.9 = (bf16[1,4,80,128]{3,2,1,0:T(8,128)(2,1)S(1)}, bf16[1,4,80,128]{3,2,1,0:T(8,128)(2,1)S(1)}, u32[]{:S(2)}, u32[]{:S(2)}) collective-permute-start(bf16[1,4,80,128]{3,2,1,0:T(8,128)(2,1)S(1)} %maximum_bitcast_fusion), channel_id=1, source_target_pairs={{0,1},{1,0},{2,3},{3,2},{4,5},{5,4},{6,7},{7,6},{8,9},{9,8},{10,11... | collective-permute-start | bytes 245768 | tf_op jit(solution)/shard_map/ppermute | solution.py:475
  30.1 11.1 %collective-permute-start.10 = (bf16[2,4,80,128]{3,2,1,0:T(8,128)(2,1)S(1)}, bf16[2,4,80,128]{3,2,1,0:T(8,128)(2,1)S(1)}, u32[]{:S(2)}, u32[]{:S(2)}) collective-permute-start(bf16[2,4,80,128]{3,2,1,0:T(8,128)(2,1)S(1)} %pad_maximum_fusion.2), channel_id=1, source_target_pairs={{0,2},{1,3},{2,0},{3,1},{4,6},{5,7},{6,4},{7,5},{8,10},{9,11},{10,... | collective-permute-start | bytes 491528 | tf_op jit(solution)/shard_map/ppermute | solution.py:475

commit v17 on v16

--- a/solution.py
+++ b/solution.py
@@ -215,24 +215,21 @@
 
 
 def expand_kernel(shared_ref, weights_ref, *, width, experts, shares, turns):
-    columns = experts * width
+    half = experts // 2
     share_rows = width // shares
-    half = experts // 2
+    columns = shares * half * share_rows
     lane = lax.broadcasted_iota(jnp.int32, (LANES, columns), 1)
     row = lax.broadcasted_iota(jnp.int32, (LANES, columns), 0)
-    source = lane // (experts * share_rows) * share_rows + lane % share_rows
-    expert_lane = lax.broadcasted_iota(jnp.int32, (half * width, columns), 1) // share_rows % experts
+    expert_lane = lax.broadcasted_iota(jnp.int32, (half * width, columns), 1) // share_rows % half
     expert_row = lax.broadcasted_iota(jnp.int32, (half * width, columns), 0) // width
+    own = expert_lane == expert_row
     for side in range(2):
+        share = jnp.bitwise_xor(lane // (half * share_rows), side)
+        source = share * share_rows + lane % share_rows
         spread = (row == source + side * width).astype(jnp.float32).astype(jnp.bfloat16)
-        own = expert_lane == expert_row + side * half
         for entry, turn in enumerate(turns):
-            placed = jnp.dot(
-                shared_ref[entry], spread, preferred_element_type=jnp.float32
-            )
-            weights_ref[turn, side * half * width : (side + 1) * half * width, :] = jnp.where(
-                own, placed, 0.0
-            ).astype(jnp.bfloat16)
+            placed = jnp.dot(shared_ref[entry], spread, preferred_element_type=jnp.float32)
+            weights_ref[turn, side] = jnp.where(own, placed, 0.0).astype(jnp.bfloat16)
 
 
 def expand(shared, turns, width, experts, shares):
@@ -240,7 +237,7 @@
     return pl.pallas_call(
         functools.partial(expand_kernel, width=width, experts=experts, shares=shares, turns=turns),
         in_specs=[VMEM],
-        out_shape=jax.ShapeDtypeStruct((owners, experts * width, experts * width), jnp.bfloat16),
+        out_shape=jax.ShapeDtypeStruct((owners, 2, experts // 2 * width, experts // 2 * width), jnp.bfloat16),
         compiler_params=pltpu.CompilerParams(vmem_limit_bytes=40 * MIB),
         cost_estimate=cost(1.3),
     )(shared)
@@ -250,9 +247,9 @@
     own_ref, near_ref, far_ref, routes_ref, weights_ref, payload_ref, value_ref, name_ref, *, top, width
 ):
     quarter = routes_ref.shape[0]
-    groups, dense_width, _ = weights_ref.shape
+    groups, sides, dense_width, _ = weights_ref.shape
     shares = payload_ref.shape[0] // groups
-    experts = dense_width // width
+    experts = sides * dense_width // width
     first = low_lanes(quarter, width)
     second = 1 - first.astype(jnp.int32)
 
@@ -268,6 +265,7 @@
         value_ref[2 * pair + 1] = jnp.where(first, swapped, both)
     for k in range(top):
         name_ref[k] = jnp.broadcast_to(routes_ref[:, k : k + 1], (quarter, LANES)) - second
+
     def one_group(step, carry):
         group = jnp.bitwise_xor(lax.axis_index("expert"), step)
         dense = []
@@ -277,12 +275,20 @@
             for k in range(top):
                 chosen = jnp.where(name_ref[k] == base, value_ref[k], chosen)
             dense.append(chosen.astype(jnp.bfloat16))
-        result = jnp.dot(
-            jnp.concatenate(dense, axis=1), weights_ref[step], preferred_element_type=jnp.float32
-        ).astype(jnp.bfloat16)
-        share_width = result.shape[1] // shares
+        per_side = len(dense) // sides
+        results = [
+            jnp.dot(
+                jnp.concatenate(dense[side * per_side : (side + 1) * per_side], axis=1),
+                weights_ref[step, side],
+                preferred_element_type=jnp.float32,
+            )
+            for side in range(sides)
+        ]
         for share in range(shares):
-            payload_ref[listed(group, groups, groups // 2) * shares + share] = result[:, share * share_width : (share + 1) * share_width]
+            lanes = slice(share // 2 * LANES, (share // 2 + 1) * LANES)
+            low, high = (results[side][:, lanes] for side in ((0, 1) if share % 2 == 0 else (1, 0)))
+            place = listed(group, groups, groups // 2) * shares + share
+            payload_ref[place] = jnp.where(first, low, high).astype(jnp.bfloat16)
         return carry
 
     lax.fori_loop(0, groups, one_group, 0, unroll=groups <= 4)
@@ -327,7 +333,8 @@
             factor_ref[e], query, (((1,), (1,)), ((), ())), preferred_element_type=jnp.float32
         )
         result = result[: 2 * width] + result[2 * width :]
-        start = e * (rows // experts) + 2 * step
+        slot = (e + experts // 2 * (lax.axis_index("proj") % 2)) % experts
+        start = slot * (rows // experts) + 2 * step
         for tile in range(wide_ref.shape[0]):
             part = result[:, tile * LANES : (tile + 1) * LANES]
             wide_ref[tile, pl.ds(start, width, stride=pitch), :] = part[:width]

time: 57 us -> 57 us (level)
  no operation moved by 1% of the time
where the time goes in v17:
time: 57 us; the launch traced here: 56.5 us
  Pallas kernels  24.8 us (44%)
  starting transfers between devices  19.5 us (34%)
  blocking collectives  9.07 us (16%)
  waiting for transfers between devices  2.72 us (5%)
    ppermute x11, starting transfers between devices, exchange(): return lax.ppermute(block, axis, [(i, i ^ turn) for i in range(size)])  14.4 us
    pallas_call x1, Pallas kernels, condition_queries(): pl.pallas_call(query_kernel, grid=(flat // LANES,), in_specs=[pl.BlockSpe...  9.59 us
    all_to_all x1, blocking collectives, send_to_all(): lax.all_to_all(blocks, ('expert', 'proj'), 0, 0, tiled=True, axis_index_g...  9.07 us
    pallas_call x1, Pallas kernels, score(): pl.pallas_call(functools.partial(score_kernel, width=width, doc_count=doc...  5.55 us
    all_to_all x1, starting transfers between devices, send_to_all(): lax.all_to_all(blocks, ('expert', 'proj'), 0, 0, tiled=True, axis_index_g...  5.14 us
    pallas_call x1, Pallas kernels, project_outer(): pl.pallas_call(functools.partial(outer_kernel, top=top), in_specs=[HBM] *...  4.25 us
    ppermute x11, waiting for transfers between devices, exchange(): return lax.ppermute(block, axis, [(i, i ^ turn) for i in range(size)])  2.72 us
    pallas_call x1, Pallas kernels, project_inner(): pl.pallas_call(inner_kernel, in_specs=[HBM] * 3, out_specs=[VMEM] * 3, ou...  2.58 us
  transfers between devices with their start and end apart: 12, of which 3 were waited for; matrix products, arithmetic and copies ran while one was open for 0% of the time, Pallas kernels for 29%

profile of v17, /device:TPU:0, one launch (start us, length us, event | category | flops | bytes accessed | tf_op | source)
XLA Modules:
  0.0 56.5 jit_solution(5700970737043249642)
XLA Ops:
  0.0 0.0 copy-start
  0.0 0.0 copy-start.2
  0.0 2.6 %shard_map.92 = (bf16[2,128,128]{2,1,0:T(8,128)(2,1)S(1)}, bf16[2,128,128]{2,1,0:T(8,128)(2,1)S(1)}, bf16[256,128]{1,0:T(8,128)(2,1)S(1)}) custom-call(bf16[512,1792]{1,0:T(8,128)(2,1)} %act_hbm.1, bf16[64,1792]{1,0:T(8,128)(2,1)} %in_proj_hbm.1, f32[8,64,64]{2,1,0:T(8,128)} %inverse_hbm.1), custom_call_target="tpu_custom_call" | custom-call | bytes 8250000 | tf_op jit(solution)/shard_map/pallas_call | solution.py:106
  2.6 3.0 %collective-permute-start.1 = (bf16[2,128,128]{2,1,0:T(8,128)(2,1)S(1)}, bf16[2,128,128]{2,1,0:T(8,128)(2,1)S(1)}, u32[]{:S(2)}, u32[]{:S(2)}) collective-permute-start(bf16[2,128,128]{2,1,0:T(8,128)(2,1)S(1)} %get-tuple-element.24), channel_id=1, source_target_pairs={{0,2},{1,3},{2,0},{3,1},{4,6},{5,7},{6,4},{7,5},{8,10},{9,11},{10,... | collective-permute-start | bytes 196616 | tf_op jit(solution)/shard_map/ppermute | solution.py:482
  5.6 2.6 %collective-permute-start = (bf16[256,128]{1,0:T(8,128)(2,1)S(1)}, bf16[256,128]{1,0:T(8,128)(2,1)S(1)}, u32[]{:S(2)}, u32[]{:S(2)}) collective-permute-start(bf16[256,128]{1,0:T(8,128)(2,1)S(1)} %get-tuple-element.23), channel_id=1, source_target_pairs={{0,8},{4,12},{8,0},{12,4},{1,9},{5,13},{9,1},{13,5},{2,10},{6,14},... | collective-permute-start | bytes 196616 | tf_op jit(solution)/shard_map/ppermute | solution.py:482
  8.2 4.2 %shard_map.91 = (bf16[2,512,128]{2,1,0:T(8,128)(2,1)S(1)}, bf16[2,512,128]{2,1,0:T(8,128)(2,1)S(1)}) custom-call(bf16[4096,512]{1,0:T(8,128)(2,1)} %bitcast.17, bf16[64,512]{1,0:T(8,128)(2,1)} %out_proj_hbm.1), custom_call_target="tpu_custom_call" | custom-call | bytes 13200000 | tf_op jit(solution)/shard_map/pallas_call | solution.py:157
  12.4 0.0 copy-start.1
  12.5 0.0 collective-permute-done.1.near_ref.first_ref
  12.5 0.0 collective-permute-done
  12.5 0.1 collective-permute-start.2
  12.6 1.6 %collective-permute-start.4 = (bf16[2,256,128]{2,1,0:T(8,128)(2,1)S(1)}, bf16[2,256,128]{2,1,0:T(8,128)(2,1)S(1)}, u32[]{:S(2)}, u32[]{:S(2)}) collective-permute-start(bf16[2,256,128]{2,1,0:T(8,128)(2,1)S(1)} %pad_maximum_fusion.3), channel_id=1, source_target_pairs={{0,4},{4,0},{8,12},{12,8},{1,5},{5,1},{9,13},{13,9},{2,6},{6,2},{1... | collective-permute-start | bytes 393224 | tf_op jit(solution)/shard_map/ppermute | solution.py:482
  14.2 0.3 collective-permute-start.5
  14.5 0.0 collective-permute-done.2.near_ref
  14.6 0.6 %collective-permute-start.3 = (bf16[512,128]{1,0:T(8,128)(2,1)S(1)}, bf16[512,128]{1,0:T(8,128)(2,1)S(1)}, u32[]{:S(2)}, u32[]{:S(2)}) collective-permute-start(bf16[512,128]{1,0:T(8,128)(2,1)S(1)} %shard_map.93), channel_id=1, source_target_pairs={{0,2},{1,3},{2,0},{3,1},{4,6},{5,7},{6,4},{7,5},{8,10},{9,11},{10,... | collective-permute-start | bytes 393224 | tf_op jit(solution)/shard_map/ppermute | solution.py:482
  15.2 0.0 copy-done
  15.2 0.1 copy.11.routes_ref
  15.3 0.2 collective-permute-done.5.second_ref
  15.5 0.0 copy-done.2
  15.5 0.1 shard_map.97
  15.6 1.0 %collective-permute-start.8 = (bf16[80,128]{1,0:T(8,128)(2,1)S(1)}, bf16[80,128]{1,0:T(8,128)(2,1)S(1)}, u32[]{:S(2)}, u32[]{:S(2)}) collective-permute-start(bf16[80,128]{1,0:T(8,128)(2,1)S(1)} %shard_map.97), channel_id=1, source_target_pairs={{0,4},{4,0},{8,12},{12,8},{1,5},{5,1},{9,13},{13,9},{2,6},{6,2},{1... | collective-permute-start | bytes 61448 | tf_op jit(solution)/shard_map/ppermute | solution.py:482
  16.6 1.4 %collective-permute-start.7 = (bf16[80,128]{1,0:T(8,128)(2,1)S(1)}, bf16[80,128]{1,0:T(8,128)(2,1)S(1)}, u32[]{:S(2)}, u32[]{:S(2)}) collective-permute-start(bf16[80,128]{1,0:T(8,128)(2,1)S(1)} %shard_map.97), channel_id=1, source_target_pairs={{0,8},{4,12},{8,0},{12,4},{1,9},{5,13},{9,1},{13,5},{2,10},{6,14},... | collective-permute-start | bytes 61448 | tf_op jit(solution)/shard_map/ppermute | solution.py:482
  18.0 2.1 %collective-permute-start.6 = (bf16[80,128]{1,0:T(8,128)(2,1)S(1)}, bf16[80,128]{1,0:T(8,128)(2,1)S(1)}, u32[]{:S(2)}, u32[]{:S(2)}) collective-permute-start(bf16[80,128]{1,0:T(8,128)(2,1)S(1)} %shard_map.97), channel_id=1, source_target_pairs={{0,12},{4,8},{8,4},{12,0},{1,13},{5,9},{9,5},{13,1},{2,14},{6,10},... | collective-permute-start | bytes 61448 | tf_op jit(solution)/shard_map/ppermute | solution.py:482
  20.1 0.0 collective-permute-done.4
  20.1 0.4 shard_map.94.weights_ref
  20.5 0.0 collective-permute-done.3.far_ref
  20.6 1.7 %shard_map.95 = bf16[16,128,128]{2,1,0:T(8,128)(2,1)} custom-call(bf16[2,512,128]{2,1,0:T(8,128)(2,1)S(1)} %get-tuple-element.22.own_ref, bf16[2,512,128]{2,1,0:T(8,128)(2,1)S(1)} %collective-permute-done.2.near_ref, bf16[512,128]{1,0:T(8,128)(2,1)S(1)} %collective-permute-done.3.far_ref, s32[128,8]{1,0:T(8,128)S(1)} %copy.11.routes_ref, ...), custom_call_target="tpu_custom_call" | custom-call | bytes 6600000 | tf_op jit(solution)/shard_map/pallas_call | solution.py:300
  22.2 0.0 collective-permute-done.8
  22.3 0.0 collective-permute-done.7
  22.3 1.3 %collective-permute-done.6 = bf16[80,128]{1,0:T(8,128)(2,1)S(1)} collective-permute-done((bf16[80,128]{1,0:T(8,128)(2,1)S(1)}, bf16[80,128]{1,0:T(8,128)(2,1)S(1)}, u32[]{:S(2)}, u32[]{:S(2)}) %collective-permute-start.6) | collective-permute-done | bytes 20512 | tf_op jit(solution)/shard_map/ppermute | solution.py:482
  23.6 5.1 %all-to-all-start = ((bf16[16,128,128]{2,1,0:T(8,128)(2,1)}), bf16[16,128,128]{2,1,0:T(8,128)(2,1)S(1)}, u32[]{:S(2)}, u32[]{:S(2)}) async-start(bf16[16,128,128]{2,1,0:T(8,128)(2,1)} %shard_map.95), calls=%async_computation | async-start | bytes 1048576 | tf_op jit(solution)/shard_map/all_to_all | solution.py:32
  28.7 0.2 collective-permute-start.9
  29.0 1.1 %collective-permute-done.9 = bf16[1,4,80,128]{3,2,1,0:T(8,128)(2,1)S(1)} collective-permute-done((bf16[1,4,80,128]{3,2,1,0:T(8,128)(2,1)S(1)}, bf16[1,4,80,128]{3,2,1,0:T(8,128)(2,1)S(1)}, u32[]{:S(2)}, u32[]{:S(2)}) %collective-permute-start.9) | collective-permute-done | bytes 81952 | tf_op jit(solution)/shard_map/ppermute | solution.py:482
  30.1 1.5 %collective-permute-start.10 = (bf16[2,4,80,128]{3,2,1,0:T(8,128)(2,1)S(1)}, bf16[2,4,80,128]{3,2,1,0:T(8,128)(2,1)S(1)}, u32[]{:S(2)}, u32[]{:S(2)}) collective-permute-start(bf16[2,4,80,128]{3,2,1,0:T(8,128)(2,1)S(1)} %pad_maximum_fusion.2), channel_id=1, source_target_pairs={{0,2},{1,3},{2,0},{3,1},{4,6},{5,7},{6,4},{7,5},{8,10},{9,11},{10,... | collective-permute-start | bytes 491528 | tf_op jit(solution)/shard_map/ppermute | solution.py:482
  31.6 0.0 copy-done.1
  31.6 9.6 %shard_map.98.far_ref = bf16[8192,256]{1,0:T(8,128)(2,1)} custom-call(bf16[256,8,1024]{2,1,0:T(8,128)(2,1)} %query_ref, f32[8,64,64]{2,1,0:T(8,128)S(1)} %copy-done.1), custom_call_target="tpu_custom_call" | custom-call | bytes 33000000 | tf_op jit(solution)/shard_map/pallas_call | solution.py:364
  41.2 0.0 collective-permute-done.10
  41.3 0.0 all-to-all-done.arrived_ref
  41.3 5.5 %shard_map.99 = f32[16,8,128]{2,1,0:T(8,128)S(1)} custom-call(bf16[16,128,128]{2,1,0:T(8,128)(2,1)S(1)} %all-to-all-done.arrived_ref, bf16[16,80,128]{2,1,0:T(8,128)(2,1)S(1)} %bitcast.12, bf16[8192,256]{1,0:T(8,128)(2,1)} %shard_map.98.far_ref), custom_call_target="tpu_custom_call" | custom-call | bytes 16500000 | tf_op jit(solution)/shard_map/pallas_call | solution.py:451
  46.8 9.1 %all_to_all.10.pieces_ref = f32[16,8,128]{2,1,0:T(8,128)S(1)} all-to-all(f32[16,8,128]{2,1,0:T(8,128)S(1)} %shard_map.99), channel_id=1, replica_groups={{12,13,14,15,0,1,2,3,4,5,6,7,8,9,10,11},{28,29,30,31,16,17,18,19,20,21,..., dimensions={0} | all-to-all | bytes 131072 | tf_op jit(solution)/shard_map/all_to_all | solution.py:32
  55.9 0.6 %shard_map.100 = f32[8,64]{1,0:T(8,128)} custom-call(f32[16,8,128]{2,1,0:T(8,128)S(1)} %all_to_all.10.pieces_ref), custom_call_target="tpu_custom_call" | custom-call | tf_op jit(solution)/shard_map/pallas_call | solution.py:473
  (8 shorter events, 0.2 us)
Async XLA Ops:
  0.0 15.2 %copy-start = (s32[512,8]{0,1:T(8,128)S(1)}, s32[512,8]{0,1:T(8,128)}, u32[]{:S(2)}) copy-start(s32[512,8]{0,1:T(8,128)} %param.11) | copy-start | bytes 49156
  0.0 15.5 %copy-start.2 = (s32[512]{0:T(512)S(1)}, s32[512]{0:T(512)}, u32[]{:S(2)}) copy-start(s32[512]{0:T(512)} %param.12) | copy-start | bytes 6148
  2.6 9.9 %collective-permute-start.1 = (bf16[2,128,128]{2,1,0:T(8,128)(2,1)S(1)}, bf16[2,128,128]{2,1,0:T(8,128)(2,1)S(1)}, u32[]{:S(2)}, u32[]{:S(2)}) collective-permute-start(bf16[2,128,128]{2,1,0:T(8,128)(2,1)S(1)} %get-tuple-element.24), channel_id=1, source_target_pairs={{0,2},{1,3},{2,0},{3,1},{4,6},{5,7},{6,4},{7,5},{8,10},{9,11},{10,... | collective-permute-start | bytes 196616 | tf_op jit(solution)/shard_map/ppermute | solution.py:482
  5.6 6.9 %collective-permute-start = (bf16[256,128]{1,0:T(8,128)(2,1)S(1)}, bf16[256,128]{1,0:T(8,128)(2,1)S(1)}, u32[]{:S(2)}, u32[]{:S(2)}) collective-permute-start(bf16[256,128]{1,0:T(8,128)(2,1)S(1)} %get-tuple-element.23), channel_id=1, source_target_pairs={{0,8},{4,12},{8,0},{12,4},{1,9},{5,13},{9,1},{13,5},{2,10},{6,14},... | collective-permute-start | bytes 196616 | tf_op jit(solution)/shard_map/ppermute | solution.py:482
  12.4 19.2 %copy-start.1 = (f32[8,64,64]{2,1,0:T(8,128)S(1)}, f32[8,64,64]{2,1,0:T(8,128)}, u32[]{:S(2)}) copy-start(f32[8,64,64]{2,1,0:T(8,128)} %inverse_ref.1) | copy-start | bytes 393220
  12.5 2.0 %collective-permute-start.2 = (bf16[2,512,128]{2,1,0:T(8,128)(2,1)S(1)}, bf16[2,512,128]{2,1,0:T(8,128)(2,1)S(1)}, u32[]{:S(2)}, u32[]{:S(2)}) collective-permute-start(bf16[2,512,128]{2,1,0:T(8,128)(2,1)S(1)} %get-tuple-element.26), channel_id=1, source_target_pairs={{0,1},{1,0},{2,3},{3,2},{4,5},{5,4},{6,7},{7,6},{8,9},{9,8},{10,11... | collective-permute-start | bytes 786440 | tf_op jit(solution)/shard_map/ppermute | solution.py:482
  12.6 7.5 %collective-permute-start.4 = (bf16[2,256,128]{2,1,0:T(8,128)(2,1)S(1)}, bf16[2,256,128]{2,1,0:T(8,128)(2,1)S(1)}, u32[]{:S(2)}, u32[]{:S(2)}) collective-permute-start(bf16[2,256,128]{2,1,0:T(8,128)(2,1)S(1)} %pad_maximum_fusion.3), channel_id=1, source_target_pairs={{0,4},{4,0},{8,12},{12,8},{1,5},{5,1},{9,13},{13,9},{2,6},{6,2},{1... | collective-permute-start | bytes 393224 | tf_op jit(solution)/shard_map/ppermute | solution.py:482
  14.2 1.3 %collective-permute-start.5 = (bf16[128,128]{1,0:T(8,128)(2,1)S(1)}, bf16[128,128]{1,0:T(8,128)(2,1)S(1)}, u32[]{:S(2)}, u32[]{:S(2)}) collective-permute-start(bf16[128,128]{1,0:T(8,128)(2,1)S(1)} %shard_map.96), channel_id=1, source_target_pairs={{0,1},{1,0},{2,3},{3,2},{4,5},{5,4},{6,7},{7,6},{8,9},{9,8},{10,11... | collective-permute-start | bytes 98312 | tf_op jit(solution)/shard_map/ppermute | solution.py:482
  14.6 6.0 %collective-permute-start.3 = (bf16[512,128]{1,0:T(8,128)(2,1)S(1)}, bf16[512,128]{1,0:T(8,128)(2,1)S(1)}, u32[]{:S(2)}, u32[]{:S(2)}) collective-permute-start(bf16[512,128]{1,0:T(8,128)(2,1)S(1)} %shard_map.93), channel_id=1, source_target_pairs={{0,2},{1,3},{2,0},{3,1},{4,6},{5,7},{6,4},{7,5},{8,10},{9,11},{10,... | collective-permute-start | bytes 393224 | tf_op jit(solution)/shard_map/ppermute | solution.py:482
  15.6 6.6 %collective-permute-start.8 = (bf16[80,128]{1,0:T(8,128)(2,1)S(1)}, bf16[80,128]{1,0:T(8,128)(2,1)S(1)}, u32[]{:S(2)}, u32[]{:S(2)}) collective-permute-start(bf16[80,128]{1,0:T(8,128)(2,1)S(1)} %shard_map.97), channel_id=1, source_target_pairs={{0,4},{4,0},{8,12},{12,8},{1,5},{5,1},{9,13},{13,9},{2,6},{6,2},{1... | collective-permute-start | bytes 61448 | tf_op jit(solution)/shard_map/ppermute | solution.py:482
  16.6 5.7 %collective-permute-start.7 = (bf16[80,128]{1,0:T(8,128)(2,1)S(1)}, bf16[80,128]{1,0:T(8,128)(2,1)S(1)}, u32[]{:S(2)}, u32[]{:S(2)}) collective-permute-start(bf16[80,128]{1,0:T(8,128)(2,1)S(1)} %shard_map.97), channel_id=1, source_target_pairs={{0,8},{4,12},{8,0},{12,4},{1,9},{5,13},{9,1},{13,5},{2,10},{6,14},... | collective-permute-start | bytes 61448 | tf_op jit(solution)/shard_map/ppermute | solution.py:482
  18.0 5.6 %collective-permute-start.6 = (bf16[80,128]{1,0:T(8,128)(2,1)S(1)}, bf16[80,128]{1,0:T(8,128)(2,1)S(1)}, u32[]{:S(2)}, u32[]{:S(2)}) collective-permute-start(bf16[80,128]{1,0:T(8,128)(2,1)S(1)} %shard_map.97), channel_id=1, source_target_pairs={{0,12},{4,8},{8,4},{12,0},{1,13},{5,9},{9,5},{13,1},{2,14},{6,10},... | collective-permute-start | bytes 61448 | tf_op jit(solution)/shard_map/ppermute | solution.py:482
  23.6 17.7 %all-to-all-start = ((bf16[16,128,128]{2,1,0:T(8,128)(2,1)}), bf16[16,128,128]{2,1,0:T(8,128)(2,1)S(1)}, u32[]{:S(2)}, u32[]{:S(2)}) async-start(bf16[16,128,128]{2,1,0:T(8,128)(2,1)} %shard_map.95), calls=%async_computation | async-start | bytes 1048576 | tf_op jit(solution)/shard_map/all_to_all | solution.py:32
  28.7 1.3 %collective-permute-start.9 = (bf16[1,4,80,128]{3,2,1,0:T(8,128)(2,1)S(1)}, bf16[1,4,80,128]{3,2,1,0:T(8,128)(2,1)S(1)}, u32[]{:S(2)}, u32[]{:S(2)}) collective-permute-start(bf16[1,4,80,128]{3,2,1,0:T(8,128)(2,1)S(1)} %maximum_bitcast_fusion), channel_id=1, source_target_pairs={{0,1},{1,0},{2,3},{3,2},{4,5},{5,4},{6,7},{7,6},{8,9},{9,8},{10,11... | collective-permute-start | bytes 245768 | tf_op jit(solution)/shard_map/ppermute | solution.py:482
  30.1 11.1 %collective-permute-start.10 = (bf16[2,4,80,128]{3,2,1,0:T(8,128)(2,1)S(1)}, bf16[2,4,80,128]{3,2,1,0:T(8,128)(2,1)S(1)}, u32[]{:S(2)}, u32[]{:S(2)}) collective-permute-start(bf16[2,4,80,128]{3,2,1,0:T(8,128)(2,1)S(1)} %pad_maximum_fusion.2), channel_id=1, source_target_pairs={{0,2},{1,3},{2,0},{3,1},{4,6},{5,7},{6,4},{7,5},{8,10},{9,11},{10,... | collective-permute-start | bytes 491528 | tf_op jit(solution)/shard_map/ppermute | solution.py:482

commit v18 on v17

--- a/solution.py
+++ b/solution.py
@@ -60,54 +60,50 @@
     return jnp.concatenate([once, once], axis=1).astype(jnp.bfloat16)
 
 
-def inner_kernel(
-    act_hbm, in_proj_hbm, inverse_hbm, leaving_ref, own_ref, shared_ref, act_ref, in_proj_ref, inverse_ref, sems
-):
-    turns = (2, 3, 1, 0)
-    quarter = act_ref.shape[1]
+def inner_kernel(act_hbm, in_proj_hbm, inverse_hbm, wire_ref, shared_ref, act_ref, in_proj_ref, inverse_ref, sems):
+    quarters, quarter, model = act_ref.shape
     width = in_proj_ref.shape[0]
     half = quarter // 2
-    place = lax.axis_index("proj")
     pairs = [(in_proj_hbm, in_proj_ref)]
-    for g, turn in enumerate(turns):
-        rows = pl.ds(pl.multiple_of(jnp.bitwise_xor(place, turn) * quarter, quarter), quarter)
-        pairs.append((act_hbm.at[rows], act_ref.at[g]))
-        if g == 0:
+    for q in range(quarters):
+        pairs.append((act_hbm.at[pl.ds(q * quarter, quarter)], act_ref.at[q]))
+        if q == 0:
             pairs.append((inverse_hbm, inverse_ref))
     take = in_order([pltpu.make_async_copy(*pair, sems.at[i]) for i, pair in enumerate(pairs)], 5)
     take()
     first = low_lanes(half, width)
     weights = twice_transposed(in_proj_ref[...])
-    for wire_ref in (leaving_ref, own_ref):
+    for q in range(0, quarters, 2):
         take()
-        if wire_ref is leaving_ref:
+        if q == 0:
             take()
             experts = inverse_ref.shape[0] // 2
             for e in range(experts):
                 pair = jnp.concatenate([inverse_ref[e], inverse_ref[experts + e]], axis=1)
                 shared_ref[e * width : (e + 1) * width, :] = pair.astype(jnp.bfloat16)
         take()
-        g = 0 if wire_ref is leaving_ref else 2
-        rows = act_ref[g : g + 2].reshape(2 * quarter, act_ref.shape[2])
+        rows = act_ref[q : q + 2].reshape(2 * quarter, model)
         inner = jnp.dot(rows, weights, preferred_element_type=jnp.float32)
         for i in range(2):
             start = i * quarter
             high, low = split(jnp.where(first, inner[start : start + half], inner[start + half : start + quarter]))
-            wire_ref[i, :half, :] = high
-            wire_ref[i, half:, :] = low
+            wire_ref[q + i, :half, :] = high
+            wire_ref[q + i, half:, :] = low
 
 
 def project_inner(activations, in_projection, inverse_out, quarters):
     tokens, model = activations.shape
     quarter = tokens // quarters
     experts, width, _ = inverse_out.shape
-    wire = jax.ShapeDtypeStruct((quarters // 2, quarter, LANES), jnp.bfloat16)
     fixed = (in_projection, inverse_out)
     return pl.pallas_call(
         inner_kernel,
         in_specs=[HBM] * 3,
-        out_specs=[VMEM] * 3,
-        out_shape=[wire, wire, jax.ShapeDtypeStruct((experts // 2 * width, LANES), jnp.bfloat16)],
+        out_specs=[VMEM] * 2,
+        out_shape=[
+            jax.ShapeDtypeStruct((quarters, quarter, LANES), jnp.bfloat16),
+            jax.ShapeDtypeStruct((experts // 2 * width, LANES), jnp.bfloat16),
+        ],
         scratch_shapes=[pltpu.VMEM((quarters, quarter, model), jnp.bfloat16)]
         + [pltpu.VMEM(array.shape, array.dtype) for array in fixed]
         + [pltpu.SemaphoreType.DMA((quarters + len(fixed),))],
@@ -175,43 +171,46 @@
     return rows[:half].astype(jnp.float32) + rows[half:].astype(jnp.float32)
 
 
-def combine_inner_kernel(own_ref, near_ref, out_ref):
-    high, low = split(exact_rows(own_ref[0]) + exact_rows(near_ref[1]))
-    out_ref[: high.shape[0], :] = high
-    out_ref[high.shape[0] :, :] = low
+def combine_inner_kernel(own_ref, other_ref, out_ref):
+    half = out_ref.shape[1] // 2
+    for q in range(out_ref.shape[0]):
+        high, low = split(exact_rows(own_ref[q]) + exact_rows(other_ref[q]))
+        out_ref[q, :half, :] = high
+        out_ref[q, half:, :] = low
 
 
 def combine_outer_kernel(own_ref, near_ref, out_ref):
     out_ref[...] = (own_ref[0].astype(jnp.float32) + near_ref[1].astype(jnp.float32)).astype(jnp.bfloat16)
 
 
-def combine(kernel, own, near):
+def combine(kernel, own, near, shape):
     return pl.pallas_call(
         kernel,
         in_specs=[VMEM, VMEM],
-        out_shape=jax.ShapeDtypeStruct(own.shape[1:], jnp.bfloat16),
+        out_shape=jax.ShapeDtypeStruct(shape, jnp.bfloat16),
         compiler_params=pltpu.CompilerParams(vmem_limit_bytes=40 * MIB),
         cost_estimate=cost(0.5),
     )(own, near)
 
 
-def finish_inner_kernel(own_ref, first_ref, second_ref, docs_ref, out_ref):
-    total = exact_rows(own_ref[1]) + exact_rows(first_ref[0]) + exact_rows(second_ref[...])
-    width = out_ref.shape[0] - DOC_ROWS
-    total = jnp.concatenate([total[:, :width], total[:, width:]], axis=0)
-    out_ref[:width, :] = jnp.transpose(total).astype(jnp.bfloat16)
-    docs = docs_ref[pl.ds(lax.axis_index("proj"), 1), :].astype(jnp.float32)
-    out_ref[width:, :] = jnp.broadcast_to(docs, (DOC_ROWS, LANES)).astype(jnp.bfloat16)
-
-
-def finish_inner(own, first, second, doc_rows, width):
+def finish_inner_kernel(own_ref, other_ref, docs_ref, out_ref):
+    width = out_ref.shape[1] - DOC_ROWS
+    for q in range(out_ref.shape[0]):
+        total = exact_rows(own_ref[q]) + exact_rows(other_ref[q])
+        total = jnp.concatenate([total[:, :width], total[:, width:]], axis=0)
+        out_ref[q, :width, :] = jnp.transpose(total).astype(jnp.bfloat16)
+        docs = docs_ref[q : q + 1, :].astype(jnp.float32)
+        out_ref[q, width:, :] = jnp.broadcast_to(docs, (DOC_ROWS, LANES)).astype(jnp.bfloat16)
+
+
+def finish_inner(own, other, doc_rows, width):
     return pl.pallas_call(
         finish_inner_kernel,
-        in_specs=[VMEM] * 4,
-        out_shape=jax.ShapeDtypeStruct((width + DOC_ROWS, own.shape[1]), jnp.bfloat16),
+        in_specs=[VMEM] * 3,
+        out_shape=jax.ShapeDtypeStruct((own.shape[0], width + DOC_ROWS, own.shape[1]), jnp.bfloat16),
         compiler_params=pltpu.CompilerParams(vmem_limit_bytes=40 * MIB),
         cost_estimate=cost(0.5),
-    )(own, first, second, doc_rows)
+    )(own, other, doc_rows)
 
 
 def expand_kernel(shared_ref, weights_ref, *, width, experts, shares, turns):
@@ -391,12 +390,14 @@
     shares = lax.axis_size("proj")
     owners = sources // shares
     outer, inner, docs = [], [], []
-    for entry, (owner_turn, share_turn) in enumerate(turns):
-        owner = jnp.bitwise_xor(lax.axis_index("expert"), owner_turn)
-        share = jnp.bitwise_xor(lax.axis_index("proj"), share_turn)
-        outer.append(arrived_ref[listed(owner, owners, owners // 2) * shares + share])
-        docs.append(inner_ref[entry, width:, :].astype(jnp.float32).astype(jnp.int32))
-        inner.append(inner_ref[entry, :width, :])
+    for t, turn in enumerate(turns):
+        for k in range(inner_ref.shape[1]):
+            away = k * shares + jnp.bitwise_xor(lax.axis_index("proj"), turn)
+            owner = jnp.bitwise_xor(lax.axis_index("expert"), away)
+            for q in range(shares):
+                outer.append(arrived_ref[listed(owner, owners, owners // 2) * shares + q])
+                docs.append(inner_ref[t, k, q, width:, :].astype(jnp.float32).astype(jnp.int32))
+                inner.append(inner_ref[t, k, q, :width, :])
     outer = jnp.concatenate(outer, axis=0)
     inner = jnp.concatenate(inner, axis=1)
     docs = jnp.concatenate(docs, axis=1)
@@ -446,7 +447,7 @@
 
 def score(arrived, inner, queries, turns, owners):
     sources = arrived.shape[0]
-    width = inner.shape[1] - DOC_ROWS
+    width = inner.shape[3] - DOC_ROWS
     doc_count = DOC_DEV * owners
     return pl.pallas_call(
         functools.partial(score_kernel, width=width, doc_count=doc_count, turns=turns),
@@ -504,41 +505,47 @@
     shares = lax.axis_size("proj")
     quarter = tokens // shares
     assert quarter == LANES and 2 * width == LANES and experts * width // shares == LANES
-    assert shares == 4 and owners & (owners - 1) == 0
+    assert shares == 4 and owners & (owners - 1) == 0 and owners >= shares
     assert DOC_DEV * owners <= 256
 
     flat_hidden = grad_hidden.reshape(tokens * top, grad_hidden.shape[2])
-    inner_leaving, inner_own, shared = project_inner(activations, in_projection, inverse_out, shares)
-    inner_first = exchange(inner_leaving, "proj", shares, 2)
+    inner_wire, shared = project_inner(activations, in_projection, inverse_out, shares)
+    inner_other = exchange(inner_wire, "proj", shares, 2)
     far_shared = exchange(shared, "expert", owners, owners // 2)
     leaving, own = project_outer(flat_hidden, out_projection, shares, top)
-    far_shared, inner_first, leaving = lax.optimization_barrier((far_shared, inner_first, leaving))
+    far_shared, inner_other, leaving = lax.optimization_barrier((far_shared, inner_other, leaving))
     near = exchange(leaving, "proj", shares, 1)
     shared, turns = jnp.stack([shared, far_shared]), (0, owners // 2)
     for bit in reversed(range((owners // 2).bit_length() - 1)):
         shared, turns = double(shared, turns, "expert", owners, 1 << bit)
-    inner_second = exchange(combine(combine_inner_kernel, inner_own, inner_first), "proj", shares, 1)
-    sent = combine(combine_outer_kernel, own, near)
+    inner_half = combine(combine_inner_kernel, inner_wire, inner_other, inner_wire.shape)
+    inner_other = exchange(inner_half, "proj", shares, 1)
+    sent = combine(combine_outer_kernel, own, near, own.shape[1:])
     far = exchange(sent, "proj", shares, 2)
-    inner = finish_inner(inner_own, inner_first, inner_second, doc_ids.reshape(shares, quarter), width)
+    inner = finish_inner(inner_half, inner_other, doc_ids.reshape(shares, quarter), width)
     inner, _ = lax.optimization_barrier((inner, sent))
-    owner_turns = tuple(reversed(range(owners)))
-    arriving = [exchange(inner, "expert", owners, turn) for turn in owner_turns if turn]
+    arriving = []
+    for k in range(owners // shares):
+        pairs = [
+            (o * shares + p, (o ^ (k * shares + p)) * shares + p)
+            for o in range(owners)
+            for p in range(shares)
+            if k or p
+        ]
+        arriving.append(lax.ppermute(inner, ("expert", "proj"), pairs))
     weights = expand(shared, turns, width, experts, shares)
     far, weights = lax.optimization_barrier((far, weights))
     quarter_routes = lax.dynamic_slice_in_dim(routes, lax.axis_index("proj") * quarter, quarter, 0)
     payload = condition(own, near, far, quarter_routes, weights, shares, width)
     payload, arriving = lax.optimization_barrier((payload, arriving))
     arrived = send_to_all(payload, owners, shares, owners // 2)
-    inner = jnp.stack(arriving + [inner])
-    inner, share_turns = inner[None], (0,)
+    arriving[0] = jnp.where(lax.axis_index("proj") == 0, inner, arriving[0])
+    inner, share_turns = jnp.stack(arriving)[None], (0,)
     inner, share_turns = double(inner, share_turns, "proj", shares, 1)
     inner, query_grads = lax.optimization_barrier((inner, query_grads))
     inner, share_turns = double(inner, share_turns, "proj", shares, 2)
-    inner = inner.reshape(owners * shares, width + DOC_ROWS, quarter)
-    all_turns = tuple((o, p) for p in share_turns for o in owner_turns)
     queries = condition_queries(query_grads, inverse_in)
-    pieces = score(arrived, inner, queries, all_turns, owners)
+    pieces = score(arrived, inner, queries, share_turns, owners)
     pieces = send_to_all(pieces, owners, shares, owners - 1)
     return sum_pieces(pieces, query_grads.shape[0] // shares).T
 

time: 57 us -> 57.6 us (1.011)
  waiting for transfers between devices: 2.72 us -> 4.26 us
  starting transfers between devices: 19.5 us -> 18.4 us
    ppermute x11 -> x8, starting transfers between devices: 14.4 us -> 10.2 us  [exchange(): return lax.ppermute(block, axis, [(i, i ^ turn) for i in range(size)])]
    all_to_all x1, starting transfers between devices: 5.14 us -> 7.58 us  [send_to_all(): lax.all_to_all(blocks, ('expert', 'proj'), 0, 0, tiled=True, axis_index_g...]
    ppermute x11 -> x8, waiting for transfers between devices: 2.72 us -> 4.26 us  [exchange(): return lax.ppermute(block, axis, [(i, i ^ turn) for i in range(size)])]
    ppermute x0 -> x1, starting transfers between devices: none -> 0.67 us  [local(): arriving.append(lax.ppermute(inner, ('expert', 'proj'), pairs))]
  transfers between devices with their start and end apart: 12 -> 10, of which waited for: 3 -> 3; matrix products, arithmetic and copies ran while one was open for 0% -> 0% of each run, Pallas kernels for 29% -> 28%
where the time goes in v18:
time: 57.6 us; the launch traced here: 57.1 us
  Pallas kernels  25 us (43%)
  starting transfers between devices  18.4 us (32%)
  blocking collectives  9.08 us (16%)
  waiting for transfers between devices  4.26 us (7%)
    ppermute x8, starting transfers between devices, exchange(): return lax.ppermute(block, axis, [(i, i ^ turn) for i in range(size)])  10.2 us
    pallas_call x1, Pallas kernels, condition_queries(): pl.pallas_call(query_kernel, grid=(flat // LANES,), in_specs=[pl.BlockSpe...  9.58 us
    all_to_all x1, blocking collectives, send_to_all(): lax.all_to_all(blocks, ('expert', 'proj'), 0, 0, tiled=True, axis_index_g...  9.08 us
    all_to_all x1, starting transfers between devices, send_to_all(): lax.all_to_all(blocks, ('expert', 'proj'), 0, 0, tiled=True, axis_index_g...  7.58 us
    pallas_call x1, Pallas kernels, score(): pl.pallas_call(functools.partial(score_kernel, width=width, doc_count=doc...  5.55 us
    ppermute x8, waiting for transfers between devices, exchange(): return lax.ppermute(block, axis, [(i, i ^ turn) for i in range(size)])  4.26 us
    pallas_call x1, Pallas kernels, project_outer(): pl.pallas_call(functools.partial(outer_kernel, top=top), in_specs=[HBM] *...  4.25 us
    pallas_call x1, Pallas kernels, project_inner(): pl.pallas_call(inner_kernel, in_specs=[HBM] * 3, out_specs=[VMEM] * 2, ou...  2.58 us
  transfers between devices with their start and end apart: 10, of which 3 were waited for; matrix products, arithmetic and copies ran while one was open for 0% of the time, Pallas kernels for 28%

profile of v18, /device:TPU:0, one launch (start us, length us, event | category | flops | bytes accessed | tf_op | source)
XLA Modules:
  0.0 57.1 jit_solution(17839384010419588595)
XLA Ops:
  0.0 0.0 copy-start
  0.0 0.0 copy-start.2
  0.0 2.6 %shard_map.92 = (bf16[4,128,128]{2,1,0:T(8,128)(2,1)S(1)}, bf16[256,128]{1,0:T(8,128)(2,1)S(1)}) custom-call(bf16[512,1792]{1,0:T(8,128)(2,1)} %act_hbm.1, bf16[64,1792]{1,0:T(8,128)(2,1)} %in_proj_hbm.1, f32[8,64,64]{2,1,0:T(8,128)} %inverse_hbm.1), custom_call_target="tpu_custom_call" | custom-call | bytes 8250000 | tf_op jit(solution)/shard_map/pallas_call | solution.py:99
  2.6 3.0 %collective-permute-start.1 = (bf16[4,128,128]{2,1,0:T(8,128)(2,1)S(1)}, bf16[4,128,128]{2,1,0:T(8,128)(2,1)S(1)}, u32[]{:S(2)}, u32[]{:S(2)}) collective-permute-start(bf16[4,128,128]{2,1,0:T(8,128)(2,1)S(1)} %get-tuple-element.21.own_ref), channel_id=1, source_target_pairs={{0,2},{1,3},{2,0},{3,1},{4,6},{5,7},{6,4},{7,5},{8,10},{9,11},{10,... | collective-permute-start | bytes 393224 | tf_op jit(solution)/shard_map/ppermute | solution.py:483
  5.6 2.6 %collective-permute-start = (bf16[256,128]{1,0:T(8,128)(2,1)S(1)}, bf16[256,128]{1,0:T(8,128)(2,1)S(1)}, u32[]{:S(2)}, u32[]{:S(2)}) collective-permute-start(bf16[256,128]{1,0:T(8,128)(2,1)S(1)} %get-tuple-element.20), channel_id=1, source_target_pairs={{0,8},{4,12},{8,0},{12,4},{1,9},{5,13},{9,1},{13,5},{2,10},{6,14},... | collective-permute-start | bytes 196616 | tf_op jit(solution)/shard_map/ppermute | solution.py:483
  8.2 4.2 %shard_map.91 = (bf16[2,512,128]{2,1,0:T(8,128)(2,1)S(1)}, bf16[2,512,128]{2,1,0:T(8,128)(2,1)S(1)}) custom-call(bf16[4096,512]{1,0:T(8,128)(2,1)} %bitcast.10, bf16[64,512]{1,0:T(8,128)(2,1)} %out_proj_hbm.1), custom_call_target="tpu_custom_call" | custom-call | bytes 13200000 | tf_op jit(solution)/shard_map/pallas_call | solution.py:153
  12.4 0.0 copy-start.1
  12.5 0.0 collective-permute-done
  12.5 0.0 collective-permute-done.1.other_ref
  12.5 0.1 collective-permute-start.2
  12.6 0.6 collective-permute-start.5
  13.2 1.6 %collective-permute-start.4 = (bf16[2,256,128]{2,1,0:T(8,128)(2,1)S(1)}, bf16[2,256,128]{2,1,0:T(8,128)(2,1)S(1)}, u32[]{:S(2)}, u32[]{:S(2)}) collective-permute-start(bf16[2,256,128]{2,1,0:T(8,128)(2,1)S(1)} %pad_maximum_fusion.3), channel_id=1, source_target_pairs={{0,4},{4,0},{8,12},{12,8},{1,5},{5,1},{9,13},{13,9},{2,6},{6,2},{1... | collective-permute-start | bytes 393224 | tf_op jit(solution)/shard_map/ppermute | solution.py:483
  14.8 0.0 collective-permute-done.2.near_ref
  14.9 0.6 %collective-permute-start.3 = (bf16[512,128]{1,0:T(8,128)(2,1)S(1)}, bf16[512,128]{1,0:T(8,128)(2,1)S(1)}, u32[]{:S(2)}, u32[]{:S(2)}) collective-permute-start(bf16[512,128]{1,0:T(8,128)(2,1)S(1)} %shard_map.93), channel_id=1, source_target_pairs={{0,2},{1,3},{2,0},{3,1},{4,6},{5,7},{6,4},{7,5},{8,10},{9,11},{10,... | collective-permute-start | bytes 393224 | tf_op jit(solution)/shard_map/ppermute | solution.py:483
  15.5 0.0 copy-done
  15.5 0.1 copy.11.routes_ref
  15.6 0.0 collective-permute-done.5.other_ref
  15.6 0.0 copy-done.2
  15.6 0.2 shard_map.97
  15.8 0.7 %collective-permute-start.6 = (bf16[4,80,128]{2,1,0:T(8,128)(2,1)S(1)}, bf16[4,80,128]{2,1,0:T(8,128)(2,1)S(1)}, u32[]{:S(2)}, u32[]{:S(2)}) collective-permute-start(bf16[4,80,128]{2,1,0:T(8,128)(2,1)S(1)} %shard_map.97), channel_id=1, source_target_pairs={{1,5},{2,10},{3,15},{5,1},{6,14},{7,11},{9,13},{10,2},{11,7},{13,9... | collective-permute-start | bytes 245768 | tf_op jit(solution)/shard_map/ppermute | solution.py:535
  16.5 2.2 %collective-permute-done.4 = bf16[2,256,128]{2,1,0:T(8,128)(2,1)S(1)} collective-permute-done((bf16[2,256,128]{2,1,0:T(8,128)(2,1)S(1)}, bf16[2,256,128]{2,1,0:T(8,128)(2,1)S(1)}, u32[]{:S(2)}, u32[]{:S(2)}) %collective-permute-start.4) | collective-permute-done | bytes 131104 | tf_op jit(solution)/shard_map/ppermute | solution.py:483
  18.7 0.4 shard_map.94.weights_ref
  19.1 0.9 %collective-permute-done.3.far_ref = bf16[512,128]{1,0:T(8,128)(2,1)S(1)} collective-permute-done((bf16[512,128]{1,0:T(8,128)(2,1)S(1)}, bf16[512,128]{1,0:T(8,128)(2,1)S(1)}, u32[]{:S(2)}, u32[]{:S(2)}) %collective-permute-start.3) | collective-permute-done | bytes 131104 | tf_op jit(solution)/shard_map/ppermute | solution.py:483
  20.1 1.7 %shard_map.95 = bf16[16,128,128]{2,1,0:T(8,128)(2,1)} custom-call(bf16[2,512,128]{2,1,0:T(8,128)(2,1)S(1)} %get-tuple-element.19.own_ref, bf16[2,512,128]{2,1,0:T(8,128)(2,1)S(1)} %collective-permute-done.2.near_ref, bf16[512,128]{1,0:T(8,128)(2,1)S(1)} %collective-permute-done.3.far_ref, s32[128,8]{1,0:T(8,128)S(1)} %copy.11.routes_ref, ...), custom_call_target="tpu_custom_call" | custom-call | bytes 6600000 | tf_op jit(solution)/shard_map/pallas_call | solution.py:299
  21.8 0.0 collective-permute-done.6
  21.8 7.6 %all-to-all-start = ((bf16[16,128,128]{2,1,0:T(8,128)(2,1)}), bf16[16,128,128]{2,1,0:T(8,128)(2,1)S(1)}, u32[]{:S(2)}, u32[]{:S(2)}) async-start(bf16[16,128,128]{2,1,0:T(8,128)(2,1)} %shard_map.95), calls=%async_computation | async-start | bytes 1048576 | tf_op jit(solution)/shard_map/all_to_all | solution.py:32
  29.4 0.2 collective-permute-start.7
  29.6 1.1 %collective-permute-done.7 = bf16[1,1,4,80,128]{4,3,2,1,0:T(8,128)(2,1)S(1)} collective-permute-done((bf16[1,1,4,80,128]{4,3,2,1,0:T(8,128)(2,1)S(1)}, bf16[1,1,4,80,128]{4,3,2,1,0:T(8,128)(2,1)S(1)}, u32[]{:S(2)}, u32[]{:S(2)}) %collective-permute-start.7) | collective-permute-done | bytes 81952 | tf_op jit(solution)/shard_map/ppermute | solution.py:483
  30.7 1.5 %collective-permute-start.8 = (bf16[2,1,4,80,128]{4,3,2,1,0:T(8,128)(2,1)S(1)}, bf16[2,1,4,80,128]{4,3,2,1,0:T(8,128)(2,1)S(1)}, u32[]{:S(2)}, u32[]{:S(2)}) collective-permute-start(bf16[2,1,4,80,128]{4,3,2,1,0:T(8,128)(2,1)S(1)} %pad_maximum_fusion.2), channel_id=1, source_target_pairs={{0,2},{1,3},{2,0},{3,1},{4,6},{5,7},{6,4},{7,5},{8,10},{9,11},{10,... | collective-permute-start | bytes 491528 | tf_op jit(solution)/shard_map/ppermute | solution.py:483
  32.3 0.0 copy-done.1
  32.3 9.6 %shard_map.98.far_ref = bf16[8192,256]{1,0:T(8,128)(2,1)} custom-call(bf16[256,8,1024]{2,1,0:T(8,128)(2,1)} %query_ref, f32[8,64,64]{2,1,0:T(8,128)S(1)} %copy-done.1), custom_call_target="tpu_custom_call" | custom-call | bytes 33000000 | tf_op jit(solution)/shard_map/pallas_call | solution.py:363
  41.8 0.0 collective-permute-done.8
  41.9 0.0 all-to-all-done.arrived_ref
  41.9 5.5 %shard_map.99 = f32[16,8,128]{2,1,0:T(8,128)S(1)} custom-call(bf16[16,128,128]{2,1,0:T(8,128)(2,1)S(1)} %all-to-all-done.arrived_ref, bf16[4,1,4,80,128]{4,3,2,1,0:T(8,128)(2,1)S(1)} %pad_maximum_fusion.inner_ref, bf16[8192,256]{1,0:T(8,128)(2,1)} %shard_map.98.far_ref), custom_call_target="tpu_custom_call" | custom-call | bytes 16500000 | tf_op jit(solution)/shard_map/pallas_call | solution.py:452
  47.5 9.1 %all_to_all.10.pieces_ref = f32[16,8,128]{2,1,0:T(8,128)S(1)} all-to-all(f32[16,8,128]{2,1,0:T(8,128)S(1)} %shard_map.99), channel_id=1, replica_groups={{12,13,14,15,0,1,2,3,4,5,6,7,8,9,10,11},{28,29,30,31,16,17,18,19,20,21,..., dimensions={0} | all-to-all | bytes 131072 | tf_op jit(solution)/shard_map/all_to_all | solution.py:32
  56.5 0.6 %shard_map.100 = f32[8,64]{1,0:T(8,128)} custom-call(f32[16,8,128]{2,1,0:T(8,128)S(1)} %all_to_all.10.pieces_ref), custom_call_target="tpu_custom_call" | custom-call | tf_op jit(solution)/shard_map/pallas_call | solution.py:474
  (8 shorter events, 0.2 us)
Async XLA Ops:
  0.0 15.5 %copy-start = (s32[512,8]{0,1:T(8,128)S(1)}, s32[512,8]{0,1:T(8,128)}, u32[]{:S(2)}) copy-start(s32[512,8]{0,1:T(8,128)} %param.11) | copy-start | bytes 49156
  0.0 15.6 %copy-start.2 = (s32[512]{0:T(512)S(1)}, s32[512]{0:T(512)}, u32[]{:S(2)}) copy-start(s32[512]{0:T(512)} %param.12) | copy-start | bytes 6148
  2.6 9.9 %collective-permute-start.1 = (bf16[4,128,128]{2,1,0:T(8,128)(2,1)S(1)}, bf16[4,128,128]{2,1,0:T(8,128)(2,1)S(1)}, u32[]{:S(2)}, u32[]{:S(2)}) collective-permute-start(bf16[4,128,128]{2,1,0:T(8,128)(2,1)S(1)} %get-tuple-element.21.own_ref), channel_id=1, source_target_pairs={{0,2},{1,3},{2,0},{3,1},{4,6},{5,7},{6,4},{7,5},{8,10},{9,11},{10,... | collective-permute-start | bytes 393224 | tf_op jit(solution)/shard_map/ppermute | solution.py:483
  5.6 6.9 %collective-permute-start = (bf16[256,128]{1,0:T(8,128)(2,1)S(1)}, bf16[256,128]{1,0:T(8,128)(2,1)S(1)}, u32[]{:S(2)}, u32[]{:S(2)}) collective-permute-start(bf16[256,128]{1,0:T(8,128)(2,1)S(1)} %get-tuple-element.20), channel_id=1, source_target_pairs={{0,8},{4,12},{8,0},{12,4},{1,9},{5,13},{9,1},{13,5},{2,10},{6,14},... | collective-permute-start | bytes 196616 | tf_op jit(solution)/shard_map/ppermute | solution.py:483
  12.4 19.8 %copy-start.1 = (f32[8,64,64]{2,1,0:T(8,128)S(1)}, f32[8,64,64]{2,1,0:T(8,128)}, u32[]{:S(2)}) copy-start(f32[8,64,64]{2,1,0:T(8,128)} %inverse_ref.1) | copy-start | bytes 393220
  12.5 2.4 %collective-permute-start.2 = (bf16[2,512,128]{2,1,0:T(8,128)(2,1)S(1)}, bf16[2,512,128]{2,1,0:T(8,128)(2,1)S(1)}, u32[]{:S(2)}, u32[]{:S(2)}) collective-permute-start(bf16[2,512,128]{2,1,0:T(8,128)(2,1)S(1)} %get-tuple-element.23), channel_id=1, source_target_pairs={{0,1},{1,0},{2,3},{3,2},{4,5},{5,4},{6,7},{7,6},{8,9},{9,8},{10,11... | collective-permute-start | bytes 786440 | tf_op jit(solution)/shard_map/ppermute | solution.py:483
  12.6 3.0 %collective-permute-start.5 = (bf16[4,128,128]{2,1,0:T(8,128)(2,1)S(1)}, bf16[4,128,128]{2,1,0:T(8,128)(2,1)S(1)}, u32[]{:S(2)}, u32[]{:S(2)}) collective-permute-start(bf16[4,128,128]{2,1,0:T(8,128)(2,1)S(1)} %shard_map.96.own_ref), channel_id=1, source_target_pairs={{0,1},{1,0},{2,3},{3,2},{4,5},{5,4},{6,7},{7,6},{8,9},{9,8},{10,11... | collective-permute-start | bytes 393224 | tf_op jit(solution)/shard_map/ppermute | solution.py:483
  13.2 5.5 %collective-permute-start.4 = (bf16[2,256,128]{2,1,0:T(8,128)(2,1)S(1)}, bf16[2,256,128]{2,1,0:T(8,128)(2,1)S(1)}, u32[]{:S(2)}, u32[]{:S(2)}) collective-permute-start(bf16[2,256,128]{2,1,0:T(8,128)(2,1)S(1)} %pad_maximum_fusion.3), channel_id=1, source_target_pairs={{0,4},{4,0},{8,12},{12,8},{1,5},{5,1},{9,13},{13,9},{2,6},{6,2},{1... | collective-permute-start | bytes 393224 | tf_op jit(solution)/shard_map/ppermute | solution.py:483
  14.9 5.2 %collective-permute-start.3 = (bf16[512,128]{1,0:T(8,128)(2,1)S(1)}, bf16[512,128]{1,0:T(8,128)(2,1)S(1)}, u32[]{:S(2)}, u32[]{:S(2)}) collective-permute-start(bf16[512,128]{1,0:T(8,128)(2,1)S(1)} %shard_map.93), channel_id=1, source_target_pairs={{0,2},{1,3},{2,0},{3,1},{4,6},{5,7},{6,4},{7,5},{8,10},{9,11},{10,... | collective-permute-start | bytes 393224 | tf_op jit(solution)/shard_map/ppermute | solution.py:483
  15.8 5.9 %collective-permute-start.6 = (bf16[4,80,128]{2,1,0:T(8,128)(2,1)S(1)}, bf16[4,80,128]{2,1,0:T(8,128)(2,1)S(1)}, u32[]{:S(2)}, u32[]{:S(2)}) collective-permute-start(bf16[4,80,128]{2,1,0:T(8,128)(2,1)S(1)} %shard_map.97), channel_id=1, source_target_pairs={{1,5},{2,10},{3,15},{5,1},{6,14},{7,11},{9,13},{10,2},{11,7},{13,9... | collective-permute-start | bytes 245768 | tf_op jit(solution)/shard_map/ppermute | solution.py:535
  21.8 20.1 %all-to-all-start = ((bf16[16,128,128]{2,1,0:T(8,128)(2,1)}), bf16[16,128,128]{2,1,0:T(8,128)(2,1)S(1)}, u32[]{:S(2)}, u32[]{:S(2)}) async-start(bf16[16,128,128]{2,1,0:T(8,128)(2,1)} %shard_map.95), calls=%async_computation | async-start | bytes 1048576 | tf_op jit(solution)/shard_map/all_to_all | solution.py:32
  29.4 1.3 %collective-permute-start.7 = (bf16[1,1,4,80,128]{4,3,2,1,0:T(8,128)(2,1)S(1)}, bf16[1,1,4,80,128]{4,3,2,1,0:T(8,128)(2,1)S(1)}, u32[]{:S(2)}, u32[]{:S(2)}) collective-permute-start(bf16[1,1,4,80,128]{4,3,2,1,0:T(8,128)(2,1)S(1)} %select_bitcast_fusion), channel_id=1, source_target_pairs={{0,1},{1,0},{2,3},{3,2},{4,5},{5,4},{6,7},{7,6},{8,9},{9,8},{10,11... | collective-permute-start | bytes 245768 | tf_op jit(solution)/shard_map/ppermute | solution.py:483
  30.7 11.1 %collective-permute-start.8 = (bf16[2,1,4,80,128]{4,3,2,1,0:T(8,128)(2,1)S(1)}, bf16[2,1,4,80,128]{4,3,2,1,0:T(8,128)(2,1)S(1)}, u32[]{:S(2)}, u32[]{:S(2)}) collective-permute-start(bf16[2,1,4,80,128]{4,3,2,1,0:T(8,128)(2,1)S(1)} %pad_maximum_fusion.2), channel_id=1, source_target_pairs={{0,2},{1,3},{2,0},{3,1},{4,6},{5,7},{6,4},{7,5},{8,10},{9,11},{10,... | collective-permute-start | bytes 491528 | tf_op jit(solution)/shard_map/ppermute | solution.py:483

commit v19 on v17

--- a/solution.py
+++ b/solution.py
@@ -10,6 +10,7 @@
 DOC_DEV = 8
 LANES = 128
 DOC_ROWS = 16
+DIAGONAL_ROWS = 16
 MIB = 1024 * 1024
 VMEM = pl.BlockSpec(memory_space=pltpu.VMEM)
 HBM = pl.BlockSpec(memory_space=pltpu.HBM)
@@ -60,8 +61,61 @@
     return jnp.concatenate([once, once], axis=1).astype(jnp.bfloat16)
 
 
+def triangles(width):
+    row = lax.broadcasted_iota(jnp.int32, (width, LANES), 0)
+    column = lax.broadcasted_iota(jnp.int32, (width, LANES), 1) % width
+    return row, column
+
+
+def pack_factors(inverse_ref, shared_ref):
+    experts, width, _ = inverse_ref.shape
+    quarter = experts // 4
+    row, column = triangles(width)
+    diagonals = []
+    for e in range(quarter):
+        lower, upper = (
+            jnp.concatenate([inverse_ref[first], inverse_ref[first + 2 * quarter]], axis=1) for first in (e, e + quarter)
+        )
+        shared_ref[e * width : (e + 1) * width, :] = jnp.where(row >= column, lower, upper).astype(jnp.bfloat16)
+        diagonals.append(jnp.sum(jnp.where(row == column, upper, 0.0), axis=0, keepdims=True))
+    fill = jnp.zeros((DIAGONAL_ROWS - quarter, LANES), jnp.float32)
+    shared_ref[quarter * width :, :] = jnp.concatenate(diagonals + [fill], axis=0).astype(jnp.bfloat16)
+
+
+def unpack_factors(packed, width, quarter):
+    row, column = triangles(width)
+    packed = packed.astype(jnp.float32)
+    lower, upper = [], []
+    for e in range(quarter):
+        square = packed[e * width : (e + 1) * width]
+        turned = jnp.transpose(square)
+        turned = jnp.concatenate([turned[:width], turned[width:]], axis=1)
+        diagonal = packed[quarter * width + e : quarter * width + e + 1]
+        lower.append(jnp.where(row >= column, square, turned))
+        upper.append(jnp.where(row == column, diagonal, jnp.where(row < column, square, turned)))
+    return jnp.concatenate(lower + upper, axis=0).astype(jnp.bfloat16)
+
+
+OUTER_TURNS = (1, 3, 2, 0)
+
+
+def quarter_rows(place, turn, rows):
+    return pl.ds(pl.multiple_of(jnp.bitwise_xor(place, turn) * rows, rows), rows)
+
+
 def inner_kernel(
-    act_hbm, in_proj_hbm, inverse_hbm, leaving_ref, own_ref, shared_ref, act_ref, in_proj_ref, inverse_ref, sems
+    act_hbm,
+    in_proj_hbm,
+    inverse_hbm,
+    hidden_hbm,
+    leaving_ref,
+    own_ref,
+    shared_ref,
+    hidden_ref,
+    act_ref,
+    in_proj_ref,
+    inverse_ref,
+    sems,
 ):
     turns = (2, 3, 1, 0)
     quarter = act_ref.shape[1]
@@ -74,7 +128,9 @@
         pairs.append((act_hbm.at[rows], act_ref.at[g]))
         if g == 0:
             pairs.append((inverse_hbm, inverse_ref))
-    take = in_order([pltpu.make_async_copy(*pair, sems.at[i]) for i, pair in enumerate(pairs)], 5)
+    for g in range(hidden_ref.shape[0]):
+        pairs.append((hidden_hbm.at[quarter_rows(place, OUTER_TURNS[g], hidden_ref.shape[1])], hidden_ref.at[g]))
+    take = in_order([pltpu.make_async_copy(*pair, sems.at[i]) for i, pair in enumerate(pairs)], 4)
     take()
     first = low_lanes(half, width)
     weights = twice_transposed(in_proj_ref[...])
@@ -82,10 +138,7 @@
         take()
         if wire_ref is leaving_ref:
             take()
-            experts = inverse_ref.shape[0] // 2
-            for e in range(experts):
-                pair = jnp.concatenate([inverse_ref[e], inverse_ref[experts + e]], axis=1)
-                shared_ref[e * width : (e + 1) * width, :] = pair.astype(jnp.bfloat16)
+            pack_factors(inverse_ref, shared_ref)
         take()
         g = 0 if wire_ref is leaving_ref else 2
         rows = act_ref[g : g + 2].reshape(2 * quarter, act_ref.shape[2])
@@ -95,9 +148,11 @@
             high, low = split(jnp.where(first, inner[start : start + half], inner[start + half : start + quarter]))
             wire_ref[i, :half, :] = high
             wire_ref[i, half:, :] = low
-
-
-def project_inner(activations, in_projection, inverse_out, quarters):
+    for _ in range(hidden_ref.shape[0]):
+        take()
+
+
+def project_inner(activations, in_projection, inverse_out, flat_hidden, quarters):
     tokens, model = activations.shape
     quarter = tokens // quarters
     experts, width, _ = inverse_out.shape
@@ -105,69 +160,69 @@
     fixed = (in_projection, inverse_out)
     return pl.pallas_call(
         inner_kernel,
-        in_specs=[HBM] * 3,
-        out_specs=[VMEM] * 3,
-        out_shape=[wire, wire, jax.ShapeDtypeStruct((experts // 2 * width, LANES), jnp.bfloat16)],
+        in_specs=[HBM] * 4,
+        out_specs=[VMEM] * 4,
+        out_shape=[
+            wire,
+            wire,
+            jax.ShapeDtypeStruct((experts // 4 * width + DIAGONAL_ROWS, LANES), jnp.bfloat16),
+            jax.ShapeDtypeStruct((quarters // 2, flat_hidden.shape[0] // quarters, flat_hidden.shape[1]), jnp.bfloat16),
+        ],
         scratch_shapes=[pltpu.VMEM((quarters, quarter, model), jnp.bfloat16)]
         + [pltpu.VMEM(array.shape, array.dtype) for array in fixed]
-        + [pltpu.SemaphoreType.DMA((quarters + len(fixed),))],
+        + [pltpu.SemaphoreType.DMA((quarters + len(fixed) + quarters // 2,))],
         compiler_params=pltpu.CompilerParams(vmem_limit_bytes=40 * MIB),
         cost_estimate=cost(2.5),
-    )(*[stay(array) for array in (activations, *fixed)])
-
-
-def outer_kernel(hidden_hbm, out_proj_hbm, leaving_ref, own_ref, hidden_ref, out_proj_ref, rows_ref, sems, *, top):
-    turns = (1, 3, 2, 0)
-    chunks, chunk_rows, _ = hidden_ref.shape
-    chunk = chunk_rows // top
-    split_by = chunks // len(turns)
-    quarter = chunk * split_by
+    )(*[stay(array) for array in (activations, *fixed, flat_hidden)])
+
+
+def outer_kernel(near_ref, hidden_hbm, out_proj_hbm, leaving_ref, own_ref, hidden_ref, out_proj_ref, rows_ref, sems, *, top):
+    ready, rows, _ = near_ref.shape
+    quarter = rows // top
     width = out_proj_ref.shape[0]
     place = lax.axis_index("proj")
     pairs = [(out_proj_hbm, out_proj_ref)]
-    for i in range(chunks):
-        start = (jnp.bitwise_xor(place, turns[i // split_by]) * split_by + i % split_by) * chunk_rows
-        pairs.append((hidden_hbm.at[pl.ds(pl.multiple_of(start, chunk_rows), chunk_rows)], hidden_ref.at[i]))
-    take = in_order([pltpu.make_async_copy(*pair, sems.at[i]) for i, pair in enumerate(pairs)], 3)
+    for i, turn in enumerate(OUTER_TURNS[ready:]):
+        pairs.append((hidden_hbm.at[quarter_rows(place, turn, rows)], hidden_ref.at[i]))
+    take = in_order([pltpu.make_async_copy(*pair, sems.at[i]) for i, pair in enumerate(pairs)], len(pairs))
     take()
-    first = low_lanes(chunk, width)
+    first = low_lanes(quarter, width)
     weights = twice_transposed(out_proj_ref[...])
 
-    def pack_rows(i):
-        g, part = i // split_by, i % split_by
+    def pack_rows(g):
         wire_ref = leaving_ref.at[g] if g < 2 else own_ref.at[g - 2]
         for pair in range(top // 2):
-            even = rows_ref[i % 2, pl.ds(2 * pair, chunk, stride=top), :]
-            odd = rows_ref[i % 2, pl.ds(2 * pair + 1, chunk, stride=top), :]
-            start = pair * quarter + part * chunk
-            wire_ref[start : start + chunk, :] = jnp.where(first, even, odd).astype(jnp.bfloat16)
-
-    for i in range(chunks):
-        take()
-        rows_ref[i % 2] = jnp.dot(hidden_ref[i], weights, preferred_element_type=jnp.float32)
-        if i:
-            pack_rows(i - 1)
-    pack_rows(chunks - 1)
-
-
-def project_outer(flat_hidden, out_projection, quarters, top):
+            even = rows_ref[g % 2, pl.ds(2 * pair, quarter, stride=top), :]
+            odd = rows_ref[g % 2, pl.ds(2 * pair + 1, quarter, stride=top), :]
+            wire_ref[pair * quarter : (pair + 1) * quarter, :] = jnp.where(first, even, odd).astype(jnp.bfloat16)
+
+    for g in range(len(OUTER_TURNS)):
+        if g >= ready:
+            take()
+        hidden = near_ref[g] if g < ready else hidden_ref[g - ready]
+        rows_ref[g % 2] = jnp.dot(hidden, weights, preferred_element_type=jnp.float32)
+        if g:
+            pack_rows(g - 1)
+    pack_rows(len(OUTER_TURNS) - 1)
+
+
+def project_outer(near_hidden, flat_hidden, out_projection, quarters, top):
     rows, hidden = flat_hidden.shape
-    chunks = quarters
     wire = jax.ShapeDtypeStruct((quarters // 2, rows // quarters // 2, LANES), jnp.bfloat16)
     return pl.pallas_call(
         functools.partial(outer_kernel, top=top),
-        in_specs=[HBM] * 2,
+        in_specs=[VMEM, HBM, HBM],
         out_specs=[VMEM] * 2,
         out_shape=[wire, wire],
         scratch_shapes=[
-            pltpu.VMEM((chunks, rows // chunks, hidden), jnp.bfloat16),
+            pltpu.VMEM((quarters // 2, rows // quarters, hidden), jnp.bfloat16),
             pltpu.VMEM(out_projection.shape, out_projection.dtype),
-            pltpu.VMEM((2, rows // chunks, LANES), jnp.float32),
-            pltpu.SemaphoreType.DMA((chunks + 1,)),
+            pltpu.VMEM((2, rows // quarters, LANES), jnp.float32),
+            pltpu.SemaphoreType.DMA((quarters // 2 + 1,)),
         ],
         compiler_params=pltpu.CompilerParams(vmem_limit_bytes=40 * MIB),
         cost_estimate=cost(4),
-    )(stay(flat_hidden), stay(out_projection))
+    )(near_hidden, stay(flat_hidden), stay(out_projection))
 
 
 def exact_rows(rows):
@@ -223,13 +278,14 @@
     expert_lane = lax.broadcasted_iota(jnp.int32, (half * width, columns), 1) // share_rows % half
     expert_row = lax.broadcasted_iota(jnp.int32, (half * width, columns), 0) // width
     own = expert_lane == expert_row
+    factors = [unpack_factors(shared_ref[entry], width, half // 2) for entry in range(len(turns))]
     for side in range(2):
         share = jnp.bitwise_xor(lane // (half * share_rows), side)
         source = share * share_rows + lane % share_rows
         spread = (row == source + side * width).astype(jnp.float32).astype(jnp.bfloat16)
         for entry, turn in enumerate(turns):
-            placed = jnp.dot(shared_ref[entry], spread, preferred_element_type=jnp.float32)
-            weights_ref[turn, side] = jnp.where(own, placed, 0.0).astype(jnp.bfloat16)
+            placed = jnp.dot(factors[entry], spread, preferred_element_type=jnp.float32)
+            weights_ref[turn // 2, side] = jnp.where(own, placed, 0.0).astype(jnp.bfloat16)
 
 
 def expand(shared, turns, width, experts, shares):
@@ -239,15 +295,16 @@
         in_specs=[VMEM],
         out_shape=jax.ShapeDtypeStruct((owners, 2, experts // 2 * width, experts // 2 * width), jnp.bfloat16),
         compiler_params=pltpu.CompilerParams(vmem_limit_bytes=40 * MIB),
-        cost_estimate=cost(1.3),
+        cost_estimate=cost(1),
     )(shared)
 
 
 def condition_kernel(
-    own_ref, near_ref, far_ref, routes_ref, weights_ref, payload_ref, value_ref, name_ref, *, top, width
+    own_ref, near_ref, far_ref, routes_ref, even_ref, odd_ref, payload_ref, value_ref, name_ref, *, top, width
 ):
     quarter = routes_ref.shape[0]
-    groups, sides, dense_width, _ = weights_ref.shape
+    pairs, sides, dense_width, _ = even_ref.shape
+    groups = 2 * pairs
     shares = payload_ref.shape[0] // groups
     experts = sides * dense_width // width
     first = low_lanes(quarter, width)
@@ -266,8 +323,9 @@
     for k in range(top):
         name_ref[k] = jnp.broadcast_to(routes_ref[:, k : k + 1], (quarter, LANES)) - second
 
-    def one_group(step, carry):
-        group = jnp.bitwise_xor(lax.axis_index("expert"), step)
+    def one_group(step, carry, parity):
+        weights_ref = odd_ref if parity else even_ref
+        group = jnp.bitwise_xor(lax.axis_index("expert"), 2 * step + parity)
         dense = []
         for pair in range(experts // 2):
             base = group * experts + 2 * pair
@@ -291,15 +349,16 @@
             payload_ref[place] = jnp.where(first, low, high).astype(jnp.bfloat16)
         return carry
 
-    lax.fori_loop(0, groups, one_group, 0, unroll=groups <= 4)
-
-
-def condition(own, near, far, quarter_routes, weights, shares, width):
+    for parity in range(2):
+        lax.fori_loop(0, pairs, functools.partial(one_group, parity=parity), 0, unroll=pairs <= 2)
+
+
+def condition(own, near, far, quarter_routes, even, odd, shares, width):
     quarter, top = quarter_routes.shape
-    groups = weights.shape[0]
+    groups = 2 * even.shape[0]
     return pl.pallas_call(
         functools.partial(condition_kernel, top=top, width=width),
-        in_specs=[VMEM] * 5,
+        in_specs=[VMEM] * 6,
         out_shape=jax.ShapeDtypeStruct((groups * shares, quarter, LANES), jnp.bfloat16),
         scratch_shapes=[
             pltpu.VMEM((top, quarter, LANES), jnp.float32),
@@ -307,7 +366,7 @@
         ],
         compiler_params=pltpu.CompilerParams(vmem_limit_bytes=40 * MIB),
         cost_estimate=cost(2),
-    )(own, near, far, quarter_routes, weights)
+    )(own, near, far, quarter_routes, even, odd)
 
 
 def query_kernel(query_ref, inverse_ref, out_hbm, factor_ref, spread_ref, wide_ref, out_ref, sems):
@@ -504,19 +563,25 @@
     shares = lax.axis_size("proj")
     quarter = tokens // shares
     assert quarter == LANES and 2 * width == LANES and experts * width // shares == LANES
+    assert experts % 4 == 0 and experts // 4 <= DIAGONAL_ROWS
     assert shares == 4 and owners & (owners - 1) == 0
     assert DOC_DEV * owners <= 256
 
     flat_hidden = grad_hidden.reshape(tokens * top, grad_hidden.shape[2])
-    inner_leaving, inner_own, shared = project_inner(activations, in_projection, inverse_out, shares)
+    inner_leaving, inner_own, shared, near_hidden = project_inner(
+        activations, in_projection, inverse_out, flat_hidden, shares
+    )
     inner_first = exchange(inner_leaving, "proj", shares, 2)
     far_shared = exchange(shared, "expert", owners, owners // 2)
-    leaving, own = project_outer(flat_hidden, out_projection, shares, top)
+    leaving, own = project_outer(near_hidden, flat_hidden, out_projection, shares, top)
     far_shared, inner_first, leaving = lax.optimization_barrier((far_shared, inner_first, leaving))
     near = exchange(leaving, "proj", shares, 1)
     shared, turns = jnp.stack([shared, far_shared]), (0, owners // 2)
-    for bit in reversed(range((owners // 2).bit_length() - 1)):
+    for bit in reversed(range(1, (owners // 2).bit_length() - 1)):
         shared, turns = double(shared, turns, "expert", owners, 1 << bit)
+    even = expand(shared, turns, width, experts, shares)
+    shared = exchange(shared, "expert", owners, 1)
+    near, even = lax.optimization_barrier((near, even))
     inner_second = exchange(combine(combine_inner_kernel, inner_own, inner_first), "proj", shares, 1)
     sent = combine(combine_outer_kernel, own, near)
     far = exchange(sent, "proj", shares, 2)
@@ -524,10 +589,10 @@
     inner, _ = lax.optimization_barrier((inner, sent))
     owner_turns = tuple(reversed(range(owners)))
     arriving = [exchange(inner, "expert", owners, turn) for turn in owner_turns if turn]
-    weights = expand(shared, turns, width, experts, shares)
-    far, weights = lax.optimization_barrier((far, weights))
+    odd = expand(shared, turns, width, experts, shares)
+    far, odd = lax.optimization_barrier((far, odd))
     quarter_routes = lax.dynamic_slice_in_dim(routes, lax.axis_index("proj") * quarter, quarter, 0)
-    payload = condition(own, near, far, quarter_routes, weights, shares, width)
+    payload = condition(own, near, far, quarter_routes, even, odd, shares, width)
     payload, arriving = lax.optimization_barrier((payload, arriving))
     arrived = send_to_all(payload, owners, shares, owners // 2)
     inner = jnp.stack(arriving + [inner])

time: 57 us -> 57 us (level)
  transfers between devices with their start and end apart: 12 -> 12, of which waited for: 3 -> 3; matrix products, arithmetic and copies ran while one was open for 0% -> 0% of each run, Pallas kernels for 29% -> 28%
where the time goes in v19:
time: 57 us; the launch traced here: 56.6 us
  Pallas kernels  24.8 us (44%)
  starting transfers between devices  19.8 us (35%)
  blocking collectives  9.08 us (16%)
  waiting for transfers between devices  2.51 us (4%)
    ppermute x11, starting transfers between devices, exchange(): return lax.ppermute(block, axis, [(i, i ^ turn) for i in range(size)])  14.6 us
    pallas_call x1, Pallas kernels, condition_queries(): pl.pallas_call(query_kernel, grid=(flat // LANES,), in_specs=[pl.BlockSpe...  9.58 us
    all_to_all x1, blocking collectives, send_to_all(): lax.all_to_all(blocks, ('expert', 'proj'), 0, 0, tiled=True, axis_index_g...  9.08 us
    pallas_call x1, Pallas kernels, score(): pl.pallas_call(functools.partial(score_kernel, width=width, doc_count=doc...  5.55 us
    all_to_all x1, starting transfers between devices, send_to_all(): lax.all_to_all(blocks, ('expert', 'proj'), 0, 0, tiled=True, axis_index_g...  5.21 us
    pallas_call x1, Pallas kernels, project_outer(): pl.pallas_call(functools.partial(outer_kernel, top=top), in_specs=[VMEM,...  3.28 us
    pallas_call x1, Pallas kernels, project_inner(): pl.pallas_call(inner_kernel, in_specs=[HBM] * 4, out_specs=[VMEM] * 4, ou...  3.08 us
    ppermute x11, waiting for transfers between devices, exchange(): return lax.ppermute(block, axis, [(i, i ^ turn) for i in range(size)])  2.51 us
  transfers between devices with their start and end apart: 12, of which 3 were waited for; matrix products, arithmetic and copies ran while one was open for 0% of the time, Pallas kernels for 28%

profile of v19, /device:TPU:0, one launch (start us, length us, event | category | flops | bytes accessed | tf_op | source)
XLA Modules:
  0.0 56.6 jit_solution(13895206463415297568)
XLA Ops:
  0.0 0.0 copy-start
  0.0 3.1 %shard_map.91 = (bf16[2,128,128]{2,1,0:T(8,128)(2,1)S(1)}, bf16[2,128,128]{2,1,0:T(8,128)(2,1)S(1)}, bf16[144,128]{1,0:T(8,128)(2,1)S(1)}, bf16[2,1024,512]{2,1,0:T(8,128)(2,1)S(1)}) custom-call(bf16[512,1792]{1,0:T(8,128)(2,1)} %act_hbm.1, bf16[64,1792]{1,0:T(8,128)(2,1)} %in_proj_hbm.1, f32[8,64,64]{2,1,0:T(8,128)} %inverse_hbm.1, bf16[4096,512]{1,0:T(8,128)(2,1)} %bitcast.16), custom_call_target="tpu_custom_call" | custom-call | bytes 8250000 | tf_op jit(solution)/shard_map/pallas_call | solution.py:161
  3.1 0.0 copy-start.2
  3.1 3.0 %collective-permute-start.1 = (bf16[2,128,128]{2,1,0:T(8,128)(2,1)S(1)}, bf16[2,128,128]{2,1,0:T(8,128)(2,1)S(1)}, u32[]{:S(2)}, u32[]{:S(2)}) collective-permute-start(bf16[2,128,128]{2,1,0:T(8,128)(2,1)S(1)} %get-tuple-element.28), channel_id=1, source_target_pairs={{0,2},{1,3},{2,0},{3,1},{4,6},{5,7},{6,4},{7,5},{8,10},{9,11},{10,... | collective-permute-start | bytes 196616 | tf_op jit(solution)/shard_map/ppermute | solution.py:541
  6.1 2.6 %collective-permute-start = (bf16[144,128]{1,0:T(8,128)(2,1)S(1)}, bf16[144,128]{1,0:T(8,128)(2,1)S(1)}, u32[]{:S(2)}, u32[]{:S(2)}) collective-permute-start(bf16[144,128]{1,0:T(8,128)(2,1)S(1)} %get-tuple-element.27), channel_id=1, source_target_pairs={{0,8},{4,12},{8,0},{12,4},{1,9},{5,13},{9,1},{13,5},{2,10},{6,14},... | collective-permute-start | bytes 110600 | tf_op jit(solution)/shard_map/ppermute | solution.py:541
  8.7 3.3 %shard_map.92 = (bf16[2,512,128]{2,1,0:T(8,128)(2,1)S(1)}, bf16[2,512,128]{2,1,0:T(8,128)(2,1)S(1)}) custom-call(bf16[2,1024,512]{2,1,0:T(8,128)(2,1)S(1)} %get-tuple-element.25.near_ref, bf16[4096,512]{1,0:T(8,128)(2,1)} %bitcast.17, bf16[64,512]{1,0:T(8,128)(2,1)} %out_proj_hbm.1), custom_call_target="tpu_custom_call" | custom-call | bytes 13200000 | tf_op jit(solution)/shard_map/pallas_call | solution.py:212
  12.0 0.0 copy-start.1
  12.0 0.0 collective-permute-done
  12.0 0.0 collective-permute-done.1.near_ref.first_ref
  12.0 0.1 collective-permute-start.2
  12.1 0.6 collective-permute-start.5
  12.7 0.4 shard_map.93.even_ref
  13.1 0.5 collective-permute-done.2.near_ref
  13.7 0.6 %collective-permute-start.3 = (bf16[512,128]{1,0:T(8,128)(2,1)S(1)}, bf16[512,128]{1,0:T(8,128)(2,1)S(1)}, u32[]{:S(2)}, u32[]{:S(2)}) collective-permute-start(bf16[512,128]{1,0:T(8,128)(2,1)S(1)} %shard_map.94), channel_id=1, source_target_pairs={{0,2},{1,3},{2,0},{3,1},{4,6},{5,7},{6,4},{7,5},{8,10},{9,11},{10,... | collective-permute-start | bytes 393224 | tf_op jit(solution)/shard_map/ppermute | solution.py:541
  14.3 1.6 %collective-permute-start.4 = (bf16[2,144,128]{2,1,0:T(8,128)(2,1)S(1)}, bf16[2,144,128]{2,1,0:T(8,128)(2,1)S(1)}, u32[]{:S(2)}, u32[]{:S(2)}) collective-permute-start(bf16[2,144,128]{2,1,0:T(8,128)(2,1)S(1)} %pad_maximum_fusion.2.shared_ref), channel_id=1, source_target_pairs={{0,4},{4,0},{8,12},{12,8},{1,5},{5,1},{9,13},{13,9},{2,6},{6,2},{1... | collective-permute-start | bytes 221192 | tf_op jit(solution)/shard_map/ppermute | solution.py:541
  15.8 0.0 collective-permute-done.5.second_ref
  15.8 0.0 copy-done.2
  15.8 0.1 shard_map.98
  16.0 0.5 collective-permute-start.8
  16.5 1.5 %collective-permute-start.7 = (bf16[80,128]{1,0:T(8,128)(2,1)S(1)}, bf16[80,128]{1,0:T(8,128)(2,1)S(1)}, u32[]{:S(2)}, u32[]{:S(2)}) collective-permute-start(bf16[80,128]{1,0:T(8,128)(2,1)S(1)} %shard_map.98), channel_id=1, source_target_pairs={{0,8},{4,12},{8,0},{12,4},{1,9},{5,13},{9,1},{13,5},{2,10},{6,14},... | collective-permute-start | bytes 61448 | tf_op jit(solution)/shard_map/ppermute | solution.py:541
  18.0 2.4 %collective-permute-start.6 = (bf16[80,128]{1,0:T(8,128)(2,1)S(1)}, bf16[80,128]{1,0:T(8,128)(2,1)S(1)}, u32[]{:S(2)}, u32[]{:S(2)}) collective-permute-start(bf16[80,128]{1,0:T(8,128)(2,1)S(1)} %shard_map.98), channel_id=1, source_target_pairs={{0,12},{4,8},{8,4},{12,0},{1,13},{5,9},{9,5},{13,1},{2,14},{6,10},... | collective-permute-start | bytes 61448 | tf_op jit(solution)/shard_map/ppermute | solution.py:541
  20.4 0.0 copy-done
  20.4 0.1 copy.11.routes_ref
  20.5 0.0 collective-permute-done.4.shared_ref
  20.5 0.4 shard_map.95.odd_ref
  21.0 0.0 collective-permute-done.3.far_ref
  21.0 1.7 %shard_map.96 = bf16[16,128,128]{2,1,0:T(8,128)(2,1)} custom-call(bf16[2,512,128]{2,1,0:T(8,128)(2,1)S(1)} %get-tuple-element.26.own_ref, bf16[2,512,128]{2,1,0:T(8,128)(2,1)S(1)} %collective-permute-done.2.near_ref, bf16[512,128]{1,0:T(8,128)(2,1)S(1)} %collective-permute-done.3.far_ref, s32[128,8]{1,0:T(8,128)S(1)} %copy.11.routes_ref, ...), custom_call_target="tpu_custom_call" | custom-call | bytes 6600000 | tf_op jit(solution)/shard_map/pallas_call | solution.py:359
  22.7 0.0 collective-permute-done.8
  22.7 0.0 collective-permute-done.7
  22.7 0.9 %collective-permute-done.6 = bf16[80,128]{1,0:T(8,128)(2,1)S(1)} collective-permute-done((bf16[80,128]{1,0:T(8,128)(2,1)S(1)}, bf16[80,128]{1,0:T(8,128)(2,1)S(1)}, u32[]{:S(2)}, u32[]{:S(2)}) %collective-permute-start.6) | collective-permute-done | bytes 20512 | tf_op jit(solution)/shard_map/ppermute | solution.py:541
  23.6 5.2 %all-to-all-start = ((bf16[16,128,128]{2,1,0:T(8,128)(2,1)}), bf16[16,128,128]{2,1,0:T(8,128)(2,1)S(1)}, u32[]{:S(2)}, u32[]{:S(2)}) async-start(bf16[16,128,128]{2,1,0:T(8,128)(2,1)} %shard_map.96), calls=%async_computation | async-start | bytes 1048576 | tf_op jit(solution)/shard_map/all_to_all | solution.py:33
  28.8 0.2 collective-permute-start.9
  29.0 1.1 %collective-permute-done.9 = bf16[1,4,80,128]{3,2,1,0:T(8,128)(2,1)S(1)} collective-permute-done((bf16[1,4,80,128]{3,2,1,0:T(8,128)(2,1)S(1)}, bf16[1,4,80,128]{3,2,1,0:T(8,128)(2,1)S(1)}, u32[]{:S(2)}, u32[]{:S(2)}) %collective-permute-start.9) | collective-permute-done | bytes 81952 | tf_op jit(solution)/shard_map/ppermute | solution.py:541
  30.1 1.5 %collective-permute-start.10 = (bf16[2,4,80,128]{3,2,1,0:T(8,128)(2,1)S(1)}, bf16[2,4,80,128]{3,2,1,0:T(8,128)(2,1)S(1)}, u32[]{:S(2)}, u32[]{:S(2)}) collective-permute-start(bf16[2,4,80,128]{3,2,1,0:T(8,128)(2,1)S(1)} %pad_maximum_fusion.1), channel_id=1, source_target_pairs={{0,2},{1,3},{2,0},{3,1},{4,6},{5,7},{6,4},{7,5},{8,10},{9,11},{10,... | collective-permute-start | bytes 491528 | tf_op jit(solution)/shard_map/ppermute | solution.py:541
  31.7 0.0 copy-done.1
  31.7 9.6 %shard_map.99.far_ref = bf16[8192,256]{1,0:T(8,128)(2,1)} custom-call(bf16[256,8,1024]{2,1,0:T(8,128)(2,1)} %query_ref, f32[8,64,64]{2,1,0:T(8,128)S(1)} %copy-done.1), custom_call_target="tpu_custom_call" | custom-call | bytes 33000000 | tf_op jit(solution)/shard_map/pallas_call | solution.py:423
  41.3 0.0 collective-permute-done.10
  41.3 0.0 all-to-all-done.arrived_ref
  41.3 5.5 %shard_map.100 = f32[16,8,128]{2,1,0:T(8,128)S(1)} custom-call(bf16[16,128,128]{2,1,0:T(8,128)(2,1)S(1)} %all-to-all-done.arrived_ref, bf16[16,80,128]{2,1,0:T(8,128)(2,1)S(1)} %bitcast.12, bf16[8192,256]{1,0:T(8,128)(2,1)} %shard_map.99.far_ref), custom_call_target="tpu_custom_call" | custom-call | bytes 16500000 | tf_op jit(solution)/shard_map/pallas_call | solution.py:510
  46.9 9.1 %all_to_all.10.pieces_ref = f32[16,8,128]{2,1,0:T(8,128)S(1)} all-to-all(f32[16,8,128]{2,1,0:T(8,128)S(1)} %shard_map.100), channel_id=1, replica_groups={{12,13,14,15,0,1,2,3,4,5,6,7,8,9,10,11},{28,29,30,31,16,17,18,19,20,21,..., dimensions={0} | all-to-all | bytes 131072 | tf_op jit(solution)/shard_map/all_to_all | solution.py:33
  56.0 0.6 %shard_map.101 = f32[8,64]{1,0:T(8,128)} custom-call(f32[16,8,128]{2,1,0:T(8,128)S(1)} %all_to_all.10.pieces_ref), custom_call_target="tpu_custom_call" | custom-call | tf_op jit(solution)/shard_map/pallas_call | solution.py:532
  (7 shorter events, 0.1 us)
Async XLA Ops:
  0.0 20.4 %copy-start = (s32[512,8]{0,1:T(8,128)S(1)}, s32[512,8]{0,1:T(8,128)}, u32[]{:S(2)}) copy-start(s32[512,8]{0,1:T(8,128)} %param.11) | copy-start | bytes 49156
  3.1 12.8 %copy-start.2 = (s32[512]{0:T(512)S(1)}, s32[512]{0:T(512)}, u32[]{:S(2)}) copy-start(s32[512]{0:T(512)} %param.12) | copy-start | bytes 6148
  3.1 8.9 %collective-permute-start.1 = (bf16[2,128,128]{2,1,0:T(8,128)(2,1)S(1)}, bf16[2,128,128]{2,1,0:T(8,128)(2,1)S(1)}, u32[]{:S(2)}, u32[]{:S(2)}) collective-permute-start(bf16[2,128,128]{2,1,0:T(8,128)(2,1)S(1)} %get-tuple-element.28), channel_id=1, source_target_pairs={{0,2},{1,3},{2,0},{3,1},{4,6},{5,7},{6,4},{7,5},{8,10},{9,11},{10,... | collective-permute-start | bytes 196616 | tf_op jit(solution)/shard_map/ppermute | solution.py:541
  6.1 5.9 %collective-permute-start = (bf16[144,128]{1,0:T(8,128)(2,1)S(1)}, bf16[144,128]{1,0:T(8,128)(2,1)S(1)}, u32[]{:S(2)}, u32[]{:S(2)}) collective-permute-start(bf16[144,128]{1,0:T(8,128)(2,1)S(1)} %get-tuple-element.27), channel_id=1, source_target_pairs={{0,8},{4,12},{8,0},{12,4},{1,9},{5,13},{9,1},{13,5},{2,10},{6,14},... | collective-permute-start | bytes 110600 | tf_op jit(solution)/shard_map/ppermute | solution.py:541
  12.0 19.7 %copy-start.1 = (f32[8,64,64]{2,1,0:T(8,128)S(1)}, f32[8,64,64]{2,1,0:T(8,128)}, u32[]{:S(2)}) copy-start(f32[8,64,64]{2,1,0:T(8,128)} %inverse_ref.1) | copy-start | bytes 393220
  12.0 1.6 %collective-permute-start.2 = (bf16[2,512,128]{2,1,0:T(8,128)(2,1)S(1)}, bf16[2,512,128]{2,1,0:T(8,128)(2,1)S(1)}, u32[]{:S(2)}, u32[]{:S(2)}) collective-permute-start(bf16[2,512,128]{2,1,0:T(8,128)(2,1)S(1)} %get-tuple-element.30), channel_id=1, source_target_pairs={{0,1},{1,0},{2,3},{3,2},{4,5},{5,4},{6,7},{7,6},{8,9},{9,8},{10,11... | collective-permute-start | bytes 786440 | tf_op jit(solution)/shard_map/ppermute | solution.py:541
  12.1 3.7 %collective-permute-start.5 = (bf16[128,128]{1,0:T(8,128)(2,1)S(1)}, bf16[128,128]{1,0:T(8,128)(2,1)S(1)}, u32[]{:S(2)}, u32[]{:S(2)}) collective-permute-start(bf16[128,128]{1,0:T(8,128)(2,1)S(1)} %shard_map.97), channel_id=1, source_target_pairs={{0,1},{1,0},{2,3},{3,2},{4,5},{5,4},{6,7},{7,6},{8,9},{9,8},{10,11... | collective-permute-start | bytes 98312 | tf_op jit(solution)/shard_map/ppermute | solution.py:541
  13.7 7.3 %collective-permute-start.3 = (bf16[512,128]{1,0:T(8,128)(2,1)S(1)}, bf16[512,128]{1,0:T(8,128)(2,1)S(1)}, u32[]{:S(2)}, u32[]{:S(2)}) collective-permute-start(bf16[512,128]{1,0:T(8,128)(2,1)S(1)} %shard_map.94), channel_id=1, source_target_pairs={{0,2},{1,3},{2,0},{3,1},{4,6},{5,7},{6,4},{7,5},{8,10},{9,11},{10,... | collective-permute-start | bytes 393224 | tf_op jit(solution)/shard_map/ppermute | solution.py:541
  14.3 6.3 %collective-permute-start.4 = (bf16[2,144,128]{2,1,0:T(8,128)(2,1)S(1)}, bf16[2,144,128]{2,1,0:T(8,128)(2,1)S(1)}, u32[]{:S(2)}, u32[]{:S(2)}) collective-permute-start(bf16[2,144,128]{2,1,0:T(8,128)(2,1)S(1)} %pad_maximum_fusion.2.shared_ref), channel_id=1, source_target_pairs={{0,4},{4,0},{8,12},{12,8},{1,5},{5,1},{9,13},{13,9},{2,6},{6,2},{1... | collective-permute-start | bytes 221192 | tf_op jit(solution)/shard_map/ppermute | solution.py:541
  16.0 6.7 %collective-permute-start.8 = (bf16[80,128]{1,0:T(8,128)(2,1)S(1)}, bf16[80,128]{1,0:T(8,128)(2,1)S(1)}, u32[]{:S(2)}, u32[]{:S(2)}) collective-permute-start(bf16[80,128]{1,0:T(8,128)(2,1)S(1)} %shard_map.98), channel_id=1, source_target_pairs={{0,4},{4,0},{8,12},{12,8},{1,5},{5,1},{9,13},{13,9},{2,6},{6,2},{1... | collective-permute-start | bytes 61448 | tf_op jit(solution)/shard_map/ppermute | solution.py:541
  16.5 6.2 %collective-permute-start.7 = (bf16[80,128]{1,0:T(8,128)(2,1)S(1)}, bf16[80,128]{1,0:T(8,128)(2,1)S(1)}, u32[]{:S(2)}, u32[]{:S(2)}) collective-permute-start(bf16[80,128]{1,0:T(8,128)(2,1)S(1)} %shard_map.98), channel_id=1, source_target_pairs={{0,8},{4,12},{8,0},{12,4},{1,9},{5,13},{9,1},{13,5},{2,10},{6,14},... | collective-permute-start | bytes 61448 | tf_op jit(solution)/shard_map/ppermute | solution.py:541
  18.0 5.6 %collective-permute-start.6 = (bf16[80,128]{1,0:T(8,128)(2,1)S(1)}, bf16[80,128]{1,0:T(8,128)(2,1)S(1)}, u32[]{:S(2)}, u32[]{:S(2)}) collective-permute-start(bf16[80,128]{1,0:T(8,128)(2,1)S(1)} %shard_map.98), channel_id=1, source_target_pairs={{0,12},{4,8},{8,4},{12,0},{1,13},{5,9},{9,5},{13,1},{2,14},{6,10},... | collective-permute-start | bytes 61448 | tf_op jit(solution)/shard_map/ppermute | solution.py:541
  23.6 17.8 %all-to-all-start = ((bf16[16,128,128]{2,1,0:T(8,128)(2,1)}), bf16[16,128,128]{2,1,0:T(8,128)(2,1)S(1)}, u32[]{:S(2)}, u32[]{:S(2)}) async-start(bf16[16,128,128]{2,1,0:T(8,128)(2,1)} %shard_map.96), calls=%async_computation | async-start | bytes 1048576 | tf_op jit(solution)/shard_map/all_to_all | solution.py:33
  28.8 1.3 %collective-permute-start.9 = (bf16[1,4,80,128]{3,2,1,0:T(8,128)(2,1)S(1)}, bf16[1,4,80,128]{3,2,1,0:T(8,128)(2,1)S(1)}, u32[]{:S(2)}, u32[]{:S(2)}) collective-permute-start(bf16[1,4,80,128]{3,2,1,0:T(8,128)(2,1)S(1)} %maximum_bitcast_fusion), channel_id=1, source_target_pairs={{0,1},{1,0},{2,3},{3,2},{4,5},{5,4},{6,7},{7,6},{8,9},{9,8},{10,11... | collective-permute-start | bytes 245768 | tf_op jit(solution)/shard_map/ppermute | solution.py:541
  30.1 11.1 %collective-permute-start.10 = (bf16[2,4,80,128]{3,2,1,0:T(8,128)(2,1)S(1)}, bf16[2,4,80,128]{3,2,1,0:T(8,128)(2,1)S(1)}, u32[]{:S(2)}, u32[]{:S(2)}) collective-permute-start(bf16[2,4,80,128]{3,2,1,0:T(8,128)(2,1)S(1)} %pad_maximum_fusion.1), channel_id=1, source_target_pairs={{0,2},{1,3},{2,0},{3,1},{4,6},{5,7},{6,4},{7,5},{8,10},{9,11},{10,... | collective-permute-start | bytes 491528 | tf_op jit(solution)/shard_map/ppermute | solution.py:541

commit v20 on v19

--- a/solution.py
+++ b/solution.py
@@ -278,7 +278,10 @@
     expert_lane = lax.broadcasted_iota(jnp.int32, (half * width, columns), 1) // share_rows % half
     expert_row = lax.broadcasted_iota(jnp.int32, (half * width, columns), 0) // width
     own = expert_lane == expert_row
-    factors = [unpack_factors(shared_ref[entry], width, half // 2) for entry in range(len(turns))]
+    rows = half // 2 * width + DIAGONAL_ROWS
+    factors = [
+        unpack_factors(shared_ref[entry * rows : (entry + 1) * rows], width, half // 2) for entry in range(len(turns))
+    ]
     for side in range(2):
         share = jnp.bitwise_xor(lane // (half * share_rows), side)
         source = share * share_rows + lane % share_rows
@@ -289,7 +292,7 @@
 
 
 def expand(shared, turns, width, experts, shares):
-    owners = shared.shape[0]
+    owners = len(turns)
     return pl.pallas_call(
         functools.partial(expand_kernel, width=width, experts=experts, shares=shares, turns=turns),
         in_specs=[VMEM],
@@ -579,17 +582,19 @@
     shared, turns = jnp.stack([shared, far_shared]), (0, owners // 2)
     for bit in reversed(range(1, (owners // 2).bit_length() - 1)):
         shared, turns = double(shared, turns, "expert", owners, 1 << bit)
+    shared = shared.reshape(-1, LANES)
     even = expand(shared, turns, width, experts, shares)
-    shared = exchange(shared, "expert", owners, 1)
     near, even = lax.optimization_barrier((near, even))
     inner_second = exchange(combine(combine_inner_kernel, inner_own, inner_first), "proj", shares, 1)
     sent = combine(combine_outer_kernel, own, near)
     far = exchange(sent, "proj", shares, 2)
     inner = finish_inner(inner_own, inner_first, inner_second, doc_ids.reshape(shares, quarter), width)
+    packet = exchange(jnp.concatenate([shared, inner], axis=0), "expert", owners, 1)
     inner, _ = lax.optimization_barrier((inner, sent))
     owner_turns = tuple(reversed(range(owners)))
-    arriving = [exchange(inner, "expert", owners, turn) for turn in owner_turns if turn]
-    odd = expand(shared, turns, width, experts, shares)
+    arriving = [exchange(inner, "expert", owners, turn) for turn in owner_turns if turn > 1]
+    arriving.append(packet[shared.shape[0] :])
+    odd = expand(packet, turns, width, experts, shares)
     far, odd = lax.optimization_barrier((far, odd))
     quarter_routes = lax.dynamic_slice_in_dim(routes, lax.axis_index("proj") * quarter, quarter, 0)
     payload = condition(own, near, far, quarter_routes, even, odd, shares, width)

time: 57 us -> 56.9 us (level)
  starting transfers between devices: 19.8 us -> 18.2 us
  waiting for transfers between devices: 2.51 us -> 3.95 us
    ppermute x11 -> x10, starting transfers between devices: 14.6 us -> 13 us  [exchange(): return lax.ppermute(block, axis, [(i, i ^ turn) for i in range(size)])]
    ppermute x11 -> x10, waiting for transfers between devices: 2.51 us -> 3.95 us  [exchange(): return lax.ppermute(block, axis, [(i, i ^ turn) for i in range(size)])]
  transfers between devices with their start and end apart: 12 -> 11, of which waited for: 3 -> 4; matrix products, arithmetic and copies ran while one was open for 0% -> 0% of each run, Pallas kernels for 28% -> 28%
where the time goes in v20:
time: 56.9 us; the launch traced here: 56.4 us
  Pallas kernels  24.8 us (44%)
  starting transfers between devices  18.2 us (32%)
  blocking collectives  9.07 us (16%)
  waiting for transfers between devices  3.95 us (7%)
    ppermute x10, starting transfers between devices, exchange(): return lax.ppermute(block, axis, [(i, i ^ turn) for i in range(size)])  13 us
    pallas_call x1, Pallas kernels, condition_queries(): pl.pallas_call(query_kernel, grid=(flat // LANES,), in_specs=[pl.BlockSpe...  9.59 us
    all_to_all x1, blocking collectives, send_to_all(): lax.all_to_all(blocks, ('expert', 'proj'), 0, 0, tiled=True, axis_index_g...  9.07 us
    pallas_call x1, Pallas kernels, score(): pl.pallas_call(functools.partial(score_kernel, width=width, doc_count=doc...  5.55 us
    all_to_all x1, starting transfers between devices, send_to_all(): lax.all_to_all(blocks, ('expert', 'proj'), 0, 0, tiled=True, axis_index_g...  5.14 us
    ppermute x10, waiting for transfers between devices, exchange(): return lax.ppermute(block, axis, [(i, i ^ turn) for i in range(size)])  3.95 us
    pallas_call x1, Pallas kernels, project_outer(): pl.pallas_call(functools.partial(outer_kernel, top=top), in_specs=[VMEM,...  3.28 us
    pallas_call x1, Pallas kernels, project_inner(): pl.pallas_call(inner_kernel, in_specs=[HBM] * 4, out_specs=[VMEM] * 4, ou...  3.08 us
  transfers between devices with their start and end apart: 11, of which 4 were waited for; matrix products, arithmetic and copies ran while one was open for 0% of the time, Pallas kernels for 28%

profile of v20, /device:TPU:0, one launch (start us, length us, event | category | flops | bytes accessed | tf_op | source)
XLA Modules:
  0.0 56.4 jit_solution(12810750301368715973)
XLA Ops:
  0.0 0.0 copy-start
  0.0 3.1 %shard_map.91 = (bf16[2,128,128]{2,1,0:T(8,128)(2,1)S(1)}, bf16[2,128,128]{2,1,0:T(8,128)(2,1)S(1)}, bf16[144,128]{1,0:T(8,128)(2,1)S(1)}, bf16[2,1024,512]{2,1,0:T(8,128)(2,1)S(1)}) custom-call(bf16[512,1792]{1,0:T(8,128)(2,1)} %act_hbm.1, bf16[64,1792]{1,0:T(8,128)(2,1)} %in_proj_hbm.1, f32[8,64,64]{2,1,0:T(8,128)} %inverse_hbm.1, bf16[4096,512]{1,0:T(8,128)(2,1)} %bitcast.19), custom_call_target="tpu_custom_call" | custom-call | bytes 8250000 | tf_op jit(solution)/shard_map/pallas_call | solution.py:161
  3.1 0.0 copy-start.2
  3.1 3.0 %collective-permute-start.1 = (bf16[2,128,128]{2,1,0:T(8,128)(2,1)S(1)}, bf16[2,128,128]{2,1,0:T(8,128)(2,1)S(1)}, u32[]{:S(2)}, u32[]{:S(2)}) collective-permute-start(bf16[2,128,128]{2,1,0:T(8,128)(2,1)S(1)} %get-tuple-element.28), channel_id=1, source_target_pairs={{0,2},{1,3},{2,0},{3,1},{4,6},{5,7},{6,4},{7,5},{8,10},{9,11},{10,... | collective-permute-start | bytes 196616 | tf_op jit(solution)/shard_map/ppermute | solution.py:544
  6.1 2.6 %collective-permute-start = (bf16[144,128]{1,0:T(8,128)(2,1)S(1)}, bf16[144,128]{1,0:T(8,128)(2,1)S(1)}, u32[]{:S(2)}, u32[]{:S(2)}) collective-permute-start(bf16[144,128]{1,0:T(8,128)(2,1)S(1)} %get-tuple-element.27), channel_id=1, source_target_pairs={{0,8},{4,12},{8,0},{12,4},{1,9},{5,13},{9,1},{13,5},{2,10},{6,14},... | collective-permute-start | bytes 110600 | tf_op jit(solution)/shard_map/ppermute | solution.py:544
  8.7 3.3 %shard_map.92 = (bf16[2,512,128]{2,1,0:T(8,128)(2,1)S(1)}, bf16[2,512,128]{2,1,0:T(8,128)(2,1)S(1)}) custom-call(bf16[2,1024,512]{2,1,0:T(8,128)(2,1)S(1)} %get-tuple-element.25.near_ref, bf16[4096,512]{1,0:T(8,128)(2,1)} %bitcast.20, bf16[64,512]{1,0:T(8,128)(2,1)} %out_proj_hbm.1), custom_call_target="tpu_custom_call" | custom-call | bytes 13200000 | tf_op jit(solution)/shard_map/pallas_call | solution.py:212
  12.0 0.0 copy-start.1
  12.0 0.0 collective-permute-done
  12.0 0.0 collective-permute-done.1.near_ref.first_ref
  12.0 0.1 collective-permute-start.2
  12.1 0.6 collective-permute-start.4
  12.7 0.4 shard_map.93.even_ref
  13.1 0.5 collective-permute-done.4.second_ref
  13.7 0.0 copy-done.2
  13.7 0.1 shard_map.96
  13.8 0.0 collective-permute-done.2.near_ref
  13.9 0.6 %collective-permute-start.3 = (bf16[512,128]{1,0:T(8,128)(2,1)S(1)}, bf16[512,128]{1,0:T(8,128)(2,1)S(1)}, u32[]{:S(2)}, u32[]{:S(2)}) collective-permute-start(bf16[512,128]{1,0:T(8,128)(2,1)S(1)} %shard_map.94), channel_id=1, source_target_pairs={{0,2},{1,3},{2,0},{3,1},{4,6},{5,7},{6,4},{7,5},{8,10},{9,11},{10,... | collective-permute-start | bytes 393224 | tf_op jit(solution)/shard_map/ppermute | solution.py:544
  14.5 1.6 %collective-permute-start.5 = (bf16[368,128]{1,0:T(8,128)(2,1)S(1)}, bf16[368,128]{1,0:T(8,128)(2,1)S(1)}, u32[]{:S(2)}, u32[]{:S(2)}) collective-permute-start(bf16[368,128]{1,0:T(8,128)(2,1)S(1)} %pad_maximum_fusion.2), channel_id=1, source_target_pairs={{0,4},{4,0},{8,12},{12,8},{1,5},{5,1},{9,13},{13,9},{2,6},{6,2},{1... | collective-permute-start | bytes 282632 | tf_op jit(solution)/shard_map/ppermute | solution.py:544
  16.1 1.8 %collective-permute-start.7 = (bf16[80,128]{1,0:T(8,128)(2,1)S(1)}, bf16[80,128]{1,0:T(8,128)(2,1)S(1)}, u32[]{:S(2)}, u32[]{:S(2)}) collective-permute-start(bf16[80,128]{1,0:T(8,128)(2,1)S(1)} %shard_map.96), channel_id=1, source_target_pairs={{0,8},{4,12},{8,0},{12,4},{1,9},{5,13},{9,1},{13,5},{2,10},{6,14},... | collective-permute-start | bytes 61448 | tf_op jit(solution)/shard_map/ppermute | solution.py:544
  17.9 1.1 %collective-permute-start.6 = (bf16[80,128]{1,0:T(8,128)(2,1)S(1)}, bf16[80,128]{1,0:T(8,128)(2,1)S(1)}, u32[]{:S(2)}, u32[]{:S(2)}) collective-permute-start(bf16[80,128]{1,0:T(8,128)(2,1)S(1)} %shard_map.96), channel_id=1, source_target_pairs={{0,12},{4,8},{8,4},{12,0},{1,13},{5,9},{9,5},{13,1},{2,14},{6,10},... | collective-permute-start | bytes 61448 | tf_op jit(solution)/shard_map/ppermute | solution.py:544
  18.9 0.0 copy-done
  18.9 0.1 copy.11.routes_ref
  19.0 0.1 collective-permute-done.5.shared_ref
  19.1 0.4 shard_map.97.odd_ref
  19.5 0.0 collective-permute-done.3.far_ref
  19.6 1.7 %shard_map.98 = bf16[16,128,128]{2,1,0:T(8,128)(2,1)} custom-call(bf16[2,512,128]{2,1,0:T(8,128)(2,1)S(1)} %get-tuple-element.26.own_ref, bf16[2,512,128]{2,1,0:T(8,128)(2,1)S(1)} %collective-permute-done.2.near_ref, bf16[512,128]{1,0:T(8,128)(2,1)S(1)} %collective-permute-done.3.far_ref, s32[128,8]{1,0:T(8,128)S(1)} %copy.11.routes_ref, ...), custom_call_target="tpu_custom_call" | custom-call | bytes 6600000 | tf_op jit(solution)/shard_map/pallas_call | solution.py:362
  21.3 0.0 collective-permute-done.7
  21.3 2.2 %collective-permute-done.6 = bf16[80,128]{1,0:T(8,128)(2,1)S(1)} collective-permute-done((bf16[80,128]{1,0:T(8,128)(2,1)S(1)}, bf16[80,128]{1,0:T(8,128)(2,1)S(1)}, u32[]{:S(2)}, u32[]{:S(2)}) %collective-permute-start.6) | collective-permute-done | bytes 20512 | tf_op jit(solution)/shard_map/ppermute | solution.py:544
  23.4 5.1 %all-to-all-start = ((bf16[16,128,128]{2,1,0:T(8,128)(2,1)}), bf16[16,128,128]{2,1,0:T(8,128)(2,1)S(1)}, u32[]{:S(2)}, u32[]{:S(2)}) async-start(bf16[16,128,128]{2,1,0:T(8,128)(2,1)} %shard_map.98), calls=%async_computation | async-start | bytes 1048576 | tf_op jit(solution)/shard_map/all_to_all | solution.py:33
  28.6 0.2 collective-permute-start.8
  28.8 1.1 %collective-permute-done.8 = bf16[1,4,80,128]{3,2,1,0:T(8,128)(2,1)S(1)} collective-permute-done((bf16[1,4,80,128]{3,2,1,0:T(8,128)(2,1)S(1)}, bf16[1,4,80,128]{3,2,1,0:T(8,128)(2,1)S(1)}, u32[]{:S(2)}, u32[]{:S(2)}) %collective-permute-start.8) | collective-permute-done | bytes 81952 | tf_op jit(solution)/shard_map/ppermute | solution.py:544
  30.0 1.5 %collective-permute-start.9 = (bf16[2,4,80,128]{3,2,1,0:T(8,128)(2,1)S(1)}, bf16[2,4,80,128]{3,2,1,0:T(8,128)(2,1)S(1)}, u32[]{:S(2)}, u32[]{:S(2)}) collective-permute-start(bf16[2,4,80,128]{3,2,1,0:T(8,128)(2,1)S(1)} %pad_maximum_fusion.1), channel_id=1, source_target_pairs={{0,2},{1,3},{2,0},{3,1},{4,6},{5,7},{6,4},{7,5},{8,10},{9,11},{10,... | collective-permute-start | bytes 491528 | tf_op jit(solution)/shard_map/ppermute | solution.py:544
  31.5 0.0 copy-done.1
  31.5 9.6 %shard_map.99.far_ref = bf16[8192,256]{1,0:T(8,128)(2,1)} custom-call(bf16[256,8,1024]{2,1,0:T(8,128)(2,1)} %query_ref, f32[8,64,64]{2,1,0:T(8,128)S(1)} %copy-done.1), custom_call_target="tpu_custom_call" | custom-call | bytes 33000000 | tf_op jit(solution)/shard_map/pallas_call | solution.py:426
  41.1 0.0 collective-permute-done.9
  41.1 0.0 all-to-all-done.arrived_ref
  41.2 5.5 %shard_map.100 = f32[16,8,128]{2,1,0:T(8,128)S(1)} custom-call(bf16[16,128,128]{2,1,0:T(8,128)(2,1)S(1)} %all-to-all-done.arrived_ref, bf16[16,80,128]{2,1,0:T(8,128)(2,1)S(1)} %bitcast.13, bf16[8192,256]{1,0:T(8,128)(2,1)} %shard_map.99.far_ref), custom_call_target="tpu_custom_call" | custom-call | bytes 16500000 | tf_op jit(solution)/shard_map/pallas_call | solution.py:513
  46.7 9.1 %all_to_all.10.pieces_ref = f32[16,8,128]{2,1,0:T(8,128)S(1)} all-to-all(f32[16,8,128]{2,1,0:T(8,128)S(1)} %shard_map.100), channel_id=1, replica_groups={{12,13,14,15,0,1,2,3,4,5,6,7,8,9,10,11},{28,29,30,31,16,17,18,19,20,21,..., dimensions={0} | all-to-all | bytes 131072 | tf_op jit(solution)/shard_map/all_to_all | solution.py:33
  55.8 0.6 %shard_map.101 = f32[8,64]{1,0:T(8,128)} custom-call(f32[16,8,128]{2,1,0:T(8,128)S(1)} %all_to_all.10.pieces_ref), custom_call_target="tpu_custom_call" | custom-call | tf_op jit(solution)/shard_map/pallas_call | solution.py:535
  (9 shorter events, 0.1 us)
Async XLA Ops:
  0.0 18.9 %copy-start = (s32[512,8]{0,1:T(8,128)S(1)}, s32[512,8]{0,1:T(8,128)}, u32[]{:S(2)}) copy-start(s32[512,8]{0,1:T(8,128)} %param.11) | copy-start | bytes 49156
  3.1 10.6 %copy-start.2 = (s32[512]{0:T(512)S(1)}, s32[512]{0:T(512)}, u32[]{:S(2)}) copy-start(s32[512]{0:T(512)} %param.12) | copy-start | bytes 6148
  3.1 8.9 %collective-permute-start.1 = (bf16[2,128,128]{2,1,0:T(8,128)(2,1)S(1)}, bf16[2,128,128]{2,1,0:T(8,128)(2,1)S(1)}, u32[]{:S(2)}, u32[]{:S(2)}) collective-permute-start(bf16[2,128,128]{2,1,0:T(8,128)(2,1)S(1)} %get-tuple-element.28), channel_id=1, source_target_pairs={{0,2},{1,3},{2,0},{3,1},{4,6},{5,7},{6,4},{7,5},{8,10},{9,11},{10,... | collective-permute-start | bytes 196616 | tf_op jit(solution)/shard_map/ppermute | solution.py:544
  6.1 5.9 %collective-permute-start = (bf16[144,128]{1,0:T(8,128)(2,1)S(1)}, bf16[144,128]{1,0:T(8,128)(2,1)S(1)}, u32[]{:S(2)}, u32[]{:S(2)}) collective-permute-start(bf16[144,128]{1,0:T(8,128)(2,1)S(1)} %get-tuple-element.27), channel_id=1, source_target_pairs={{0,8},{4,12},{8,0},{12,4},{1,9},{5,13},{9,1},{13,5},{2,10},{6,14},... | collective-permute-start | bytes 110600 | tf_op jit(solution)/shard_map/ppermute | solution.py:544
  12.0 19.5 %copy-start.1 = (f32[8,64,64]{2,1,0:T(8,128)S(1)}, f32[8,64,64]{2,1,0:T(8,128)}, u32[]{:S(2)}) copy-start(f32[8,64,64]{2,1,0:T(8,128)} %inverse_ref.1) | copy-start | bytes 393220
  12.0 1.8 %collective-permute-start.2 = (bf16[2,512,128]{2,1,0:T(8,128)(2,1)S(1)}, bf16[2,512,128]{2,1,0:T(8,128)(2,1)S(1)}, u32[]{:S(2)}, u32[]{:S(2)}) collective-permute-start(bf16[2,512,128]{2,1,0:T(8,128)(2,1)S(1)} %get-tuple-element.30), channel_id=1, source_target_pairs={{0,1},{1,0},{2,3},{3,2},{4,5},{5,4},{6,7},{7,6},{8,9},{9,8},{10,11... | collective-permute-start | bytes 786440 | tf_op jit(solution)/shard_map/ppermute | solution.py:544
  12.1 1.5 %collective-permute-start.4 = (bf16[128,128]{1,0:T(8,128)(2,1)S(1)}, bf16[128,128]{1,0:T(8,128)(2,1)S(1)}, u32[]{:S(2)}, u32[]{:S(2)}) collective-permute-start(bf16[128,128]{1,0:T(8,128)(2,1)S(1)} %shard_map.95), channel_id=1, source_target_pairs={{0,1},{1,0},{2,3},{3,2},{4,5},{5,4},{6,7},{7,6},{8,9},{9,8},{10,11... | collective-permute-start | bytes 98312 | tf_op jit(solution)/shard_map/ppermute | solution.py:544
  13.9 5.7 %collective-permute-start.3 = (bf16[512,128]{1,0:T(8,128)(2,1)S(1)}, bf16[512,128]{1,0:T(8,128)(2,1)S(1)}, u32[]{:S(2)}, u32[]{:S(2)}) collective-permute-start(bf16[512,128]{1,0:T(8,128)(2,1)S(1)} %shard_map.94), channel_id=1, source_target_pairs={{0,2},{1,3},{2,0},{3,1},{4,6},{5,7},{6,4},{7,5},{8,10},{9,11},{10,... | collective-permute-start | bytes 393224 | tf_op jit(solution)/shard_map/ppermute | solution.py:544
  14.5 4.6 %collective-permute-start.5 = (bf16[368,128]{1,0:T(8,128)(2,1)S(1)}, bf16[368,128]{1,0:T(8,128)(2,1)S(1)}, u32[]{:S(2)}, u32[]{:S(2)}) collective-permute-start(bf16[368,128]{1,0:T(8,128)(2,1)S(1)} %pad_maximum_fusion.2), channel_id=1, source_target_pairs={{0,4},{4,0},{8,12},{12,8},{1,5},{5,1},{9,13},{13,9},{2,6},{6,2},{1... | collective-permute-start | bytes 282632 | tf_op jit(solution)/shard_map/ppermute | solution.py:544
  16.1 5.2 %collective-permute-start.7 = (bf16[80,128]{1,0:T(8,128)(2,1)S(1)}, bf16[80,128]{1,0:T(8,128)(2,1)S(1)}, u32[]{:S(2)}, u32[]{:S(2)}) collective-permute-start(bf16[80,128]{1,0:T(8,128)(2,1)S(1)} %shard_map.96), channel_id=1, source_target_pairs={{0,8},{4,12},{8,0},{12,4},{1,9},{5,13},{9,1},{13,5},{2,10},{6,14},... | collective-permute-start | bytes 61448 | tf_op jit(solution)/shard_map/ppermute | solution.py:544
  17.9 5.6 %collective-permute-start.6 = (bf16[80,128]{1,0:T(8,128)(2,1)S(1)}, bf16[80,128]{1,0:T(8,128)(2,1)S(1)}, u32[]{:S(2)}, u32[]{:S(2)}) collective-permute-start(bf16[80,128]{1,0:T(8,128)(2,1)S(1)} %shard_map.96), channel_id=1, source_target_pairs={{0,12},{4,8},{8,4},{12,0},{1,13},{5,9},{9,5},{13,1},{2,14},{6,10},... | collective-permute-start | bytes 61448 | tf_op jit(solution)/shard_map/ppermute | solution.py:544
  23.4 17.7 %all-to-all-start = ((bf16[16,128,128]{2,1,0:T(8,128)(2,1)}), bf16[16,128,128]{2,1,0:T(8,128)(2,1)S(1)}, u32[]{:S(2)}, u32[]{:S(2)}) async-start(bf16[16,128,128]{2,1,0:T(8,128)(2,1)} %shard_map.98), calls=%async_computation | async-start | bytes 1048576 | tf_op jit(solution)/shard_map/all_to_all | solution.py:33
  28.6 1.3 %collective-permute-start.8 = (bf16[1,4,80,128]{3,2,1,0:T(8,128)(2,1)S(1)}, bf16[1,4,80,128]{3,2,1,0:T(8,128)(2,1)S(1)}, u32[]{:S(2)}, u32[]{:S(2)}) collective-permute-start(bf16[1,4,80,128]{3,2,1,0:T(8,128)(2,1)S(1)} %maximum_bitcast_fusion), channel_id=1, source_target_pairs={{0,1},{1,0},{2,3},{3,2},{4,5},{5,4},{6,7},{7,6},{8,9},{9,8},{10,11... | collective-permute-start | bytes 245768 | tf_op jit(solution)/shard_map/ppermute | solution.py:544
  30.0 11.1 %collective-permute-start.9 = (bf16[2,4,80,128]{3,2,1,0:T(8,128)(2,1)S(1)}, bf16[2,4,80,128]{3,2,1,0:T(8,128)(2,1)S(1)}, u32[]{:S(2)}, u32[]{:S(2)}) collective-permute-start(bf16[2,4,80,128]{3,2,1,0:T(8,128)(2,1)S(1)} %pad_maximum_fusion.1), channel_id=1, source_target_pairs={{0,2},{1,3},{2,0},{3,1},{4,6},{5,7},{6,4},{7,5},{8,10},{9,11},{10,... | collective-permute-start | bytes 491528 | tf_op jit(solution)/shard_map/ppermute | solution.py:544

commit v21 on v20

--- a/solution.py
+++ b/solution.py
@@ -437,7 +437,7 @@
             pltpu.VMEM((count * experts, LANES), jnp.float32),
             pltpu.VMEM((count // LANES, rows + 8 * width, LANES), jnp.float32),
             pltpu.VMEM((rows, count), jnp.bfloat16),
-            pltpu.SemaphoreType.DMA((4,)),
+            pltpu.SemaphoreType.DMA((8,)),
         ],
         compiler_params=pltpu.CompilerParams(vmem_limit_bytes=40 * MIB),
         cost_estimate=cost(10),
@@ -489,15 +489,11 @@
 
     groups = doc_count // (2 * pair_group)
     lax.fori_loop(0, groups, one_group, 0, unroll=groups == 1)
-    high, low = [], []
-    for j in range(width):
-        parts = split(grads_ref[pl.ds(j, doc_count, stride=pitch), :])
-        high.append(parts[0])
-        low.append(parts[1])
-    flat = jnp.concatenate([jnp.concatenate(high, axis=1), jnp.concatenate(low, axis=1)], axis=0)
+    flat = jnp.concatenate(
+        [grads_ref[pl.ds(j, doc_count, stride=pitch), :].astype(jnp.bfloat16) for j in range(width)], axis=1
+    )
     fetch.wait()
     result = jnp.dot(flat, queries_ref[...], preferred_element_type=jnp.float32)
-    result = result[:doc_count] + result[doc_count:]
     columns = result.shape[1] // shares
     fill = jnp.zeros((DOC_DEV, LANES - columns), jnp.float32)
     for owner in range(owners):
@@ -591,7 +587,7 @@
     inner = finish_inner(inner_own, inner_first, inner_second, doc_ids.reshape(shares, quarter), width)
     packet = exchange(jnp.concatenate([shared, inner], axis=0), "expert", owners, 1)
     inner, _ = lax.optimization_barrier((inner, sent))
-    owner_turns = tuple(reversed(range(owners)))
+    owner_turns = (*range(2, owners), 1, 0)
     arriving = [exchange(inner, "expert", owners, turn) for turn in owner_turns if turn > 1]
     arriving.append(packet[shared.shape[0] :])
     odd = expand(packet, turns, width, experts, shares)

time: 56.9 us -> 55.6 us (0.977)
  starting transfers between devices: 18.2 us -> 17.3 us
    ppermute x10, starting transfers between devices: 13 us -> 12.1 us  [exchange(): return lax.ppermute(block, axis, [(i, i ^ turn) for i in range(size)])]
  transfers between devices with their start and end apart: 11 -> 11, of which waited for: 4 -> 5; matrix products, arithmetic and copies ran while one was open for 0% -> 0% of each run, Pallas kernels for 28% -> 28%
where the time goes in v21:
time: 55.6 us; the launch traced here: 55.1 us
  Pallas kernels  24.8 us (45%)
  starting transfers between devices  17.3 us (31%)
  blocking collectives  9.1 us (16%)
  waiting for transfers between devices  3.59 us (6%)
    ppermute x10, starting transfers between devices, exchange(): return lax.ppermute(block, axis, [(i, i ^ turn) for i in range(size)])  12.1 us
    pallas_call x1, Pallas kernels, condition_queries(): pl.pallas_call(query_kernel, grid=(flat // LANES,), in_specs=[pl.BlockSpe...  9.56 us
    all_to_all x1, blocking collectives, send_to_all(): lax.all_to_all(blocks, ('expert', 'proj'), 0, 0, tiled=True, axis_index_g...  9.1 us
    pallas_call x1, Pallas kernels, score(): pl.pallas_call(functools.partial(score_kernel, width=width, doc_count=doc...  5.51 us
    all_to_all x1, starting transfers between devices, send_to_all(): lax.all_to_all(blocks, ('expert', 'proj'), 0, 0, tiled=True, axis_index_g...  5.21 us
    ppermute x10, waiting for transfers between devices, exchange(): return lax.ppermute(block, axis, [(i, i ^ turn) for i in range(size)])  3.58 us
    pallas_call x1, Pallas kernels, project_outer(): pl.pallas_call(functools.partial(outer_kernel, top=top), in_specs=[VMEM,...  3.28 us
    pallas_call x1, Pallas kernels, project_inner(): pl.pallas_call(inner_kernel, in_specs=[HBM] * 4, out_specs=[VMEM] * 4, ou...  3.08 us
  transfers between devices with their start and end apart: 11, of which 5 were waited for; matrix products, arithmetic and copies ran while one was open for 0% of the time, Pallas kernels for 28%

profile of v21, /device:TPU:0, one launch (start us, length us, event | category | flops | bytes accessed | tf_op | source)
XLA Modules:
  0.0 55.1 jit_solution(14312916184370436235)
XLA Ops:
  0.0 0.0 copy-start
  0.0 3.1 %shard_map.91 = (bf16[2,128,128]{2,1,0:T(8,128)(2,1)S(1)}, bf16[2,128,128]{2,1,0:T(8,128)(2,1)S(1)}, bf16[144,128]{1,0:T(8,128)(2,1)S(1)}, bf16[2,1024,512]{2,1,0:T(8,128)(2,1)S(1)}) custom-call(bf16[512,1792]{1,0:T(8,128)(2,1)} %act_hbm.1, bf16[64,1792]{1,0:T(8,128)(2,1)} %in_proj_hbm.1, f32[8,64,64]{2,1,0:T(8,128)} %inverse_hbm.1, bf16[4096,512]{1,0:T(8,128)(2,1)} %bitcast.19), custom_call_target="tpu_custom_call" | custom-call | bytes 8250000 | tf_op jit(solution)/shard_map/pallas_call | solution.py:161
  3.1 0.0 copy-start.2
  3.1 3.0 %collective-permute-start.1 = (bf16[2,128,128]{2,1,0:T(8,128)(2,1)S(1)}, bf16[2,128,128]{2,1,0:T(8,128)(2,1)S(1)}, u32[]{:S(2)}, u32[]{:S(2)}) collective-permute-start(bf16[2,128,128]{2,1,0:T(8,128)(2,1)S(1)} %get-tuple-element.28), channel_id=1, source_target_pairs={{0,2},{1,3},{2,0},{3,1},{4,6},{5,7},{6,4},{7,5},{8,10},{9,11},{10,... | collective-permute-start | bytes 196616 | tf_op jit(solution)/shard_map/ppermute | solution.py:540
  6.1 2.6 %collective-permute-start = (bf16[144,128]{1,0:T(8,128)(2,1)S(1)}, bf16[144,128]{1,0:T(8,128)(2,1)S(1)}, u32[]{:S(2)}, u32[]{:S(2)}) collective-permute-start(bf16[144,128]{1,0:T(8,128)(2,1)S(1)} %get-tuple-element.27), channel_id=1, source_target_pairs={{0,8},{4,12},{8,0},{12,4},{1,9},{5,13},{9,1},{13,5},{2,10},{6,14},... | collective-permute-start | bytes 110600 | tf_op jit(solution)/shard_map/ppermute | solution.py:540
  8.7 3.3 %shard_map.92 = (bf16[2,512,128]{2,1,0:T(8,128)(2,1)S(1)}, bf16[2,512,128]{2,1,0:T(8,128)(2,1)S(1)}) custom-call(bf16[2,1024,512]{2,1,0:T(8,128)(2,1)S(1)} %get-tuple-element.25.near_ref, bf16[4096,512]{1,0:T(8,128)(2,1)} %bitcast.20, bf16[64,512]{1,0:T(8,128)(2,1)} %out_proj_hbm.1), custom_call_target="tpu_custom_call" | custom-call | bytes 13200000 | tf_op jit(solution)/shard_map/pallas_call | solution.py:212
  12.0 0.0 copy-start.1
  12.0 0.0 collective-permute-done
  12.0 0.0 collective-permute-done.1.near_ref.first_ref
  12.0 0.1 collective-permute-start.2
  12.1 0.6 %collective-permute-start.4 = (bf16[128,128]{1,0:T(8,128)(2,1)S(1)}, bf16[128,128]{1,0:T(8,128)(2,1)S(1)}, u32[]{:S(2)}, u32[]{:S(2)}) collective-permute-start(bf16[128,128]{1,0:T(8,128)(2,1)S(1)} %shard_map.95), channel_id=1, source_target_pairs={{0,1},{1,0},{2,3},{3,2},{4,5},{5,4},{6,7},{7,6},{8,9},{9,8},{10,11... | collective-permute-start | bytes 98312 | tf_op jit(solution)/shard_map/ppermute | solution.py:540
  12.7 0.4 shard_map.93.even_ref
  13.1 0.5 collective-permute-done.4.second_ref
  13.7 0.0 copy-done.2
  13.7 0.1 shard_map.96
  13.8 0.0 collective-permute-done.2.near_ref
  13.9 0.6 %collective-permute-start.3 = (bf16[512,128]{1,0:T(8,128)(2,1)S(1)}, bf16[512,128]{1,0:T(8,128)(2,1)S(1)}, u32[]{:S(2)}, u32[]{:S(2)}) collective-permute-start(bf16[512,128]{1,0:T(8,128)(2,1)S(1)} %shard_map.94), channel_id=1, source_target_pairs={{0,2},{1,3},{2,0},{3,1},{4,6},{5,7},{6,4},{7,5},{8,10},{9,11},{10,... | collective-permute-start | bytes 393224 | tf_op jit(solution)/shard_map/ppermute | solution.py:540
  14.5 1.6 %collective-permute-start.5 = (bf16[368,128]{1,0:T(8,128)(2,1)S(1)}, bf16[368,128]{1,0:T(8,128)(2,1)S(1)}, u32[]{:S(2)}, u32[]{:S(2)}) collective-permute-start(bf16[368,128]{1,0:T(8,128)(2,1)S(1)} %pad_maximum_fusion.2), channel_id=1, source_target_pairs={{0,4},{4,0},{8,12},{12,8},{1,5},{5,1},{9,13},{13,9},{2,6},{6,2},{1... | collective-permute-start | bytes 282632 | tf_op jit(solution)/shard_map/ppermute | solution.py:540
  16.1 1.4 %collective-permute-start.7 = (bf16[80,128]{1,0:T(8,128)(2,1)S(1)}, bf16[80,128]{1,0:T(8,128)(2,1)S(1)}, u32[]{:S(2)}, u32[]{:S(2)}) collective-permute-start(bf16[80,128]{1,0:T(8,128)(2,1)S(1)} %shard_map.96), channel_id=1, source_target_pairs={{0,12},{4,8},{8,4},{12,0},{1,13},{5,9},{9,5},{13,1},{2,14},{6,10},... | collective-permute-start | bytes 61448 | tf_op jit(solution)/shard_map/ppermute | solution.py:540
  17.5 0.5 collective-permute-start.6
  18.0 0.0 copy-done
  18.0 0.1 copy.11.routes_ref
  18.1 1.0 %collective-permute-done.5.shared_ref = bf16[368,128]{1,0:T(8,128)(2,1)S(1)} collective-permute-done((bf16[368,128]{1,0:T(8,128)(2,1)S(1)}, bf16[368,128]{1,0:T(8,128)(2,1)S(1)}, u32[]{:S(2)}, u32[]{:S(2)}) %collective-permute-start.5) | collective-permute-done | bytes 94240 | tf_op jit(solution)/shard_map/ppermute | solution.py:540
  19.1 0.4 shard_map.97.odd_ref
  19.5 0.0 collective-permute-done.3.far_ref
  19.6 1.7 %shard_map.98 = bf16[16,128,128]{2,1,0:T(8,128)(2,1)} custom-call(bf16[2,512,128]{2,1,0:T(8,128)(2,1)S(1)} %get-tuple-element.26.own_ref, bf16[2,512,128]{2,1,0:T(8,128)(2,1)S(1)} %collective-permute-done.2.near_ref, bf16[512,128]{1,0:T(8,128)(2,1)S(1)} %collective-permute-done.3.far_ref, s32[128,8]{1,0:T(8,128)S(1)} %copy.11.routes_ref, ...), custom_call_target="tpu_custom_call" | custom-call | bytes 6600000 | tf_op jit(solution)/shard_map/pallas_call | solution.py:362
  21.3 0.4 collective-permute-done.7
  21.7 0.5 collective-permute-done.6
  22.2 5.2 %all-to-all-start = ((bf16[16,128,128]{2,1,0:T(8,128)(2,1)}), bf16[16,128,128]{2,1,0:T(8,128)(2,1)S(1)}, u32[]{:S(2)}, u32[]{:S(2)}) async-start(bf16[16,128,128]{2,1,0:T(8,128)(2,1)} %shard_map.98), calls=%async_computation | async-start | bytes 1048576 | tf_op jit(solution)/shard_map/all_to_all | solution.py:33
  27.4 0.2 collective-permute-start.8
  27.6 1.1 %collective-permute-done.8 = bf16[1,4,80,128]{3,2,1,0:T(8,128)(2,1)S(1)} collective-permute-done((bf16[1,4,80,128]{3,2,1,0:T(8,128)(2,1)S(1)}, bf16[1,4,80,128]{3,2,1,0:T(8,128)(2,1)S(1)}, u32[]{:S(2)}, u32[]{:S(2)}) %collective-permute-start.8) | collective-permute-done | bytes 81952 | tf_op jit(solution)/shard_map/ppermute | solution.py:540
  28.8 1.5 %collective-permute-start.9 = (bf16[2,4,80,128]{3,2,1,0:T(8,128)(2,1)S(1)}, bf16[2,4,80,128]{3,2,1,0:T(8,128)(2,1)S(1)}, u32[]{:S(2)}, u32[]{:S(2)}) collective-permute-start(bf16[2,4,80,128]{3,2,1,0:T(8,128)(2,1)S(1)} %pad_maximum_fusion.1), channel_id=1, source_target_pairs={{0,2},{1,3},{2,0},{3,1},{4,6},{5,7},{6,4},{7,5},{8,10},{9,11},{10,... | collective-permute-start | bytes 491528 | tf_op jit(solution)/shard_map/ppermute | solution.py:540
  30.3 0.0 copy-done.1
  30.3 9.6 %shard_map.99.far_ref = bf16[8192,256]{1,0:T(8,128)(2,1)} custom-call(bf16[256,8,1024]{2,1,0:T(8,128)(2,1)} %query_ref, f32[8,64,64]{2,1,0:T(8,128)S(1)} %copy-done.1), custom_call_target="tpu_custom_call" | custom-call | bytes 33000000 | tf_op jit(solution)/shard_map/pallas_call | solution.py:426
  39.9 0.0 collective-permute-done.9
  39.9 0.0 all-to-all-done.arrived_ref
  39.9 5.5 %shard_map.100 = f32[16,8,128]{2,1,0:T(8,128)S(1)} custom-call(bf16[16,128,128]{2,1,0:T(8,128)(2,1)S(1)} %all-to-all-done.arrived_ref, bf16[16,80,128]{2,1,0:T(8,128)(2,1)S(1)} %bitcast.13, bf16[8192,256]{1,0:T(8,128)(2,1)} %shard_map.99.far_ref), custom_call_target="tpu_custom_call" | custom-call | bytes 16500000 | tf_op jit(solution)/shard_map/pallas_call | solution.py:509
  45.4 9.1 %all_to_all.10.pieces_ref = f32[16,8,128]{2,1,0:T(8,128)S(1)} all-to-all(f32[16,8,128]{2,1,0:T(8,128)S(1)} %shard_map.100), channel_id=1, replica_groups={{12,13,14,15,0,1,2,3,4,5,6,7,8,9,10,11},{28,29,30,31,16,17,18,19,20,21,..., dimensions={0} | all-to-all | bytes 131072 | tf_op jit(solution)/shard_map/all_to_all | solution.py:33
  54.5 0.6 %shard_map.101 = f32[8,64]{1,0:T(8,128)} custom-call(f32[16,8,128]{2,1,0:T(8,128)S(1)} %all_to_all.10.pieces_ref), custom_call_target="tpu_custom_call" | custom-call | tf_op jit(solution)/shard_map/pallas_call | solution.py:531
  (9 shorter events, 0.1 us)
Async XLA Ops:
  0.0 18.0 %copy-start = (s32[512,8]{0,1:T(8,128)S(1)}, s32[512,8]{0,1:T(8,128)}, u32[]{:S(2)}) copy-start(s32[512,8]{0,1:T(8,128)} %param.11) | copy-start | bytes 49156
  3.1 10.6 %copy-start.2 = (s32[512]{0:T(512)S(1)}, s32[512]{0:T(512)}, u32[]{:S(2)}) copy-start(s32[512]{0:T(512)} %param.12) | copy-start | bytes 6148
  3.1 8.9 %collective-permute-start.1 = (bf16[2,128,128]{2,1,0:T(8,128)(2,1)S(1)}, bf16[2,128,128]{2,1,0:T(8,128)(2,1)S(1)}, u32[]{:S(2)}, u32[]{:S(2)}) collective-permute-start(bf16[2,128,128]{2,1,0:T(8,128)(2,1)S(1)} %get-tuple-element.28), channel_id=1, source_target_pairs={{0,2},{1,3},{2,0},{3,1},{4,6},{5,7},{6,4},{7,5},{8,10},{9,11},{10,... | collective-permute-start | bytes 196616 | tf_op jit(solution)/shard_map/ppermute | solution.py:540
  6.1 5.9 %collective-permute-start = (bf16[144,128]{1,0:T(8,128)(2,1)S(1)}, bf16[144,128]{1,0:T(8,128)(2,1)S(1)}, u32[]{:S(2)}, u32[]{:S(2)}) collective-permute-start(bf16[144,128]{1,0:T(8,128)(2,1)S(1)} %get-tuple-element.27), channel_id=1, source_target_pairs={{0,8},{4,12},{8,0},{12,4},{1,9},{5,13},{9,1},{13,5},{2,10},{6,14},... | collective-permute-start | bytes 110600 | tf_op jit(solution)/shard_map/ppermute | solution.py:540
  12.0 18.3 %copy-start.1 = (f32[8,64,64]{2,1,0:T(8,128)S(1)}, f32[8,64,64]{2,1,0:T(8,128)}, u32[]{:S(2)}) copy-start(f32[8,64,64]{2,1,0:T(8,128)} %inverse_ref.1) | copy-start | bytes 393220
  12.0 1.8 %collective-permute-start.2 = (bf16[2,512,128]{2,1,0:T(8,128)(2,1)S(1)}, bf16[2,512,128]{2,1,0:T(8,128)(2,1)S(1)}, u32[]{:S(2)}, u32[]{:S(2)}) collective-permute-start(bf16[2,512,128]{2,1,0:T(8,128)(2,1)S(1)} %get-tuple-element.30), channel_id=1, source_target_pairs={{0,1},{1,0},{2,3},{3,2},{4,5},{5,4},{6,7},{7,6},{8,9},{9,8},{10,11... | collective-permute-start | bytes 786440 | tf_op jit(solution)/shard_map/ppermute | solution.py:540
  12.1 1.5 %collective-permute-start.4 = (bf16[128,128]{1,0:T(8,128)(2,1)S(1)}, bf16[128,128]{1,0:T(8,128)(2,1)S(1)}, u32[]{:S(2)}, u32[]{:S(2)}) collective-permute-start(bf16[128,128]{1,0:T(8,128)(2,1)S(1)} %shard_map.95), channel_id=1, source_target_pairs={{0,1},{1,0},{2,3},{3,2},{4,5},{5,4},{6,7},{7,6},{8,9},{9,8},{10,11... | collective-permute-start | bytes 98312 | tf_op jit(solution)/shard_map/ppermute | solution.py:540
  13.9 5.7 %collective-permute-start.3 = (bf16[512,128]{1,0:T(8,128)(2,1)S(1)}, bf16[512,128]{1,0:T(8,128)(2,1)S(1)}, u32[]{:S(2)}, u32[]{:S(2)}) collective-permute-start(bf16[512,128]{1,0:T(8,128)(2,1)S(1)} %shard_map.94), channel_id=1, source_target_pairs={{0,2},{1,3},{2,0},{3,1},{4,6},{5,7},{6,4},{7,5},{8,10},{9,11},{10,... | collective-permute-start | bytes 393224 | tf_op jit(solution)/shard_map/ppermute | solution.py:540
  14.5 4.6 %collective-permute-start.5 = (bf16[368,128]{1,0:T(8,128)(2,1)S(1)}, bf16[368,128]{1,0:T(8,128)(2,1)S(1)}, u32[]{:S(2)}, u32[]{:S(2)}) collective-permute-start(bf16[368,128]{1,0:T(8,128)(2,1)S(1)} %pad_maximum_fusion.2), channel_id=1, source_target_pairs={{0,4},{4,0},{8,12},{12,8},{1,5},{5,1},{9,13},{13,9},{2,6},{6,2},{1... | collective-permute-start | bytes 282632 | tf_op jit(solution)/shard_map/ppermute | solution.py:540
  16.1 5.6 %collective-permute-start.7 = (bf16[80,128]{1,0:T(8,128)(2,1)S(1)}, bf16[80,128]{1,0:T(8,128)(2,1)S(1)}, u32[]{:S(2)}, u32[]{:S(2)}) collective-permute-start(bf16[80,128]{1,0:T(8,128)(2,1)S(1)} %shard_map.96), channel_id=1, source_target_pairs={{0,12},{4,8},{8,4},{12,0},{1,13},{5,9},{9,5},{13,1},{2,14},{6,10},... | collective-permute-start | bytes 61448 | tf_op jit(solution)/shard_map/ppermute | solution.py:540
  17.5 4.7 %collective-permute-start.6 = (bf16[80,128]{1,0:T(8,128)(2,1)S(1)}, bf16[80,128]{1,0:T(8,128)(2,1)S(1)}, u32[]{:S(2)}, u32[]{:S(2)}) collective-permute-start(bf16[80,128]{1,0:T(8,128)(2,1)S(1)} %shard_map.96), channel_id=1, source_target_pairs={{0,8},{4,12},{8,0},{12,4},{1,9},{5,13},{9,1},{13,5},{2,10},{6,14},... | collective-permute-start | bytes 61448 | tf_op jit(solution)/shard_map/ppermute | solution.py:540
  22.2 17.7 %all-to-all-start = ((bf16[16,128,128]{2,1,0:T(8,128)(2,1)}), bf16[16,128,128]{2,1,0:T(8,128)(2,1)S(1)}, u32[]{:S(2)}, u32[]{:S(2)}) async-start(bf16[16,128,128]{2,1,0:T(8,128)(2,1)} %shard_map.98), calls=%async_computation | async-start | bytes 1048576 | tf_op jit(solution)/shard_map/all_to_all | solution.py:33
  27.4 1.3 %collective-permute-start.8 = (bf16[1,4,80,128]{3,2,1,0:T(8,128)(2,1)S(1)}, bf16[1,4,80,128]{3,2,1,0:T(8,128)(2,1)S(1)}, u32[]{:S(2)}, u32[]{:S(2)}) collective-permute-start(bf16[1,4,80,128]{3,2,1,0:T(8,128)(2,1)S(1)} %maximum_bitcast_fusion), channel_id=1, source_target_pairs={{0,1},{1,0},{2,3},{3,2},{4,5},{5,4},{6,7},{7,6},{8,9},{9,8},{10,11... | collective-permute-start | bytes 245768 | tf_op jit(solution)/shard_map/ppermute | solution.py:540
  28.8 11.1 %collective-permute-start.9 = (bf16[2,4,80,128]{3,2,1,0:T(8,128)(2,1)S(1)}, bf16[2,4,80,128]{3,2,1,0:T(8,128)(2,1)S(1)}, u32[]{:S(2)}, u32[]{:S(2)}) collective-permute-start(bf16[2,4,80,128]{3,2,1,0:T(8,128)(2,1)S(1)} %pad_maximum_fusion.1), channel_id=1, source_target_pairs={{0,2},{1,3},{2,0},{3,1},{4,6},{5,7},{6,4},{7,5},{8,10},{9,11},{10,... | collective-permute-start | bytes 491528 | tf_op jit(solution)/shard_map/ppermute | solution.py:540

commit v22 on v21

--- a/solution.py
+++ b/solution.py
@@ -445,10 +445,15 @@
 
 
 def score_kernel(
-    arrived_ref, inner_ref, far_ref, out_ref, grads_ref, queries_ref, sem, *, width, doc_count, turns
+    arrived_ref, inner_ref, far_ref, out_ref, grads_ref, queries_ref, sems, *, width, doc_count, turns
 ):
-    fetch = pltpu.make_async_copy(far_ref, queries_ref, sem)
-    fetch.start()
+    parts = sems.shape[0]
+    part_rows = queries_ref.shape[0] // parts
+    fetches = []
+    for part in range(parts):
+        rows = pl.ds(part * part_rows, part_rows)
+        fetches.append(pltpu.make_async_copy(far_ref.at[rows], queries_ref.at[rows], sems.at[part]))
+        fetches[-1].start()
     sources, quarter, lanes = arrived_ref.shape
     shares = lax.axis_size("proj")
     owners = sources // shares
@@ -489,11 +494,18 @@
 
     groups = doc_count // (2 * pair_group)
     lax.fori_loop(0, groups, one_group, 0, unroll=groups == 1)
-    flat = jnp.concatenate(
-        [grads_ref[pl.ds(j, doc_count, stride=pitch), :].astype(jnp.bfloat16) for j in range(width)], axis=1
-    )
-    fetch.wait()
-    result = jnp.dot(flat, queries_ref[...], preferred_element_type=jnp.float32)
+    result = 0
+    for part in range(parts):
+        high, low = [], []
+        for j in range(part * width // parts, (part + 1) * width // parts):
+            pieces = split(grads_ref[pl.ds(j, doc_count, stride=pitch), :])
+            high.append(pieces[0])
+            low.append(pieces[1])
+        flat = jnp.concatenate([jnp.concatenate(high, axis=1), jnp.concatenate(low, axis=1)], axis=0)
+        fetches[part].wait()
+        rows = slice(part * part_rows, (part + 1) * part_rows)
+        result = result + jnp.dot(flat, queries_ref[rows, :], preferred_element_type=jnp.float32)
+    result = result[:doc_count] + result[doc_count:]
     columns = result.shape[1] // shares
     fill = jnp.zeros((DOC_DEV, LANES - columns), jnp.float32)
     for owner in range(owners):
@@ -513,7 +525,7 @@
         scratch_shapes=[
             pltpu.VMEM((doc_count * (width + 8), arrived.shape[2]), jnp.float32),
             pltpu.VMEM(queries.shape, jnp.bfloat16),
-            pltpu.SemaphoreType.DMA,
+            pltpu.SemaphoreType.DMA((8,)),
         ],
         compiler_params=pltpu.CompilerParams(vmem_limit_bytes=40 * MIB),
         cost_estimate=cost(5),

time: 55.6 us -> 54.9 us (0.987)
  Pallas kernels: 24.8 us -> 24.1 us
    pallas_call x1, Pallas kernels: 5.51 us -> 4.82 us  [score(): pl.pallas_call(functools.partial(score_kernel, width=width, doc_count=doc...]
  transfers between devices with their start and end apart: 11 -> 11, of which waited for: 5 -> 5; matrix products, arithmetic and copies ran while one was open for 0% -> 0% of each run, Pallas kernels for 28% -> 29%
where the time goes in v22:
time: 54.9 us; the launch traced here: 54.5 us
  Pallas kernels  24.1 us (44%)
  starting transfers between devices  17.3 us (32%)
  blocking collectives  9.1 us (17%)
  waiting for transfers between devices  3.59 us (7%)
    ppermute x10, starting transfers between devices, exchange(): return lax.ppermute(block, axis, [(i, i ^ turn) for i in range(size)])  12.1 us
    pallas_call x1, Pallas kernels, condition_queries(): pl.pallas_call(query_kernel, grid=(flat // LANES,), in_specs=[pl.BlockSpe...  9.56 us
    all_to_all x1, blocking collectives, send_to_all(): lax.all_to_all(blocks, ('expert', 'proj'), 0, 0, tiled=True, axis_index_g...  9.1 us
    all_to_all x1, starting transfers between devices, send_to_all(): lax.all_to_all(blocks, ('expert', 'proj'), 0, 0, tiled=True, axis_index_g...  5.21 us
    pallas_call x1, Pallas kernels, score(): pl.pallas_call(functools.partial(score_kernel, width=width, doc_count=doc...  4.82 us
    ppermute x10, waiting for transfers between devices, exchange(): return lax.ppermute(block, axis, [(i, i ^ turn) for i in range(size)])  3.58 us
    pallas_call x1, Pallas kernels, project_outer(): pl.pallas_call(functools.partial(outer_kernel, top=top), in_specs=[VMEM,...  3.28 us
    pallas_call x1, Pallas kernels, project_inner(): pl.pallas_call(inner_kernel, in_specs=[HBM] * 4, out_specs=[VMEM] * 4, ou...  3.08 us
  transfers between devices with their start and end apart: 11, of which 5 were waited for; matrix products, arithmetic and copies ran while one was open for 0% of the time, Pallas kernels for 29%

profile of v22, /device:TPU:0, one launch (start us, length us, event | category | flops | bytes accessed | tf_op | source)
XLA Modules:
  0.0 54.5 jit_solution(11406480080539372243)
XLA Ops:
  0.0 0.0 copy-start
  0.0 3.1 %shard_map.91 = (bf16[2,128,128]{2,1,0:T(8,128)(2,1)S(1)}, bf16[2,128,128]{2,1,0:T(8,128)(2,1)S(1)}, bf16[144,128]{1,0:T(8,128)(2,1)S(1)}, bf16[2,1024,512]{2,1,0:T(8,128)(2,1)S(1)}) custom-call(bf16[512,1792]{1,0:T(8,128)(2,1)} %act_hbm.1, bf16[64,1792]{1,0:T(8,128)(2,1)} %in_proj_hbm.1, f32[8,64,64]{2,1,0:T(8,128)} %inverse_hbm.1, bf16[4096,512]{1,0:T(8,128)(2,1)} %bitcast.19), custom_call_target="tpu_custom_call" | custom-call | bytes 8250000 | tf_op jit(solution)/shard_map/pallas_call | solution.py:161
  3.1 0.0 copy-start.2
  3.1 3.0 %collective-permute-start.1 = (bf16[2,128,128]{2,1,0:T(8,128)(2,1)S(1)}, bf16[2,128,128]{2,1,0:T(8,128)(2,1)S(1)}, u32[]{:S(2)}, u32[]{:S(2)}) collective-permute-start(bf16[2,128,128]{2,1,0:T(8,128)(2,1)S(1)} %get-tuple-element.28), channel_id=1, source_target_pairs={{0,2},{1,3},{2,0},{3,1},{4,6},{5,7},{6,4},{7,5},{8,10},{9,11},{10,... | collective-permute-start | bytes 196616 | tf_op jit(solution)/shard_map/ppermute | solution.py:552
  6.1 2.6 %collective-permute-start = (bf16[144,128]{1,0:T(8,128)(2,1)S(1)}, bf16[144,128]{1,0:T(8,128)(2,1)S(1)}, u32[]{:S(2)}, u32[]{:S(2)}) collective-permute-start(bf16[144,128]{1,0:T(8,128)(2,1)S(1)} %get-tuple-element.27), channel_id=1, source_target_pairs={{0,8},{4,12},{8,0},{12,4},{1,9},{5,13},{9,1},{13,5},{2,10},{6,14},... | collective-permute-start | bytes 110600 | tf_op jit(solution)/shard_map/ppermute | solution.py:552
  8.7 3.3 %shard_map.92 = (bf16[2,512,128]{2,1,0:T(8,128)(2,1)S(1)}, bf16[2,512,128]{2,1,0:T(8,128)(2,1)S(1)}) custom-call(bf16[2,1024,512]{2,1,0:T(8,128)(2,1)S(1)} %get-tuple-element.25.near_ref, bf16[4096,512]{1,0:T(8,128)(2,1)} %bitcast.20, bf16[64,512]{1,0:T(8,128)(2,1)} %out_proj_hbm.1), custom_call_target="tpu_custom_call" | custom-call | bytes 13200000 | tf_op jit(solution)/shard_map/pallas_call | solution.py:212
  12.0 0.0 copy-start.1
  12.0 0.0 collective-permute-done
  12.0 0.0 collective-permute-done.1.near_ref.first_ref
  12.0 0.1 collective-permute-start.2
  12.1 0.6 %collective-permute-start.4 = (bf16[128,128]{1,0:T(8,128)(2,1)S(1)}, bf16[128,128]{1,0:T(8,128)(2,1)S(1)}, u32[]{:S(2)}, u32[]{:S(2)}) collective-permute-start(bf16[128,128]{1,0:T(8,128)(2,1)S(1)} %shard_map.95), channel_id=1, source_target_pairs={{0,1},{1,0},{2,3},{3,2},{4,5},{5,4},{6,7},{7,6},{8,9},{9,8},{10,11... | collective-permute-start | bytes 98312 | tf_op jit(solution)/shard_map/ppermute | solution.py:552
  12.7 0.4 shard_map.93.even_ref
  13.1 0.5 collective-permute-done.4.second_ref
  13.7 0.0 copy-done.2
  13.7 0.1 shard_map.96
  13.8 0.0 collective-permute-done.2.near_ref
  13.9 0.6 %collective-permute-start.3 = (bf16[512,128]{1,0:T(8,128)(2,1)S(1)}, bf16[512,128]{1,0:T(8,128)(2,1)S(1)}, u32[]{:S(2)}, u32[]{:S(2)}) collective-permute-start(bf16[512,128]{1,0:T(8,128)(2,1)S(1)} %shard_map.94), channel_id=1, source_target_pairs={{0,2},{1,3},{2,0},{3,1},{4,6},{5,7},{6,4},{7,5},{8,10},{9,11},{10,... | collective-permute-start | bytes 393224 | tf_op jit(solution)/shard_map/ppermute | solution.py:552
  14.5 1.6 %collective-permute-start.5 = (bf16[368,128]{1,0:T(8,128)(2,1)S(1)}, bf16[368,128]{1,0:T(8,128)(2,1)S(1)}, u32[]{:S(2)}, u32[]{:S(2)}) collective-permute-start(bf16[368,128]{1,0:T(8,128)(2,1)S(1)} %pad_maximum_fusion.2), channel_id=1, source_target_pairs={{0,4},{4,0},{8,12},{12,8},{1,5},{5,1},{9,13},{13,9},{2,6},{6,2},{1... | collective-permute-start | bytes 282632 | tf_op jit(solution)/shard_map/ppermute | solution.py:552
  16.1 1.4 %collective-permute-start.7 = (bf16[80,128]{1,0:T(8,128)(2,1)S(1)}, bf16[80,128]{1,0:T(8,128)(2,1)S(1)}, u32[]{:S(2)}, u32[]{:S(2)}) collective-permute-start(bf16[80,128]{1,0:T(8,128)(2,1)S(1)} %shard_map.96), channel_id=1, source_target_pairs={{0,12},{4,8},{8,4},{12,0},{1,13},{5,9},{9,5},{13,1},{2,14},{6,10},... | collective-permute-start | bytes 61448 | tf_op jit(solution)/shard_map/ppermute | solution.py:552
  17.5 0.5 collective-permute-start.6
  18.0 0.0 copy-done
  18.0 0.1 copy.11.routes_ref
  18.1 1.0 %collective-permute-done.5.shared_ref = bf16[368,128]{1,0:T(8,128)(2,1)S(1)} collective-permute-done((bf16[368,128]{1,0:T(8,128)(2,1)S(1)}, bf16[368,128]{1,0:T(8,128)(2,1)S(1)}, u32[]{:S(2)}, u32[]{:S(2)}) %collective-permute-start.5) | collective-permute-done | bytes 94240 | tf_op jit(solution)/shard_map/ppermute | solution.py:552
  19.1 0.4 shard_map.97.odd_ref
  19.5 0.0 collective-permute-done.3.far_ref
  19.6 1.7 %shard_map.98 = bf16[16,128,128]{2,1,0:T(8,128)(2,1)} custom-call(bf16[2,512,128]{2,1,0:T(8,128)(2,1)S(1)} %get-tuple-element.26.own_ref, bf16[2,512,128]{2,1,0:T(8,128)(2,1)S(1)} %collective-permute-done.2.near_ref, bf16[512,128]{1,0:T(8,128)(2,1)S(1)} %collective-permute-done.3.far_ref, s32[128,8]{1,0:T(8,128)S(1)} %copy.11.routes_ref, ...), custom_call_target="tpu_custom_call" | custom-call | bytes 6600000 | tf_op jit(solution)/shard_map/pallas_call | solution.py:362
  21.3 0.4 collective-permute-done.7
  21.7 0.5 collective-permute-done.6
  22.2 5.2 %all-to-all-start = ((bf16[16,128,128]{2,1,0:T(8,128)(2,1)}), bf16[16,128,128]{2,1,0:T(8,128)(2,1)S(1)}, u32[]{:S(2)}, u32[]{:S(2)}) async-start(bf16[16,128,128]{2,1,0:T(8,128)(2,1)} %shard_map.98), calls=%async_computation | async-start | bytes 1048576 | tf_op jit(solution)/shard_map/all_to_all | solution.py:33
  27.4 0.2 collective-permute-start.8
  27.6 1.1 %collective-permute-done.8 = bf16[1,4,80,128]{3,2,1,0:T(8,128)(2,1)S(1)} collective-permute-done((bf16[1,4,80,128]{3,2,1,0:T(8,128)(2,1)S(1)}, bf16[1,4,80,128]{3,2,1,0:T(8,128)(2,1)S(1)}, u32[]{:S(2)}, u32[]{:S(2)}) %collective-permute-start.8) | collective-permute-done | bytes 81952 | tf_op jit(solution)/shard_map/ppermute | solution.py:552
  28.8 1.5 %collective-permute-start.9 = (bf16[2,4,80,128]{3,2,1,0:T(8,128)(2,1)S(1)}, bf16[2,4,80,128]{3,2,1,0:T(8,128)(2,1)S(1)}, u32[]{:S(2)}, u32[]{:S(2)}) collective-permute-start(bf16[2,4,80,128]{3,2,1,0:T(8,128)(2,1)S(1)} %pad_maximum_fusion.1), channel_id=1, source_target_pairs={{0,2},{1,3},{2,0},{3,1},{4,6},{5,7},{6,4},{7,5},{8,10},{9,11},{10,... | collective-permute-start | bytes 491528 | tf_op jit(solution)/shard_map/ppermute | solution.py:552
  30.3 0.0 copy-done.1
  30.3 9.6 %shard_map.99.far_ref = bf16[8192,256]{1,0:T(8,128)(2,1)} custom-call(bf16[256,8,1024]{2,1,0:T(8,128)(2,1)} %query_ref, f32[8,64,64]{2,1,0:T(8,128)S(1)} %copy-done.1), custom_call_target="tpu_custom_call" | custom-call | bytes 33000000 | tf_op jit(solution)/shard_map/pallas_call | solution.py:426
  39.9 0.0 collective-permute-done.9
  39.9 0.0 all-to-all-done.arrived_ref
  39.9 4.8 %shard_map.100 = f32[16,8,128]{2,1,0:T(8,128)S(1)} custom-call(bf16[16,128,128]{2,1,0:T(8,128)(2,1)S(1)} %all-to-all-done.arrived_ref, bf16[16,80,128]{2,1,0:T(8,128)(2,1)S(1)} %bitcast.13, bf16[8192,256]{1,0:T(8,128)(2,1)} %shard_map.99.far_ref), custom_call_target="tpu_custom_call" | custom-call | bytes 16500000 | tf_op jit(solution)/shard_map/pallas_call | solution.py:521
  44.7 9.1 %all_to_all.10.pieces_ref = f32[16,8,128]{2,1,0:T(8,128)S(1)} all-to-all(f32[16,8,128]{2,1,0:T(8,128)S(1)} %shard_map.100), channel_id=1, replica_groups={{12,13,14,15,0,1,2,3,4,5,6,7,8,9,10,11},{28,29,30,31,16,17,18,19,20,21,..., dimensions={0} | all-to-all | bytes 131072 | tf_op jit(solution)/shard_map/all_to_all | solution.py:33
  53.8 0.6 %shard_map.101 = f32[8,64]{1,0:T(8,128)} custom-call(f32[16,8,128]{2,1,0:T(8,128)S(1)} %all_to_all.10.pieces_ref), custom_call_target="tpu_custom_call" | custom-call | tf_op jit(solution)/shard_map/pallas_call | solution.py:543
  (9 shorter events, 0.1 us)
Async XLA Ops:
  0.0 18.0 %copy-start = (s32[512,8]{0,1:T(8,128)S(1)}, s32[512,8]{0,1:T(8,128)}, u32[]{:S(2)}) copy-start(s32[512,8]{0,1:T(8,128)} %param.11) | copy-start | bytes 49156
  3.1 10.6 %copy-start.2 = (s32[512]{0:T(512)S(1)}, s32[512]{0:T(512)}, u32[]{:S(2)}) copy-start(s32[512]{0:T(512)} %param.12) | copy-start | bytes 6148
  3.1 8.9 %collective-permute-start.1 = (bf16[2,128,128]{2,1,0:T(8,128)(2,1)S(1)}, bf16[2,128,128]{2,1,0:T(8,128)(2,1)S(1)}, u32[]{:S(2)}, u32[]{:S(2)}) collective-permute-start(bf16[2,128,128]{2,1,0:T(8,128)(2,1)S(1)} %get-tuple-element.28), channel_id=1, source_target_pairs={{0,2},{1,3},{2,0},{3,1},{4,6},{5,7},{6,4},{7,5},{8,10},{9,11},{10,... | collective-permute-start | bytes 196616 | tf_op jit(solution)/shard_map/ppermute | solution.py:552
  6.1 5.9 %collective-permute-start = (bf16[144,128]{1,0:T(8,128)(2,1)S(1)}, bf16[144,128]{1,0:T(8,128)(2,1)S(1)}, u32[]{:S(2)}, u32[]{:S(2)}) collective-permute-start(bf16[144,128]{1,0:T(8,128)(2,1)S(1)} %get-tuple-element.27), channel_id=1, source_target_pairs={{0,8},{4,12},{8,0},{12,4},{1,9},{5,13},{9,1},{13,5},{2,10},{6,14},... | collective-permute-start | bytes 110600 | tf_op jit(solution)/shard_map/ppermute | solution.py:552
  12.0 18.3 %copy-start.1 = (f32[8,64,64]{2,1,0:T(8,128)S(1)}, f32[8,64,64]{2,1,0:T(8,128)}, u32[]{:S(2)}) copy-start(f32[8,64,64]{2,1,0:T(8,128)} %inverse_ref.1) | copy-start | bytes 393220
  12.0 1.8 %collective-permute-start.2 = (bf16[2,512,128]{2,1,0:T(8,128)(2,1)S(1)}, bf16[2,512,128]{2,1,0:T(8,128)(2,1)S(1)}, u32[]{:S(2)}, u32[]{:S(2)}) collective-permute-start(bf16[2,512,128]{2,1,0:T(8,128)(2,1)S(1)} %get-tuple-element.30), channel_id=1, source_target_pairs={{0,1},{1,0},{2,3},{3,2},{4,5},{5,4},{6,7},{7,6},{8,9},{9,8},{10,11... | collective-permute-start | bytes 786440 | tf_op jit(solution)/shard_map/ppermute | solution.py:552
  12.1 1.5 %collective-permute-start.4 = (bf16[128,128]{1,0:T(8,128)(2,1)S(1)}, bf16[128,128]{1,0:T(8,128)(2,1)S(1)}, u32[]{:S(2)}, u32[]{:S(2)}) collective-permute-start(bf16[128,128]{1,0:T(8,128)(2,1)S(1)} %shard_map.95), channel_id=1, source_target_pairs={{0,1},{1,0},{2,3},{3,2},{4,5},{5,4},{6,7},{7,6},{8,9},{9,8},{10,11... | collective-permute-start | bytes 98312 | tf_op jit(solution)/shard_map/ppermute | solution.py:552
  13.9 5.7 %collective-permute-start.3 = (bf16[512,128]{1,0:T(8,128)(2,1)S(1)}, bf16[512,128]{1,0:T(8,128)(2,1)S(1)}, u32[]{:S(2)}, u32[]{:S(2)}) collective-permute-start(bf16[512,128]{1,0:T(8,128)(2,1)S(1)} %shard_map.94), channel_id=1, source_target_pairs={{0,2},{1,3},{2,0},{3,1},{4,6},{5,7},{6,4},{7,5},{8,10},{9,11},{10,... | collective-permute-start | bytes 393224 | tf_op jit(solution)/shard_map/ppermute | solution.py:552
  14.5 4.6 %collective-permute-start.5 = (bf16[368,128]{1,0:T(8,128)(2,1)S(1)}, bf16[368,128]{1,0:T(8,128)(2,1)S(1)}, u32[]{:S(2)}, u32[]{:S(2)}) collective-permute-start(bf16[368,128]{1,0:T(8,128)(2,1)S(1)} %pad_maximum_fusion.2), channel_id=1, source_target_pairs={{0,4},{4,0},{8,12},{12,8},{1,5},{5,1},{9,13},{13,9},{2,6},{6,2},{1... | collective-permute-start | bytes 282632 | tf_op jit(solution)/shard_map/ppermute | solution.py:552
  16.1 5.6 %collective-permute-start.7 = (bf16[80,128]{1,0:T(8,128)(2,1)S(1)}, bf16[80,128]{1,0:T(8,128)(2,1)S(1)}, u32[]{:S(2)}, u32[]{:S(2)}) collective-permute-start(bf16[80,128]{1,0:T(8,128)(2,1)S(1)} %shard_map.96), channel_id=1, source_target_pairs={{0,12},{4,8},{8,4},{12,0},{1,13},{5,9},{9,5},{13,1},{2,14},{6,10},... | collective-permute-start | bytes 61448 | tf_op jit(solution)/shard_map/ppermute | solution.py:552
  17.5 4.7 %collective-permute-start.6 = (bf16[80,128]{1,0:T(8,128)(2,1)S(1)}, bf16[80,128]{1,0:T(8,128)(2,1)S(1)}, u32[]{:S(2)}, u32[]{:S(2)}) collective-permute-start(bf16[80,128]{1,0:T(8,128)(2,1)S(1)} %shard_map.96), channel_id=1, source_target_pairs={{0,8},{4,12},{8,0},{12,4},{1,9},{5,13},{9,1},{13,5},{2,10},{6,14},... | collective-permute-start | bytes 61448 | tf_op jit(solution)/shard_map/ppermute | solution.py:552
  22.2 17.7 %all-to-all-start = ((bf16[16,128,128]{2,1,0:T(8,128)(2,1)}), bf16[16,128,128]{2,1,0:T(8,128)(2,1)S(1)}, u32[]{:S(2)}, u32[]{:S(2)}) async-start(bf16[16,128,128]{2,1,0:T(8,128)(2,1)} %shard_map.98), calls=%async_computation | async-start | bytes 1048576 | tf_op jit(solution)/shard_map/all_to_all | solution.py:33
  27.4 1.3 %collective-permute-start.8 = (bf16[1,4,80,128]{3,2,1,0:T(8,128)(2,1)S(1)}, bf16[1,4,80,128]{3,2,1,0:T(8,128)(2,1)S(1)}, u32[]{:S(2)}, u32[]{:S(2)}) collective-permute-start(bf16[1,4,80,128]{3,2,1,0:T(8,128)(2,1)S(1)} %maximum_bitcast_fusion), channel_id=1, source_target_pairs={{0,1},{1,0},{2,3},{3,2},{4,5},{5,4},{6,7},{7,6},{8,9},{9,8},{10,11... | collective-permute-start | bytes 245768 | tf_op jit(solution)/shard_map/ppermute | solution.py:552
  28.8 11.1 %collective-permute-start.9 = (bf16[2,4,80,128]{3,2,1,0:T(8,128)(2,1)S(1)}, bf16[2,4,80,128]{3,2,1,0:T(8,128)(2,1)S(1)}, u32[]{:S(2)}, u32[]{:S(2)}) collective-permute-start(bf16[2,4,80,128]{3,2,1,0:T(8,128)(2,1)S(1)} %pad_maximum_fusion.1), channel_id=1, source_target_pairs={{0,2},{1,3},{2,0},{3,1},{4,6},{5,7},{6,4},{7,5},{8,10},{9,11},{10,... | collective-permute-start | bytes 491528 | tf_op jit(solution)/shard_map/ppermute | solution.py:552

commit v23 on v22

--- a/solution.py
+++ b/solution.py
@@ -11,6 +11,7 @@
 LANES = 128
 DOC_ROWS = 16
 DIAGONAL_ROWS = 16
+QUERY_PARTS = 4
 MIB = 1024 * 1024
 VMEM = pl.BlockSpec(memory_space=pltpu.VMEM)
 HBM = pl.BlockSpec(memory_space=pltpu.HBM)
@@ -372,8 +373,10 @@
     )(own, near, far, quarter_routes, even, odd)
 
 
-def query_kernel(query_ref, inverse_ref, out_hbm, factor_ref, spread_ref, wide_ref, out_ref, sems):
-    count, experts, _ = query_ref.shape
+def query_kernel(*refs):
+    *query_refs, inverse_ref, out_hbm, factor_ref, spread_ref, wide_ref, out_ref, sems = refs
+    part_count, experts, _ = query_refs[0].shape
+    count = part_count * len(query_refs)
     width = inverse_ref.shape[1]
     step = pl.program_id(0)
     rows = out_ref.shape[0] // width
@@ -388,7 +391,11 @@
             right = jnp.concatenate([zeros, high, zeros, low], axis=0)
             factor_ref[e] = jnp.concatenate([left, right], axis=1)
 
-    spread_ref[...] = query_ref[...].astype(jnp.float32).reshape(count * experts, LANES)
+    part_rows = part_count * experts
+    for r, query_ref in enumerate(query_refs):
+        spread_ref[r * part_rows : (r + 1) * part_rows, :] = (
+            query_ref[...].astype(jnp.float32).reshape(part_rows, LANES)
+        )
     for e in range(experts):
         query = spread_ref[pl.ds(e, count, stride=experts), :].astype(jnp.bfloat16)
         result = lax.dot_general(
@@ -427,9 +434,10 @@
         query_kernel,
         grid=(flat // LANES,),
         in_specs=[
-            pl.BlockSpec((count, experts, LANES), lambda c: (0, 0, c)),
-            pl.BlockSpec(inverse_in.shape, lambda c: (0, 0, 0)),
-        ],
+            pl.BlockSpec((count // QUERY_PARTS, experts, LANES), functools.partial(lambda r, c: (r, 0, c), r))
+            for r in range(QUERY_PARTS)
+        ]
+        + [pl.BlockSpec(inverse_in.shape, lambda c: (0, 0, 0))],
         out_specs=HBM,
         out_shape=pltpu.HBM((rows, count), jnp.bfloat16),
         scratch_shapes=[
@@ -441,7 +449,7 @@
         ],
         compiler_params=pltpu.CompilerParams(vmem_limit_bytes=40 * MIB),
         cost_estimate=cost(10),
-    )(stay(query_grads), inverse_in)
+    )(*[stay(query_grads)] * QUERY_PARTS, inverse_in)
 
 
 def score_kernel(

time: 54.9 us -> 54.9 us (level)
  no operation moved by 1% of the time
where the time goes in v23:
time: 54.9 us; the launch traced here: 54.5 us
  Pallas kernels  24.3 us (44%)
  starting transfers between devices  17.3 us (32%)
  blocking collectives  8.93 us (16%)
  waiting for transfers between devices  3.59 us (7%)
    ppermute x10, starting transfers between devices, exchange(): return lax.ppermute(block, axis, [(i, i ^ turn) for i in range(size)])  12.1 us
    pallas_call x1, Pallas kernels, condition_queries(): pl.pallas_call(query_kernel, grid=(flat // LANES,), in_specs=[pl.BlockSpe...  9.73 us
    all_to_all x1, blocking collectives, send_to_all(): lax.all_to_all(blocks, ('expert', 'proj'), 0, 0, tiled=True, axis_index_g...  8.93 us
    all_to_all x1, starting transfers between devices, send_to_all(): lax.all_to_all(blocks, ('expert', 'proj'), 0, 0, tiled=True, axis_index_g...  5.21 us
    pallas_call x1, Pallas kernels, score(): pl.pallas_call(functools.partial(score_kernel, width=width, doc_count=doc...  4.82 us
    ppermute x10, waiting for transfers between devices, exchange(): return lax.ppermute(block, axis, [(i, i ^ turn) for i in range(size)])  3.58 us
    pallas_call x1, Pallas kernels, project_outer(): pl.pallas_call(functools.partial(outer_kernel, top=top), in_specs=[VMEM,...  3.28 us
    pallas_call x1, Pallas kernels, project_inner(): pl.pallas_call(inner_kernel, in_specs=[HBM] * 4, out_specs=[VMEM] * 4, ou...  3.08 us
  transfers between devices with their start and end apart: 11, of which 5 were waited for; matrix products, arithmetic and copies ran while one was open for 0% of the time, Pallas kernels for 29%

profile of v23, /device:TPU:0, one launch (start us, length us, event | category | flops | bytes accessed | tf_op | source)
XLA Modules:
  0.0 54.5 jit_solution(1429607612546813970)
XLA Ops:
  0.0 0.0 copy-start
  0.0 3.1 %shard_map.91 = (bf16[2,128,128]{2,1,0:T(8,128)(2,1)S(1)}, bf16[2,128,128]{2,1,0:T(8,128)(2,1)S(1)}, bf16[144,128]{1,0:T(8,128)(2,1)S(1)}, bf16[2,1024,512]{2,1,0:T(8,128)(2,1)S(1)}) custom-call(bf16[512,1792]{1,0:T(8,128)(2,1)} %act_hbm.1, bf16[64,1792]{1,0:T(8,128)(2,1)} %in_proj_hbm.1, f32[8,64,64]{2,1,0:T(8,128)} %inverse_hbm.1, bf16[4096,512]{1,0:T(8,128)(2,1)} %bitcast.19), custom_call_target="tpu_custom_call" | custom-call | bytes 8250000 | tf_op jit(solution)/shard_map/pallas_call | solution.py:162
  3.1 0.0 copy-start.2
  3.1 3.0 %collective-permute-start.1 = (bf16[2,128,128]{2,1,0:T(8,128)(2,1)S(1)}, bf16[2,128,128]{2,1,0:T(8,128)(2,1)S(1)}, u32[]{:S(2)}, u32[]{:S(2)}) collective-permute-start(bf16[2,128,128]{2,1,0:T(8,128)(2,1)S(1)} %get-tuple-element.28), channel_id=1, source_target_pairs={{0,2},{1,3},{2,0},{3,1},{4,6},{5,7},{6,4},{7,5},{8,10},{9,11},{10,... | collective-permute-start | bytes 196616 | tf_op jit(solution)/shard_map/ppermute | solution.py:560
  6.1 2.6 %collective-permute-start = (bf16[144,128]{1,0:T(8,128)(2,1)S(1)}, bf16[144,128]{1,0:T(8,128)(2,1)S(1)}, u32[]{:S(2)}, u32[]{:S(2)}) collective-permute-start(bf16[144,128]{1,0:T(8,128)(2,1)S(1)} %get-tuple-element.27), channel_id=1, source_target_pairs={{0,8},{4,12},{8,0},{12,4},{1,9},{5,13},{9,1},{13,5},{2,10},{6,14},... | collective-permute-start | bytes 110600 | tf_op jit(solution)/shard_map/ppermute | solution.py:560
  8.7 3.3 %shard_map.92 = (bf16[2,512,128]{2,1,0:T(8,128)(2,1)S(1)}, bf16[2,512,128]{2,1,0:T(8,128)(2,1)S(1)}) custom-call(bf16[2,1024,512]{2,1,0:T(8,128)(2,1)S(1)} %get-tuple-element.25.near_ref, bf16[4096,512]{1,0:T(8,128)(2,1)} %bitcast.20, bf16[64,512]{1,0:T(8,128)(2,1)} %out_proj_hbm.1), custom_call_target="tpu_custom_call" | custom-call | bytes 13200000 | tf_op jit(solution)/shard_map/pallas_call | solution.py:213
  12.0 0.0 copy-start.1
  12.0 0.0 collective-permute-done
  12.0 0.0 collective-permute-done.1.near_ref.first_ref
  12.0 0.1 collective-permute-start.2
  12.1 0.6 %collective-permute-start.4 = (bf16[128,128]{1,0:T(8,128)(2,1)S(1)}, bf16[128,128]{1,0:T(8,128)(2,1)S(1)}, u32[]{:S(2)}, u32[]{:S(2)}) collective-permute-start(bf16[128,128]{1,0:T(8,128)(2,1)S(1)} %shard_map.95), channel_id=1, source_target_pairs={{0,1},{1,0},{2,3},{3,2},{4,5},{5,4},{6,7},{7,6},{8,9},{9,8},{10,11... | collective-permute-start | bytes 98312 | tf_op jit(solution)/shard_map/ppermute | solution.py:560
  12.7 0.4 shard_map.93.even_ref
  13.1 0.5 collective-permute-done.4.second_ref
  13.7 0.0 copy-done.2
  13.7 0.1 shard_map.96
  13.8 0.0 collective-permute-done.2.near_ref
  13.9 0.6 %collective-permute-start.3 = (bf16[512,128]{1,0:T(8,128)(2,1)S(1)}, bf16[512,128]{1,0:T(8,128)(2,1)S(1)}, u32[]{:S(2)}, u32[]{:S(2)}) collective-permute-start(bf16[512,128]{1,0:T(8,128)(2,1)S(1)} %shard_map.94), channel_id=1, source_target_pairs={{0,2},{1,3},{2,0},{3,1},{4,6},{5,7},{6,4},{7,5},{8,10},{9,11},{10,... | collective-permute-start | bytes 393224 | tf_op jit(solution)/shard_map/ppermute | solution.py:560
  14.5 1.6 %collective-permute-start.5 = (bf16[368,128]{1,0:T(8,128)(2,1)S(1)}, bf16[368,128]{1,0:T(8,128)(2,1)S(1)}, u32[]{:S(2)}, u32[]{:S(2)}) collective-permute-start(bf16[368,128]{1,0:T(8,128)(2,1)S(1)} %pad_maximum_fusion.2), channel_id=1, source_target_pairs={{0,4},{4,0},{8,12},{12,8},{1,5},{5,1},{9,13},{13,9},{2,6},{6,2},{1... | collective-permute-start | bytes 282632 | tf_op jit(solution)/shard_map/ppermute | solution.py:560
  16.1 1.4 %collective-permute-start.7 = (bf16[80,128]{1,0:T(8,128)(2,1)S(1)}, bf16[80,128]{1,0:T(8,128)(2,1)S(1)}, u32[]{:S(2)}, u32[]{:S(2)}) collective-permute-start(bf16[80,128]{1,0:T(8,128)(2,1)S(1)} %shard_map.96), channel_id=1, source_target_pairs={{0,12},{4,8},{8,4},{12,0},{1,13},{5,9},{9,5},{13,1},{2,14},{6,10},... | collective-permute-start | bytes 61448 | tf_op jit(solution)/shard_map/ppermute | solution.py:560
  17.5 0.5 collective-permute-start.6
  18.0 0.0 copy-done
  18.0 0.1 copy.11.routes_ref
  18.1 1.0 %collective-permute-done.5.shared_ref = bf16[368,128]{1,0:T(8,128)(2,1)S(1)} collective-permute-done((bf16[368,128]{1,0:T(8,128)(2,1)S(1)}, bf16[368,128]{1,0:T(8,128)(2,1)S(1)}, u32[]{:S(2)}, u32[]{:S(2)}) %collective-permute-start.5) | collective-permute-done | bytes 94240 | tf_op jit(solution)/shard_map/ppermute | solution.py:560
  19.1 0.4 shard_map.97.odd_ref
  19.5 0.0 collective-permute-done.3.far_ref
  19.6 1.7 %shard_map.98 = bf16[16,128,128]{2,1,0:T(8,128)(2,1)} custom-call(bf16[2,512,128]{2,1,0:T(8,128)(2,1)S(1)} %get-tuple-element.26.own_ref, bf16[2,512,128]{2,1,0:T(8,128)(2,1)S(1)} %collective-permute-done.2.near_ref, bf16[512,128]{1,0:T(8,128)(2,1)S(1)} %collective-permute-done.3.far_ref, s32[128,8]{1,0:T(8,128)S(1)} %copy.11.routes_ref, ...), custom_call_target="tpu_custom_call" | custom-call | bytes 6600000 | tf_op jit(solution)/shard_map/pallas_call | solution.py:363
  21.3 0.4 collective-permute-done.7
  21.7 0.5 collective-permute-done.6
  22.2 5.2 %all-to-all-start = ((bf16[16,128,128]{2,1,0:T(8,128)(2,1)}), bf16[16,128,128]{2,1,0:T(8,128)(2,1)S(1)}, u32[]{:S(2)}, u32[]{:S(2)}) async-start(bf16[16,128,128]{2,1,0:T(8,128)(2,1)} %shard_map.98), calls=%async_computation | async-start | bytes 1048576 | tf_op jit(solution)/shard_map/all_to_all | solution.py:34
  27.4 0.2 collective-permute-start.8
  27.6 1.1 %collective-permute-done.8 = bf16[1,4,80,128]{3,2,1,0:T(8,128)(2,1)S(1)} collective-permute-done((bf16[1,4,80,128]{3,2,1,0:T(8,128)(2,1)S(1)}, bf16[1,4,80,128]{3,2,1,0:T(8,128)(2,1)S(1)}, u32[]{:S(2)}, u32[]{:S(2)}) %collective-permute-start.8) | collective-permute-done | bytes 81952 | tf_op jit(solution)/shard_map/ppermute | solution.py:560
  28.8 1.5 %collective-permute-start.9 = (bf16[2,4,80,128]{3,2,1,0:T(8,128)(2,1)S(1)}, bf16[2,4,80,128]{3,2,1,0:T(8,128)(2,1)S(1)}, u32[]{:S(2)}, u32[]{:S(2)}) collective-permute-start(bf16[2,4,80,128]{3,2,1,0:T(8,128)(2,1)S(1)} %pad_maximum_fusion.1), channel_id=1, source_target_pairs={{0,2},{1,3},{2,0},{3,1},{4,6},{5,7},{6,4},{7,5},{8,10},{9,11},{10,... | collective-permute-start | bytes 491528 | tf_op jit(solution)/shard_map/ppermute | solution.py:560
  30.3 0.0 copy-done.1
  30.3 9.7 %shard_map.99.far_ref = bf16[8192,256]{1,0:T(8,128)(2,1)} custom-call(bf16[256,8,1024]{2,1,0:T(8,128)(2,1)} %refs_3_, bf16[256,8,1024]{2,1,0:T(8,128)(2,1)} %refs_3_, bf16[256,8,1024]{2,1,0:T(8,128)(2,1)} %refs_3_, bf16[256,8,1024]{2,1,0:T(8,128)(2,1)} %refs_3_, f32[8,64,64]{2,1,0:T(8,128)S(1)} %copy-done.1), custom_call_target="tpu_custom_call" | custom-call | bytes 33000000 | tf_op jit(solution)/shard_map/pallas_call | solution.py:433
  40.0 0.0 collective-permute-done.9
  40.1 0.0 all-to-all-done.arrived_ref
  40.1 4.8 %shard_map.100 = f32[16,8,128]{2,1,0:T(8,128)S(1)} custom-call(bf16[16,128,128]{2,1,0:T(8,128)(2,1)S(1)} %all-to-all-done.arrived_ref, bf16[16,80,128]{2,1,0:T(8,128)(2,1)S(1)} %bitcast.13, bf16[8192,256]{1,0:T(8,128)(2,1)} %shard_map.99.far_ref), custom_call_target="tpu_custom_call" | custom-call | bytes 16500000 | tf_op jit(solution)/shard_map/pallas_call | solution.py:529
  44.9 8.9 %all_to_all.10.pieces_ref = f32[16,8,128]{2,1,0:T(8,128)S(1)} all-to-all(f32[16,8,128]{2,1,0:T(8,128)S(1)} %shard_map.100), channel_id=1, replica_groups={{12,13,14,15,0,1,2,3,4,5,6,7,8,9,10,11},{28,29,30,31,16,17,18,19,20,21,..., dimensions={0} | all-to-all | bytes 131072 | tf_op jit(solution)/shard_map/all_to_all | solution.py:34
  53.8 0.6 %shard_map.101 = f32[8,64]{1,0:T(8,128)} custom-call(f32[16,8,128]{2,1,0:T(8,128)S(1)} %all_to_all.10.pieces_ref), custom_call_target="tpu_custom_call" | custom-call | tf_op jit(solution)/shard_map/pallas_call | solution.py:551
  (9 shorter events, 0.1 us)
Async XLA Ops:
  0.0 18.0 %copy-start = (s32[512,8]{0,1:T(8,128)S(1)}, s32[512,8]{0,1:T(8,128)}, u32[]{:S(2)}) copy-start(s32[512,8]{0,1:T(8,128)} %param.11) | copy-start | bytes 49156
  3.1 10.6 %copy-start.2 = (s32[512]{0:T(512)S(1)}, s32[512]{0:T(512)}, u32[]{:S(2)}) copy-start(s32[512]{0:T(512)} %param.12) | copy-start | bytes 6148
  3.1 8.9 %collective-permute-start.1 = (bf16[2,128,128]{2,1,0:T(8,128)(2,1)S(1)}, bf16[2,128,128]{2,1,0:T(8,128)(2,1)S(1)}, u32[]{:S(2)}, u32[]{:S(2)}) collective-permute-start(bf16[2,128,128]{2,1,0:T(8,128)(2,1)S(1)} %get-tuple-element.28), channel_id=1, source_target_pairs={{0,2},{1,3},{2,0},{3,1},{4,6},{5,7},{6,4},{7,5},{8,10},{9,11},{10,... | collective-permute-start | bytes 196616 | tf_op jit(solution)/shard_map/ppermute | solution.py:560
  6.1 5.9 %collective-permute-start = (bf16[144,128]{1,0:T(8,128)(2,1)S(1)}, bf16[144,128]{1,0:T(8,128)(2,1)S(1)}, u32[]{:S(2)}, u32[]{:S(2)}) collective-permute-start(bf16[144,128]{1,0:T(8,128)(2,1)S(1)} %get-tuple-element.27), channel_id=1, source_target_pairs={{0,8},{4,12},{8,0},{12,4},{1,9},{5,13},{9,1},{13,5},{2,10},{6,14},... | collective-permute-start | bytes 110600 | tf_op jit(solution)/shard_map/ppermute | solution.py:560
  12.0 18.3 %copy-start.1 = (f32[8,64,64]{2,1,0:T(8,128)S(1)}, f32[8,64,64]{2,1,0:T(8,128)}, u32[]{:S(2)}) copy-start(f32[8,64,64]{2,1,0:T(8,128)} %refs_4_.1) | copy-start | bytes 393220
  12.0 1.8 %collective-permute-start.2 = (bf16[2,512,128]{2,1,0:T(8,128)(2,1)S(1)}, bf16[2,512,128]{2,1,0:T(8,128)(2,1)S(1)}, u32[]{:S(2)}, u32[]{:S(2)}) collective-permute-start(bf16[2,512,128]{2,1,0:T(8,128)(2,1)S(1)} %get-tuple-element.30), channel_id=1, source_target_pairs={{0,1},{1,0},{2,3},{3,2},{4,5},{5,4},{6,7},{7,6},{8,9},{9,8},{10,11... | collective-permute-start | bytes 786440 | tf_op jit(solution)/shard_map/ppermute | solution.py:560
  12.1 1.5 %collective-permute-start.4 = (bf16[128,128]{1,0:T(8,128)(2,1)S(1)}, bf16[128,128]{1,0:T(8,128)(2,1)S(1)}, u32[]{:S(2)}, u32[]{:S(2)}) collective-permute-start(bf16[128,128]{1,0:T(8,128)(2,1)S(1)} %shard_map.95), channel_id=1, source_target_pairs={{0,1},{1,0},{2,3},{3,2},{4,5},{5,4},{6,7},{7,6},{8,9},{9,8},{10,11... | collective-permute-start | bytes 98312 | tf_op jit(solution)/shard_map/ppermute | solution.py:560
  13.9 5.7 %collective-permute-start.3 = (bf16[512,128]{1,0:T(8,128)(2,1)S(1)}, bf16[512,128]{1,0:T(8,128)(2,1)S(1)}, u32[]{:S(2)}, u32[]{:S(2)}) collective-permute-start(bf16[512,128]{1,0:T(8,128)(2,1)S(1)} %shard_map.94), channel_id=1, source_target_pairs={{0,2},{1,3},{2,0},{3,1},{4,6},{5,7},{6,4},{7,5},{8,10},{9,11},{10,... | collective-permute-start | bytes 393224 | tf_op jit(solution)/shard_map/ppermute | solution.py:560
  14.5 4.6 %collective-permute-start.5 = (bf16[368,128]{1,0:T(8,128)(2,1)S(1)}, bf16[368,128]{1,0:T(8,128)(2,1)S(1)}, u32[]{:S(2)}, u32[]{:S(2)}) collective-permute-start(bf16[368,128]{1,0:T(8,128)(2,1)S(1)} %pad_maximum_fusion.2), channel_id=1, source_target_pairs={{0,4},{4,0},{8,12},{12,8},{1,5},{5,1},{9,13},{13,9},{2,6},{6,2},{1... | collective-permute-start | bytes 282632 | tf_op jit(solution)/shard_map/ppermute | solution.py:560
  16.1 5.6 %collective-permute-start.7 = (bf16[80,128]{1,0:T(8,128)(2,1)S(1)}, bf16[80,128]{1,0:T(8,128)(2,1)S(1)}, u32[]{:S(2)}, u32[]{:S(2)}) collective-permute-start(bf16[80,128]{1,0:T(8,128)(2,1)S(1)} %shard_map.96), channel_id=1, source_target_pairs={{0,12},{4,8},{8,4},{12,0},{1,13},{5,9},{9,5},{13,1},{2,14},{6,10},... | collective-permute-start | bytes 61448 | tf_op jit(solution)/shard_map/ppermute | solution.py:560
  17.5 4.7 %collective-permute-start.6 = (bf16[80,128]{1,0:T(8,128)(2,1)S(1)}, bf16[80,128]{1,0:T(8,128)(2,1)S(1)}, u32[]{:S(2)}, u32[]{:S(2)}) collective-permute-start(bf16[80,128]{1,0:T(8,128)(2,1)S(1)} %shard_map.96), channel_id=1, source_target_pairs={{0,8},{4,12},{8,0},{12,4},{1,9},{5,13},{9,1},{13,5},{2,10},{6,14},... | collective-permute-start | bytes 61448 | tf_op jit(solution)/shard_map/ppermute | solution.py:560
  22.2 17.9 %all-to-all-start = ((bf16[16,128,128]{2,1,0:T(8,128)(2,1)}), bf16[16,128,128]{2,1,0:T(8,128)(2,1)S(1)}, u32[]{:S(2)}, u32[]{:S(2)}) async-start(bf16[16,128,128]{2,1,0:T(8,128)(2,1)} %shard_map.98), calls=%async_computation | async-start | bytes 1048576 | tf_op jit(solution)/shard_map/all_to_all | solution.py:34
  27.4 1.3 %collective-permute-start.8 = (bf16[1,4,80,128]{3,2,1,0:T(8,128)(2,1)S(1)}, bf16[1,4,80,128]{3,2,1,0:T(8,128)(2,1)S(1)}, u32[]{:S(2)}, u32[]{:S(2)}) collective-permute-start(bf16[1,4,80,128]{3,2,1,0:T(8,128)(2,1)S(1)} %maximum_bitcast_fusion), channel_id=1, source_target_pairs={{0,1},{1,0},{2,3},{3,2},{4,5},{5,4},{6,7},{7,6},{8,9},{9,8},{10,11... | collective-permute-start | bytes 245768 | tf_op jit(solution)/shard_map/ppermute | solution.py:560
  28.8 11.3 %collective-permute-start.9 = (bf16[2,4,80,128]{3,2,1,0:T(8,128)(2,1)S(1)}, bf16[2,4,80,128]{3,2,1,0:T(8,128)(2,1)S(1)}, u32[]{:S(2)}, u32[]{:S(2)}) collective-permute-start(bf16[2,4,80,128]{3,2,1,0:T(8,128)(2,1)S(1)} %pad_maximum_fusion.1), channel_id=1, source_target_pairs={{0,2},{1,3},{2,0},{3,1},{4,6},{5,7},{6,4},{7,5},{8,10},{9,11},{10,... | collective-permute-start | bytes 491528 | tf_op jit(solution)/shard_map/ppermute | solution.py:560

commit v24 on v23

--- a/solution.py
+++ b/solution.py
@@ -11,7 +11,7 @@
 LANES = 128
 DOC_ROWS = 16
 DIAGONAL_ROWS = 16
-QUERY_PARTS = 4
+QUERY_PARTS = 1
 MIB = 1024 * 1024
 VMEM = pl.BlockSpec(memory_space=pltpu.VMEM)
 HBM = pl.BlockSpec(memory_space=pltpu.HBM)
@@ -614,13 +614,11 @@
     far, odd = lax.optimization_barrier((far, odd))
     quarter_routes = lax.dynamic_slice_in_dim(routes, lax.axis_index("proj") * quarter, quarter, 0)
     payload = condition(own, near, far, quarter_routes, even, odd, shares, width)
-    payload, arriving = lax.optimization_barrier((payload, arriving))
+    payload, arriving, query_grads = lax.optimization_barrier((payload, arriving, query_grads))
     arrived = send_to_all(payload, owners, shares, owners // 2)
     inner = jnp.stack(arriving + [inner])
-    inner, share_turns = inner[None], (0,)
-    inner, share_turns = double(inner, share_turns, "proj", shares, 1)
-    inner, query_grads = lax.optimization_barrier((inner, query_grads))
-    inner, share_turns = double(inner, share_turns, "proj", shares, 2)
+    share_turns = tuple(range(shares))
+    inner = jnp.stack([exchange(inner, "proj", shares, turn) if turn else inner for turn in share_turns])
     inner = inner.reshape(owners * shares, width + DOC_ROWS, quarter)
     all_turns = tuple((o, p) for p in share_turns for o in owner_turns)
     queries = condition_queries(query_grads, inverse_in)

time: 54.9 us -> 54.9 us (level)
  waiting for transfers between devices: 3.59 us -> 2.77 us
    ppermute x10 -> x11, waiting for transfers between devices: 3.58 us -> 2.46 us  [exchange(): return lax.ppermute(block, axis, [(i, i ^ turn) for i in range(size)])]
    ppermute x10 -> x11, starting transfers between devices: 12.1 us -> 12.6 us  [exchange(): return lax.ppermute(block, axis, [(i, i ^ turn) for i in range(size)])]
  transfers between devices with their start and end apart: 11 -> 12, of which waited for: 5 -> 5; matrix products, arithmetic and copies ran while one was open for 0% -> 0% of each run, Pallas kernels for 29% -> 28%
where the time goes in v24:
time: 54.9 us; the launch traced here: 54.5 us
  Pallas kernels  24.1 us (44%)
  starting transfers between devices  17.8 us (32%)
  blocking collectives  9.47 us (17%)
  waiting for transfers between devices  2.77 us (5%)
    ppermute x11, starting transfers between devices, exchange(): return lax.ppermute(block, axis, [(i, i ^ turn) for i in range(size)])  12.6 us
    pallas_call x1, Pallas kernels, condition_queries(): pl.pallas_call(query_kernel, grid=(flat // LANES,), in_specs=[pl.BlockSpe...  9.55 us
    all_to_all x1, blocking collectives, send_to_all(): lax.all_to_all(blocks, ('expert', 'proj'), 0, 0, tiled=True, axis_index_g...  9.47 us
    all_to_all x1, starting transfers between devices, send_to_all(): lax.all_to_all(blocks, ('expert', 'proj'), 0, 0, tiled=True, axis_index_g...  5.21 us
    pallas_call x1, Pallas kernels, score(): pl.pallas_call(functools.partial(score_kernel, width=width, doc_count=doc...  4.81 us
    pallas_call x1, Pallas kernels, project_outer(): pl.pallas_call(functools.partial(outer_kernel, top=top), in_specs=[VMEM,...  3.28 us
    pallas_call x1, Pallas kernels, project_inner(): pl.pallas_call(inner_kernel, in_specs=[HBM] * 4, out_specs=[VMEM] * 4, ou...  3.08 us
    ppermute x11, waiting for transfers between devices, exchange(): return lax.ppermute(block, axis, [(i, i ^ turn) for i in range(size)])  2.46 us
  transfers between devices with their start and end apart: 12, of which 5 were waited for; matrix products, arithmetic and copies ran while one was open for 0% of the time, Pallas kernels for 28%

profile of v24, /device:TPU:0, one launch (start us, length us, event | category | flops | bytes accessed | tf_op | source)
XLA Modules:
  0.0 54.5 jit_solution(15466631413326432086)
XLA Ops:
  0.0 0.0 copy-start
  0.0 3.1 %shard_map.91 = (bf16[2,128,128]{2,1,0:T(8,128)(2,1)S(1)}, bf16[2,128,128]{2,1,0:T(8,128)(2,1)S(1)}, bf16[144,128]{1,0:T(8,128)(2,1)S(1)}, bf16[2,1024,512]{2,1,0:T(8,128)(2,1)S(1)}) custom-call(bf16[512,1792]{1,0:T(8,128)(2,1)} %act_hbm.1, bf16[64,1792]{1,0:T(8,128)(2,1)} %in_proj_hbm.1, f32[8,64,64]{2,1,0:T(8,128)} %inverse_hbm.1, bf16[4096,512]{1,0:T(8,128)(2,1)} %bitcast.22), custom_call_target="tpu_custom_call" | custom-call | bytes 8250000 | tf_op jit(solution)/shard_map/pallas_call | solution.py:162
  3.1 0.0 copy-start.2
  3.1 3.0 %collective-permute-start.1 = (bf16[2,128,128]{2,1,0:T(8,128)(2,1)S(1)}, bf16[2,128,128]{2,1,0:T(8,128)(2,1)S(1)}, u32[]{:S(2)}, u32[]{:S(2)}) collective-permute-start(bf16[2,128,128]{2,1,0:T(8,128)(2,1)S(1)} %get-tuple-element.27), channel_id=1, source_target_pairs={{0,2},{1,3},{2,0},{3,1},{4,6},{5,7},{6,4},{7,5},{8,10},{9,11},{10,... | collective-permute-start | bytes 196616 | tf_op jit(solution)/shard_map/ppermute | solution.py:560
  6.1 2.6 %collective-permute-start = (bf16[144,128]{1,0:T(8,128)(2,1)S(1)}, bf16[144,128]{1,0:T(8,128)(2,1)S(1)}, u32[]{:S(2)}, u32[]{:S(2)}) collective-permute-start(bf16[144,128]{1,0:T(8,128)(2,1)S(1)} %get-tuple-element.26), channel_id=1, source_target_pairs={{0,8},{4,12},{8,0},{12,4},{1,9},{5,13},{9,1},{13,5},{2,10},{6,14},... | collective-permute-start | bytes 110600 | tf_op jit(solution)/shard_map/ppermute | solution.py:560
  8.7 3.3 %shard_map.92 = (bf16[2,512,128]{2,1,0:T(8,128)(2,1)S(1)}, bf16[2,512,128]{2,1,0:T(8,128)(2,1)S(1)}) custom-call(bf16[2,1024,512]{2,1,0:T(8,128)(2,1)S(1)} %get-tuple-element.24.near_ref, bf16[4096,512]{1,0:T(8,128)(2,1)} %bitcast.23, bf16[64,512]{1,0:T(8,128)(2,1)} %out_proj_hbm.1), custom_call_target="tpu_custom_call" | custom-call | bytes 13200000 | tf_op jit(solution)/shard_map/pallas_call | solution.py:213
  12.0 0.0 copy-start.1
  12.0 0.0 collective-permute-done
  12.0 0.0 collective-permute-done.1.near_ref.first_ref
  12.0 0.1 collective-permute-start.2
  12.1 0.6 %collective-permute-start.4 = (bf16[128,128]{1,0:T(8,128)(2,1)S(1)}, bf16[128,128]{1,0:T(8,128)(2,1)S(1)}, u32[]{:S(2)}, u32[]{:S(2)}) collective-permute-start(bf16[128,128]{1,0:T(8,128)(2,1)S(1)} %shard_map.95), channel_id=1, source_target_pairs={{0,1},{1,0},{2,3},{3,2},{4,5},{5,4},{6,7},{7,6},{8,9},{9,8},{10,11... | collective-permute-start | bytes 98312 | tf_op jit(solution)/shard_map/ppermute | solution.py:560
  12.7 0.4 shard_map.93.even_ref
  13.1 0.5 collective-permute-done.4.second_ref
  13.7 0.0 copy-done.2
  13.7 0.1 shard_map.96
  13.8 0.0 collective-permute-done.2.near_ref
  13.9 0.6 %collective-permute-start.3 = (bf16[512,128]{1,0:T(8,128)(2,1)S(1)}, bf16[512,128]{1,0:T(8,128)(2,1)S(1)}, u32[]{:S(2)}, u32[]{:S(2)}) collective-permute-start(bf16[512,128]{1,0:T(8,128)(2,1)S(1)} %shard_map.94), channel_id=1, source_target_pairs={{0,2},{1,3},{2,0},{3,1},{4,6},{5,7},{6,4},{7,5},{8,10},{9,11},{10,... | collective-permute-start | bytes 393224 | tf_op jit(solution)/shard_map/ppermute | solution.py:560
  14.5 1.6 %collective-permute-start.5 = (bf16[368,128]{1,0:T(8,128)(2,1)S(1)}, bf16[368,128]{1,0:T(8,128)(2,1)S(1)}, u32[]{:S(2)}, u32[]{:S(2)}) collective-permute-start(bf16[368,128]{1,0:T(8,128)(2,1)S(1)} %pad_maximum_fusion.1), channel_id=1, source_target_pairs={{0,4},{4,0},{8,12},{12,8},{1,5},{5,1},{9,13},{13,9},{2,6},{6,2},{1... | collective-permute-start | bytes 282632 | tf_op jit(solution)/shard_map/ppermute | solution.py:560
  16.1 1.4 %collective-permute-start.7 = (bf16[80,128]{1,0:T(8,128)(2,1)S(1)}, bf16[80,128]{1,0:T(8,128)(2,1)S(1)}, u32[]{:S(2)}, u32[]{:S(2)}) collective-permute-start(bf16[80,128]{1,0:T(8,128)(2,1)S(1)} %shard_map.96), channel_id=1, source_target_pairs={{0,12},{4,8},{8,4},{12,0},{1,13},{5,9},{9,5},{13,1},{2,14},{6,10},... | collective-permute-start | bytes 61448 | tf_op jit(solution)/shard_map/ppermute | solution.py:560
  17.5 0.5 collective-permute-start.6
  18.0 0.0 copy-done
  18.0 0.1 copy.11.routes_ref
  18.1 1.0 %collective-permute-done.5.shared_ref = bf16[368,128]{1,0:T(8,128)(2,1)S(1)} collective-permute-done((bf16[368,128]{1,0:T(8,128)(2,1)S(1)}, bf16[368,128]{1,0:T(8,128)(2,1)S(1)}, u32[]{:S(2)}, u32[]{:S(2)}) %collective-permute-start.5) | collective-permute-done | bytes 94240 | tf_op jit(solution)/shard_map/ppermute | solution.py:560
  19.1 0.4 shard_map.97.odd_ref
  19.5 0.0 collective-permute-done.3.far_ref
  19.6 1.7 %shard_map.98 = bf16[16,128,128]{2,1,0:T(8,128)(2,1)} custom-call(bf16[2,512,128]{2,1,0:T(8,128)(2,1)S(1)} %get-tuple-element.25.own_ref, bf16[2,512,128]{2,1,0:T(8,128)(2,1)S(1)} %collective-permute-done.2.near_ref, bf16[512,128]{1,0:T(8,128)(2,1)S(1)} %collective-permute-done.3.far_ref, s32[128,8]{1,0:T(8,128)S(1)} %copy.11.routes_ref, ...), custom_call_target="tpu_custom_call" | custom-call | bytes 6600000 | tf_op jit(solution)/shard_map/pallas_call | solution.py:363
  21.3 0.4 collective-permute-done.7
  21.7 0.5 collective-permute-done.6
  22.2 5.2 %all-to-all-start = ((bf16[16,128,128]{2,1,0:T(8,128)(2,1)}), bf16[16,128,128]{2,1,0:T(8,128)(2,1)S(1)}, u32[]{:S(2)}, u32[]{:S(2)}) async-start(bf16[16,128,128]{2,1,0:T(8,128)(2,1)} %shard_map.98), calls=%async_computation | async-start | bytes 1048576 | tf_op jit(solution)/shard_map/all_to_all | solution.py:34
  27.4 1.5 %collective-permute-start.9 = (bf16[4,80,128]{2,1,0:T(8,128)(2,1)S(1)}, bf16[4,80,128]{2,1,0:T(8,128)(2,1)S(1)}, u32[]{:S(2)}, u32[]{:S(2)}) collective-permute-start(bf16[4,80,128]{2,1,0:T(8,128)(2,1)S(1)} %get-tuple-element.44), channel_id=1, source_target_pairs={{0,2},{1,3},{2,0},{3,1},{4,6},{5,7},{6,4},{7,5},{8,10},{9,11},{10,... | collective-permute-start | bytes 245768 | tf_op jit(solution)/shard_map/ppermute | solution.py:560
  28.9 0.0 collective-permute-start.8
  28.9 0.7 %collective-permute-start.10 = (bf16[4,80,128]{2,1,0:T(8,128)(2,1)S(1)}, bf16[4,80,128]{2,1,0:T(8,128)(2,1)S(1)}, u32[]{:S(2)}, u32[]{:S(2)}) collective-permute-start(bf16[4,80,128]{2,1,0:T(8,128)(2,1)S(1)} %get-tuple-element.44), channel_id=1, source_target_pairs={{0,3},{1,2},{2,1},{3,0},{4,7},{5,6},{6,5},{7,4},{8,11},{9,10},{10,... | collective-permute-start | bytes 245768 | tf_op jit(solution)/shard_map/ppermute | solution.py:560
  29.6 0.0 copy-done.1
  29.6 9.5 %shard_map.99.far_ref = bf16[8192,256]{1,0:T(8,128)(2,1)} custom-call(bf16[256,8,1024]{2,1,0:T(8,128)(2,1)} %refs_0_, f32[8,64,64]{2,1,0:T(8,128)S(1)} %copy-done.1), custom_call_target="tpu_custom_call" | custom-call | bytes 33000000 | tf_op jit(solution)/shard_map/pallas_call | solution.py:433
  39.2 0.0 collective-permute-done.9
  39.2 0.0 collective-permute-done.8
  39.2 0.0 collective-permute-done.10
  39.2 0.3 all-to-all-done.arrived_ref
  39.6 4.8 %shard_map.100 = f32[16,8,128]{2,1,0:T(8,128)S(1)} custom-call(bf16[16,128,128]{2,1,0:T(8,128)(2,1)S(1)} %all-to-all-done.arrived_ref, bf16[16,80,128]{2,1,0:T(8,128)(2,1)S(1)} %bitcast.16, bf16[8192,256]{1,0:T(8,128)(2,1)} %shard_map.99.far_ref), custom_call_target="tpu_custom_call" | custom-call | bytes 16500000 | tf_op jit(solution)/shard_map/pallas_call | solution.py:529
  44.4 9.5 %all_to_all.10.pieces_ref = f32[16,8,128]{2,1,0:T(8,128)S(1)} all-to-all(f32[16,8,128]{2,1,0:T(8,128)S(1)} %shard_map.100), channel_id=1, replica_groups={{12,13,14,15,0,1,2,3,4,5,6,7,8,9,10,11},{28,29,30,31,16,17,18,19,20,21,..., dimensions={0} | all-to-all | bytes 131072 | tf_op jit(solution)/shard_map/all_to_all | solution.py:34
  53.8 0.6 %shard_map.101 = f32[8,64]{1,0:T(8,128)} custom-call(f32[16,8,128]{2,1,0:T(8,128)S(1)} %all_to_all.10.pieces_ref), custom_call_target="tpu_custom_call" | custom-call | tf_op jit(solution)/shard_map/pallas_call | solution.py:551
  (8 shorter events, 0.1 us)
Async XLA Ops:
  0.0 18.0 %copy-start = (s32[512,8]{0,1:T(8,128)S(1)}, s32[512,8]{0,1:T(8,128)}, u32[]{:S(2)}) copy-start(s32[512,8]{0,1:T(8,128)} %param.11) | copy-start | bytes 49156
  3.1 10.6 %copy-start.2 = (s32[512]{0:T(512)S(1)}, s32[512]{0:T(512)}, u32[]{:S(2)}) copy-start(s32[512]{0:T(512)} %param.12) | copy-start | bytes 6148
  3.1 8.9 %collective-permute-start.1 = (bf16[2,128,128]{2,1,0:T(8,128)(2,1)S(1)}, bf16[2,128,128]{2,1,0:T(8,128)(2,1)S(1)}, u32[]{:S(2)}, u32[]{:S(2)}) collective-permute-start(bf16[2,128,128]{2,1,0:T(8,128)(2,1)S(1)} %get-tuple-element.27), channel_id=1, source_target_pairs={{0,2},{1,3},{2,0},{3,1},{4,6},{5,7},{6,4},{7,5},{8,10},{9,11},{10,... | collective-permute-start | bytes 196616 | tf_op jit(solution)/shard_map/ppermute | solution.py:560
  6.1 5.9 %collective-permute-start = (bf16[144,128]{1,0:T(8,128)(2,1)S(1)}, bf16[144,128]{1,0:T(8,128)(2,1)S(1)}, u32[]{:S(2)}, u32[]{:S(2)}) collective-permute-start(bf16[144,128]{1,0:T(8,128)(2,1)S(1)} %get-tuple-element.26), channel_id=1, source_target_pairs={{0,8},{4,12},{8,0},{12,4},{1,9},{5,13},{9,1},{13,5},{2,10},{6,14},... | collective-permute-start | bytes 110600 | tf_op jit(solution)/shard_map/ppermute | solution.py:560
  12.0 17.6 %copy-start.1 = (f32[8,64,64]{2,1,0:T(8,128)S(1)}, f32[8,64,64]{2,1,0:T(8,128)}, u32[]{:S(2)}) copy-start(f32[8,64,64]{2,1,0:T(8,128)} %refs_1_.1) | copy-start | bytes 393220
  12.0 1.8 %collective-permute-start.2 = (bf16[2,512,128]{2,1,0:T(8,128)(2,1)S(1)}, bf16[2,512,128]{2,1,0:T(8,128)(2,1)S(1)}, u32[]{:S(2)}, u32[]{:S(2)}) collective-permute-start(bf16[2,512,128]{2,1,0:T(8,128)(2,1)S(1)} %get-tuple-element.29), channel_id=1, source_target_pairs={{0,1},{1,0},{2,3},{3,2},{4,5},{5,4},{6,7},{7,6},{8,9},{9,8},{10,11... | collective-permute-start | bytes 786440 | tf_op jit(solution)/shard_map/ppermute | solution.py:560
  12.1 1.5 %collective-permute-start.4 = (bf16[128,128]{1,0:T(8,128)(2,1)S(1)}, bf16[128,128]{1,0:T(8,128)(2,1)S(1)}, u32[]{:S(2)}, u32[]{:S(2)}) collective-permute-start(bf16[128,128]{1,0:T(8,128)(2,1)S(1)} %shard_map.95), channel_id=1, source_target_pairs={{0,1},{1,0},{2,3},{3,2},{4,5},{5,4},{6,7},{7,6},{8,9},{9,8},{10,11... | collective-permute-start | bytes 98312 | tf_op jit(solution)/shard_map/ppermute | solution.py:560
  13.9 5.7 %collective-permute-start.3 = (bf16[512,128]{1,0:T(8,128)(2,1)S(1)}, bf16[512,128]{1,0:T(8,128)(2,1)S(1)}, u32[]{:S(2)}, u32[]{:S(2)}) collective-permute-start(bf16[512,128]{1,0:T(8,128)(2,1)S(1)} %shard_map.94), channel_id=1, source_target_pairs={{0,2},{1,3},{2,0},{3,1},{4,6},{5,7},{6,4},{7,5},{8,10},{9,11},{10,... | collective-permute-start | bytes 393224 | tf_op jit(solution)/shard_map/ppermute | solution.py:560
  14.5 4.6 %collective-permute-start.5 = (bf16[368,128]{1,0:T(8,128)(2,1)S(1)}, bf16[368,128]{1,0:T(8,128)(2,1)S(1)}, u32[]{:S(2)}, u32[]{:S(2)}) collective-permute-start(bf16[368,128]{1,0:T(8,128)(2,1)S(1)} %pad_maximum_fusion.1), channel_id=1, source_target_pairs={{0,4},{4,0},{8,12},{12,8},{1,5},{5,1},{9,13},{13,9},{2,6},{6,2},{1... | collective-permute-start | bytes 282632 | tf_op jit(solution)/shard_map/ppermute | solution.py:560
  16.1 5.6 %collective-permute-start.7 = (bf16[80,128]{1,0:T(8,128)(2,1)S(1)}, bf16[80,128]{1,0:T(8,128)(2,1)S(1)}, u32[]{:S(2)}, u32[]{:S(2)}) collective-permute-start(bf16[80,128]{1,0:T(8,128)(2,1)S(1)} %shard_map.96), channel_id=1, source_target_pairs={{0,12},{4,8},{8,4},{12,0},{1,13},{5,9},{9,5},{13,1},{2,14},{6,10},... | collective-permute-start | bytes 61448 | tf_op jit(solution)/shard_map/ppermute | solution.py:560
  17.5 4.7 %collective-permute-start.6 = (bf16[80,128]{1,0:T(8,128)(2,1)S(1)}, bf16[80,128]{1,0:T(8,128)(2,1)S(1)}, u32[]{:S(2)}, u32[]{:S(2)}) collective-permute-start(bf16[80,128]{1,0:T(8,128)(2,1)S(1)} %shard_map.96), channel_id=1, source_target_pairs={{0,8},{4,12},{8,0},{12,4},{1,9},{5,13},{9,1},{13,5},{2,10},{6,14},... | collective-permute-start | bytes 61448 | tf_op jit(solution)/shard_map/ppermute | solution.py:560
  22.2 17.4 %all-to-all-start = ((bf16[16,128,128]{2,1,0:T(8,128)(2,1)}), bf16[16,128,128]{2,1,0:T(8,128)(2,1)S(1)}, u32[]{:S(2)}, u32[]{:S(2)}) async-start(bf16[16,128,128]{2,1,0:T(8,128)(2,1)} %shard_map.98), calls=%async_computation | async-start | bytes 1048576 | tf_op jit(solution)/shard_map/all_to_all | solution.py:34
  27.4 11.8 %collective-permute-start.9 = (bf16[4,80,128]{2,1,0:T(8,128)(2,1)S(1)}, bf16[4,80,128]{2,1,0:T(8,128)(2,1)S(1)}, u32[]{:S(2)}, u32[]{:S(2)}) collective-permute-start(bf16[4,80,128]{2,1,0:T(8,128)(2,1)S(1)} %get-tuple-element.44), channel_id=1, source_target_pairs={{0,2},{1,3},{2,0},{3,1},{4,6},{5,7},{6,4},{7,5},{8,10},{9,11},{10,... | collective-permute-start | bytes 245768 | tf_op jit(solution)/shard_map/ppermute | solution.py:560
  28.9 10.2 %collective-permute-start.8 = (bf16[4,80,128]{2,1,0:T(8,128)(2,1)S(1)}, bf16[4,80,128]{2,1,0:T(8,128)(2,1)S(1)}, u32[]{:S(2)}, u32[]{:S(2)}) collective-permute-start(bf16[4,80,128]{2,1,0:T(8,128)(2,1)S(1)} %get-tuple-element.44), channel_id=1, source_target_pairs={{0,1},{1,0},{2,3},{3,2},{4,5},{5,4},{6,7},{7,6},{8,9},{9,8},{10,11... | collective-permute-start | bytes 245768 | tf_op jit(solution)/shard_map/ppermute | solution.py:560
  28.9 10.3 %collective-permute-start.10 = (bf16[4,80,128]{2,1,0:T(8,128)(2,1)S(1)}, bf16[4,80,128]{2,1,0:T(8,128)(2,1)S(1)}, u32[]{:S(2)}, u32[]{:S(2)}) collective-permute-start(bf16[4,80,128]{2,1,0:T(8,128)(2,1)S(1)} %get-tuple-element.44), channel_id=1, source_target_pairs={{0,3},{1,2},{2,1},{3,0},{4,7},{5,6},{6,5},{7,4},{8,11},{9,10},{10,... | collective-permute-start | bytes 245768 | tf_op jit(solution)/shard_map/ppermute | solution.py:560

commit v25 on v24

--- a/solution.py
+++ b/solution.py
@@ -108,14 +108,17 @@
     act_hbm,
     in_proj_hbm,
     inverse_hbm,
+    out_proj_hbm,
     hidden_hbm,
     leaving_ref,
     own_ref,
     shared_ref,
     hidden_ref,
+    out_weights_ref,
     act_ref,
     in_proj_ref,
     inverse_ref,
+    out_proj_ref,
     sems,
 ):
     turns = (2, 3, 1, 0)
@@ -128,7 +131,7 @@
         rows = pl.ds(pl.multiple_of(jnp.bitwise_xor(place, turn) * quarter, quarter), quarter)
         pairs.append((act_hbm.at[rows], act_ref.at[g]))
         if g == 0:
-            pairs.append((inverse_hbm, inverse_ref))
+            pairs += [(inverse_hbm, inverse_ref), (out_proj_hbm, out_proj_ref)]
     for g in range(hidden_ref.shape[0]):
         pairs.append((hidden_hbm.at[quarter_rows(place, OUTER_TURNS[g], hidden_ref.shape[1])], hidden_ref.at[g]))
     take = in_order([pltpu.make_async_copy(*pair, sems.at[i]) for i, pair in enumerate(pairs)], 4)
@@ -140,6 +143,8 @@
         if wire_ref is leaving_ref:
             take()
             pack_factors(inverse_ref, shared_ref)
+            take()
+            out_weights_ref[...] = twice_transposed(out_proj_ref[...])
         take()
         g = 0 if wire_ref is leaving_ref else 2
         rows = act_ref[g : g + 2].reshape(2 * quarter, act_ref.shape[2])
@@ -153,21 +158,22 @@
         take()
 
 
-def project_inner(activations, in_projection, inverse_out, flat_hidden, quarters):
+def project_inner(activations, in_projection, inverse_out, out_projection, flat_hidden, quarters):
     tokens, model = activations.shape
     quarter = tokens // quarters
     experts, width, _ = inverse_out.shape
     wire = jax.ShapeDtypeStruct((quarters // 2, quarter, LANES), jnp.bfloat16)
-    fixed = (in_projection, inverse_out)
+    fixed = (in_projection, inverse_out, out_projection)
     return pl.pallas_call(
         inner_kernel,
-        in_specs=[HBM] * 4,
-        out_specs=[VMEM] * 4,
+        in_specs=[HBM] * 5,
+        out_specs=[VMEM] * 5,
         out_shape=[
             wire,
             wire,
             jax.ShapeDtypeStruct((experts // 4 * width + DIAGONAL_ROWS, LANES), jnp.bfloat16),
             jax.ShapeDtypeStruct((quarters // 2, flat_hidden.shape[0] // quarters, flat_hidden.shape[1]), jnp.bfloat16),
+            jax.ShapeDtypeStruct((out_projection.shape[1], 2 * width), jnp.bfloat16),
         ],
         scratch_shapes=[pltpu.VMEM((quarters, quarter, model), jnp.bfloat16)]
         + [pltpu.VMEM(array.shape, array.dtype) for array in fixed]
@@ -177,18 +183,17 @@
     )(*[stay(array) for array in (activations, *fixed, flat_hidden)])
 
 
-def outer_kernel(near_ref, hidden_hbm, out_proj_hbm, leaving_ref, own_ref, hidden_ref, out_proj_ref, rows_ref, sems, *, top):
+def outer_kernel(near_ref, hidden_hbm, weights_ref, leaving_ref, own_ref, hidden_ref, rows_ref, sems, *, top):
     ready, rows, _ = near_ref.shape
     quarter = rows // top
-    width = out_proj_ref.shape[0]
+    width = weights_ref.shape[1] // 2
     place = lax.axis_index("proj")
-    pairs = [(out_proj_hbm, out_proj_ref)]
+    pairs = []
     for i, turn in enumerate(OUTER_TURNS[ready:]):
         pairs.append((hidden_hbm.at[quarter_rows(place, turn, rows)], hidden_ref.at[i]))
     take = in_order([pltpu.make_async_copy(*pair, sems.at[i]) for i, pair in enumerate(pairs)], len(pairs))
-    take()
     first = low_lanes(quarter, width)
-    weights = twice_transposed(out_proj_ref[...])
+    weights = weights_ref[...]
 
     def pack_rows(g):
         wire_ref = leaving_ref.at[g] if g < 2 else own_ref.at[g - 2]
@@ -207,23 +212,22 @@
     pack_rows(len(OUTER_TURNS) - 1)
 
 
-def project_outer(near_hidden, flat_hidden, out_projection, quarters, top):
+def project_outer(near_hidden, flat_hidden, weights, quarters, top):
     rows, hidden = flat_hidden.shape
     wire = jax.ShapeDtypeStruct((quarters // 2, rows // quarters // 2, LANES), jnp.bfloat16)
     return pl.pallas_call(
         functools.partial(outer_kernel, top=top),
-        in_specs=[VMEM, HBM, HBM],
+        in_specs=[VMEM, HBM, VMEM],
         out_specs=[VMEM] * 2,
         out_shape=[wire, wire],
         scratch_shapes=[
             pltpu.VMEM((quarters // 2, rows // quarters, hidden), jnp.bfloat16),
-            pltpu.VMEM(out_projection.shape, out_projection.dtype),
             pltpu.VMEM((2, rows // quarters, LANES), jnp.float32),
-            pltpu.SemaphoreType.DMA((quarters // 2 + 1,)),
+            pltpu.SemaphoreType.DMA((quarters // 2,)),
         ],
         compiler_params=pltpu.CompilerParams(vmem_limit_bytes=40 * MIB),
         cost_estimate=cost(4),
-    )(near_hidden, stay(flat_hidden), stay(out_projection))
+    )(near_hidden, stay(flat_hidden), weights)
 
 
 def exact_rows(rows):
@@ -587,12 +591,12 @@
     assert DOC_DEV * owners <= 256
 
     flat_hidden = grad_hidden.reshape(tokens * top, grad_hidden.shape[2])
-    inner_leaving, inner_own, shared, near_hidden = project_inner(
-        activations, in_projection, inverse_out, flat_hidden, shares
+    inner_leaving, inner_own, shared, near_hidden, out_weights = project_inner(
+        activations, in_projection, inverse_out, out_projection, flat_hidden, shares
     )
     inner_first = exchange(inner_leaving, "proj", shares, 2)
     far_shared = exchange(shared, "expert", owners, owners // 2)
-    leaving, own = project_outer(near_hidden, flat_hidden, out_projection, shares, top)
+    leaving, own = project_outer(near_hidden, flat_hidden, out_weights, shares, top)
     far_shared, inner_first, leaving = lax.optimization_barrier((far_shared, inner_first, leaving))
     near = exchange(leaving, "proj", shares, 1)
     shared, turns = jnp.stack([shared, far_shared]), (0, owners // 2)

time: 54.9 us -> 55.4 us (level)
  no operation moved by 1% of the time
where the time goes in v25:
time: 55.4 us; the launch traced here: 54.9 us
  Pallas kernels  24.5 us (44%)
  starting transfers between devices  17.8 us (32%)
  blocking collectives  9.46 us (17%)
  waiting for transfers between devices  2.72 us (5%)
    ppermute x11, starting transfers between devices, exchange(): return lax.ppermute(block, axis, [(i, i ^ turn) for i in range(size)])  12.6 us
    pallas_call x1, Pallas kernels, condition_queries(): pl.pallas_call(query_kernel, grid=(flat // LANES,), in_specs=[pl.BlockSpe...  9.54 us
    all_to_all x1, blocking collectives, send_to_all(): lax.all_to_all(blocks, ('expert', 'proj'), 0, 0, tiled=True, axis_index_g...  9.46 us
    all_to_all x1, starting transfers between devices, send_to_all(): lax.all_to_all(blocks, ('expert', 'proj'), 0, 0, tiled=True, axis_index_g...  5.27 us
    pallas_call x1, Pallas kernels, score(): pl.pallas_call(functools.partial(score_kernel, width=width, doc_count=doc...  4.82 us
    pallas_call x1, Pallas kernels, project_inner(): pl.pallas_call(inner_kernel, in_specs=[HBM] * 5, out_specs=[VMEM] * 5, ou...  3.47 us
    pallas_call x1, Pallas kernels, project_outer(): pl.pallas_call(functools.partial(outer_kernel, top=top), in_specs=[VMEM,...  3.33 us
    ppermute x11, waiting for transfers between devices, exchange(): return lax.ppermute(block, axis, [(i, i ^ turn) for i in range(size)])  2.41 us
  transfers between devices with their start and end apart: 12, of which 5 were waited for; matrix products, arithmetic and copies ran while one was open for 0% of the time, Pallas kernels for 28%

profile of v25, /device:TPU:0, one launch (start us, length us, event | category | flops | bytes accessed | tf_op | source)
XLA Modules:
  0.0 54.9 jit_solution(7677468934314204906)
XLA Ops:
  0.0 0.0 copy-start
  0.0 3.5 %shard_map.91 = (bf16[2,128,128]{2,1,0:T(8,128)(2,1)S(1)}, bf16[2,128,128]{2,1,0:T(8,128)(2,1)S(1)}, bf16[144,128]{1,0:T(8,128)(2,1)S(1)}, bf16[2,1024,512]{2,1,0:T(8,128)(2,1)S(1)}, bf16[512,128]{1,0:T(8,128)(2,1)S(1)}) custom-call(bf16[512,1792]{1,0:T(8,128)(2,1)} %act_hbm.1, bf16[64,1792]{1,0:T(8,128)(2,1)} %in_proj_hbm.1, f32[8,64,64]{2,1,0:T(8,128)} %inverse_hbm.1, ...), custom_call_target="tpu_custom_call" | custom-call | bytes 8250000 | tf_op jit(solution)/shard_map/pallas_call | solution.py:167
  3.5 0.0 copy-start.2
  3.5 3.0 %collective-permute-start.1 = (bf16[2,128,128]{2,1,0:T(8,128)(2,1)S(1)}, bf16[2,128,128]{2,1,0:T(8,128)(2,1)S(1)}, u32[]{:S(2)}, u32[]{:S(2)}) collective-permute-start(bf16[2,128,128]{2,1,0:T(8,128)(2,1)S(1)} %get-tuple-element.29), channel_id=1, source_target_pairs={{0,2},{1,3},{2,0},{3,1},{4,6},{5,7},{6,4},{7,5},{8,10},{9,11},{10,... | collective-permute-start | bytes 196616 | tf_op jit(solution)/shard_map/ppermute | solution.py:564
  6.5 2.6 %collective-permute-start = (bf16[144,128]{1,0:T(8,128)(2,1)S(1)}, bf16[144,128]{1,0:T(8,128)(2,1)S(1)}, u32[]{:S(2)}, u32[]{:S(2)}) collective-permute-start(bf16[144,128]{1,0:T(8,128)(2,1)S(1)} %get-tuple-element.28), channel_id=1, source_target_pairs={{0,8},{4,12},{8,0},{12,4},{1,9},{5,13},{9,1},{13,5},{2,10},{6,14},... | collective-permute-start | bytes 110600 | tf_op jit(solution)/shard_map/ppermute | solution.py:564
  9.1 3.3 %shard_map.92 = (bf16[2,512,128]{2,1,0:T(8,128)(2,1)S(1)}, bf16[2,512,128]{2,1,0:T(8,128)(2,1)S(1)}) custom-call(bf16[2,1024,512]{2,1,0:T(8,128)(2,1)S(1)} %get-tuple-element.25.near_ref, bf16[4096,512]{1,0:T(8,128)(2,1)} %bitcast.23, bf16[512,128]{1,0:T(8,128)(2,1)S(1)} %get-tuple-element.26.weights_ref), custom_call_target="tpu_custom_call" | custom-call | bytes 13200000 | tf_op jit(solution)/shard_map/pallas_call | solution.py:218
  12.4 0.0 copy-start.1
  12.4 0.0 collective-permute-done
  12.5 0.0 collective-permute-done.1.near_ref.first_ref
  12.5 0.1 collective-permute-start.2
  12.6 0.6 %collective-permute-start.4 = (bf16[128,128]{1,0:T(8,128)(2,1)S(1)}, bf16[128,128]{1,0:T(8,128)(2,1)S(1)}, u32[]{:S(2)}, u32[]{:S(2)}) collective-permute-start(bf16[128,128]{1,0:T(8,128)(2,1)S(1)} %shard_map.95), channel_id=1, source_target_pairs={{0,1},{1,0},{2,3},{3,2},{4,5},{5,4},{6,7},{7,6},{8,9},{9,8},{10,11... | collective-permute-start | bytes 98312 | tf_op jit(solution)/shard_map/ppermute | solution.py:564
  13.1 0.4 shard_map.93.even_ref
  13.6 0.5 collective-permute-done.4.second_ref
  14.1 0.0 copy-done.2
  14.1 0.1 shard_map.96
  14.2 0.0 collective-permute-done.2.near_ref
  14.3 0.6 %collective-permute-start.3 = (bf16[512,128]{1,0:T(8,128)(2,1)S(1)}, bf16[512,128]{1,0:T(8,128)(2,1)S(1)}, u32[]{:S(2)}, u32[]{:S(2)}) collective-permute-start(bf16[512,128]{1,0:T(8,128)(2,1)S(1)} %shard_map.94), channel_id=1, source_target_pairs={{0,2},{1,3},{2,0},{3,1},{4,6},{5,7},{6,4},{7,5},{8,10},{9,11},{10,... | collective-permute-start | bytes 393224 | tf_op jit(solution)/shard_map/ppermute | solution.py:564
  14.9 1.6 %collective-permute-start.5 = (bf16[368,128]{1,0:T(8,128)(2,1)S(1)}, bf16[368,128]{1,0:T(8,128)(2,1)S(1)}, u32[]{:S(2)}, u32[]{:S(2)}) collective-permute-start(bf16[368,128]{1,0:T(8,128)(2,1)S(1)} %pad_maximum_fusion.1), channel_id=1, source_target_pairs={{0,4},{4,0},{8,12},{12,8},{1,5},{5,1},{9,13},{13,9},{2,6},{6,2},{1... | collective-permute-start | bytes 282632 | tf_op jit(solution)/shard_map/ppermute | solution.py:564
  16.6 1.3 %collective-permute-start.7 = (bf16[80,128]{1,0:T(8,128)(2,1)S(1)}, bf16[80,128]{1,0:T(8,128)(2,1)S(1)}, u32[]{:S(2)}, u32[]{:S(2)}) collective-permute-start(bf16[80,128]{1,0:T(8,128)(2,1)S(1)} %shard_map.96), channel_id=1, source_target_pairs={{0,12},{4,8},{8,4},{12,0},{1,13},{5,9},{9,5},{13,1},{2,14},{6,10},... | collective-permute-start | bytes 61448 | tf_op jit(solution)/shard_map/ppermute | solution.py:564
  17.9 0.6 %collective-permute-start.6 = (bf16[80,128]{1,0:T(8,128)(2,1)S(1)}, bf16[80,128]{1,0:T(8,128)(2,1)S(1)}, u32[]{:S(2)}, u32[]{:S(2)}) collective-permute-start(bf16[80,128]{1,0:T(8,128)(2,1)S(1)} %shard_map.96), channel_id=1, source_target_pairs={{0,8},{4,12},{8,0},{12,4},{1,9},{5,13},{9,1},{13,5},{2,10},{6,14},... | collective-permute-start | bytes 61448 | tf_op jit(solution)/shard_map/ppermute | solution.py:564
  18.5 0.0 copy-done
  18.5 0.1 copy.11.routes_ref
  18.6 1.0 %collective-permute-done.5.shared_ref = bf16[368,128]{1,0:T(8,128)(2,1)S(1)} collective-permute-done((bf16[368,128]{1,0:T(8,128)(2,1)S(1)}, bf16[368,128]{1,0:T(8,128)(2,1)S(1)}, u32[]{:S(2)}, u32[]{:S(2)}) %collective-permute-start.5) | collective-permute-done | bytes 94240 | tf_op jit(solution)/shard_map/ppermute | solution.py:564
  19.5 0.4 shard_map.97.odd_ref
  20.0 0.0 collective-permute-done.3.far_ref
  20.0 1.7 %shard_map.98 = bf16[16,128,128]{2,1,0:T(8,128)(2,1)} custom-call(bf16[2,512,128]{2,1,0:T(8,128)(2,1)S(1)} %get-tuple-element.27.own_ref, bf16[2,512,128]{2,1,0:T(8,128)(2,1)S(1)} %collective-permute-done.2.near_ref, bf16[512,128]{1,0:T(8,128)(2,1)S(1)} %collective-permute-done.3.far_ref, s32[128,8]{1,0:T(8,128)S(1)} %copy.11.routes_ref, ...), custom_call_target="tpu_custom_call" | custom-call | bytes 6600000 | tf_op jit(solution)/shard_map/pallas_call | solution.py:367
  21.7 0.4 collective-permute-done.7
  22.1 0.4 collective-permute-done.6
  22.6 5.3 %all-to-all-start = ((bf16[16,128,128]{2,1,0:T(8,128)(2,1)}), bf16[16,128,128]{2,1,0:T(8,128)(2,1)S(1)}, u32[]{:S(2)}, u32[]{:S(2)}) async-start(bf16[16,128,128]{2,1,0:T(8,128)(2,1)} %shard_map.98), calls=%async_computation | async-start | bytes 1048576 | tf_op jit(solution)/shard_map/all_to_all | solution.py:34
  27.9 1.5 %collective-permute-start.9 = (bf16[4,80,128]{2,1,0:T(8,128)(2,1)S(1)}, bf16[4,80,128]{2,1,0:T(8,128)(2,1)S(1)}, u32[]{:S(2)}, u32[]{:S(2)}) collective-permute-start(bf16[4,80,128]{2,1,0:T(8,128)(2,1)S(1)} %get-tuple-element.46), channel_id=1, source_target_pairs={{0,2},{1,3},{2,0},{3,1},{4,6},{5,7},{6,4},{7,5},{8,10},{9,11},{10,... | collective-permute-start | bytes 245768 | tf_op jit(solution)/shard_map/ppermute | solution.py:564
  29.4 0.0 collective-permute-start.8
  29.4 0.7 %collective-permute-start.10 = (bf16[4,80,128]{2,1,0:T(8,128)(2,1)S(1)}, bf16[4,80,128]{2,1,0:T(8,128)(2,1)S(1)}, u32[]{:S(2)}, u32[]{:S(2)}) collective-permute-start(bf16[4,80,128]{2,1,0:T(8,128)(2,1)S(1)} %get-tuple-element.46), channel_id=1, source_target_pairs={{0,3},{1,2},{2,1},{3,0},{4,7},{5,6},{6,5},{7,4},{8,11},{9,10},{10,... | collective-permute-start | bytes 245768 | tf_op jit(solution)/shard_map/ppermute | solution.py:564
  30.1 0.0 copy-done.1
  30.1 9.5 %shard_map.99.far_ref = bf16[8192,256]{1,0:T(8,128)(2,1)} custom-call(bf16[256,8,1024]{2,1,0:T(8,128)(2,1)} %refs_0_, f32[8,64,64]{2,1,0:T(8,128)S(1)} %copy-done.1), custom_call_target="tpu_custom_call" | custom-call | bytes 33000000 | tf_op jit(solution)/shard_map/pallas_call | solution.py:437
  39.6 0.0 collective-permute-done.9
  39.6 0.0 collective-permute-done.8
  39.6 0.0 collective-permute-done.10
  39.7 0.3 all-to-all-done.arrived_ref
  40.0 4.8 %shard_map.100 = f32[16,8,128]{2,1,0:T(8,128)S(1)} custom-call(bf16[16,128,128]{2,1,0:T(8,128)(2,1)S(1)} %all-to-all-done.arrived_ref, bf16[16,80,128]{2,1,0:T(8,128)(2,1)S(1)} %bitcast.16, bf16[8192,256]{1,0:T(8,128)(2,1)} %shard_map.99.far_ref), custom_call_target="tpu_custom_call" | custom-call | bytes 16500000 | tf_op jit(solution)/shard_map/pallas_call | solution.py:533
  44.8 9.5 %all_to_all.10.pieces_ref = f32[16,8,128]{2,1,0:T(8,128)S(1)} all-to-all(f32[16,8,128]{2,1,0:T(8,128)S(1)} %shard_map.100), channel_id=1, replica_groups={{12,13,14,15,0,1,2,3,4,5,6,7,8,9,10,11},{28,29,30,31,16,17,18,19,20,21,..., dimensions={0} | all-to-all | bytes 131072 | tf_op jit(solution)/shard_map/all_to_all | solution.py:34
  54.3 0.6 %shard_map.101 = f32[8,64]{1,0:T(8,128)} custom-call(f32[16,8,128]{2,1,0:T(8,128)S(1)} %all_to_all.10.pieces_ref), custom_call_target="tpu_custom_call" | custom-call | tf_op jit(solution)/shard_map/pallas_call | solution.py:555
  (8 shorter events, 0.1 us)
Async XLA Ops:
  0.0 18.5 %copy-start = (s32[512,8]{0,1:T(8,128)S(1)}, s32[512,8]{0,1:T(8,128)}, u32[]{:S(2)}) copy-start(s32[512,8]{0,1:T(8,128)} %param.11) | copy-start | bytes 49156
  3.5 10.6 %copy-start.2 = (s32[512]{0:T(512)S(1)}, s32[512]{0:T(512)}, u32[]{:S(2)}) copy-start(s32[512]{0:T(512)} %param.12) | copy-start | bytes 6148
  3.5 9.0 %collective-permute-start.1 = (bf16[2,128,128]{2,1,0:T(8,128)(2,1)S(1)}, bf16[2,128,128]{2,1,0:T(8,128)(2,1)S(1)}, u32[]{:S(2)}, u32[]{:S(2)}) collective-permute-start(bf16[2,128,128]{2,1,0:T(8,128)(2,1)S(1)} %get-tuple-element.29), channel_id=1, source_target_pairs={{0,2},{1,3},{2,0},{3,1},{4,6},{5,7},{6,4},{7,5},{8,10},{9,11},{10,... | collective-permute-start | bytes 196616 | tf_op jit(solution)/shard_map/ppermute | solution.py:564
  6.5 5.9 %collective-permute-start = (bf16[144,128]{1,0:T(8,128)(2,1)S(1)}, bf16[144,128]{1,0:T(8,128)(2,1)S(1)}, u32[]{:S(2)}, u32[]{:S(2)}) collective-permute-start(bf16[144,128]{1,0:T(8,128)(2,1)S(1)} %get-tuple-element.28), channel_id=1, source_target_pairs={{0,8},{4,12},{8,0},{12,4},{1,9},{5,13},{9,1},{13,5},{2,10},{6,14},... | collective-permute-start | bytes 110600 | tf_op jit(solution)/shard_map/ppermute | solution.py:564
  12.4 17.6 %copy-start.1 = (f32[8,64,64]{2,1,0:T(8,128)S(1)}, f32[8,64,64]{2,1,0:T(8,128)}, u32[]{:S(2)}) copy-start(f32[8,64,64]{2,1,0:T(8,128)} %refs_1_.1) | copy-start | bytes 393220
  12.5 1.8 %collective-permute-start.2 = (bf16[2,512,128]{2,1,0:T(8,128)(2,1)S(1)}, bf16[2,512,128]{2,1,0:T(8,128)(2,1)S(1)}, u32[]{:S(2)}, u32[]{:S(2)}) collective-permute-start(bf16[2,512,128]{2,1,0:T(8,128)(2,1)S(1)} %get-tuple-element.31), channel_id=1, source_target_pairs={{0,1},{1,0},{2,3},{3,2},{4,5},{5,4},{6,7},{7,6},{8,9},{9,8},{10,11... | collective-permute-start | bytes 786440 | tf_op jit(solution)/shard_map/ppermute | solution.py:564
  12.6 1.5 %collective-permute-start.4 = (bf16[128,128]{1,0:T(8,128)(2,1)S(1)}, bf16[128,128]{1,0:T(8,128)(2,1)S(1)}, u32[]{:S(2)}, u32[]{:S(2)}) collective-permute-start(bf16[128,128]{1,0:T(8,128)(2,1)S(1)} %shard_map.95), channel_id=1, source_target_pairs={{0,1},{1,0},{2,3},{3,2},{4,5},{5,4},{6,7},{7,6},{8,9},{9,8},{10,11... | collective-permute-start | bytes 98312 | tf_op jit(solution)/shard_map/ppermute | solution.py:564
  14.3 5.7 %collective-permute-start.3 = (bf16[512,128]{1,0:T(8,128)(2,1)S(1)}, bf16[512,128]{1,0:T(8,128)(2,1)S(1)}, u32[]{:S(2)}, u32[]{:S(2)}) collective-permute-start(bf16[512,128]{1,0:T(8,128)(2,1)S(1)} %shard_map.94), channel_id=1, source_target_pairs={{0,2},{1,3},{2,0},{3,1},{4,6},{5,7},{6,4},{7,5},{8,10},{9,11},{10,... | collective-permute-start | bytes 393224 | tf_op jit(solution)/shard_map/ppermute | solution.py:564
  14.9 4.6 %collective-permute-start.5 = (bf16[368,128]{1,0:T(8,128)(2,1)S(1)}, bf16[368,128]{1,0:T(8,128)(2,1)S(1)}, u32[]{:S(2)}, u32[]{:S(2)}) collective-permute-start(bf16[368,128]{1,0:T(8,128)(2,1)S(1)} %pad_maximum_fusion.1), channel_id=1, source_target_pairs={{0,4},{4,0},{8,12},{12,8},{1,5},{5,1},{9,13},{13,9},{2,6},{6,2},{1... | collective-permute-start | bytes 282632 | tf_op jit(solution)/shard_map/ppermute | solution.py:564
  16.6 5.6 %collective-permute-start.7 = (bf16[80,128]{1,0:T(8,128)(2,1)S(1)}, bf16[80,128]{1,0:T(8,128)(2,1)S(1)}, u32[]{:S(2)}, u32[]{:S(2)}) collective-permute-start(bf16[80,128]{1,0:T(8,128)(2,1)S(1)} %shard_map.96), channel_id=1, source_target_pairs={{0,12},{4,8},{8,4},{12,0},{1,13},{5,9},{9,5},{13,1},{2,14},{6,10},... | collective-permute-start | bytes 61448 | tf_op jit(solution)/shard_map/ppermute | solution.py:564
  17.9 4.7 %collective-permute-start.6 = (bf16[80,128]{1,0:T(8,128)(2,1)S(1)}, bf16[80,128]{1,0:T(8,128)(2,1)S(1)}, u32[]{:S(2)}, u32[]{:S(2)}) collective-permute-start(bf16[80,128]{1,0:T(8,128)(2,1)S(1)} %shard_map.96), channel_id=1, source_target_pairs={{0,8},{4,12},{8,0},{12,4},{1,9},{5,13},{9,1},{13,5},{2,10},{6,14},... | collective-permute-start | bytes 61448 | tf_op jit(solution)/shard_map/ppermute | solution.py:564
  22.6 17.5 %all-to-all-start = ((bf16[16,128,128]{2,1,0:T(8,128)(2,1)}), bf16[16,128,128]{2,1,0:T(8,128)(2,1)S(1)}, u32[]{:S(2)}, u32[]{:S(2)}) async-start(bf16[16,128,128]{2,1,0:T(8,128)(2,1)} %shard_map.98), calls=%async_computation | async-start | bytes 1048576 | tf_op jit(solution)/shard_map/all_to_all | solution.py:34
  27.9 11.8 %collective-permute-start.9 = (bf16[4,80,128]{2,1,0:T(8,128)(2,1)S(1)}, bf16[4,80,128]{2,1,0:T(8,128)(2,1)S(1)}, u32[]{:S(2)}, u32[]{:S(2)}) collective-permute-start(bf16[4,80,128]{2,1,0:T(8,128)(2,1)S(1)} %get-tuple-element.46), channel_id=1, source_target_pairs={{0,2},{1,3},{2,0},{3,1},{4,6},{5,7},{6,4},{7,5},{8,10},{9,11},{10,... | collective-permute-start | bytes 245768 | tf_op jit(solution)/shard_map/ppermute | solution.py:564
  29.4 10.2 %collective-permute-start.8 = (bf16[4,80,128]{2,1,0:T(8,128)(2,1)S(1)}, bf16[4,80,128]{2,1,0:T(8,128)(2,1)S(1)}, u32[]{:S(2)}, u32[]{:S(2)}) collective-permute-start(bf16[4,80,128]{2,1,0:T(8,128)(2,1)S(1)} %get-tuple-element.46), channel_id=1, source_target_pairs={{0,1},{1,0},{2,3},{3,2},{4,5},{5,4},{6,7},{7,6},{8,9},{9,8},{10,11... | collective-permute-start | bytes 245768 | tf_op jit(solution)/shard_map/ppermute | solution.py:564
  29.4 10.3 %collective-permute-start.10 = (bf16[4,80,128]{2,1,0:T(8,128)(2,1)S(1)}, bf16[4,80,128]{2,1,0:T(8,128)(2,1)S(1)}, u32[]{:S(2)}, u32[]{:S(2)}) collective-permute-start(bf16[4,80,128]{2,1,0:T(8,128)(2,1)S(1)} %get-tuple-element.46), channel_id=1, source_target_pairs={{0,3},{1,2},{2,1},{3,0},{4,7},{5,6},{6,5},{7,4},{8,11},{9,10},{10,... | collective-permute-start | bytes 245768 | tf_op jit(solution)/shard_map/ppermute | solution.py:564

commit v26 on v24

--- a/solution.py
+++ b/solution.py
@@ -167,11 +167,11 @@
             wire,
             wire,
             jax.ShapeDtypeStruct((experts // 4 * width + DIAGONAL_ROWS, LANES), jnp.bfloat16),
-            jax.ShapeDtypeStruct((quarters // 2, flat_hidden.shape[0] // quarters, flat_hidden.shape[1]), jnp.bfloat16),
+            jax.ShapeDtypeStruct((1, flat_hidden.shape[0] // quarters, flat_hidden.shape[1]), jnp.bfloat16),
         ],
         scratch_shapes=[pltpu.VMEM((quarters, quarter, model), jnp.bfloat16)]
         + [pltpu.VMEM(array.shape, array.dtype) for array in fixed]
-        + [pltpu.SemaphoreType.DMA((quarters + len(fixed) + quarters // 2,))],
+        + [pltpu.SemaphoreType.DMA((quarters + len(fixed) + 1,))],
         compiler_params=pltpu.CompilerParams(vmem_limit_bytes=40 * MIB),
         cost_estimate=cost(2.5),
     )(*[stay(array) for array in (activations, *fixed, flat_hidden)])
@@ -216,10 +216,10 @@
         out_specs=[VMEM] * 2,
         out_shape=[wire, wire],
         scratch_shapes=[
-            pltpu.VMEM((quarters // 2, rows // quarters, hidden), jnp.bfloat16),
+            pltpu.VMEM((quarters - 1, rows // quarters, hidden), jnp.bfloat16),
             pltpu.VMEM(out_projection.shape, out_projection.dtype),
             pltpu.VMEM((2, rows // quarters, LANES), jnp.float32),
-            pltpu.SemaphoreType.DMA((quarters // 2 + 1,)),
+            pltpu.SemaphoreType.DMA((quarters,)),
         ],
         compiler_params=pltpu.CompilerParams(vmem_limit_bytes=40 * MIB),
         cost_estimate=cost(4),

time: 54.9 us -> 55.3 us (level)
    pallas_call x1, Pallas kernels: 3.28 us -> 3.97 us  [project_outer(): pl.pallas_call(functools.partial(outer_kernel, top=top), in_specs=[VMEM,...]
  transfers between devices with their start and end apart: 12 -> 12, of which waited for: 5 -> 4; matrix products, arithmetic and copies ran while one was open for 0% -> 0% of each run, Pallas kernels for 28% -> 30%
where the time goes in v26:
time: 55.3 us; the launch traced here: 54.9 us
  Pallas kernels  24.5 us (44%)
  starting transfers between devices  18.3 us (33%)
  blocking collectives  9.46 us (17%)
  waiting for transfers between devices  2.3 us (4%)
    ppermute x11, starting transfers between devices, exchange(): return lax.ppermute(block, axis, [(i, i ^ turn) for i in range(size)])  12.6 us
    pallas_call x1, Pallas kernels, condition_queries(): pl.pallas_call(query_kernel, grid=(flat // LANES,), in_specs=[pl.BlockSpe...  9.55 us
    all_to_all x1, blocking collectives, send_to_all(): lax.all_to_all(blocks, ('expert', 'proj'), 0, 0, tiled=True, axis_index_g...  9.46 us
    all_to_all x1, starting transfers between devices, send_to_all(): lax.all_to_all(blocks, ('expert', 'proj'), 0, 0, tiled=True, axis_index_g...  5.69 us
    pallas_call x1, Pallas kernels, score(): pl.pallas_call(functools.partial(score_kernel, width=width, doc_count=doc...  4.82 us
    pallas_call x1, Pallas kernels, project_outer(): pl.pallas_call(functools.partial(outer_kernel, top=top), in_specs=[VMEM,...  3.97 us
    pallas_call x1, Pallas kernels, project_inner(): pl.pallas_call(inner_kernel, in_specs=[HBM] * 4, out_specs=[VMEM] * 4, ou...  2.84 us
    ppermute x11, waiting for transfers between devices, exchange(): return lax.ppermute(block, axis, [(i, i ^ turn) for i in range(size)])  1.99 us
  transfers between devices with their start and end apart: 12, of which 4 were waited for; matrix products, arithmetic and copies ran while one was open for 0% of the time, Pallas kernels for 30%

profile of v26, /device:TPU:0, one launch (start us, length us, event | category | flops | bytes accessed | tf_op | source)
XLA Modules:
  0.0 54.9 jit_solution(9507822618245678843)
XLA Ops:
  0.0 0.0 copy-start
  0.0 2.8 %shard_map.91 = (bf16[2,128,128]{2,1,0:T(8,128)(2,1)S(1)}, bf16[2,128,128]{2,1,0:T(8,128)(2,1)S(1)}, bf16[144,128]{1,0:T(8,128)(2,1)S(1)}, bf16[1,1024,512]{2,1,0:T(8,128)(2,1)S(1)}) custom-call(bf16[512,1792]{1,0:T(8,128)(2,1)} %act_hbm.1, bf16[64,1792]{1,0:T(8,128)(2,1)} %in_proj_hbm.1, f32[8,64,64]{2,1,0:T(8,128)} %inverse_hbm.1, bf16[4096,512]{1,0:T(8,128)(2,1)} %bitcast.22), custom_call_target="tpu_custom_call" | custom-call | bytes 8250000 | tf_op jit(solution)/shard_map/pallas_call | solution.py:162
  2.8 0.0 copy-start.2
  2.9 3.0 %collective-permute-start.1 = (bf16[2,128,128]{2,1,0:T(8,128)(2,1)S(1)}, bf16[2,128,128]{2,1,0:T(8,128)(2,1)S(1)}, u32[]{:S(2)}, u32[]{:S(2)}) collective-permute-start(bf16[2,128,128]{2,1,0:T(8,128)(2,1)S(1)} %get-tuple-element.27), channel_id=1, source_target_pairs={{0,2},{1,3},{2,0},{3,1},{4,6},{5,7},{6,4},{7,5},{8,10},{9,11},{10,... | collective-permute-start | bytes 196616 | tf_op jit(solution)/shard_map/ppermute | solution.py:560
  5.9 2.6 %collective-permute-start = (bf16[144,128]{1,0:T(8,128)(2,1)S(1)}, bf16[144,128]{1,0:T(8,128)(2,1)S(1)}, u32[]{:S(2)}, u32[]{:S(2)}) collective-permute-start(bf16[144,128]{1,0:T(8,128)(2,1)S(1)} %get-tuple-element.26), channel_id=1, source_target_pairs={{0,8},{4,12},{8,0},{12,4},{1,9},{5,13},{9,1},{13,5},{2,10},{6,14},... | collective-permute-start | bytes 110600 | tf_op jit(solution)/shard_map/ppermute | solution.py:560
  8.5 4.0 %shard_map.92 = (bf16[2,512,128]{2,1,0:T(8,128)(2,1)S(1)}, bf16[2,512,128]{2,1,0:T(8,128)(2,1)S(1)}) custom-call(bf16[1,1024,512]{2,1,0:T(8,128)(2,1)S(1)} %get-tuple-element.24.near_ref, bf16[4096,512]{1,0:T(8,128)(2,1)} %bitcast.23, bf16[64,512]{1,0:T(8,128)(2,1)} %out_proj_hbm.1), custom_call_target="tpu_custom_call" | custom-call | bytes 13200000 | tf_op jit(solution)/shard_map/pallas_call | solution.py:213
  12.4 0.0 copy-start.1
  12.4 0.0 collective-permute-done
  12.5 0.0 collective-permute-done.1.near_ref.first_ref
  12.5 0.1 collective-permute-start.2
  12.6 0.6 %collective-permute-start.4 = (bf16[128,128]{1,0:T(8,128)(2,1)S(1)}, bf16[128,128]{1,0:T(8,128)(2,1)S(1)}, u32[]{:S(2)}, u32[]{:S(2)}) collective-permute-start(bf16[128,128]{1,0:T(8,128)(2,1)S(1)} %shard_map.95), channel_id=1, source_target_pairs={{0,1},{1,0},{2,3},{3,2},{4,5},{5,4},{6,7},{7,6},{8,9},{9,8},{10,11... | collective-permute-start | bytes 98312 | tf_op jit(solution)/shard_map/ppermute | solution.py:560
  13.1 0.4 shard_map.93.even_ref
  13.6 0.5 collective-permute-done.4.second_ref
  14.1 0.0 copy-done.2
  14.1 0.1 shard_map.96
  14.2 0.0 collective-permute-done.2.near_ref
  14.3 0.6 %collective-permute-start.3 = (bf16[512,128]{1,0:T(8,128)(2,1)S(1)}, bf16[512,128]{1,0:T(8,128)(2,1)S(1)}, u32[]{:S(2)}, u32[]{:S(2)}) collective-permute-start(bf16[512,128]{1,0:T(8,128)(2,1)S(1)} %shard_map.94), channel_id=1, source_target_pairs={{0,2},{1,3},{2,0},{3,1},{4,6},{5,7},{6,4},{7,5},{8,10},{9,11},{10,... | collective-permute-start | bytes 393224 | tf_op jit(solution)/shard_map/ppermute | solution.py:560
  14.9 1.6 %collective-permute-start.5 = (bf16[368,128]{1,0:T(8,128)(2,1)S(1)}, bf16[368,128]{1,0:T(8,128)(2,1)S(1)}, u32[]{:S(2)}, u32[]{:S(2)}) collective-permute-start(bf16[368,128]{1,0:T(8,128)(2,1)S(1)} %pad_maximum_fusion.1), channel_id=1, source_target_pairs={{0,4},{4,0},{8,12},{12,8},{1,5},{5,1},{9,13},{13,9},{2,6},{6,2},{1... | collective-permute-start | bytes 282632 | tf_op jit(solution)/shard_map/ppermute | solution.py:560
  16.6 0.7 %collective-permute-start.7 = (bf16[80,128]{1,0:T(8,128)(2,1)S(1)}, bf16[80,128]{1,0:T(8,128)(2,1)S(1)}, u32[]{:S(2)}, u32[]{:S(2)}) collective-permute-start(bf16[80,128]{1,0:T(8,128)(2,1)S(1)} %shard_map.96), channel_id=1, source_target_pairs={{0,12},{4,8},{8,4},{12,0},{1,13},{5,9},{9,5},{13,1},{2,14},{6,10},... | collective-permute-start | bytes 61448 | tf_op jit(solution)/shard_map/ppermute | solution.py:560
  17.2 1.2 %collective-permute-start.6 = (bf16[80,128]{1,0:T(8,128)(2,1)S(1)}, bf16[80,128]{1,0:T(8,128)(2,1)S(1)}, u32[]{:S(2)}, u32[]{:S(2)}) collective-permute-start(bf16[80,128]{1,0:T(8,128)(2,1)S(1)} %shard_map.96), channel_id=1, source_target_pairs={{0,8},{4,12},{8,0},{12,4},{1,9},{5,13},{9,1},{13,5},{2,10},{6,14},... | collective-permute-start | bytes 61448 | tf_op jit(solution)/shard_map/ppermute | solution.py:560
  18.5 0.0 copy-done
  18.5 0.1 copy.11.routes_ref
  18.6 1.0 %collective-permute-done.5.shared_ref = bf16[368,128]{1,0:T(8,128)(2,1)S(1)} collective-permute-done((bf16[368,128]{1,0:T(8,128)(2,1)S(1)}, bf16[368,128]{1,0:T(8,128)(2,1)S(1)}, u32[]{:S(2)}, u32[]{:S(2)}) %collective-permute-start.5) | collective-permute-done | bytes 94240 | tf_op jit(solution)/shard_map/ppermute | solution.py:560
  19.6 0.4 shard_map.97.odd_ref
  20.0 0.0 collective-permute-done.3.far_ref
  20.0 1.7 %shard_map.98 = bf16[16,128,128]{2,1,0:T(8,128)(2,1)} custom-call(bf16[2,512,128]{2,1,0:T(8,128)(2,1)S(1)} %get-tuple-element.25.own_ref, bf16[2,512,128]{2,1,0:T(8,128)(2,1)S(1)} %collective-permute-done.2.near_ref, bf16[512,128]{1,0:T(8,128)(2,1)S(1)} %collective-permute-done.3.far_ref, s32[128,8]{1,0:T(8,128)S(1)} %copy.11.routes_ref, ...), custom_call_target="tpu_custom_call" | custom-call | bytes 6600000 | tf_op jit(solution)/shard_map/pallas_call | solution.py:363
  21.7 0.4 collective-permute-done.7
  22.1 0.0 collective-permute-done.6
  22.2 5.7 %all-to-all-start = ((bf16[16,128,128]{2,1,0:T(8,128)(2,1)}), bf16[16,128,128]{2,1,0:T(8,128)(2,1)S(1)}, u32[]{:S(2)}, u32[]{:S(2)}) async-start(bf16[16,128,128]{2,1,0:T(8,128)(2,1)} %shard_map.98), calls=%async_computation | async-start | bytes 1048576 | tf_op jit(solution)/shard_map/all_to_all | solution.py:34
  27.9 1.5 %collective-permute-start.9 = (bf16[4,80,128]{2,1,0:T(8,128)(2,1)S(1)}, bf16[4,80,128]{2,1,0:T(8,128)(2,1)S(1)}, u32[]{:S(2)}, u32[]{:S(2)}) collective-permute-start(bf16[4,80,128]{2,1,0:T(8,128)(2,1)S(1)} %get-tuple-element.44), channel_id=1, source_target_pairs={{0,2},{1,3},{2,0},{3,1},{4,6},{5,7},{6,4},{7,5},{8,10},{9,11},{10,... | collective-permute-start | bytes 245768 | tf_op jit(solution)/shard_map/ppermute | solution.py:560
  29.4 0.0 collective-permute-start.8
  29.4 0.7 %collective-permute-start.10 = (bf16[4,80,128]{2,1,0:T(8,128)(2,1)S(1)}, bf16[4,80,128]{2,1,0:T(8,128)(2,1)S(1)}, u32[]{:S(2)}, u32[]{:S(2)}) collective-permute-start(bf16[4,80,128]{2,1,0:T(8,128)(2,1)S(1)} %get-tuple-element.44), channel_id=1, source_target_pairs={{0,3},{1,2},{2,1},{3,0},{4,7},{5,6},{6,5},{7,4},{8,11},{9,10},{10,... | collective-permute-start | bytes 245768 | tf_op jit(solution)/shard_map/ppermute | solution.py:560
  30.1 0.0 copy-done.1
  30.1 9.5 %shard_map.99.far_ref = bf16[8192,256]{1,0:T(8,128)(2,1)} custom-call(bf16[256,8,1024]{2,1,0:T(8,128)(2,1)} %refs_0_, f32[8,64,64]{2,1,0:T(8,128)S(1)} %copy-done.1), custom_call_target="tpu_custom_call" | custom-call | bytes 33000000 | tf_op jit(solution)/shard_map/pallas_call | solution.py:433
  39.6 0.0 collective-permute-done.9
  39.6 0.0 collective-permute-done.8
  39.6 0.0 collective-permute-done.10
  39.7 0.3 all-to-all-done.arrived_ref
  40.0 4.8 %shard_map.100 = f32[16,8,128]{2,1,0:T(8,128)S(1)} custom-call(bf16[16,128,128]{2,1,0:T(8,128)(2,1)S(1)} %all-to-all-done.arrived_ref, bf16[16,80,128]{2,1,0:T(8,128)(2,1)S(1)} %bitcast.16, bf16[8192,256]{1,0:T(8,128)(2,1)} %shard_map.99.far_ref), custom_call_target="tpu_custom_call" | custom-call | bytes 16500000 | tf_op jit(solution)/shard_map/pallas_call | solution.py:529
  44.8 9.5 %all_to_all.10.pieces_ref = f32[16,8,128]{2,1,0:T(8,128)S(1)} all-to-all(f32[16,8,128]{2,1,0:T(8,128)S(1)} %shard_map.100), channel_id=1, replica_groups={{12,13,14,15,0,1,2,3,4,5,6,7,8,9,10,11},{28,29,30,31,16,17,18,19,20,21,..., dimensions={0} | all-to-all | bytes 131072 | tf_op jit(solution)/shard_map/all_to_all | solution.py:34
  54.3 0.6 %shard_map.101 = f32[8,64]{1,0:T(8,128)} custom-call(f32[16,8,128]{2,1,0:T(8,128)S(1)} %all_to_all.10.pieces_ref), custom_call_target="tpu_custom_call" | custom-call | tf_op jit(solution)/shard_map/pallas_call | solution.py:551
  (8 shorter events, 0.1 us)
Async XLA Ops:
  0.0 18.5 %copy-start = (s32[512,8]{0,1:T(8,128)S(1)}, s32[512,8]{0,1:T(8,128)}, u32[]{:S(2)}) copy-start(s32[512,8]{0,1:T(8,128)} %param.11) | copy-start | bytes 49156
  2.8 11.3 %copy-start.2 = (s32[512]{0:T(512)S(1)}, s32[512]{0:T(512)}, u32[]{:S(2)}) copy-start(s32[512]{0:T(512)} %param.12) | copy-start | bytes 6148
  2.9 9.6 %collective-permute-start.1 = (bf16[2,128,128]{2,1,0:T(8,128)(2,1)S(1)}, bf16[2,128,128]{2,1,0:T(8,128)(2,1)S(1)}, u32[]{:S(2)}, u32[]{:S(2)}) collective-permute-start(bf16[2,128,128]{2,1,0:T(8,128)(2,1)S(1)} %get-tuple-element.27), channel_id=1, source_target_pairs={{0,2},{1,3},{2,0},{3,1},{4,6},{5,7},{6,4},{7,5},{8,10},{9,11},{10,... | collective-permute-start | bytes 196616 | tf_op jit(solution)/shard_map/ppermute | solution.py:560
  5.9 6.6 %collective-permute-start = (bf16[144,128]{1,0:T(8,128)(2,1)S(1)}, bf16[144,128]{1,0:T(8,128)(2,1)S(1)}, u32[]{:S(2)}, u32[]{:S(2)}) collective-permute-start(bf16[144,128]{1,0:T(8,128)(2,1)S(1)} %get-tuple-element.26), channel_id=1, source_target_pairs={{0,8},{4,12},{8,0},{12,4},{1,9},{5,13},{9,1},{13,5},{2,10},{6,14},... | collective-permute-start | bytes 110600 | tf_op jit(solution)/shard_map/ppermute | solution.py:560
  12.4 17.6 %copy-start.1 = (f32[8,64,64]{2,1,0:T(8,128)S(1)}, f32[8,64,64]{2,1,0:T(8,128)}, u32[]{:S(2)}) copy-start(f32[8,64,64]{2,1,0:T(8,128)} %refs_1_.1) | copy-start | bytes 393220
  12.5 1.8 %collective-permute-start.2 = (bf16[2,512,128]{2,1,0:T(8,128)(2,1)S(1)}, bf16[2,512,128]{2,1,0:T(8,128)(2,1)S(1)}, u32[]{:S(2)}, u32[]{:S(2)}) collective-permute-start(bf16[2,512,128]{2,1,0:T(8,128)(2,1)S(1)} %get-tuple-element.29), channel_id=1, source_target_pairs={{0,1},{1,0},{2,3},{3,2},{4,5},{5,4},{6,7},{7,6},{8,9},{9,8},{10,11... | collective-permute-start | bytes 786440 | tf_op jit(solution)/shard_map/ppermute | solution.py:560
  12.6 1.5 %collective-permute-start.4 = (bf16[128,128]{1,0:T(8,128)(2,1)S(1)}, bf16[128,128]{1,0:T(8,128)(2,1)S(1)}, u32[]{:S(2)}, u32[]{:S(2)}) collective-permute-start(bf16[128,128]{1,0:T(8,128)(2,1)S(1)} %shard_map.95), channel_id=1, source_target_pairs={{0,1},{1,0},{2,3},{3,2},{4,5},{5,4},{6,7},{7,6},{8,9},{9,8},{10,11... | collective-permute-start | bytes 98312 | tf_op jit(solution)/shard_map/ppermute | solution.py:560
  14.3 5.7 %collective-permute-start.3 = (bf16[512,128]{1,0:T(8,128)(2,1)S(1)}, bf16[512,128]{1,0:T(8,128)(2,1)S(1)}, u32[]{:S(2)}, u32[]{:S(2)}) collective-permute-start(bf16[512,128]{1,0:T(8,128)(2,1)S(1)} %shard_map.94), channel_id=1, source_target_pairs={{0,2},{1,3},{2,0},{3,1},{4,6},{5,7},{6,4},{7,5},{8,10},{9,11},{10,... | collective-permute-start | bytes 393224 | tf_op jit(solution)/shard_map/ppermute | solution.py:560
  14.9 4.6 %collective-permute-start.5 = (bf16[368,128]{1,0:T(8,128)(2,1)S(1)}, bf16[368,128]{1,0:T(8,128)(2,1)S(1)}, u32[]{:S(2)}, u32[]{:S(2)}) collective-permute-start(bf16[368,128]{1,0:T(8,128)(2,1)S(1)} %pad_maximum_fusion.1), channel_id=1, source_target_pairs={{0,4},{4,0},{8,12},{12,8},{1,5},{5,1},{9,13},{13,9},{2,6},{6,2},{1... | collective-permute-start | bytes 282632 | tf_op jit(solution)/shard_map/ppermute | solution.py:560
  16.6 5.6 %collective-permute-start.7 = (bf16[80,128]{1,0:T(8,128)(2,1)S(1)}, bf16[80,128]{1,0:T(8,128)(2,1)S(1)}, u32[]{:S(2)}, u32[]{:S(2)}) collective-permute-start(bf16[80,128]{1,0:T(8,128)(2,1)S(1)} %shard_map.96), channel_id=1, source_target_pairs={{0,12},{4,8},{8,4},{12,0},{1,13},{5,9},{9,5},{13,1},{2,14},{6,10},... | collective-permute-start | bytes 61448 | tf_op jit(solution)/shard_map/ppermute | solution.py:560
  17.2 4.9 %collective-permute-start.6 = (bf16[80,128]{1,0:T(8,128)(2,1)S(1)}, bf16[80,128]{1,0:T(8,128)(2,1)S(1)}, u32[]{:S(2)}, u32[]{:S(2)}) collective-permute-start(bf16[80,128]{1,0:T(8,128)(2,1)S(1)} %shard_map.96), channel_id=1, source_target_pairs={{0,8},{4,12},{8,0},{12,4},{1,9},{5,13},{9,1},{13,5},{2,10},{6,14},... | collective-permute-start | bytes 61448 | tf_op jit(solution)/shard_map/ppermute | solution.py:560
  22.2 17.9 %all-to-all-start = ((bf16[16,128,128]{2,1,0:T(8,128)(2,1)}), bf16[16,128,128]{2,1,0:T(8,128)(2,1)S(1)}, u32[]{:S(2)}, u32[]{:S(2)}) async-start(bf16[16,128,128]{2,1,0:T(8,128)(2,1)} %shard_map.98), calls=%async_computation | async-start | bytes 1048576 | tf_op jit(solution)/shard_map/all_to_all | solution.py:34
  27.9 11.8 %collective-permute-start.9 = (bf16[4,80,128]{2,1,0:T(8,128)(2,1)S(1)}, bf16[4,80,128]{2,1,0:T(8,128)(2,1)S(1)}, u32[]{:S(2)}, u32[]{:S(2)}) collective-permute-start(bf16[4,80,128]{2,1,0:T(8,128)(2,1)S(1)} %get-tuple-element.44), channel_id=1, source_target_pairs={{0,2},{1,3},{2,0},{3,1},{4,6},{5,7},{6,4},{7,5},{8,10},{9,11},{10,... | collective-permute-start | bytes 245768 | tf_op jit(solution)/shard_map/ppermute | solution.py:560
  29.4 10.3 %collective-permute-start.8 = (bf16[4,80,128]{2,1,0:T(8,128)(2,1)S(1)}, bf16[4,80,128]{2,1,0:T(8,128)(2,1)S(1)}, u32[]{:S(2)}, u32[]{:S(2)}) collective-permute-start(bf16[4,80,128]{2,1,0:T(8,128)(2,1)S(1)} %get-tuple-element.44), channel_id=1, source_target_pairs={{0,1},{1,0},{2,3},{3,2},{4,5},{5,4},{6,7},{7,6},{8,9},{9,8},{10,11... | collective-permute-start | bytes 245768 | tf_op jit(solution)/shard_map/ppermute | solution.py:560
  29.4 10.3 %collective-permute-start.10 = (bf16[4,80,128]{2,1,0:T(8,128)(2,1)S(1)}, bf16[4,80,128]{2,1,0:T(8,128)(2,1)S(1)}, u32[]{:S(2)}, u32[]{:S(2)}) collective-permute-start(bf16[4,80,128]{2,1,0:T(8,128)(2,1)S(1)} %get-tuple-element.44), channel_id=1, source_target_pairs={{0,3},{1,2},{2,1},{3,0},{4,7},{5,6},{6,5},{7,4},{8,11},{9,10},{10,... | collective-permute-start | bytes 245768 | tf_op jit(solution)/shard_map/ppermute | solution.py:560
